TPU v7x, 32 devices: a whole 2x2x4 slice. The times are simulated.
32 devices in a mesh: head: 4 (over z), blk: 8 (over y, x, core).
Axes of the slice: x: 2, y: 2, z: 4, core: 2. Of those that a mesh axis runs over, the one named last changes fastest.
Arguments:
- tokens: bfloat16 [2, 2048, 1536], P(None, ('head', 'blk')), may hold values from -6 to 6
- lengths: int32 [2], replicated, may hold values from 256 to 2048, as said below
- routes: int32 [2, 2, 2048, 8], P(None, None, ('head', 'blk')), may hold values from 0 to 39, as said below
- queue_ranks: int32 [2, 2, 2048, 8], P(None, None, ('head', 'blk')), may hold values from 0 to 26, as said below
- query_key_value_weight: bfloat16 [2, 1536, 2560], P(None, ('head', 'blk')), may hold values from -0.15625 to 0.15625
- w_out: bfloat16 [2, 1536, 1536], P(None, ('head', 'blk')), may hold values from -2.5 to 2.5
- router: bfloat16 [2, 1536, 40], P(None, ('head', 'blk')), may hold values from -0.078125 to 0.078125
- norm_gains: bfloat16 [2, 2, 1536], P(None, None, ('head', 'blk')), may hold values from 0.5 to 1.5
- w_in: bfloat16 [2, 40, 1536, 1024], P(None, 'head', 'blk'), may hold values from -0.15625 to 0.15625
- w_down: bfloat16 [2, 40, 512, 1536], P(None, 'head', 'blk'), may hold values from -0.75 to 0.75
- cotangent: bfloat16 [2, 2048, 1536], P(None, ('head', 'blk')), may hold values from -6 to 6
Outputs:
- out: bfloat16 [2, 2048, 1536], P(None, ('head', 'blk'))
- grad_tokens: float32 [2, 2048, 1536], P(None, ('head', 'blk'))
- grad_w_qkv: float32 [2, 1536, 2560], P(None, ('head', 'blk'))
- grad_w_out: float32 [2, 1536, 1536], P(None, ('head', 'blk'))
- grad_router: float32 [2, 1536, 40], P(None, ('head', 'blk'))
- grad_attn_gains: float32 [2, 1536], P(None, ('head', 'blk'))
- grad_expert_gains: float32 [2, 1536], P(None, ('head', 'blk'))
- grad_w_in: float32 [2, 40, 1536, 1024], P(None, 'head', 'blk')
- grad_w_down: float32 [2, 40, 512, 1536], P(None, 'head', 'blk')
Inputs may be any that keep to these rules, and one draw needn't show every extreme that they name: One slot, chosen by the seed, is full; in each slot positions from lengths[s] on are padding. `routes`: each token names 8 different experts in each layer. `queue_ranks`: positions are cut into aligned blocks of 64; a block's pairs are those of its positions in both slots. In each layer and block, the pairs of valid tokens naming one expert hold distinct ranks 0, 1, 2 and so on, with every rank from 26 on written as 26; every pair of a padding token has rank 26.
All inputs are finite; a program needn't handle non-finite values.
Results may differ from a plain program's by a relative error of at most 0.028.
Values may be sent and summed in bfloat16 or wider, within the bound.
A program may use at most 384 MiB of HBM per device.

v0:
```python
import jax
import jax.numpy as jnp
from jax import lax
from jax.sharding import PartitionSpec as P

MODEL_WIDTH = 1536
QUERY_HEAD_COUNT = 24
KEY_VALUE_HEADS = 8
HEAD_SIZE = 64
FF = 512
EXPERTS = 40
TOP = 8
DECODER_LAYERS = 2
SEQUENCE_SLOTS = 2
CAP = 26


highest = lax.Precision.HIGHEST
epsilon = 1e-06
negative = -1e30
theta_log = 9.210340371976184


def rotate(values, positions, direction):
    half_width = values.shape[-1] // 2
    frequency = jnp.exp(
        jnp.arange(half_width, dtype=jnp.float32) * (-2.0 * theta_log / values.shape[-1])
    )
    angles = positions[:, None, None] * frequency
    cosine = jnp.cos(angles)
    sine_part = jnp.sin(angles) * direction
    first_half = values[..., :half_width]
    second_half = values[..., half_width:]
    return jnp.concatenate(
        [
            first_half * cosine - second_half * sine_part,
            second_half * cosine + first_half * sine_part,
        ],
        axis=-1,
    )


def norm_rows(hidden):
    inverse = lax.rsqrt(jnp.mean(hidden * hidden, axis=-1, keepdims=True) + epsilon)
    return (hidden * inverse, inverse)


def norm_back(grad_normed, scaled, inverse, gain_row):
    grad_gain = jnp.sum(grad_normed * scaled, axis=(0, 1))
    grad_scaled = grad_normed * gain_row
    grad_hidden = inverse * (
        grad_scaled - scaled * jnp.mean(grad_scaled * scaled, axis=-1, keepdims=True)
    )
    return (grad_hidden, grad_gain)


def gather_keys(kv_heads):
    return lax.all_gather(kv_heads, "blk", axis=1, tiled=True)


def gather_experts(layer_in, layer_down):
    return (
        lax.all_gather(layer_in, "blk", axis=1, tiled=True),
        lax.all_gather(layer_down, "blk", axis=1, tiled=True),
    )


def shards(
    tokens,
    lengths,
    routes,
    queue_ranks,
    query_key_value_weight,
    w_out,
    router,
    norm_gains,
    w_in,
    w_down,
    cotangent,
):
    head_total_count = lax.axis_size("head")
    blocks_count = lax.axis_size("blk")
    head_index = lax.axis_index("head")
    blk_index = lax.axis_index("blk")
    sequence_resident = tokens.shape[1]
    rows_local = head_total_count * sequence_resident
    keys_total = blocks_count * rows_local
    key_value_resident = KEY_VALUE_HEADS // head_total_count
    query_group_width = QUERY_HEAD_COUNT // KEY_VALUE_HEADS
    block_size = min(512, keys_total)
    block_count = keys_total // block_size
    slot_rows = SEQUENCE_SLOTS * sequence_resident
    own_places = (head_index * blocks_count + blk_index) * sequence_resident + jnp.arange(
        sequence_resident, dtype=jnp.int32
    )
    own_float = own_places.astype(jnp.float32)
    valid_rows = (own_places[None, :] < lengths[:, None]).astype(jnp.float32)
    local_ids = jnp.arange(rows_local, dtype=jnp.int32)
    query_places = (
        local_ids // sequence_resident * blocks_count + blk_index
    ) * sequence_resident + local_ids % sequence_resident

    def key_places(row_ids):
        within = row_ids % rows_local
        return (
            within // sequence_resident * blocks_count + row_ids // rows_local
        ) * sequence_resident + within % sequence_resident

    def block_scores(query_matrix, keys_all, offset):
        key_piece = lax.dynamic_slice_in_dim(keys_all, offset, block_size, 1)
        scores = (
            jnp.einsum(
                "sqgrd,skgd->sqgrk",
                query_matrix,
                key_piece[:, :, :, 0, :],
                preferred_element_type=jnp.float32,
            )
            * 0.125
        )
        places = key_places(offset + jnp.arange(block_size, dtype=jnp.int32))
        allowed = (places[None, None, :] <= query_places[None, :, None]) & (
            places[None, None, :] < lengths[:, None, None]
        )
        return (jnp.where(allowed[:, :, None, None, :], scores, negative), key_piece)

    def attend_back(query_matrix, keys_all, grad_attended, attended, log_total):
        row_delta = jnp.sum(grad_attended.astype(jnp.float32) * attended, axis=-1)

        def revisit(running, block_index):
            grad_queries, grad_keys_all = running
            offset = block_index * block_size
            scores, key_piece = block_scores(query_matrix, keys_all, offset)
            probabilities = jnp.exp(scores - log_total[..., None])
            grad_values = jnp.einsum(
                "sqgrk,sqgrd->skgd",
                probabilities.astype(jnp.bfloat16),
                grad_attended,
                preferred_element_type=jnp.float32,
            )
            grad_probs = jnp.einsum(
                "sqgrd,skgd->sqgrk",
                grad_attended,
                key_piece[:, :, :, 1, :],
                preferred_element_type=jnp.float32,
            )
            grad_scores = (probabilities * (grad_probs - row_delta[..., None])).astype(jnp.bfloat16)
            grad_queries = grad_queries + 0.125 * jnp.einsum(
                "sqgrk,skgd->sqgrd",
                grad_scores,
                key_piece[:, :, :, 0, :],
                preferred_element_type=jnp.float32,
            )
            grad_keys = 0.125 * jnp.einsum(
                "sqgrk,sqgrd->skgd", grad_scores, query_matrix, preferred_element_type=jnp.float32
            )
            grad_keys_all = lax.dynamic_update_slice_in_dim(
                grad_keys_all, jnp.stack([grad_keys, grad_values], axis=3), offset, 1
            )
            return ((grad_queries, grad_keys_all), None)

        start_state = (
            jnp.zeros(query_matrix.shape, jnp.float32),
            jnp.zeros(keys_all.shape, jnp.float32),
        )
        (grad_queries, grad_keys_all), unused = lax.scan(
            revisit, start_state, jnp.arange(block_count, dtype=jnp.int32)
        )
        return (grad_queries, grad_keys_all)

    hidden = tokens.astype(jnp.float32)
    stored_all = []
    for layer_index in range(DECODER_LAYERS):
        forward_qkv_full = lax.all_gather(
            query_key_value_weight[layer_index], ("head", "blk"), axis=0, tiled=True
        )
        forward_out_full = lax.all_gather(w_out[layer_index], ("head", "blk"), axis=0, tiled=True)
        forward_router_full = lax.all_gather(
            router[layer_index], ("head", "blk"), axis=0, tiled=True
        )
        forward_gains_full = lax.all_gather(
            norm_gains[layer_index], ("head", "blk"), axis=1, tiled=True
        )
        forward_scaled_a, forward_inverse_a = norm_rows(hidden)
        forward_normed_a = (forward_scaled_a * forward_gains_full[0]).astype(jnp.bfloat16)
        projected_rows = jnp.einsum(
            "std,de->ste", forward_normed_a, forward_qkv_full, preferred_element_type=jnp.float32
        )
        forward_query_matrix = rotate(
            projected_rows[..., : QUERY_HEAD_COUNT * HEAD_SIZE].reshape(
                SEQUENCE_SLOTS, sequence_resident, QUERY_HEAD_COUNT, HEAD_SIZE
            ),
            own_float,
            1.0,
        )
        pair_columns = projected_rows[..., QUERY_HEAD_COUNT * HEAD_SIZE :].reshape(
            SEQUENCE_SLOTS, sequence_resident, KEY_VALUE_HEADS, 2, HEAD_SIZE
        )
        keys_rot = rotate(pair_columns[:, :, :, 0, :], own_float, 1.0)
        pair_send = (
            jnp.stack([keys_rot, pair_columns[:, :, :, 1, :]], axis=3)
            .astype(jnp.bfloat16)
            .reshape(SEQUENCE_SLOTS, sequence_resident, KEY_VALUE_HEADS * 2 * HEAD_SIZE)
        )
        query_send = forward_query_matrix.astype(jnp.bfloat16).reshape(
            SEQUENCE_SLOTS, sequence_resident, QUERY_HEAD_COUNT * HEAD_SIZE
        )
        forward_query_heads = lax.all_to_all(
            query_send, "head", split_axis=2, concat_axis=1, tiled=True
        )
        forward_kv_heads = lax.all_to_all(
            pair_send, "head", split_axis=2, concat_axis=1, tiled=True
        )
        forward_query_heads = forward_query_heads.reshape(
            SEQUENCE_SLOTS, rows_local, key_value_resident, query_group_width, HEAD_SIZE
        )
        forward_keys_all = gather_keys(forward_kv_heads).reshape(
            SEQUENCE_SLOTS, keys_total, key_value_resident, 2, HEAD_SIZE
        )
        attend_query_matrix = forward_query_heads
        attend_keys_all = forward_keys_all

        def visit(running, block_index):
            row_peak, row_total, weighted = running
            scores, key_piece = block_scores(
                attend_query_matrix, attend_keys_all, block_index * block_size
            )
            new_peak = jnp.maximum(row_peak, jnp.max(scores, axis=-1))
            exponents = jnp.exp(scores - new_peak[..., None])
            factor = jnp.exp(row_peak - new_peak)
            row_total = row_total * factor + jnp.sum(exponents, axis=-1)
            weighted = weighted * factor[..., None] + jnp.einsum(
                "sqgrk,skgd->sqgrd",
                exponents.astype(jnp.bfloat16),
                key_piece[:, :, :, 1, :],
                preferred_element_type=jnp.float32,
            )
            return ((new_peak, row_total, weighted), None)

        stat_shape = attend_query_matrix.shape[:-1]
        attend_start_state = (
            jnp.full(stat_shape, negative, jnp.float32),
            jnp.zeros(stat_shape, jnp.float32),
            jnp.zeros(attend_query_matrix.shape, jnp.float32),
        )
        (row_peak, row_total, weighted), attend_unused = lax.scan(
            visit, attend_start_state, jnp.arange(block_count, dtype=jnp.int32)
        )
        forward_attended = weighted / row_total[..., None]
        forward_log_total = row_peak + jnp.log(row_total)
        heads_out = forward_attended.astype(jnp.bfloat16).reshape(
            SEQUENCE_SLOTS, rows_local, key_value_resident * query_group_width * HEAD_SIZE
        )
        forward_attended_tokens = lax.all_to_all(
            heads_out, "head", split_axis=1, concat_axis=2, tiled=True
        )
        branch = jnp.einsum(
            "stf,fd->std",
            forward_attended_tokens,
            forward_out_full,
            preferred_element_type=jnp.float32,
        )
        middle = hidden + valid_rows[..., None] * branch
        forward_scaled_b, forward_inverse_b = norm_rows(middle)
        forward_normed_b = (forward_scaled_b * forward_gains_full[1]).astype(jnp.bfloat16)
        logits = jnp.einsum(
            "std,de->ste", forward_normed_b, forward_router_full, preferred_element_type=jnp.float32
        )
        forward_route_hots = (
            routes[layer_index][..., None] == jnp.arange(EXPERTS, dtype=jnp.int32)
        ).astype(jnp.float32)
        forward_gate_weights = jax.nn.softmax(
            jnp.einsum("stke,ste->stk", forward_route_hots, logits, precision=highest), axis=-1
        )
        layer_ranks = queue_ranks[layer_index]
        forward_targets = jnp.where(
            layer_ranks < CAP, routes[layer_index] * CAP + layer_ranks, EXPERTS * CAP
        )
        token_ids = jnp.broadcast_to(
            jnp.arange(slot_rows, dtype=jnp.int32).reshape(SEQUENCE_SLOTS, sequence_resident, 1),
            forward_targets.shape,
        )
        source = (
            jnp.full((EXPERTS * CAP + 1,), slot_rows, jnp.int32)
            .at[forward_targets.reshape(-1)]
            .set(token_ids.reshape(-1))[: EXPERTS * CAP]
        )
        flat_rows = jnp.concatenate(
            [
                forward_normed_b.reshape(slot_rows, MODEL_WIDTH),
                jnp.zeros((1, MODEL_WIDTH), jnp.bfloat16),
            ],
            axis=0,
        )
        forward_incoming = lax.all_to_all(
            flat_rows[source].reshape(EXPERTS, CAP, MODEL_WIDTH),
            "head",
            split_axis=0,
            concat_axis=1,
            tiled=True,
        )
        forward_experts_in, forward_experts_down = gather_experts(
            w_in[layer_index], w_down[layer_index]
        )
        forward_gate_up = jnp.einsum(
            "erd,edf->erf", forward_incoming, forward_experts_in, preferred_element_type=jnp.float32
        )
        forward_hidden_units = (
            jax.nn.silu(forward_gate_up[..., :FF]) * forward_gate_up[..., FF:]
        ).astype(jnp.bfloat16)
        produced = jnp.einsum(
            "erf,efd->erd",
            forward_hidden_units,
            forward_experts_down,
            preferred_element_type=jnp.float32,
        ).astype(jnp.bfloat16)
        returned = lax.all_to_all(produced, "head", split_axis=1, concat_axis=0, tiled=True)
        flat_out = jnp.concatenate(
            [
                returned.reshape(EXPERTS * CAP, MODEL_WIDTH),
                jnp.zeros((1, MODEL_WIDTH), jnp.bfloat16),
            ],
            axis=0,
        )
        forward_per_pair = flat_out[forward_targets]
        mixture = jnp.einsum(
            "stk,stkd->std",
            forward_gate_weights,
            forward_per_pair.astype(jnp.float32),
            precision=highest,
        )
        output = middle + valid_rows[..., None] * mixture
        forward_stored = (
            forward_qkv_full,
            forward_out_full,
            forward_router_full,
            forward_gains_full,
            forward_scaled_a,
            forward_inverse_a,
            forward_normed_a,
            forward_query_heads,
            forward_kv_heads,
            forward_keys_all,
            forward_attended,
            forward_log_total,
            forward_attended_tokens,
            forward_scaled_b,
            forward_inverse_b,
            forward_normed_b,
            forward_route_hots,
            forward_gate_weights,
            forward_targets,
            forward_incoming,
            forward_experts_in,
            forward_experts_down,
            forward_gate_up,
            forward_hidden_units,
            forward_per_pair,
        )
        hidden = output
        stored_all.append(forward_stored)
    result = (valid_rows[..., None] * hidden).astype(jnp.bfloat16)
    grad_hidden = valid_rows[..., None] * cotangent.astype(jnp.float32)
    small_list = [None] * DECODER_LAYERS
    expert_list = [None] * DECODER_LAYERS
    for layer_index in reversed(range(DECODER_LAYERS)):
        backward_stored = stored_all[layer_index]
        (
            qkv_full,
            out_full,
            router_full,
            gains_full,
            scaled_a,
            inverse_a,
            normed_a,
            query_heads,
            kv_heads,
            backward_keys_all,
            backward_attended,
            backward_log_total,
            attended_tokens,
            scaled_b,
            inverse_b,
            normed_b,
            route_hots,
            gate_weights,
            targets,
            incoming,
            experts_in,
            experts_down,
            gate_up,
            hidden_units,
            per_pair,
        ) = backward_stored
        grad_mixture = valid_rows[..., None] * grad_hidden
        grad_gates = jnp.einsum(
            "stkd,std->stk", per_pair.astype(jnp.float32), grad_mixture, precision=highest
        )
        grad_pairs = (gate_weights[..., None] * grad_mixture[:, :, None, :]).astype(jnp.bfloat16)
        pair_ids = jnp.arange(slot_rows * TOP, dtype=jnp.int32).reshape(targets.shape)
        slot_owner = (
            jnp.full((EXPERTS * CAP + 1,), slot_rows * TOP, jnp.int32)
            .at[targets.reshape(-1)]
            .set(pair_ids.reshape(-1))[: EXPERTS * CAP]
        )
        flat_pairs = jnp.concatenate(
            [
                grad_pairs.reshape(slot_rows * TOP, MODEL_WIDTH),
                jnp.zeros((1, MODEL_WIDTH), jnp.bfloat16),
            ],
            axis=0,
        )
        grad_produced = lax.all_to_all(
            flat_pairs[slot_owner].reshape(EXPERTS, CAP, MODEL_WIDTH),
            "head",
            split_axis=0,
            concat_axis=1,
            tiled=True,
        )
        in_again, down_again = gather_experts(w_in[layer_index], w_down[layer_index])
        grad_units = jnp.einsum(
            "erd,efd->erf", grad_produced, down_again, preferred_element_type=jnp.float32
        )
        grad_down = jnp.einsum(
            "erf,erd->efd", hidden_units, grad_produced, preferred_element_type=jnp.float32
        )
        gate_part = gate_up[..., :FF]
        up_part = gate_up[..., FF:]
        sigmoid_part = jax.nn.sigmoid(gate_part)
        grad_gate_up = jnp.concatenate(
            [
                grad_units * up_part * sigmoid_part * (1.0 + gate_part * (1.0 - sigmoid_part)),
                grad_units * gate_part * sigmoid_part,
            ],
            axis=-1,
        ).astype(jnp.bfloat16)
        grad_in = jnp.einsum(
            "erd,erf->edf", incoming, grad_gate_up, preferred_element_type=jnp.float32
        )
        grad_incoming = jnp.einsum(
            "erf,edf->erd", grad_gate_up, in_again, preferred_element_type=jnp.float32
        ).astype(jnp.bfloat16)
        grad_rows = lax.all_to_all(grad_incoming, "head", split_axis=1, concat_axis=0, tiled=True)
        flat_grads = jnp.concatenate(
            [
                grad_rows.reshape(EXPERTS * CAP, MODEL_WIDTH),
                jnp.zeros((1, MODEL_WIDTH), jnp.bfloat16),
            ],
            axis=0,
        )
        grad_normed_b = jnp.sum(flat_grads[targets].astype(jnp.float32), axis=2)
        grad_chosen = gate_weights * (
            grad_gates - jnp.sum(gate_weights * grad_gates, axis=-1, keepdims=True)
        )
        grad_logits = jnp.einsum("stke,stk->ste", route_hots, grad_chosen, precision=highest)
        backward_grad_router = jnp.einsum(
            "std,ste->de", normed_b.astype(jnp.float32), grad_logits, precision=highest
        )
        grad_normed_b = grad_normed_b + jnp.einsum(
            "ste,de->std", grad_logits, router_full.astype(jnp.float32), precision=highest
        )
        grad_norm_b, grad_gain_b = norm_back(grad_normed_b, scaled_b, inverse_b, gains_full[1])
        grad_middle = grad_hidden + grad_norm_b
        grad_branch = (valid_rows[..., None] * grad_middle).astype(jnp.bfloat16)
        grad_out_w = jnp.einsum(
            "stf,std->fd", attended_tokens, grad_branch, preferred_element_type=jnp.float32
        )
        grad_tokens_att = jnp.einsum(
            "std,fd->stf", grad_branch, out_full, preferred_element_type=jnp.float32
        ).astype(jnp.bfloat16)
        grad_heads = lax.all_to_all(
            grad_tokens_att, "head", split_axis=2, concat_axis=1, tiled=True
        ).reshape(SEQUENCE_SLOTS, rows_local, key_value_resident, query_group_width, HEAD_SIZE)
        keys_again = gather_keys(kv_heads).reshape(
            SEQUENCE_SLOTS, keys_total, key_value_resident, 2, HEAD_SIZE
        )
        backward_grad_queries, backward_grad_keys_all = attend_back(
            query_heads, keys_again, grad_heads, backward_attended, backward_log_total
        )
        grad_pairs_own = lax.psum_scatter(
            backward_grad_keys_all.astype(jnp.bfloat16), "blk", scatter_dimension=1, tiled=True
        )
        grad_query_send = backward_grad_queries.astype(jnp.bfloat16).reshape(
            SEQUENCE_SLOTS, rows_local, key_value_resident * query_group_width * HEAD_SIZE
        )
        grad_pair_send = grad_pairs_own.reshape(
            SEQUENCE_SLOTS, rows_local, key_value_resident * 2 * HEAD_SIZE
        )
        grad_query_tok = lax.all_to_all(
            grad_query_send, "head", split_axis=1, concat_axis=2, tiled=True
        )
        gradient_pair_token = lax.all_to_all(
            grad_pair_send, "head", split_axis=1, concat_axis=2, tiled=True
        )
        grad_query_rot = rotate(
            grad_query_tok.astype(jnp.float32).reshape(
                SEQUENCE_SLOTS, sequence_resident, QUERY_HEAD_COUNT, HEAD_SIZE
            ),
            own_float,
            -1.0,
        )
        gradient_pair_complete = gradient_pair_token.astype(jnp.float32).reshape(
            SEQUENCE_SLOTS, sequence_resident, KEY_VALUE_HEADS, 2, HEAD_SIZE
        )
        grad_key_rot = rotate(gradient_pair_complete[:, :, :, 0, :], own_float, -1.0)
        grad_pair_cols = jnp.stack(
            [grad_key_rot, gradient_pair_complete[:, :, :, 1, :]], axis=3
        ).reshape(SEQUENCE_SLOTS, sequence_resident, KEY_VALUE_HEADS * 2 * HEAD_SIZE)
        grad_projected = jnp.concatenate(
            [
                grad_query_rot.reshape(
                    SEQUENCE_SLOTS, sequence_resident, QUERY_HEAD_COUNT * HEAD_SIZE
                ),
                grad_pair_cols,
            ],
            axis=-1,
        ).astype(jnp.bfloat16)
        grad_qkv = jnp.einsum(
            "std,ste->de", normed_a, grad_projected, preferred_element_type=jnp.float32
        )
        grad_normed_a = jnp.einsum(
            "ste,de->std", grad_projected, qkv_full, preferred_element_type=jnp.float32
        )
        grad_norm_a, grad_gain_a = norm_back(grad_normed_a, scaled_a, inverse_a, gains_full[0])
        grad_hidden_in = grad_middle + grad_norm_a
        small_grads = (
            lax.psum_scatter(grad_qkv, ("head", "blk"), scatter_dimension=0, tiled=True),
            lax.psum_scatter(grad_out_w, ("head", "blk"), scatter_dimension=0, tiled=True),
            lax.psum_scatter(
                backward_grad_router, ("head", "blk"), scatter_dimension=0, tiled=True
            ),
            lax.psum_scatter(
                jnp.stack([grad_gain_a, grad_gain_b]),
                ("head", "blk"),
                scatter_dimension=1,
                tiled=True,
            ),
        )
        expert_grads = (
            lax.psum_scatter(
                grad_in.astype(jnp.bfloat16), "blk", scatter_dimension=1, tiled=True
            ).astype(jnp.float32),
            lax.psum_scatter(
                grad_down.astype(jnp.bfloat16), "blk", scatter_dimension=1, tiled=True
            ).astype(jnp.float32),
        )
        grad_hidden, small_grads, expert_grads = (grad_hidden_in, small_grads, expert_grads)
        small_list[layer_index] = small_grads
        expert_list[layer_index] = expert_grads
    grad_w_qkv = jnp.stack([small_list[layer_index][0] for layer_index in range(DECODER_LAYERS)])
    grad_w_out = jnp.stack([small_list[layer_index][1] for layer_index in range(DECODER_LAYERS)])
    grad_router = jnp.stack([small_list[layer_index][2] for layer_index in range(DECODER_LAYERS)])
    grad_gains = jnp.stack([small_list[layer_index][3] for layer_index in range(DECODER_LAYERS)])
    grad_w_in = jnp.stack([expert_list[layer_index][0] for layer_index in range(DECODER_LAYERS)])
    grad_w_down = jnp.stack([expert_list[layer_index][1] for layer_index in range(DECODER_LAYERS)])
    return (
        result,
        grad_hidden,
        grad_w_qkv,
        grad_w_out,
        grad_router,
        grad_gains[:, 0, :],
        grad_gains[:, 1, :],
        grad_w_in,
        grad_w_down,
    )


def solution(mesh):
    in_specs = (
        P(None, ("head", "blk"), None),
        P(),
        P(None, None, ("head", "blk"), None),
        P(None, None, ("head", "blk"), None),
        P(None, ("head", "blk"), None),
        P(None, ("head", "blk"), None),
        P(None, ("head", "blk"), None),
        P(None, None, ("head", "blk")),
        P(None, "head", "blk", None),
        P(None, "head", "blk", None),
        P(None, ("head", "blk"), None),
    )
    out_specs = (
        P(None, ("head", "blk"), None),
        P(None, ("head", "blk"), None),
        P(None, ("head", "blk"), None),
        P(None, ("head", "blk"), None),
        P(None, ("head", "blk"), None),
        P(None, ("head", "blk")),
        P(None, ("head", "blk")),
        P(None, "head", "blk", None),
        P(None, "head", "blk", None),
    )
    return jax.shard_map(shards, mesh=mesh, in_specs=in_specs, out_specs=out_specs, check_vma=False)
```

profile of v0, /device:TPU:0, one launch (start us, length us, event | category | flops | bytes accessed | tf_op | source)
XLA Modules:
  0.0 3848.7 jit_solution(8926712495782325605)
XLA Ops:
  10.0 46.0 %all-gather = bf16[1,2,1536]{1,0,2:T(2,128)(2,1)S(1)} all-gather(bf16[1,2,48]{1,0,2:T(2,128)(2,1)S(1)} %copy.403), channel_id=2, replica_groups=mesh['head'=4,'blk'=8] {'head','blk'}, dimensions={2}, use_global_device_ids=true | all-gather | bytes 6336 | tf_op jit(solution)/shard_map/all_gather | solution.py:180
  58.0 25.6 fusion.225
  151.1 64.8 %while.68 = (s32[]{:T(128)}, f32[2,256,2,3]{1,3,2,0:T(4,128)S(1)}, f32[2,256,2,3]{1,3,2,0:T(4,128)S(1)}, f32[2,256,2,3,64]{1,4,3,2,0:T(8,128)}, s32[4]{0:T(128)S...) while((s32[]{:T(128)}, f32[2,256,2,3]{1,3,2,0:T(4,128)S(1)}, ...), condition=%wide.region_4.5_spmd.clone, body=%wide.region_1.4_spmd.clone.sunk | while | flops 420980224 | bytes 29174064 | solution.py:245
  248.1 89.4 %all_to_all.301 = bf16[40,26,1536]{2,1,0:T(8,128)(2,1)S(1)} all-to-all(bf16[40,26,1536]{2,1,0:T(8,128)(2,1)} %reshape.1101), channel_id=1, replica_groups=mesh['head'=4,'blk'=8] {'head'}, dimensions={0} | all-to-all | bytes 6389760 | tf_op jit(solution)/shard_map/all_to_all | solution.py:294
  379.2 67.7 %all-gather.33.cloned.1.call-done = bf16[1,10,512,1536]{3,2,1,0:T(8,128)(2,1)} async-done(((bf16[1,10,64,1536]{3,2,1,0:T(8,128)(2,1)}), bf16[1,10,512,1536]{3,2,1,0:T(8,128)(2,1)}) %all-gather.33.cloned.1.call-update) | async-done | bytes 15728656 | tf_op jit(solution)/shard_map/all_gather | solution.py:64
  464.8 140.4 %all-gather.3 = bf16[1,1536,40]{2,0,1:T(2,128)(2,1)S(1)} all-gather(bf16[1,48,40]{2,0,1:T(2,128)(2,1)S(1)} %copy.404), channel_id=5, replica_groups=mesh['head'=4,'blk'=8] {'head','blk'}, dimensions={1}, use_global_device_ids=true | all-gather | bytes 126720 | tf_op jit(solution)/shard_map/all_gather | solution.py:177
  607.0 70.9 %all-gather.6 = bf16[1,2,1536]{1,0,2:T(2,128)(2,1)S(1)} all-gather(bf16[1,2,48]{1,0,2:T(2,128)(2,1)S(1)} %copy.405), channel_id=8, replica_groups=mesh['head'=4,'blk'=8] {'head','blk'}, dimensions={2}, use_global_device_ids=true | all-gather | bytes 6336 | tf_op jit(solution)/shard_map/all_gather | solution.py:180
  677.8 26.1 fusion.223
  785.3 67.9 %while.69 = (s32[]{:T(128)}, f32[2,256,2,3]{1,3,2,0:T(4,128)}, f32[2,256,2,3]{1,3,2,0:T(4,128)}, f32[2,256,2,3,64]{1,4,3,2,0:T(8,128)}, s32[4]{0:T(128)S(1)}, /*...) while((s32[]{:T(128)}, f32[2,256,2,3]{1,3,2,0:T(4,128)}, ...), condition=%wide.region_13.14_spmd.clone, body=%wide.region_10.13_spmd.clone.sunk | while | flops 420980224 | bytes 29321604 | solution.py:245
  855.1 16.5 all_to_all.306
  887.5 91.3 %all_to_all.303 = bf16[40,26,1536]{2,1,0:T(8,128)(2,1)S(1)} all-to-all(bf16[40,26,1536]{2,1,0:T(8,128)(2,1)} %reshape.1109), channel_id=1, replica_groups=mesh['head'=4,'blk'=8] {'head'}, dimensions={0} | all-to-all | bytes 6389760 | tf_op jit(solution)/shard_map/all_to_all | solution.py:294
  1019.7 67.7 %all-gather.41.cloned.1.call-done = bf16[1,10,512,1536]{3,2,1,0:T(8,128)(2,1)} async-done(((bf16[1,10,64,1536]{3,2,1,0:T(8,128)(2,1)}), bf16[1,10,512,1536]{3,2,1,0:T(8,128)(2,1)}) %all-gather.41.cloned.1.call-update) | async-done | bytes 15728656 | tf_op jit(solution)/shard_map/all_gather | solution.py:64
  1104.7 138.0 %all-gather.9 = bf16[1,1536,40]{2,0,1:T(2,128)(2,1)S(1)} all-gather(bf16[1,48,40]{2,0,1:T(2,128)(2,1)S(1)} %copy.406), channel_id=11, replica_groups=mesh['head'=4,'blk'=8] {'head','blk'}, dimensions={1}, use_global_device_ids=true | all-gather | bytes 126720 | tf_op jit(solution)/shard_map/all_gather | solution.py:177
  1294.7 94.4 %all_to_all.304 = bf16[40,26,1536]{2,1,0:T(8,128)(2,1)S(1)} all-to-all(bf16[40,26,1536]{2,1,0:T(8,128)(2,1)} %reshape.1111), channel_id=1, replica_groups=mesh['head'=4,'blk'=8] {'head'}, dimensions={0} | all-to-all | bytes 6389760 | tf_op jit(solution)/shard_map/all_to_all | solution.py:412
  1438.6 108.4 %all-to-all-done.11 = bf16[10,104,1536]{2,0,1:T(8,128)(2,1)} async-done(((bf16[10,104,1536]{2,0,1:T(8,128)(2,1)}), bf16[10,104,1536]{2,0,1:T(8,128)(2,1)}, u32[]{:S(2)}, u32[]{:S(2)}) %all-to-all-start.11) | async-done | bytes 3194912 | tf_op jit(solution)/shard_map/all_to_all | solution.py:442
  1600.1 85.4 %while.70 = (s32[]{:T(128)}, f32[2,256,2,3,64]{1,4,3,2,0:T(8,128)}, bf16[2,2048,2,2,64]{1,4,3,2,0:T(8,128)(2,1)}, s32[4]{0:T(128)S(1)}, bf16[2,2048,2,2,64]{1,4,...) while((s32[]{:T(128)}, f32[2,256,2,3,64]{1,4,3,2,0:T(8,128)}, ...), condition=%wide.region_24.25_spmd.clone, body=%wide.region_23.24_spmd.clone.sunk | while | flops 1023896064 | bytes 36018504 | solution.py:165
  1702.4 21.8 reduce-scatter.23.cloned.1.call-done
  1762.6 90.1 %all_to_all.305 = bf16[40,26,1536]{2,1,0:T(8,128)(2,1)S(1)} all-to-all(bf16[40,26,1536]{2,1,0:T(8,128)(2,1)} %reshape.1118), channel_id=1, replica_groups=mesh['head'=4,'blk'=8] {'head'}, dimensions={0} | all-to-all | bytes 6389760 | tf_op jit(solution)/shard_map/all_to_all | solution.py:412
  1906.3 103.5 %all-to-all-done.16 = bf16[10,104,1536]{2,0,1:T(8,128)(2,1)} async-done(((bf16[10,104,1536]{2,0,1:T(8,128)(2,1)}), bf16[10,104,1536]{2,0,1:T(8,128)(2,1)}, u32[]{:S(2)}, u32[]{:S(2)}) %all-to-all-start.16) | async-done | bytes 3194912 | tf_op jit(solution)/shard_map/all_to_all | solution.py:442
  2062.3 84.7 %while.71 = (s32[]{:T(128)}, f32[2,256,2,3,64]{1,4,3,2,0:T(8,128)}, bf16[2,2048,2,2,64]{1,4,3,2,0:T(8,128)(2,1)}, s32[4]{0:T(128)S(1)}, bf16[2,2048,2,2,64]{1,4,...) while((s32[]{:T(128)}, f32[2,256,2,3,64]{1,4,3,2,0:T(8,128)}, ...), condition=%wide.region_33.34_spmd.clone, body=%wide.region_32.33_spmd.clone.sunk | while | flops 1023896064 | bytes 36018504 | solution.py:165
  2164.1 22.4 reduce-scatter.25.cloned.1.call-done
  2299.4 88.0 %reduce-scatter.49.cloned.1.call-done = f32[48,2]{1,0:T(8,128)} async-done(((f32[1536,2]{1,0:T(8,128)}), f32[48,2]{1,0:T(8,128)}) %reduce-scatter.49.cloned.1.call-update) | async-done | bytes 400
  2388.2 98.8 %reduce-scatter.43.cloned.1.call-done = f32[48,40]{1,0:T(8,128)} async-done(((f32[1536,40]{1,0:T(8,128)}), f32[48,40]{1,0:T(8,128)}) %reduce-scatter.43.cloned.1.call-update) | async-done | bytes 7696
  2489.6 96.9 %reduce-scatter.47.cloned.1.call-done = f32[48,2]{1,0:T(8,128)} async-done(((f32[1536,2]{1,0:T(8,128)}), f32[48,2]{1,0:T(8,128)}) %reduce-scatter.47.cloned.1.call-update) | async-done | bytes 400
  2588.0 139.1 %reduce-scatter.33.cloned.1.call-done = f32[48,1536]{1,0:T(8,128)} async-done(((f32[1536,1536]{1,0:T(8,128)}), f32[48,1536]{1,0:T(8,128)}) %reduce-scatter.33.cloned.1.call-update) | async-done | bytes 294928 | tf_op jit(solution)/shard_map/reduce_scatter | solution.py:527
  2727.1 141.5 %reduce-scatter.31.cloned.1.call-done = f32[48,1536]{1,0:T(8,128)} async-done(((f32[1536,1536]{1,0:T(8,128)}), f32[48,1536]{1,0:T(8,128)}) %reduce-scatter.31.cloned.1.call-update) | async-done | bytes 294928 | tf_op jit(solution)/shard_map/reduce_scatter | solution.py:527
  2870.4 109.8 %reduce-scatter.41.cloned.1.call-done = bf16[10,64,1536]{2,1,0:T(8,128)(2,1)} async-done(((bf16[10,512,1536]{2,1,0:T(8,128)(2,1)}), bf16[10,64,1536]{2,1,0:T(8,128)(2,1)}) %reduce-scatter.41.cloned.1.call-update) | async-done | bytes 1966096 | tf_op jit(solution)/shard_map/reduce_scatter | solution.py:542
  2980.2 112.6 %reduce-scatter.39.cloned.1.call-done = bf16[10,64,1536]{2,1,0:T(8,128)(2,1)} async-done(((bf16[10,512,1536]{2,1,0:T(8,128)(2,1)}), bf16[10,64,1536]{2,1,0:T(8,128)(2,1)}) %reduce-scatter.39.cloned.1.call-update) | async-done | bytes 1966096 | tf_op jit(solution)/shard_map/reduce_scatter | solution.py:542
  3098.6 171.2 %reduce-scatter.29.cloned.1.call-done = f32[48,2560]{1,0:T(8,128)} async-done(((f32[1536,2560]{1,0:T(8,128)}), f32[48,2560]{1,0:T(8,128)}) %reduce-scatter.29.cloned.1.call-update) | async-done | bytes 491536 | tf_op jit(solution)/shard_map/reduce_scatter | solution.py:526
  3269.8 175.7 %reduce-scatter.27.cloned.1.call-done = f32[48,2560]{1,0:T(8,128)} async-done(((f32[1536,2560]{1,0:T(8,128)}), f32[48,2560]{1,0:T(8,128)}) %reduce-scatter.27.cloned.1.call-update) | async-done | bytes 491536 | tf_op jit(solution)/shard_map/reduce_scatter | solution.py:526
  3447.8 190.4 %reduce-scatter.37.cloned.1.call-done = bf16[10,192,1024]{2,1,0:T(8,128)(2,1)} async-done(((bf16[10,1536,1024]{2,1,0:T(8,128)(2,1)}), bf16[10,192,1024]{2,1,0:T(8,128)(2,1)}) %reduce-scatter.37.cloned.1.call-update) | async-done | bytes 3932176 | tf_op jit(solution)/shard_map/reduce_scatter | solution.py:539
  3638.2 193.3 %reduce-scatter.35.cloned.1.call-done = bf16[10,192,1024]{2,1,0:T(8,128)(2,1)} async-done(((bf16[10,1536,1024]{2,1,0:T(8,128)(2,1)}), bf16[10,192,1024]{2,1,0:T(8,128)(2,1)}) %reduce-scatter.35.cloned.1.call-update) | async-done | bytes 3932176 | tf_op jit(solution)/shard_map/reduce_scatter | solution.py:539
  (900 shorter events, 1082.1 us)
Async XLA Ops:
  7.2 84.4 %all-gather.27.cloned.1.call-start = ((), (), s32[]{:S(2)}) async-start(), calls=%async_computation.46 | async-start | bytes 8110080 | tf_op jit(solution)/shard_map/all_gather | solution.py:173
  9.2 137.4 %all-gather.23.cloned.1.call-start = ((), (), s32[]{:S(2)}) async-start(), calls=%async_computation.34 | async-start | bytes 2359296 | tf_op jit(solution)/shard_map/all_gather | solution.py:58
  113.2 119.3 %all-gather.29.cloned.1.call-start = ((), (), s32[]{:S(2)}) async-start(), calls=%async_computation.47 | async-start | bytes 4866048 | tf_op jit(solution)/shard_map/all_gather | solution.py:176
  115.0 244.7 %all-gather.31.cloned.1.call-start = ((), (), s32[]{:S(2)}) async-start(), calls=%async_computation.48 | async-start | bytes 35389440 | tf_op jit(solution)/shard_map/all_gather | solution.py:63
  120.8 326.1 %all-gather.33.cloned.1.call-start = ((), (), s32[]{:S(2)}) async-start(), calls=%async_computation.49 | async-start | bytes 17694720 | tf_op jit(solution)/shard_map/all_gather | solution.py:64
  125.3 606.8 %all-gather.35.cloned.1.call-start = ((), (), s32[]{:S(2)}) async-start(), calls=%async_computation.50 | async-start | bytes 8110080 | tf_op jit(solution)/shard_map/all_gather | solution.py:173
  130.7 14.2 all-to-all-start.1
  458.9 247.1 %all-to-all-start.4 = ((bf16[10,104,1536]{2,0,1:T(8,128)(2,1)}), bf16[10,104,1536]{2,0,1:T(8,128)(2,1)}, u32[]{:S(2)}, u32[]{:S(2)}) async-start(bf16[10,104,1536]{2,0,1:T(8,128)(2,1)} %copy.273), calls=%async_computation.4 | async-start | bytes 10223616 | tf_op jit(solution)/shard_map/all_to_all | solution.py:316
  464.1 316.8 %all-gather.25.cloned.1.call-start = ((), (), s32[]{:S(2)}) async-start(), calls=%async_computation.35 | async-start | bytes 2359296 | tf_op jit(solution)/shard_map/all_gather | solution.py:58
  755.6 116.1 %all-gather.37.cloned.1.call-start = ((), (), s32[]{:S(2)}) async-start(), calls=%async_computation.51 | async-start | bytes 4866048 | tf_op jit(solution)/shard_map/all_gather | solution.py:176
  756.4 243.8 %all-gather.39.cloned.1.call-start = ((), (), s32[]{:S(2)}) async-start(), calls=%async_computation.52 | async-start | bytes 35389440 | tf_op jit(solution)/shard_map/all_gather | solution.py:63
  757.1 330.3 %all-gather.41.cloned.1.call-start = ((), (), s32[]{:S(2)}) async-start(), calls=%async_computation.53 | async-start | bytes 17694720 | tf_op jit(solution)/shard_map/all_gather | solution.py:64
  763.4 14.6 all-to-all-start.6
  1099.4 155.4 %all-to-all-start.9 = ((bf16[10,104,1536]{2,0,1:T(8,128)(2,1)}), bf16[10,104,1536]{2,0,1:T(8,128)(2,1)}, u32[]{:S(2)}, u32[]{:S(2)}) async-start(bf16[10,104,1536]{2,0,1:T(8,128)(2,1)} %copy.297), calls=%async_computation.9 | async-start | bytes 10223616 | tf_op jit(solution)/shard_map/all_to_all | solution.py:316
  1428.8 118.2 %all-to-all-start.11 = ((bf16[10,104,1536]{2,0,1:T(8,128)(2,1)}), bf16[10,104,1536]{2,0,1:T(8,128)(2,1)}, u32[]{:S(2)}, u32[]{:S(2)}) async-start(bf16[10,104,1536]{2,0,1:T(8,128)(2,1)} %copy.302), calls=%async_computation.11 | async-start | bytes 10223616 | tf_op jit(solution)/shard_map/all_to_all | solution.py:442
  1579.8 14.6 all-to-all-start.12
  1583.3 140.9 %reduce-scatter.23.cloned.1.call-start = ((), (), s32[]{:S(2)}) async-start(), calls=%async_computation.36 | async-start | bytes 2359296 | tf_op jit(solution)/shard_map/reduce_scatter | solution.py:479
  1892.4 117.4 %all-to-all-start.16 = ((bf16[10,104,1536]{2,0,1:T(8,128)(2,1)}), bf16[10,104,1536]{2,0,1:T(8,128)(2,1)}, u32[]{:S(2)}, u32[]{:S(2)}) async-start(bf16[10,104,1536]{2,0,1:T(8,128)(2,1)} %copy.319), calls=%async_computation.17 | async-start | bytes 10223616 | tf_op jit(solution)/shard_map/all_to_all | solution.py:442
  2042.0 14.6 all-to-all-start.17
  2045.5 141.0 %reduce-scatter.25.cloned.1.call-start = ((), (), s32[]{:S(2)}) async-start(), calls=%async_computation.37 | async-start | bytes 2359296 | tf_op jit(solution)/shard_map/reduce_scatter | solution.py:479
  2153.1 145.3 %reduce-scatter.45.cloned.1.call-start = ((), (), s32[]{:S(2)}) async-start(), calls=%async_computation.55 | async-start | bytes 811008
  2154.6 232.8 %reduce-scatter.49.cloned.1.call-start = ((), (), s32[]{:S(2)}) async-start(), calls=%async_computation.57 | async-start | bytes 811008
  2155.9 331.1 %reduce-scatter.43.cloned.1.call-start = ((), (), s32[]{:S(2)}) async-start(), calls=%async_computation.54 | async-start | bytes 811008
  2192.9 393.6 %reduce-scatter.47.cloned.1.call-start = ((), (), s32[]{:S(2)}) async-start(), calls=%async_computation.56 | async-start | bytes 811008
  2213.2 513.8 %reduce-scatter.33.cloned.1.call-start = ((), (), s32[]{:S(2)}) async-start(), calls=%async_computation.41 | async-start | bytes 9732096 | tf_op jit(solution)/shard_map/reduce_scatter | solution.py:527
  2218.3 650.2 %reduce-scatter.31.cloned.1.call-start = ((), (), s32[]{:S(2)}) async-start(), calls=%async_computation.40 | async-start | bytes 9732096 | tf_op jit(solution)/shard_map/reduce_scatter | solution.py:527
  2224.6 755.6 %reduce-scatter.41.cloned.1.call-start = ((), (), s32[]{:S(2)}) async-start(), calls=%async_computation.45 | async-start | bytes 17694720 | tf_op jit(solution)/shard_map/reduce_scatter | solution.py:542
  2235.6 857.1 %reduce-scatter.39.cloned.1.call-start = ((), (), s32[]{:S(2)}) async-start(), calls=%async_computation.44 | async-start | bytes 17694720 | tf_op jit(solution)/shard_map/reduce_scatter | solution.py:542
  2246.5 1023.3 %reduce-scatter.29.cloned.1.call-start = ((), (), s32[]{:S(2)}) async-start(), calls=%async_computation.39 | async-start | bytes 16220160 | tf_op jit(solution)/shard_map/reduce_scatter | solution.py:526
  2255.9 1189.6 %reduce-scatter.27.cloned.1.call-start = ((), (), s32[]{:S(2)}) async-start(), calls=%async_computation.38 | async-start | bytes 16220160 | tf_op jit(solution)/shard_map/reduce_scatter | solution.py:526
  2263.8 1374.3 %reduce-scatter.37.cloned.1.call-start = ((), (), s32[]{:S(2)}) async-start(), calls=%async_computation.43 | async-start | bytes 35389440 | tf_op jit(solution)/shard_map/reduce_scatter | solution.py:539
  2281.3 1550.2 %reduce-scatter.35.cloned.1.call-start = ((), (), s32[]{:S(2)}) async-start(), calls=%async_computation.42 | async-start | bytes 35389440 | tf_op jit(solution)/shard_map/reduce_scatter | solution.py:539
  (165 other events, 4152.1 us)
Sparse Core Ops, SparseCore 0:
  11.5 80.0 all-gather.26
  113.3 26.0 all-gather.22
  142.9 63.6 all-gather.28
  208.9 150.7 all-gather.30
  361.4 85.4 all-gather.32
  449.7 163.9 all-gather.34
  755.7 25.1 all-gather.24
  783.8 63.6 all-gather.36
  849.4 150.7 all-gather.38
  1001.9 85.4 all-gather.40
  1685.7 38.4 reduce-scatter.22
  2147.2 39.2 reduce-scatter.24
  2192.2 95.5 reduce-scatter.44
  2292.7 94.6 reduce-scatter.48
  2392.3 94.5 reduce-scatter.42
  2491.9 94.5 reduce-scatter.46
  2592.3 134.6 reduce-scatter.32
  2733.8 134.6 reduce-scatter.30
  2872.0 108.1 reduce-scatter.40
  2983.5 109.1 reduce-scatter.38
  3099.3 170.4 reduce-scatter.28
  3275.8 169.6 reduce-scatter.26
  3449.2 188.9 reduce-scatter.36
  3641.7 189.7 reduce-scatter.34
where the time goes:
time: 3860 us; the launch traced here: 3850 us
  waiting for transfers between devices  2020 us (52%)
  blocking collectives  801 us (21%)
  matrix products  471 us (12%)
  local copies, waits for them, and re-layouts  293 us (8%)
  other arithmetic  173 us (4%)
  starting transfers between devices  57.3 us (1%)
    reduce_scatter x2, waiting for transfers between devices, shards(): lax.psum_scatter(grad_in.astype(jnp.bfloat16), 'blk', scatter_dimension=1...  384 us
    reduce_scatter x2, waiting for transfers between devices, shards(): lax.psum_scatter(grad_qkv, ('head', 'blk'), scatter_dimension=0, tiled=True)  347 us
    unnamed x28, waiting for transfers between devices  287 us
    reduce_scatter x2, waiting for transfers between devices, shards(): lax.psum_scatter(grad_out_w, ('head', 'blk'), scatter_dimension=0, tiled=...  281 us
    all_gather x2, blocking collectives, shards(): lax.all_gather(router[layer_index], ('head', 'blk'), axis=0, tiled=True)  278 us
    reduce_scatter x2, waiting for transfers between devices, shards(): lax.psum_scatter(grad_down.astype(jnp.bfloat16), 'blk', scatter_dimension...  222 us
    all_to_all x2, waiting for transfers between devices, shards(): lax.all_to_all(grad_incoming, 'head', split_axis=1, concat_axis=0, tiled=...  212 us
    all_to_all x2, blocking collectives, shards(): lax.all_to_all(flat_pairs[slot_owner].reshape(EXPERTS, CAP, MODEL_WIDTH),...  185 us
  transfers between devices with their start and end apart: 37, of which 30 were waited for; matrix products, arithmetic and copies ran while one was open for 13% of the time, Pallas kernels for 0%

commit v1 on v0

v1 whole, which is shorter than its diff:
```python
import jax
import jax.numpy as jnp
from jax import lax
from jax.sharding import PartitionSpec as P

MODEL_WIDTH = 1536
QUERY_HEAD_COUNT = 24
KEY_VALUE_HEADS = 8
HEAD_SIZE = 64
FF = 512
EXPERTS = 40
TOP = 8
DECODER_LAYERS = 2
SEQUENCE_SLOTS = 2
CAP = 26


epsilon = 1e-06
negative = -1e30
theta_log = 9.210340371976184


def rotate(values, positions, direction):
    half_width = values.shape[-1] // 2
    frequency = jnp.exp(
        jnp.arange(half_width, dtype=jnp.float32) * (-2.0 * theta_log / values.shape[-1])
    )
    angles = positions[:, None, None] * frequency
    cosine = jnp.cos(angles)
    sine_part = jnp.sin(angles) * direction
    first_half = values[..., :half_width]
    second_half = values[..., half_width:]
    return jnp.concatenate(
        [
            first_half * cosine - second_half * sine_part,
            second_half * cosine + first_half * sine_part,
        ],
        axis=-1,
    )


def norm_rows(hidden):
    inverse = lax.rsqrt(jnp.mean(hidden * hidden, axis=-1, keepdims=True) + epsilon)
    return (hidden * inverse, inverse)


def norm_back(grad_normed, scaled, inverse, gain_row):
    grad_gain = jnp.sum(grad_normed * scaled, axis=0)
    grad_scaled = grad_normed * gain_row
    grad_hidden = inverse * (
        grad_scaled - scaled * jnp.mean(grad_scaled * scaled, axis=-1, keepdims=True)
    )
    return (grad_hidden, grad_gain)


def gather_keys(kv_heads):
    return lax.all_gather(kv_heads, "blk", axis=1, tiled=True)


def ring(count, offset):
    return [(i, (i + offset) % count) for i in range(count)]


def rows_to_owner(matrices, blocks_count, owned, blk_index):
    rows, columns = matrices.shape[1:]
    whole = jnp.zeros((owned, blocks_count * rows, columns), matrices.dtype)
    for offset in range(blocks_count):
        target = (blk_index + offset) % blocks_count
        origin = (blk_index - offset) % blocks_count
        piece = lax.dynamic_slice_in_dim(matrices, target * owned, owned, 0)
        if offset:
            piece = lax.ppermute(piece, "blk", ring(blocks_count, offset))
        whole = lax.dynamic_update_slice_in_dim(whole, piece, origin * rows, 1)
    return whole


def rows_from_owner(whole, blocks_count, owned, blk_index):
    rows = whole.shape[1] // blocks_count
    matrices = jnp.zeros((owned * blocks_count, rows, whole.shape[2]), whole.dtype)
    for offset in range(blocks_count):
        target = (blk_index + offset) % blocks_count
        origin = (blk_index - offset) % blocks_count
        piece = lax.dynamic_slice_in_dim(whole, target * rows, rows, 1)
        if offset:
            piece = lax.ppermute(piece, "blk", ring(blocks_count, offset))
        matrices = lax.dynamic_update_slice_in_dim(matrices, piece, origin * owned, 0)
    return matrices


def head_gather(rows):
    heads = lax.axis_size("head")
    copies = jnp.broadcast_to(rows[None], (heads,) + rows.shape)
    return lax.all_to_all(copies, "head", 0, 0, tiled=True).reshape(-1, rows.shape[-1])


def head_scatter(partial):
    heads = lax.axis_size("head")
    parts = partial.astype(jnp.bfloat16).reshape(heads, -1, partial.shape[-1])
    parts = lax.all_to_all(parts, "head", 0, 0, tiled=True)
    return jnp.sum(parts.astype(jnp.float32), axis=0)


def mm(spec, left, right):
    return jnp.einsum(spec, left, right, preferred_element_type=jnp.float32)


def shards(
    tokens,
    lengths,
    routes,
    queue_ranks,
    query_key_value_weight,
    w_out,
    router,
    norm_gains,
    w_in,
    w_down,
    cotangent,
):
    heads_count = lax.axis_size("head")
    blocks_count = lax.axis_size("blk")
    head_index = lax.axis_index("head")
    blk_index = lax.axis_index("blk")
    resident = tokens.shape[1]
    width = tokens.shape[2]
    rows_local = heads_count * resident
    keys_total = blocks_count * rows_local
    kv_local = KEY_VALUE_HEADS // heads_count
    group = QUERY_HEAD_COUNT // KEY_VALUE_HEADS
    block_size = min(512, keys_total)
    block_count = keys_total // block_size
    slot_rows = SEQUENCE_SLOTS * resident
    experts_local = EXPERTS // heads_count
    owned = experts_local // blocks_count
    owned_total = owned * blocks_count
    slot = heads_count * CAP
    own_places = (head_index * blocks_count + blk_index) * resident + jnp.arange(
        resident, dtype=jnp.int32
    )
    own_float = own_places.astype(jnp.float32)
    valid_rows = (own_places[None, :] < lengths[:, None]).astype(jnp.float32)
    valid_column = valid_rows.reshape(slot_rows, 1)
    local_ids = jnp.arange(rows_local, dtype=jnp.int32)
    query_places = (local_ids // resident * blocks_count + blk_index) * resident + local_ids % resident

    def key_places(row_ids):
        within = row_ids % rows_local
        return (
            within // resident * blocks_count + row_ids // rows_local
        ) * resident + within % resident

    def block_scores(query_matrix, keys_all, offset):
        key_piece = lax.dynamic_slice_in_dim(keys_all, offset, block_size, 1)
        scores = mm("sqgrd,skgd->sqgrk", query_matrix, key_piece[:, :, :, 0, :]) * 0.125
        places = key_places(offset + jnp.arange(block_size, dtype=jnp.int32))
        allowed = (places[None, None, :] <= query_places[None, :, None]) & (
            places[None, None, :] < lengths[:, None, None]
        )
        return (jnp.where(allowed[:, :, None, None, :], scores, negative), key_piece)

    def attend(query_matrix, keys_all):
        def visit(running, block_index):
            row_peak, row_total, weighted = running
            scores, key_piece = block_scores(query_matrix, keys_all, block_index * block_size)
            new_peak = jnp.maximum(row_peak, jnp.max(scores, axis=-1))
            exponents = jnp.exp(scores - new_peak[..., None])
            factor = jnp.exp(row_peak - new_peak)
            row_total = row_total * factor + jnp.sum(exponents, axis=-1)
            weighted = weighted * factor[..., None] + mm(
                "sqgrk,skgd->sqgrd", exponents.astype(jnp.bfloat16), key_piece[:, :, :, 1, :]
            )
            return ((new_peak, row_total, weighted), None)

        stat_shape = query_matrix.shape[:-1]
        start_state = (
            jnp.full(stat_shape, negative, jnp.float32),
            jnp.zeros(stat_shape, jnp.float32),
            jnp.zeros(query_matrix.shape, jnp.float32),
        )
        (row_peak, row_total, weighted), unused = lax.scan(
            visit, start_state, jnp.arange(block_count, dtype=jnp.int32)
        )
        return (weighted / row_total[..., None], row_peak + jnp.log(row_total))

    def attend_back(query_matrix, keys_all, grad_attended, attended, log_total):
        row_delta = jnp.sum(grad_attended.astype(jnp.float32) * attended, axis=-1)

        def revisit(running, block_index):
            grad_queries, grad_keys_all = running
            offset = block_index * block_size
            scores, key_piece = block_scores(query_matrix, keys_all, offset)
            probabilities = jnp.exp(scores - log_total[..., None])
            grad_values = mm("sqgrk,sqgrd->skgd", probabilities.astype(jnp.bfloat16), grad_attended)
            grad_probs = mm("sqgrd,skgd->sqgrk", grad_attended, key_piece[:, :, :, 1, :])
            grad_scores = (probabilities * (grad_probs - row_delta[..., None])).astype(jnp.bfloat16)
            grad_queries = grad_queries + 0.125 * mm(
                "sqgrk,skgd->sqgrd", grad_scores, key_piece[:, :, :, 0, :]
            )
            grad_keys = 0.125 * mm("sqgrk,sqgrd->skgd", grad_scores, query_matrix)
            grad_keys_all = lax.dynamic_update_slice_in_dim(
                grad_keys_all, jnp.stack([grad_keys, grad_values], axis=3), offset, 1
            )
            return ((grad_queries, grad_keys_all), None)

        start_state = (
            jnp.zeros(query_matrix.shape, jnp.float32),
            jnp.zeros(keys_all.shape, jnp.float32),
        )
        (grad_queries, grad_keys_all), unused = lax.scan(
            revisit, start_state, jnp.arange(block_count, dtype=jnp.int32)
        )
        return (grad_queries, grad_keys_all)

    plan = lax.all_gather(
        jnp.stack([routes, queue_ranks]).reshape(2, DECODER_LAYERS, slot_rows, TOP), "head", axis=0
    )
    expert_ids = jnp.arange(EXPERTS, dtype=jnp.int32)
    row_ids = jnp.arange(experts_local * slot, dtype=jnp.int32)
    spread = (
        row_ids[None, :] // slot == jnp.arange(experts_local, dtype=jnp.int32)[:, None]
    ).astype(jnp.bfloat16)
    all_tokens = heads_count * slot_rows
    token_head = jnp.arange(all_tokens, dtype=jnp.int32)[:, None] // slot_rows
    row_head = row_ids[None, :] % slot // CAP
    row_rank = (row_ids % CAP).astype(jnp.float32)[None, :]

    def layer_plan(layer_index):
        plan_routes = plan[:, 0, layer_index].reshape(all_tokens, TOP)
        plan_ranks = plan[:, 1, layer_index].reshape(all_tokens, TOP)
        named = plan_routes[:, :, None] == expert_ids
        chosen = jnp.any(named, axis=1)
        marks = jnp.sum(
            jnp.where(named & (plan_ranks < CAP)[:, :, None], plan_ranks[:, :, None] + 1, 0), axis=1
        )
        marks = lax.dynamic_slice_in_dim(marks, head_index * experts_local, experts_local, 1)
        wide = mm("te,er->tr", marks.astype(jnp.bfloat16), spread) - 1.0
        places = ((wide == row_rank) & (token_head == row_head)).astype(jnp.bfloat16)
        return (chosen, places)

    def to_experts(rows):
        rows = rows.reshape(experts_local, slot, width)
        own = lax.all_to_all(rows[:owned_total], "blk", 0, 1, tiled=True) if owned else None
        return (own, rows[owned_total:])

    def from_experts(own, shared):
        parts = [shared]
        if owned:
            parts = [lax.all_to_all(own, "blk", 1, 0, tiled=True), shared]
        return jnp.concatenate(parts, axis=0).reshape(experts_local * slot, width)

    def expert_weights(layer_index):
        sets = []
        if owned:
            sets.append(
                tuple(
                    rows_to_owner(matrix[layer_index, :owned_total], blocks_count, owned, blk_index)
                    for matrix in (w_in, w_down)
                )
            )
        if owned_total < experts_local:
            sets.append(
                tuple(
                    lax.all_gather(matrix[layer_index, owned_total:], "blk", axis=1, tiled=True)
                    for matrix in (w_in, w_down)
                )
            )
        return sets

    def experts_forward(incoming, weights):
        gate_up = mm("erd,edf->erf", incoming, weights[0])
        units = (jax.nn.silu(gate_up[..., :FF]) * gate_up[..., FF:]).astype(jnp.bfloat16)
        produced = mm("erf,efd->erd", units, weights[1]).astype(jnp.bfloat16)
        return (produced, (incoming, gate_up, units))

    def experts_backward(grad_produced, weights, kept):
        incoming, gate_up, units = kept
        grad_units = mm("erd,efd->erf", grad_produced, weights[1])
        grad_down = mm("erf,erd->efd", units, grad_produced).astype(jnp.bfloat16)
        gate_part = gate_up[..., :FF]
        up_part = gate_up[..., FF:]
        sigmoid_part = jax.nn.sigmoid(gate_part)
        grad_gate_up = jnp.concatenate(
            [
                grad_units * up_part * sigmoid_part * (1.0 + gate_part * (1.0 - sigmoid_part)),
                grad_units * gate_part * sigmoid_part,
            ],
            axis=-1,
        ).astype(jnp.bfloat16)
        grad_in = mm("erd,erf->edf", incoming, grad_gate_up).astype(jnp.bfloat16)
        grad_incoming = mm("erf,edf->erd", grad_gate_up, weights[0]).astype(jnp.bfloat16)
        return (grad_incoming, (grad_in, grad_down))

    hidden = tokens.reshape(slot_rows, width).astype(jnp.float32)
    stored_all = []
    for layer_index in range(DECODER_LAYERS):
        qkv_full = lax.all_gather(
            query_key_value_weight[layer_index], ("head", "blk"), axis=0, tiled=True
        )
        out_full = lax.all_gather(w_out[layer_index], ("head", "blk"), axis=0, tiled=True)
        router_full = lax.all_gather(router[layer_index], ("head", "blk"), axis=0, tiled=True)
        gains_full = lax.all_gather(norm_gains[layer_index], ("head", "blk"), axis=1, tiled=True)
        weight_sets = expert_weights(layer_index)
        chosen, places = layer_plan(layer_index)
        scaled_a, inverse_a = norm_rows(hidden)
        normed_a = (scaled_a * gains_full[0]).astype(jnp.bfloat16)
        projected = mm("td,de->te", normed_a, qkv_full).reshape(SEQUENCE_SLOTS, resident, -1)
        queries = rotate(
            projected[..., : QUERY_HEAD_COUNT * HEAD_SIZE].reshape(
                SEQUENCE_SLOTS, resident, QUERY_HEAD_COUNT, HEAD_SIZE
            ),
            own_float,
            1.0,
        )
        pair_columns = projected[..., QUERY_HEAD_COUNT * HEAD_SIZE :].reshape(
            SEQUENCE_SLOTS, resident, KEY_VALUE_HEADS, 2, HEAD_SIZE
        )
        keys_rot = rotate(pair_columns[:, :, :, 0, :], own_float, 1.0)
        pair_send = (
            jnp.stack([keys_rot, pair_columns[:, :, :, 1, :]], axis=3)
            .astype(jnp.bfloat16)
            .reshape(SEQUENCE_SLOTS, resident, KEY_VALUE_HEADS * 2 * HEAD_SIZE)
        )
        query_send = queries.astype(jnp.bfloat16).reshape(
            SEQUENCE_SLOTS, resident, QUERY_HEAD_COUNT * HEAD_SIZE
        )
        query_heads = lax.all_to_all(query_send, "head", split_axis=2, concat_axis=1, tiled=True)
        kv_heads = lax.all_to_all(pair_send, "head", split_axis=2, concat_axis=1, tiled=True)
        query_heads = query_heads.reshape(SEQUENCE_SLOTS, rows_local, kv_local, group, HEAD_SIZE)
        keys_all = gather_keys(kv_heads).reshape(SEQUENCE_SLOTS, keys_total, kv_local, 2, HEAD_SIZE)
        attended, log_total = attend(query_heads, keys_all)
        heads_out = attended.astype(jnp.bfloat16).reshape(
            SEQUENCE_SLOTS, rows_local, kv_local * group * HEAD_SIZE
        )
        attended_tokens = lax.all_to_all(
            heads_out, "head", split_axis=1, concat_axis=2, tiled=True
        ).reshape(slot_rows, -1)
        middle = hidden + valid_column * mm("tf,fd->td", attended_tokens, out_full)
        scaled_b, inverse_b = norm_rows(middle)
        normed_b = (scaled_b * gains_full[1]).astype(jnp.bfloat16)
        plane_rows = head_gather(normed_b)
        logits = mm("td,de->te", plane_rows, router_full)
        peaks = jnp.max(jnp.where(chosen, logits, negative), axis=-1, keepdims=True)
        lifted = jnp.where(chosen, jnp.exp(logits - peaks), 0.0)
        gates_all = lifted / jnp.sum(lifted, axis=-1, keepdims=True)
        gates = lax.dynamic_slice_in_dim(gates_all, head_index * slot_rows, slot_rows, 0)
        plane_gates = lax.dynamic_slice_in_dim(
            gates_all, head_index * experts_local, experts_local, 1
        )
        weighted_places = (
            mm("te,er->tr", plane_gates.astype(jnp.bfloat16), spread).astype(jnp.bfloat16) * places
        )
        queues = mm("tr,td->rd", places, plane_rows).astype(jnp.bfloat16)
        own_in, shared_in = to_experts(queues)
        kept_sets = []
        produced = []
        for incoming, weights in zip([own_in, shared_in] if owned else [shared_in], weight_sets):
            made, kept = experts_forward(incoming, weights)
            produced.append(made)
            kept_sets.append(kept)
        returned = from_experts(*(produced if owned else [None] + produced))
        mixture = head_scatter(mm("tr,rd->td", weighted_places, returned))
        stored_all.append(
            (
                qkv_full,
                out_full,
                router_full,
                gains_full,
                weight_sets,
                places,
                scaled_a,
                inverse_a,
                normed_a,
                query_heads,
                keys_all,
                attended,
                log_total,
                attended_tokens,
                scaled_b,
                inverse_b,
                normed_b,
                gates,
                weighted_places,
                kept_sets,
                returned,
            )
        )
        hidden = middle + valid_column * mixture
    result = (valid_column * hidden).astype(jnp.bfloat16).reshape(tokens.shape)
    grad_hidden = valid_column * cotangent.reshape(slot_rows, width).astype(jnp.float32)
    small_list = [None] * DECODER_LAYERS
    expert_list = [None] * DECODER_LAYERS
    for layer_index in reversed(range(DECODER_LAYERS)):
        (
            qkv_full,
            out_full,
            router_full,
            gains_full,
            weight_sets,
            places,
            scaled_a,
            inverse_a,
            normed_a,
            query_heads,
            keys_all,
            attended,
            log_total,
            attended_tokens,
            scaled_b,
            inverse_b,
            normed_b,
            gates,
            weighted_places,
            kept_sets,
            returned,
        ) = stored_all[layer_index]
        plane_grads = head_gather((valid_column * grad_hidden).astype(jnp.bfloat16))
        queue_grads = mm("tr,td->rd", weighted_places, plane_grads).astype(jnp.bfloat16)
        own_grad, shared_grad = to_experts(queue_grads)
        grad_in_sets = []
        grad_weight_sets = []
        for grad_produced, weights, kept in zip(
            [own_grad, shared_grad] if owned else [shared_grad], weight_sets, kept_sets
        ):
            grad_incoming, grad_weights = experts_backward(grad_produced, weights, kept)
            grad_in_sets.append(grad_incoming)
            grad_weight_sets.append(grad_weights)
        grad_rows = from_experts(*(grad_in_sets if owned else [None] + grad_in_sets))
        grad_normed_b = head_scatter(mm("tr,rd->td", places, grad_rows))
        pair_dots = mm("td,rd->tr", plane_grads, returned) * places
        plane_grad_gates = mm("tr,er->te", pair_dots, spread.astype(jnp.float32)).reshape(
            heads_count, slot_rows, experts_local
        )
        grad_gates = (
            lax.all_to_all(plane_grad_gates, "head", 0, 0, tiled=True)
            .transpose(1, 0, 2)
            .reshape(slot_rows, EXPERTS)
        )
        grad_logits = gates * (grad_gates - jnp.sum(gates * grad_gates, axis=-1, keepdims=True))
        grad_router = mm("td,te->de", normed_b.astype(jnp.float32), grad_logits)
        grad_normed_b = grad_normed_b + mm(
            "te,de->td", grad_logits, router_full.astype(jnp.float32)
        )
        grad_norm_b, grad_gain_b = norm_back(grad_normed_b, scaled_b, inverse_b, gains_full[1])
        grad_middle = grad_hidden + grad_norm_b
        grad_branch = (valid_column * grad_middle).astype(jnp.bfloat16)
        grad_out_w = mm("tf,td->fd", attended_tokens, grad_branch).astype(jnp.bfloat16)
        grad_tokens_att = (
            mm("td,fd->tf", grad_branch, out_full)
            .astype(jnp.bfloat16)
            .reshape(SEQUENCE_SLOTS, resident, -1)
        )
        grad_heads = lax.all_to_all(
            grad_tokens_att, "head", split_axis=2, concat_axis=1, tiled=True
        ).reshape(SEQUENCE_SLOTS, rows_local, kv_local, group, HEAD_SIZE)
        grad_queries, grad_keys_all = attend_back(
            query_heads, keys_all, grad_heads, attended, log_total
        )
        grad_pairs_own = lax.psum_scatter(
            grad_keys_all.astype(jnp.bfloat16), "blk", scatter_dimension=1, tiled=True
        )
        grad_query_send = grad_queries.astype(jnp.bfloat16).reshape(
            SEQUENCE_SLOTS, rows_local, kv_local * group * HEAD_SIZE
        )
        grad_pair_send = grad_pairs_own.reshape(
            SEQUENCE_SLOTS, rows_local, kv_local * 2 * HEAD_SIZE
        )
        grad_query_tok = lax.all_to_all(
            grad_query_send, "head", split_axis=1, concat_axis=2, tiled=True
        )
        grad_pair_tok = lax.all_to_all(
            grad_pair_send, "head", split_axis=1, concat_axis=2, tiled=True
        )
        grad_query_rot = rotate(
            grad_query_tok.astype(jnp.float32).reshape(
                SEQUENCE_SLOTS, resident, QUERY_HEAD_COUNT, HEAD_SIZE
            ),
            own_float,
            -1.0,
        )
        grad_pair = grad_pair_tok.astype(jnp.float32).reshape(
            SEQUENCE_SLOTS, resident, KEY_VALUE_HEADS, 2, HEAD_SIZE
        )
        grad_key_rot = rotate(grad_pair[:, :, :, 0, :], own_float, -1.0)
        grad_projected = jnp.concatenate(
            [
                grad_query_rot.reshape(slot_rows, QUERY_HEAD_COUNT * HEAD_SIZE),
                jnp.stack([grad_key_rot, grad_pair[:, :, :, 1, :]], axis=3).reshape(
                    slot_rows, KEY_VALUE_HEADS * 2 * HEAD_SIZE
                ),
            ],
            axis=-1,
        ).astype(jnp.bfloat16)
        grad_qkv = mm("td,te->de", normed_a, grad_projected).astype(jnp.bfloat16)
        grad_normed_a = mm("te,de->td", grad_projected, qkv_full)
        grad_norm_a, grad_gain_a = norm_back(grad_normed_a, scaled_a, inverse_a, gains_full[0])
        grad_hidden = grad_middle + grad_norm_a
        small_list[layer_index] = tuple(
            lax.psum_scatter(term, ("head", "blk"), scatter_dimension=0, tiled=True)
            for term in (
                grad_qkv,
                grad_out_w,
                grad_router,
                jnp.stack([grad_gain_a, grad_gain_b], axis=1),
            )
        )
        own_and_shared = []
        if owned:
            own_and_shared.append(
                tuple(
                    rows_from_owner(term, blocks_count, owned, blk_index)
                    for term in grad_weight_sets[0]
                )
            )
        if owned_total < experts_local:
            own_and_shared.append(
                tuple(
                    lax.psum_scatter(term, "blk", scatter_dimension=1, tiled=True)
                    for term in grad_weight_sets[-1]
                )
            )
        expert_list[layer_index] = tuple(
            jnp.concatenate(terms, axis=0).astype(jnp.float32) for terms in zip(*own_and_shared)
        )
    grad_w_qkv = jnp.stack([terms[0].astype(jnp.float32) for terms in small_list])
    grad_w_out = jnp.stack([terms[1].astype(jnp.float32) for terms in small_list])
    grad_router = jnp.stack([terms[2] for terms in small_list])
    grad_gains = jnp.stack([terms[3] for terms in small_list])
    grad_w_in = jnp.stack([terms[0] for terms in expert_list])
    grad_w_down = jnp.stack([terms[1] for terms in expert_list])
    return (
        result,
        grad_hidden.reshape(tokens.shape),
        grad_w_qkv,
        grad_w_out,
        grad_router,
        grad_gains[:, :, 0],
        grad_gains[:, :, 1],
        grad_w_in,
        grad_w_down,
    )


def solution(mesh):
    in_specs = (
        P(None, ("head", "blk"), None),
        P(),
        P(None, None, ("head", "blk"), None),
        P(None, None, ("head", "blk"), None),
        P(None, ("head", "blk"), None),
        P(None, ("head", "blk"), None),
        P(None, ("head", "blk"), None),
        P(None, None, ("head", "blk")),
        P(None, "head", "blk", None),
        P(None, "head", "blk", None),
        P(None, ("head", "blk"), None),
    )
    out_specs = (
        P(None, ("head", "blk"), None),
        P(None, ("head", "blk"), None),
        P(None, ("head", "blk"), None),
        P(None, ("head", "blk"), None),
        P(None, ("head", "blk"), None),
        P(None, ("head", "blk")),
        P(None, ("head", "blk")),
        P(None, "head", "blk", None),
        P(None, "head", "blk", None),
    )
    return jax.shard_map(shards, mesh=mesh, in_specs=in_specs, out_specs=out_specs, check_vma=False)
```

time: 3860 us -> 3160 us (0.82)
  waiting for transfers between devices: 2020 us -> 1380 us
  blocking collectives: 801 us -> 448 us
  other arithmetic: 173 us -> 396 us
  starting transfers between devices: 57.3 us -> 160 us
  matrix products: 471 us -> 419 us
    reduce_scatter x10, waiting for transfers between devices: 1280 us -> 647 us  [the longest x4 476 us: shards(): lax.psum_scatter(term, ('head', 'blk'), scatter_dimension=0, tiled=True)]
    all_to_all x4, blocking collectives: 365 us -> 128 us  [the longest x2 79.5 us: head_gather(): lax.all_to_all(copies, 'head', 0, 0, tiled=True).reshape(-1, rows.shape[-1])]
    unnamed x8 -> x12, other arithmetic: 0.01 us -> 221 us
    ppermute x0 -> x56, waiting for transfers between devices: none -> 209 us  [the longest x28 130 us: rows_from_owner(): piece = lax.ppermute(piece, 'blk', ring(blocks_count, offset))]
    all_gather x4, waiting for transfers between devices: 166 us -> 0.08 us  [expert_weights(): lax.all_gather(matrix[layer_index, owned_total:], 'blk', axis=1, tiled=True)]
    all_gather x2, blocking collectives: 278 us -> 154 us  [shards(): lax.all_gather(router[layer_index], ('head', 'blk'), axis=0, tiled=True)]
    unnamed x262 -> x391, local copies, waits for them, and re-layouts: 32 us -> 106 us
    convert_element_type x13 -> x10, other arithmetic: 66.2 us -> 5.49 us  [the longest x2 2.63 us: shards(): attended.astype(jnp.bfloat16)]
  transfers between devices with their start and end apart: 37 -> 103, of which waited for: 30 -> 52; matrix products, arithmetic and copies ran while one was open for 13% -> 24% of each run, Pallas kernels for 0% -> 0%
where the time goes in v1:
time: 3160 us; the launch traced here: 3150 us
  waiting for transfers between devices  1380 us (44%)
  blocking collectives  448 us (14%)
  matrix products  419 us (13%)
  other arithmetic  396 us (13%)
  local copies, waits for them, and re-layouts  317 us (10%)
  starting transfers between devices  160 us (5%)
    reduce_scatter x4, waiting for transfers between devices, shards(): lax.psum_scatter(term, ('head', 'blk'), scatter_dimension=0, tiled=True)  476 us
    dot_general x110, matrix products, mm(): return jnp.einsum(spec, left, right, preferred_element_type=jnp.float32)  415 us
    unnamed x28, waiting for transfers between devices  271 us
    unnamed x12, other arithmetic  221 us
    all_gather x2, blocking collectives, shards(): lax.all_gather(router[layer_index], ('head', 'blk'), axis=0, tiled=True)  154 us
    reduce_scatter x4, waiting for transfers between devices, shards(): lax.psum_scatter(term, 'blk', scatter_dimension=1, tiled=True)  145 us
    ppermute x28, waiting for transfers between devices, rows_from_owner(): piece = lax.ppermute(piece, 'blk', ring(blocks_count, offset))  130 us
    all_gather x2, blocking collectives, shards(): lax.all_gather(norm_gains[layer_index], ('head', 'blk'), axis=1, tiled=True)  111 us
  transfers between devices with their start and end apart: 103, of which 52 were waited for; matrix products, arithmetic and copies ran while one was open for 24% of the time, Pallas kernels for 0%

profile of v1, /device:TPU:0, one launch (start us, length us, event | category | flops | bytes accessed | tf_op | source)
XLA Modules:
  0.0 3149.8 jit_solution(9329253238179177214)
XLA Ops:
  10.6 47.5 %all-gather = bf16[1,2,1536]{1,0,2:T(2,128)(2,1)S(1)} all-gather(bf16[1,2,48]{1,0,2:T(2,128)(2,1)S(1)} %copy.427), channel_id=2, replica_groups=mesh['head'=4,'blk'=8] {'head','blk'}, dimensions={2}, use_global_device_ids=true | all-gather | bytes 6336 | tf_op jit(solution)/shard_map/all_gather | solution.py:301
  60.6 25.7 fusion.236
  202.4 69.0 %while.68 = (s32[]{:T(128)}, f32[2,256,2,3]{1,3,2,0:T(4,128)S(1)}, f32[2,256,2,3]{1,3,2,0:T(4,128)S(1)}, f32[2,256,2,3,64]{1,4,3,2,0:T(8,128)}, s32[4]{0:T(128)S...) while((s32[]{:T(128)}, f32[2,256,2,3]{1,3,2,0:T(4,128)S(1)}, ...), condition=%wide.region_4.5_spmd.clone, body=%wide.region_1.4_spmd.clone.sunk | while | flops 420980224 | bytes 29174064 | solution.py:180
  364.5 43.2 %collective-permute-done.2 = bf16[1,192,1024]{2,1,0:T(8,128)(2,1)S(1)} collective-permute-done((bf16[1,192,1024]{2,1,0:T(8,128)(2,1)}, bf16[1,192,1024]{2,1,0:T(8,128)(2,1)S(1)}, u32[]{:S(2)}, u32[]{:S(2)}) %collective-permute-start.2) | collective-permute-done | bytes 393248 | tf_op jit(solution)/shard_map/ppermute | solution.py:72
  439.0 56.6 %reduce.9 = bf16[832,1536]{1,0:T(8,128)(2,1)} reduce(bf16[832,1,1536]{2,1,0:T(2,128)(2,1)} %bitcast.968, bf16[]{:T(256)} %broadcast.1827), dimensions={1}, to_apply=%bitcast.863.reduce_sub_computation | reduce | bytes 5111810
  520.1 63.7 %all-gather.3 = bf16[1,1536,40]{2,0,1:T(2,128)(2,1)S(1)} all-gather(bf16[1,48,40]{2,0,1:T(2,128)(2,1)S(1)} %copy.428), channel_id=5, replica_groups=mesh['head'=4,'blk'=8] {'head','blk'}, dimensions={1}, use_global_device_ids=true | all-gather | bytes 126720 | tf_op jit(solution)/shard_map/all_gather | solution.py:300
  612.3 63.3 %all-gather.6 = bf16[1,2,1536]{1,0,2:T(2,128)(2,1)S(1)} all-gather(bf16[1,2,48]{1,0,2:T(2,128)(2,1)S(1)} %copy.429), channel_id=8, replica_groups=mesh['head'=4,'blk'=8] {'head','blk'}, dimensions={2}, use_global_device_ids=true | all-gather | bytes 6336 | tf_op jit(solution)/shard_map/all_gather | solution.py:301
  675.6 25.9 fusion.234
  759.7 68.7 %while.69 = (s32[]{:T(128)}, f32[2,256,2,3]{1,3,2,0:T(4,128)S(1)}, f32[2,256,2,3]{1,3,2,0:T(4,128)}, f32[2,256,2,3,64]{1,4,3,2,0:T(8,128)}, s32[4]{0:T(128)S(1)}...) while((s32[]{:T(128)}, f32[2,256,2,3]{1,3,2,0:T(4,128)S(1)}, ...), condition=%wide.region_15.16_spmd.clone, body=%wide.region_12.15_spmd.clone.sunk | while | flops 420980224 | bytes 29272424 | solution.py:180
  851.4 40.7 %all_to_all.299 = bf16[4,128,1536]{2,1,0:T(8,128)(2,1)} all-to-all(bf16[4,128,1536]{2,1,0:T(8,128)(2,1)S(1)} %broadcast_in_dim.134), channel_id=1, replica_groups=mesh['head'=4,'blk'=8] {'head'}, dimensions={0} | all-to-all | bytes 3145728 | tf_op jit(solution)/shard_map/all_to_all | solution.py:93
  903.9 29.6 all-to-all-done.14
  947.3 89.9 %all-gather.9 = bf16[1,1536,40]{2,0,1:T(2,128)(2,1)} all-gather(bf16[1,48,40]{2,0,1:T(2,128)(2,1)} %copy.430), channel_id=11, replica_groups=mesh['head'=4,'blk'=8] {'head','blk'}, dimensions={1}, use_global_device_ids=true | all-gather | bytes 126720 | tf_op jit(solution)/shard_map/all_gather | solution.py:300
  1062.1 27.6 collective-permute-done.20
  1115.9 54.7 %reduce.10 = bf16[832,1536]{1,0:T(8,128)(2,1)S(1)} reduce(bf16[832,1,1536]{2,1,0:T(2,128)(2,1)} %bitcast.971, bf16[]{:T(256)} %broadcast.1827), dimensions={1}, to_apply=%bitcast.861.reduce_sub_computation | reduce | bytes 5111810
  1188.2 54.7 %reduce.11 = bf16[832,1536]{1,0:T(8,128)(2,1)S(1)} reduce(bf16[832,1,1536]{2,1,0:T(2,128)(2,1)} %bitcast.972, bf16[]{:T(256)} %broadcast.1827), dimensions={1}, to_apply=%bitcast.862.reduce_sub_computation | reduce | bytes 5111810
  1319.0 28.6 all-to-all-done.17
  1357.6 31.3 all-to-all-done.13
  1418.4 90.3 %while.70 = (s32[]{:T(128)}, f32[2,256,2,3,64]{1,4,3,2,0:T(8,128)}, bf16[2,2048,2,2,64]{1,4,3,2,0:T(8,128)(2,1)}, s32[4]{0:T(128)}, bf16[2,2048,2,2,64]{1,4,2,0,...) while((s32[]{:T(128)}, f32[2,256,2,3,64]{1,4,3,2,0:T(8,128)}, ...), condition=%wide.region_27.28_spmd.clone, body=%wide.region_26.27_spmd.clone.sunk | while | flops 1023896064 | bytes 36014408 | solution.py:209
  1576.7 38.8 %all_to_all.301 = bf16[4,128,1536]{2,1,0:T(8,128)(2,1)S(1)} all-to-all(bf16[4,128,1536]{2,1,0:T(8,128)(2,1)S(1)} %broadcast_in_dim.136), channel_id=1, replica_groups=mesh['head'=4,'blk'=8] {'head'}, dimensions={0} | all-to-all | bytes 3145728 | tf_op jit(solution)/shard_map/all_to_all | solution.py:93
  1620.1 34.7 %all_to_all.302 = bf16[8,104,1536]{2,1,0:T(8,128)(2,1)S(1)} all-to-all(bf16[8,104,1536]{2,1,0:T(8,128)(2,1)S(1)} %bitcast.979), channel_id=1, replica_groups=mesh['head'=4,'blk'=8] {'blk'}, dimensions={0} | all-to-all | bytes 5111808 | tf_op jit(solution)/shard_map/all_to_all | solution.py:242
  1671.4 54.7 %reduce.12 = bf16[832,1536]{1,0:T(8,128)(2,1)S(1)} reduce(bf16[832,1,1536]{2,1,0:T(2,128)(2,1)} %bitcast.969, bf16[]{:T(256)} %broadcast.1827), dimensions={1}, to_apply=%bitcast.860.reduce_sub_computation | reduce | bytes 5111810
  1785.9 33.8 %all-to-all-done.25 = bf16[4,128,1536]{2,1,0:T(8,128)(2,1)S(1)} async-done(((bf16[4,128,1536]{2,1,0:T(8,128)(2,1)}), bf16[4,128,1536]{2,1,0:T(8,128)(2,1)S(1)}, u32[]{:S(2)}, u32[]{:S(2)}) %all-to-all-start.25) | async-done | bytes 1572896 | tf_op jit(solution)/shard_map/all_to_all | solution.py:99
  1847.9 90.3 %while.71 = (s32[]{:T(128)}, f32[2,256,2,3,64]{1,4,3,2,0:T(8,128)}, bf16[2,2048,2,2,64]{1,4,3,2,0:T(8,128)(2,1)}, s32[4]{0:T(128)}, bf16[2,2048,2,2,64]{1,4,2,0,...) while((s32[]{:T(128)}, f32[2,256,2,3,64]{1,4,3,2,0:T(8,128)}, ...), condition=%wide.region_35.36_spmd.clone, body=%wide.region_34.35_spmd.clone.sunk | while | flops 1023896064 | bytes 36018504 | solution.py:209
  2119.2 79.9 %reduce-scatter.49.cloned.1.call-done = f32[48,2]{1,0:T(8,128)} async-done(((f32[1536,2]{1,0:T(8,128)}), f32[48,2]{1,0:T(8,128)}) %reduce-scatter.49.cloned.1.call-update) | async-done | bytes 400
  2200.0 98.8 %reduce-scatter.43.cloned.1.call-done = f32[48,40]{1,0:T(8,128)} async-done(((f32[1536,40]{1,0:T(8,128)}), f32[48,40]{1,0:T(8,128)}) %reduce-scatter.43.cloned.1.call-update) | async-done | bytes 7696
  2434.3 60.8 %reduce-scatter.37.cloned.1.call-done = bf16[2,192,1024]{2,1,0:T(8,128)(2,1)} async-done(((bf16[2,1536,1024]{2,1,0:T(8,128)(2,1)}), bf16[2,192,1024]{2,1,0:T(8,128)(2,1)}) %reduce-scatter.37.cloned.1.call-update) | async-done | bytes 786448 | tf_op jit(solution)/shard_map/reduce_scatter | solution.py:517
  2495.2 65.6 %reduce-scatter.35.cloned.1.call-done = bf16[2,192,1024]{2,1,0:T(8,128)(2,1)} async-done(((bf16[2,1536,1024]{2,1,0:T(8,128)(2,1)}), bf16[2,192,1024]{2,1,0:T(8,128)(2,1)}) %reduce-scatter.35.cloned.1.call-update) | async-done | bytes 786448 | tf_op jit(solution)/shard_map/reduce_scatter | solution.py:517
  2571.1 90.1 %reduce-scatter.47.cloned.1.call-done = f32[48,2]{1,0:T(8,128)} async-done(((f32[1536,2]{1,0:T(8,128)}), f32[48,2]{1,0:T(8,128)}) %reduce-scatter.47.cloned.1.call-update) | async-done | bytes 400
  2662.6 110.1 %reduce-scatter.33.cloned.1.call-done = bf16[48,1536]{1,0:T(8,128)(2,1)} async-done(((bf16[1536,1536]{1,0:T(8,128)(2,1)}), bf16[48,1536]{1,0:T(8,128)(2,1)}) %reduce-scatter.33.cloned.1.call-update) | async-done | bytes 147472 | tf_op jit(solution)/shard_map/reduce_scatter | solution.py:498
  2772.8 112.5 %reduce-scatter.31.cloned.1.call-done = bf16[48,1536]{1,0:T(8,128)(2,1)} async-done(((bf16[1536,1536]{1,0:T(8,128)(2,1)}), bf16[48,1536]{1,0:T(8,128)(2,1)}) %reduce-scatter.31.cloned.1.call-update) | async-done | bytes 147472 | tf_op jit(solution)/shard_map/reduce_scatter | solution.py:498
  2887.1 125.3 %reduce-scatter.29.cloned.1.call-done = bf16[48,2560]{1,0:T(8,128)(2,1)} async-done(((bf16[1536,2560]{1,0:T(8,128)(2,1)}), bf16[48,2560]{1,0:T(8,128)(2,1)}) %reduce-scatter.29.cloned.1.call-update) | async-done | bytes 245776 | tf_op jit(solution)/shard_map/reduce_scatter | solution.py:498
  3012.4 128.2 %reduce-scatter.27.cloned.1.call-done = bf16[48,2560]{1,0:T(8,128)(2,1)} async-done(((bf16[1536,2560]{1,0:T(8,128)(2,1)}), bf16[48,2560]{1,0:T(8,128)(2,1)}) %reduce-scatter.27.cloned.1.call-update) | async-done | bytes 245776 | tf_op jit(solution)/shard_map/reduce_scatter | solution.py:498
  (1222 shorter events, 1403.5 us)
Async XLA Ops:
  9.2 188.6 %all-gather.23.cloned.1.call-start = ((), (), s32[]{:S(2)}) async-start(), calls=%async_computation.44 | async-start | bytes 2359296 | tf_op jit(solution)/shard_map/all_gather | solution.py:57
  113.9 176.1 %all-gather.29.cloned.1.call-start = ((), (), s32[]{:S(2)}) async-start(), calls=%async_computation.57 | async-start | bytes 4866048 | tf_op jit(solution)/shard_map/all_gather | solution.py:299
  114.7 471.5 %all-gather.31.cloned.1.call-start = ((), (), s32[]{:S(2)}) async-start(), calls=%async_computation.58 | async-start | bytes 7077888 | tf_op jit(solution)/shard_map/all_gather | solution.py:263
  117.4 474.2 %all-gather.33.cloned.1.call-start = ((), (), s32[]{:S(2)}) async-start(), calls=%async_computation.59 | async-start | bytes 3538944 | tf_op jit(solution)/shard_map/all_gather | solution.py:263
  119.5 584.3 %all-gather.35.cloned.1.call-start = ((), (), s32[]{:S(2)}) async-start(), calls=%async_computation.60 | async-start | bytes 8110080 | tf_op jit(solution)/shard_map/all_gather | solution.py:296
  126.7 151.8 %collective-permute-start.23 = (bf16[1,64,1536]{2,1,0:T(8,128)(2,1)}, bf16[1,64,1536]{2,1,0:T(8,128)(2,1)}, u32[]{:S(2)}, u32[]{:S(2)}) collective-permute-start(bf16[1,64,1536]{2,1,0:T(8,128)(2,1)} %get-tuple-element.1216), channel_id=1, source_target_pairs={{0,3},{1,4},{2,5},{3,6},{4,7},{5,0},{6,1},{7,2},{8,11},{9,12},{10,... | collective-permute-start | bytes 589832 | tf_op jit(solution)/shard_map/ppermute | solution.py:72
  128.1 173.5 %collective-permute-start.24 = (bf16[1,64,1536]{2,1,0:T(8,128)(2,1)}, bf16[1,64,1536]{2,1,0:T(8,128)(2,1)}, u32[]{:S(2)}, u32[]{:S(2)}) collective-permute-start(bf16[1,64,1536]{2,1,0:T(8,128)(2,1)} %get-tuple-element.1215), channel_id=1, source_target_pairs={{0,4},{1,5},{2,6},{3,7},{4,0},{5,1},{6,2},{7,3},{8,12},{9,13},{10,... | collective-permute-start | bytes 589832 | tf_op jit(solution)/shard_map/ppermute | solution.py:72
  129.6 179.7 %collective-permute-start.25 = (bf16[1,64,1536]{2,1,0:T(8,128)(2,1)}, bf16[1,64,1536]{2,1,0:T(8,128)(2,1)}, u32[]{:S(2)}, u32[]{:S(2)}) collective-permute-start(bf16[1,64,1536]{2,1,0:T(8,128)(2,1)} %get-tuple-element.1214), channel_id=1, source_target_pairs={{0,5},{1,6},{2,7},{3,0},{4,1},{5,2},{6,3},{7,4},{8,13},{9,14},{10,... | collective-permute-start | bytes 589832 | tf_op jit(solution)/shard_map/ppermute | solution.py:72
  179.5 132.5 %collective-permute-start.26 = (bf16[1,64,1536]{2,1,0:T(8,128)(2,1)}, bf16[1,64,1536]{2,1,0:T(8,128)(2,1)}, u32[]{:S(2)}, u32[]{:S(2)}) collective-permute-start(bf16[1,64,1536]{2,1,0:T(8,128)(2,1)} %get-tuple-element.1213), channel_id=1, source_target_pairs={{0,6},{1,7},{2,0},{3,1},{4,2},{5,3},{6,4},{7,5},{8,14},{9,15},{10,... | collective-permute-start | bytes 589832 | tf_op jit(solution)/shard_map/ppermute | solution.py:72
  612.2 142.7 %all-gather.25.cloned.1.call-start = ((), (), s32[]{:S(2)}) async-start(), calls=%async_computation.45 | async-start | bytes 2359296 | tf_op jit(solution)/shard_map/all_gather | solution.py:57
  729.6 117.3 %all-gather.37.cloned.1.call-start = ((), (), s32[]{:S(2)}) async-start(), calls=%async_computation.61 | async-start | bytes 4866048 | tf_op jit(solution)/shard_map/all_gather | solution.py:299
  737.5 516.4 %all-gather.39.cloned.1.call-start = ((), (), s32[]{:S(2)}) async-start(), calls=%async_computation.62 | async-start | bytes 7077888 | tf_op jit(solution)/shard_map/all_gather | solution.py:263
  934.7 113.9 %all-to-all-start.11 = ((bf16[8,104,1536]{2,1,0:T(8,128)(2,1)}), bf16[8,104,1536]{2,1,0:T(8,128)(2,1)}, u32[]{:S(2)}, u32[]{:S(2)}) async-start(bf16[8,104,1536]{2,1,0:T(8,128)(2,1)} %bitcast.978), calls=%async_computation.11 | async-start | bytes 5111808 | tf_op jit(solution)/shard_map/all_to_all | solution.py:242
  939.3 318.6 %all-gather.41.cloned.1.call-start = ((), (), s32[]{:S(2)}) async-start(), calls=%async_computation.63 | async-start | bytes 3538944 | tf_op jit(solution)/shard_map/all_gather | solution.py:263
  941.3 113.0 %collective-permute-start.15 = (bf16[1,192,1024]{2,1,0:T(8,128)(2,1)}, bf16[1,192,1024]{2,1,0:T(8,128)(2,1)}, u32[]{:S(2)}, u32[]{:S(2)}) collective-permute-start(bf16[1,192,1024]{2,1,0:T(8,128)(2,1)} %get-tuple-element.1181), channel_id=1, source_target_pairs={{0,2},{1,3},{2,4},{3,5},{4,6},{5,7},{6,0},{7,1},{8,10},{9,11},{10,... | collective-permute-start | bytes 1179656 | tf_op jit(solution)/shard_map/ppermute | solution.py:72
  943.0 115.0 %collective-permute-start.16 = (bf16[1,192,1024]{2,1,0:T(8,128)(2,1)}, bf16[1,192,1024]{2,1,0:T(8,128)(2,1)}, u32[]{:S(2)}, u32[]{:S(2)}) collective-permute-start(bf16[1,192,1024]{2,1,0:T(8,128)(2,1)} %get-tuple-element.1180), channel_id=1, source_target_pairs={{0,3},{1,4},{2,5},{3,6},{4,7},{5,0},{6,1},{7,2},{8,11},{9,12},{10,... | collective-permute-start | bytes 1179656 | tf_op jit(solution)/shard_map/ppermute | solution.py:72
  945.2 113.8 %collective-permute-start.17 = (bf16[1,192,1024]{2,1,0:T(8,128)(2,1)}, bf16[1,192,1024]{2,1,0:T(8,128)(2,1)}, u32[]{:S(2)}, u32[]{:S(2)}) collective-permute-start(bf16[1,192,1024]{2,1,0:T(8,128)(2,1)} %get-tuple-element.1179), channel_id=1, source_target_pairs={{0,4},{1,5},{2,6},{3,7},{4,0},{5,1},{6,2},{7,3},{8,12},{9,13},{10,... | collective-permute-start | bytes 1179656 | tf_op jit(solution)/shard_map/ppermute | solution.py:72
  945.7 114.3 %collective-permute-start.18 = (bf16[1,192,1024]{2,1,0:T(8,128)(2,1)}, bf16[1,192,1024]{2,1,0:T(8,128)(2,1)}, u32[]{:S(2)}, u32[]{:S(2)}) collective-permute-start(bf16[1,192,1024]{2,1,0:T(8,128)(2,1)} %get-tuple-element.1178), channel_id=1, source_target_pairs={{0,5},{1,6},{2,7},{3,0},{4,1},{5,2},{6,3},{7,4},{8,13},{9,14},{10,... | collective-permute-start | bytes 1179656 | tf_op jit(solution)/shard_map/ppermute | solution.py:72
  1401.6 148.4 %reduce-scatter.23.cloned.1.call-start = ((), (), s32[]{:S(2)}) async-start(), calls=%async_computation.46 | async-start | bytes 2359296 | tf_op jit(solution)/shard_map/reduce_scatter | solution.py:458
  1830.5 149.4 %reduce-scatter.25.cloned.1.call-start = ((), (), s32[]{:S(2)}) async-start(), calls=%async_computation.47 | async-start | bytes 2359296 | tf_op jit(solution)/shard_map/reduce_scatter | solution.py:458
  1938.3 180.1 %reduce-scatter.45.cloned.1.call-start = ((), (), s32[]{:S(2)}) async-start(), calls=%async_computation.65 | async-start | bytes 811008
  1940.7 258.5 %reduce-scatter.49.cloned.1.call-start = ((), (), s32[]{:S(2)}) async-start(), calls=%async_computation.67 | async-start | bytes 811008
  1942.1 356.7 %reduce-scatter.43.cloned.1.call-start = ((), (), s32[]{:S(2)}) async-start(), calls=%async_computation.64 | async-start | bytes 811008
  1944.1 466.8 %reduce-scatter.41.cloned.1.call-start = ((), (), s32[]{:S(2)}) async-start(), calls=%async_computation.55 | async-start | bytes 3538944 | tf_op jit(solution)/shard_map/reduce_scatter | solution.py:517
  1946.9 482.7 %reduce-scatter.39.cloned.1.call-start = ((), (), s32[]{:S(2)}) async-start(), calls=%async_computation.54 | async-start | bytes 3538944 | tf_op jit(solution)/shard_map/reduce_scatter | solution.py:517
  1950.8 544.4 %reduce-scatter.37.cloned.1.call-start = ((), (), s32[]{:S(2)}) async-start(), calls=%async_computation.53 | async-start | bytes 7077888 | tf_op jit(solution)/shard_map/reduce_scatter | solution.py:517
  1956.5 604.2 %reduce-scatter.35.cloned.1.call-start = ((), (), s32[]{:S(2)}) async-start(), calls=%async_computation.52 | async-start | bytes 7077888 | tf_op jit(solution)/shard_map/reduce_scatter | solution.py:517
  1986.4 674.9 %reduce-scatter.47.cloned.1.call-start = ((), (), s32[]{:S(2)}) async-start(), calls=%async_computation.66 | async-start | bytes 811008
  2007.2 765.6 %reduce-scatter.33.cloned.1.call-start = ((), (), s32[]{:S(2)}) async-start(), calls=%async_computation.51 | async-start | bytes 4866048 | tf_op jit(solution)/shard_map/reduce_scatter | solution.py:498
  2011.0 874.3 %reduce-scatter.31.cloned.1.call-start = ((), (), s32[]{:S(2)}) async-start(), calls=%async_computation.50 | async-start | bytes 4866048 | tf_op jit(solution)/shard_map/reduce_scatter | solution.py:498
  2015.8 996.6 %reduce-scatter.29.cloned.1.call-start = ((), (), s32[]{:S(2)}) async-start(), calls=%async_computation.49 | async-start | bytes 8110080 | tf_op jit(solution)/shard_map/reduce_scatter | solution.py:498
  2022.6 1118.0 %reduce-scatter.27.cloned.1.call-start = ((), (), s32[]{:S(2)}) async-start(), calls=%async_computation.48 | async-start | bytes 8110080 | tf_op jit(solution)/shard_map/reduce_scatter | solution.py:498
  (282 other events, 5229.7 us)
Sparse Core Ops, SparseCore 0:
  11.5 79.5 all-gather.26
  114.0 36.6 all-gather.22
  153.6 66.0 all-gather.28
  222.0 44.3 all-gather.30
  268.1 35.4 all-gather.32
  306.4 112.6 all-gather.34
  729.8 25.1 all-gather.24
  757.8 63.6 all-gather.36
  823.4 44.3 all-gather.38
  946.1 65.5 all-gather.40
  1508.8 41.1 reduce-scatter.22
  1938.4 41.4 reduce-scatter.24
  1985.1 114.5 reduce-scatter.44
  2104.6 94.5 reduce-scatter.48
  2204.1 94.5 reduce-scatter.42
  2302.5 66.0 reduce-scatter.40
  2372.3 57.2 reduce-scatter.38
  2433.4 61.7 reduce-scatter.36
  2498.9 61.7 reduce-scatter.34
  2565.7 95.5 reduce-scatter.46
  2666.7 105.9 reduce-scatter.32
  2779.1 106.1 reduce-scatter.30
  2891.0 121.4 reduce-scatter.28
  3018.9 121.7 reduce-scatter.26

commit v2 on v1

v2 whole, which is shorter than its diff:
```python
import functools

import jax
import jax.numpy as jnp
from jax import lax
from jax.experimental import pallas as pl
from jax.experimental.pallas import tpu as pltpu
from jax.sharding import PartitionSpec as P

MODEL_WIDTH = 1536
QUERY_HEAD_COUNT = 24
KEY_VALUE_HEADS = 8
HEAD_SIZE = 64
FF = 512
EXPERTS = 40
TOP = 8
DECODER_LAYERS = 2
SEQUENCE_SLOTS = 2
CAP = 26


epsilon = 1e-06
negative = -1e30
theta_log = 9.210340371976184


MESH = pl.DeviceIdType.MESH


def mm(spec, left, right):
    return jnp.einsum(spec, left, right, preferred_element_type=jnp.float32)


def rotate(values, cosine, sine):
    rows = values.shape[0]
    half = HEAD_SIZE // 2
    heads = values.reshape(rows, -1, HEAD_SIZE)
    first_half = heads[..., :half]
    second_half = heads[..., half:]
    cosine = cosine[:, None, :]
    sine = sine[:, None, :]
    return jnp.concatenate(
        [first_half * cosine - second_half * sine, second_half * cosine + first_half * sine],
        axis=-1,
    ).reshape(values.shape)


def norm_rows(hidden):
    inverse = lax.rsqrt(jnp.mean(hidden * hidden, axis=-1, keepdims=True) + epsilon)
    return (hidden * inverse, inverse)


def norm_back(grad_normed, scaled, inverse, gain_row):
    grad_gain = jnp.sum(grad_normed * scaled, axis=0)
    grad_scaled = grad_normed * gain_row
    grad_hidden = inverse * (
        grad_scaled - scaled * jnp.mean(grad_scaled * scaled, axis=-1, keepdims=True)
    )
    return (grad_hidden, grad_gain)


def ring(count, offset):
    return [(i, (i + offset) % count) for i in range(count)]


def rows_to_owner(matrices, blocks_count, owned, blk_index):
    rows, columns = matrices.shape[1:]
    whole = jnp.zeros((owned, blocks_count * rows, columns), matrices.dtype)
    for offset in range(blocks_count):
        target = (blk_index + offset) % blocks_count
        origin = (blk_index - offset) % blocks_count
        piece = lax.dynamic_slice_in_dim(matrices, target * owned, owned, 0)
        if offset:
            piece = lax.ppermute(piece, "blk", ring(blocks_count, offset))
        whole = lax.dynamic_update_slice_in_dim(whole, piece, origin * rows, 1)
    return whole


def rows_from_owner(whole, blocks_count, owned, blk_index):
    rows = whole.shape[1] // blocks_count
    matrices = jnp.zeros((owned * blocks_count, rows, whole.shape[2]), whole.dtype)
    for offset in range(blocks_count):
        target = (blk_index + offset) % blocks_count
        origin = (blk_index - offset) % blocks_count
        piece = lax.dynamic_slice_in_dim(whole, target * rows, rows, 1)
        if offset:
            piece = lax.ppermute(piece, "blk", ring(blocks_count, offset))
        matrices = lax.dynamic_update_slice_in_dim(matrices, piece, origin * owned, 0)
    return matrices


def head_gather_kernel(heads, own_ref, all_ref, send_sems, recv_sems, local_sem):
    head = lax.axis_index("head")
    blk = lax.axis_index("blk")
    peers = [lax.rem(head + step, heads) for step in range(1, heads)]
    barrier = pltpu.get_barrier_semaphore()
    for peer in peers:
        pl.semaphore_signal(barrier, inc=1, device_id=(peer, blk), device_id_type=MESH)
    pl.semaphore_wait(barrier, heads - 1)
    copies = []
    for step, peer in enumerate(peers):
        copy = pltpu.make_async_remote_copy(
            src_ref=own_ref,
            dst_ref=all_ref.at[head],
            send_sem=send_sems.at[step],
            recv_sem=recv_sems.at[step],
            device_id=(peer, blk),
            device_id_type=MESH,
        )
        copy.start()
        copies.append(copy)
    local = pltpu.make_async_copy(own_ref, all_ref.at[head], local_sem)
    local.start()
    local.wait()
    for copy in copies:
        copy.wait()


def head_gather(rows):
    heads = lax.axis_size("head")
    gathered = pl.pallas_call(
        functools.partial(head_gather_kernel, heads),
        out_shape=jax.ShapeDtypeStruct((heads,) + rows.shape, rows.dtype),
        in_specs=[pl.BlockSpec(memory_space=pl.ANY)],
        out_specs=pl.BlockSpec(memory_space=pl.ANY),
        scratch_shapes=[
            pltpu.SemaphoreType.DMA((heads - 1,)),
            pltpu.SemaphoreType.DMA((heads - 1,)),
            pltpu.SemaphoreType.DMA,
        ],
        compiler_params=pltpu.CompilerParams(collective_id=1, has_side_effects=True),
        name="head_gather",
    )(rows)
    return gathered.reshape(-1, rows.shape[-1])


def head_scatter(partial):
    heads = lax.axis_size("head")
    parts = partial.astype(jnp.bfloat16).reshape(heads, -1, partial.shape[-1])
    parts = lax.all_to_all(parts, "head", 0, 0, tiled=True)
    return jnp.sum(parts.astype(jnp.float32), axis=0)


def dot_last(left, right):
    return lax.dot_general(
        left, right, (((1,), (1,)), ((), ())), preferred_element_type=jnp.float32
    )


def dot_first(left, right):
    return lax.dot_general(
        left, right, (((0,), (0,)), ((), ())), preferred_element_type=jnp.float32
    )


def head_columns(ref, rows, first, group, shift):
    pieces = []
    for member in range(group):
        start = (first + member) * HEAD_SIZE
        piece = ref[0, rows, start : start + HEAD_SIZE]
        empty = jnp.zeros_like(piece)
        pieces.append(jnp.concatenate([empty, piece] if shift else [piece, empty], axis=1))
    return jnp.concatenate(pieces, axis=0)


def unit_scores(queries, pairs, blk, resident, chunk):
    scores = dot_last(queries, pairs) * 0.125
    count, keys = scores.shape
    places = lax.broadcasted_iota(jnp.int32, (count, chunk), 1)
    own = blk * resident + lax.broadcasted_iota(jnp.int32, (count, chunk), 0) % resident
    last = jnp.where(places <= own, scores[:, keys - chunk :], negative)
    if keys > chunk:
        scores = jnp.concatenate([scores[:, : keys - chunk], last], axis=1)
    else:
        scores = last
    exponents = jnp.exp(scores - jnp.max(scores, axis=1, keepdims=True))
    return (exponents, jnp.sum(exponents, axis=1, keepdims=True))


def attend_kernel(heads, blocks, resident, group, kv_local, info_ref, query_ref, pair_ref, out_ref):
    slot_index = pl.program_id(0)
    blk = info_ref[0]
    length = info_ref[1 + slot_index]
    chunk = blocks * resident
    for head in range(heads):
        rows = pl.ds(head * resident, resident)
        live = head * chunk + blk * resident < length

        @pl.when(live)
        def _(head=head, rows=rows):
            keys = (head + 1) * chunk
            for kv_head in range(kv_local):
                lanes = pl.ds(kv_head * 2 * HEAD_SIZE, 2 * HEAD_SIZE)
                pairs = pair_ref[0, pl.ds(0, keys), lanes]
                queries = head_columns(query_ref, rows, kv_head * group, group, False)
                exponents, totals = unit_scores(queries, pairs, blk, resident, chunk)
                weighted = jnp.dot(
                    exponents.astype(jnp.bfloat16), pairs, preferred_element_type=jnp.float32
                )
                weighted = weighted / totals
                for member in range(group):
                    start = (kv_head * group + member) * HEAD_SIZE
                    out_ref[0, rows, start : start + HEAD_SIZE] = weighted[
                        member * resident : (member + 1) * resident, HEAD_SIZE:
                    ].astype(out_ref.dtype)

        @pl.when(jnp.logical_not(live))
        def _(rows=rows):
            out_ref[0, rows, :] = jnp.zeros((resident, out_ref.shape[2]), out_ref.dtype)


def attend_back_kernel(
    heads,
    blocks,
    resident,
    group,
    kv_local,
    info_ref,
    query_ref,
    pair_ref,
    grad_ref,
    grad_query_ref,
    grad_pair_ref,
    total_ref,
):
    slot_index = pl.program_id(0)
    blk = info_ref[0]
    length = info_ref[1 + slot_index]
    chunk = blocks * resident
    total_ref[...] = jnp.zeros_like(total_ref)
    for head in range(heads):
        rows = pl.ds(head * resident, resident)
        live = head * chunk + blk * resident < length

        @pl.when(live)
        def _(head=head, rows=rows):
            keys = (head + 1) * chunk
            for kv_head in range(kv_local):
                lanes = pl.ds(kv_head * 2 * HEAD_SIZE, 2 * HEAD_SIZE)
                pairs = pair_ref[0, pl.ds(0, keys), lanes]
                queries = head_columns(query_ref, rows, kv_head * group, group, False)
                grads = head_columns(grad_ref, rows, kv_head * group, group, True)
                exponents, totals = unit_scores(queries, pairs, blk, resident, chunk)
                probabilities = exponents * (1.0 / totals)
                grad_probs = dot_last(grads, pairs)
                delta = jnp.sum(probabilities * grad_probs, axis=1, keepdims=True)
                grad_scores = (probabilities * (grad_probs - delta)).astype(jnp.bfloat16)
                grad_queries = 0.125 * jnp.dot(
                    grad_scores, pairs, preferred_element_type=jnp.float32
                )
                for member in range(group):
                    start = (kv_head * group + member) * HEAD_SIZE
                    grad_query_ref[0, rows, start : start + HEAD_SIZE] = grad_queries[
                        member * resident : (member + 1) * resident, :HEAD_SIZE
                    ].astype(grad_query_ref.dtype)
                total_ref[pl.ds(0, keys), lanes] += dot_first(
                    grad_scores, queries * jnp.bfloat16(0.125)
                ) + dot_first(probabilities.astype(jnp.bfloat16), grads)

        @pl.when(jnp.logical_not(live))
        def _(rows=rows):
            grad_query_ref[0, rows, :] = jnp.zeros(
                (resident, grad_query_ref.shape[2]), grad_query_ref.dtype
            )

    grad_pair_ref[0] = total_ref[...].astype(grad_pair_ref.dtype)


def attention_call(kernel, info, arrays, outs, scratch, flops, name):
    def spec(array):
        shape = array.shape
        return pl.BlockSpec((1,) + shape[1:], lambda slot, info: (slot, 0, 0))

    return pl.pallas_call(
        kernel,
        grid_spec=pltpu.PrefetchScalarGridSpec(
            num_scalar_prefetch=1,
            grid=(SEQUENCE_SLOTS,),
            in_specs=[spec(array) for array in arrays],
            out_specs=[spec(array) for array in outs],
            scratch_shapes=scratch,
        ),
        out_shape=outs,
        compiler_params=pltpu.CompilerParams(vmem_limit_bytes=56 * 1024 * 1024),
        cost_estimate=pl.CostEstimate(
            flops=flops, bytes_accessed=8 << 20, transcendentals=flops // 256
        ),
        name=name,
    )(info, *arrays)


def shards(
    tokens,
    lengths,
    routes,
    queue_ranks,
    query_key_value_weight,
    w_out,
    router,
    norm_gains,
    w_in,
    w_down,
    cotangent,
):
    heads_count = lax.axis_size("head")
    blocks_count = lax.axis_size("blk")
    head_index = lax.axis_index("head")
    blk_index = lax.axis_index("blk")
    resident = tokens.shape[1]
    width = tokens.shape[2]
    weight_rows = w_out.shape[1]
    rows_local = heads_count * resident
    keys_total = blocks_count * rows_local
    kv_local = KEY_VALUE_HEADS // heads_count
    group = QUERY_HEAD_COUNT // KEY_VALUE_HEADS
    query_columns = kv_local * group * HEAD_SIZE
    pair_columns = kv_local * 2 * HEAD_SIZE
    slot_rows = SEQUENCE_SLOTS * resident
    all_tokens = heads_count * slot_rows
    experts_local = EXPERTS // heads_count
    owned = experts_local // blocks_count
    owned_total = owned * blocks_count
    slot = -(-heads_count * CAP // 16) * 16
    half = HEAD_SIZE // 2

    own_places = (head_index * blocks_count + blk_index) * resident + jnp.arange(
        resident, dtype=jnp.int32
    )
    valid_column = (
        (own_places[None, :] < lengths[:, None]).astype(jnp.float32).reshape(slot_rows, 1)
    )
    plane_ids = jnp.arange(all_tokens, dtype=jnp.int32)
    plane_places = (
        (plane_ids // slot_rows * blocks_count + blk_index) * resident + plane_ids % resident
    ).astype(jnp.float32)
    frequency = jnp.exp(jnp.arange(half, dtype=jnp.float32) * (-2.0 * theta_log / HEAD_SIZE))
    angles = plane_places[:, None] * frequency[None, :]
    cosine = jnp.cos(angles)
    sine = jnp.sin(angles)
    info = jnp.concatenate([blk_index[None].astype(jnp.int32), lengths])

    plan = lax.all_gather(
        jnp.stack([routes, queue_ranks]).reshape(2, DECODER_LAYERS, slot_rows, TOP), "head", axis=0
    )
    expert_ids = jnp.arange(EXPERTS, dtype=jnp.int32)
    row_ids = jnp.arange(experts_local * slot, dtype=jnp.int32)
    spread = (
        row_ids[None, :] // slot == jnp.arange(experts_local, dtype=jnp.int32)[:, None]
    ).astype(jnp.bfloat16)
    token_head = plane_ids[:, None] // slot_rows
    row_head = row_ids[None, :] % slot // CAP
    row_rank = (row_ids % slot % CAP).astype(jnp.float32)[None, :]

    def layer_plan(layer_index):
        plan_routes = plan[:, 0, layer_index].reshape(all_tokens, TOP)
        plan_ranks = plan[:, 1, layer_index].reshape(all_tokens, TOP)
        named = plan_routes[:, :, None] == expert_ids
        chosen = jnp.any(named, axis=1)
        marks = jnp.sum(
            jnp.where(named & (plan_ranks < CAP)[:, :, None], plan_ranks[:, :, None] + 1, 0), axis=1
        )
        marks = lax.dynamic_slice_in_dim(marks, head_index * experts_local, experts_local, 1)
        wide = mm("te,er->tr", marks.astype(jnp.bfloat16), spread) - 1.0
        places = ((wide == row_rank) & (token_head == row_head)).astype(jnp.bfloat16)
        return (chosen, places)

    def to_experts(rows):
        rows = rows.reshape(experts_local, slot, width)
        own = None
        if owned:
            own = rows[:owned_total].reshape(blocks_count, owned * slot, width)
            own = lax.all_to_all(own, "blk", 0, 0, tiled=True)
            own = own.reshape(blocks_count, owned, slot, width).transpose(1, 0, 2, 3)
            own = own.reshape(owned, blocks_count * slot, width)
        return (own, rows[owned_total:])

    def from_experts(own, shared):
        parts = [shared]
        if owned:
            own = own.reshape(owned, blocks_count, slot, width).transpose(1, 0, 2, 3)
            own = own.reshape(blocks_count, owned * slot, width)
            own = lax.all_to_all(own, "blk", 0, 0, tiled=True)
            parts = [own.reshape(owned_total, slot, width), shared]
        return jnp.concatenate(parts, axis=0).reshape(experts_local * slot, width)

    def expert_weights(layer_index):
        sets = []
        if owned:
            sets.append(
                tuple(
                    rows_to_owner(matrix[layer_index, :owned_total], blocks_count, owned, blk_index)
                    for matrix in (w_in, w_down)
                )
            )
        if owned_total < experts_local:
            sets.append(
                tuple(
                    lax.all_gather(matrix[layer_index, owned_total:], "blk", axis=1, tiled=True)
                    for matrix in (w_in, w_down)
                )
            )
        return sets

    def experts_forward(incoming, weights):
        gate_up = mm("erd,edf->erf", incoming, weights[0])
        units = (jax.nn.silu(gate_up[..., :FF]) * gate_up[..., FF:]).astype(jnp.bfloat16)
        produced = mm("erf,efd->erd", units, weights[1]).astype(jnp.bfloat16)
        return (produced, (incoming, gate_up, units))

    def experts_backward(grad_produced, weights, kept):
        incoming, gate_up, units = kept
        grad_units = mm("erd,efd->erf", grad_produced, weights[1])
        grad_down = mm("erf,erd->efd", units, grad_produced).astype(jnp.bfloat16)
        gate_part = gate_up[..., :FF]
        up_part = gate_up[..., FF:]
        sigmoid_part = jax.nn.sigmoid(gate_part)
        grad_gate_up = jnp.concatenate(
            [
                grad_units * up_part * sigmoid_part * (1.0 + gate_part * (1.0 - sigmoid_part)),
                grad_units * gate_part * sigmoid_part,
            ],
            axis=-1,
        ).astype(jnp.bfloat16)
        grad_in = mm("erd,erf->edf", incoming, grad_gate_up).astype(jnp.bfloat16)
        grad_incoming = mm("erf,edf->erd", grad_gate_up, weights[0]).astype(jnp.bfloat16)
        return (grad_incoming, (grad_in, grad_down))

    def by_slot(rows):
        return (
            rows.reshape(heads_count, SEQUENCE_SLOTS, resident, -1)
            .transpose(1, 0, 2, 3)
            .reshape(SEQUENCE_SLOTS, rows_local, -1)
        )

    def by_head(rows):
        return (
            rows.reshape(SEQUENCE_SLOTS, heads_count, resident, -1)
            .transpose(1, 0, 2, 3)
            .reshape(all_tokens, -1)
        )

    small_columns = 128
    send = []
    for layer_index in range(DECODER_LAYERS):
        weight = query_key_value_weight[layer_index]
        split = QUERY_HEAD_COUNT * HEAD_SIZE
        small = jnp.concatenate([router[layer_index], norm_gains[layer_index].T], axis=1)
        small = jnp.pad(small, ((0, 0), (0, small_columns - small.shape[1])))
        send.append(
            jnp.concatenate(
                [
                    weight[:, :split]
                    .reshape(weight_rows, heads_count, query_columns)
                    .transpose(1, 0, 2),
                    weight[:, split:]
                    .reshape(weight_rows, heads_count, pair_columns)
                    .transpose(1, 0, 2),
                    jnp.broadcast_to(small[None], (heads_count,) + small.shape),
                ],
                axis=-1,
            )
        )
    send = lax.all_to_all(jnp.stack(send, axis=1), "head", 0, 0, tiled=True)
    attention_weights = []
    for layer_index in range(DECODER_LAYERS):
        wide = lax.all_gather(send[:, layer_index], "blk", axis=1, tiled=True).reshape(width, -1)
        out_full = lax.all_gather(w_out[layer_index], "blk", axis=0, tiled=True)
        columns = query_columns + pair_columns
        small = wide[:, columns:]
        gains = small.T[EXPERTS : EXPERTS + 2].astype(jnp.float32)
        attention_weights.append((wide[:, :columns], out_full, small[:, :EXPERTS], gains))

    hidden = tokens.reshape(slot_rows, width).astype(jnp.float32)
    plane_tokens = head_gather(tokens.reshape(slot_rows, width))
    stored_all = []
    for layer_index in range(DECODER_LAYERS):
        qkv_full, out_full, router_full, gains = attention_weights[layer_index]
        weight_sets = expert_weights(layer_index)
        chosen, places = layer_plan(layer_index)
        scaled_a, inverse_a = norm_rows(hidden)
        if layer_index:
            plane_normed_a = head_gather((scaled_a * gains[:1]).astype(jnp.bfloat16))
        else:
            plane_normed_a = (
                norm_rows(plane_tokens.astype(jnp.float32))[0] * gains[:1]
            ).astype(jnp.bfloat16)
        projected = mm("td,de->te", plane_normed_a, qkv_full)
        queries = by_slot(rotate(projected[:, :query_columns], cosine, sine).astype(jnp.bfloat16))
        pairs = projected[:, query_columns:].reshape(all_tokens, kv_local, 2, HEAD_SIZE)
        keys = rotate(pairs[:, :, 0].reshape(all_tokens, -1), cosine, sine)
        pairs = jnp.stack([keys.reshape(all_tokens, kv_local, HEAD_SIZE), pairs[:, :, 1]], axis=2)
        pairs = pairs.reshape(all_tokens, pair_columns).astype(jnp.bfloat16)
        pairs = lax.all_to_all(
            jnp.broadcast_to(pairs[None], (blocks_count,) + pairs.shape), "blk", 0, 0, tiled=True
        )
        pairs_all = (
            pairs.reshape(blocks_count, heads_count, SEQUENCE_SLOTS, resident, pair_columns)
            .transpose(2, 1, 0, 3, 4)
            .reshape(SEQUENCE_SLOTS, keys_total, pair_columns)
        )
        (attended,) = attention_call(
            functools.partial(
                attend_kernel, heads_count, blocks_count, resident, group, kv_local
            ),
            info,
            [queries, pairs_all],
            [jax.ShapeDtypeStruct(queries.shape, jnp.bfloat16)],
            [],
            4 * rows_local * keys_total * query_columns,
            "attend",
        )
        attended = by_head(attended)
        middle = hidden + valid_column * head_scatter(mm("tf,fd->td", attended, out_full))
        scaled_b, inverse_b = norm_rows(middle)
        normed_b = (scaled_b * gains[1:]).astype(jnp.bfloat16)
        plane_rows = head_gather(normed_b)
        logits = mm("td,de->te", plane_rows, router_full)
        peaks = jnp.max(jnp.where(chosen, logits, negative), axis=-1, keepdims=True)
        lifted = jnp.where(chosen, jnp.exp(logits - peaks), 0.0)
        gates_all = lifted / jnp.sum(lifted, axis=-1, keepdims=True)
        plane_gates = lax.dynamic_slice_in_dim(
            gates_all, head_index * experts_local, experts_local, 1
        )
        weighted_places = (
            mm("te,er->tr", plane_gates.astype(jnp.bfloat16), spread).astype(jnp.bfloat16) * places
        )
        queues = mm("tr,td->rd", places, plane_rows).astype(jnp.bfloat16)
        own_in, shared_in = to_experts(queues)
        kept_sets = []
        produced = []
        for incoming, weights in zip([own_in, shared_in] if owned else [shared_in], weight_sets):
            made, kept = experts_forward(incoming, weights)
            produced.append(made)
            kept_sets.append(kept)
        returned = from_experts(*(produced if owned else [None] + produced))
        mixture = head_scatter(mm("tr,rd->td", weighted_places, returned))
        stored_all.append(
            (
                weight_sets,
                places,
                scaled_a,
                inverse_a,
                plane_normed_a,
                queries,
                pairs_all,
                attended,
                scaled_b,
                inverse_b,
                plane_rows,
                gates_all,
                weighted_places,
                kept_sets,
                returned,
            )
        )
        hidden = middle + valid_column * mixture
    result = (valid_column * hidden).astype(jnp.bfloat16).reshape(tokens.shape)
    grad_hidden = valid_column * cotangent.reshape(slot_rows, width).astype(jnp.float32)
    qkv_list = [None] * DECODER_LAYERS
    out_list = [None] * DECODER_LAYERS
    router_list = [None] * DECODER_LAYERS
    gains_list = [None] * DECODER_LAYERS
    expert_list = [None] * DECODER_LAYERS
    for layer_index in reversed(range(DECODER_LAYERS)):
        qkv_full, out_full, router_full, gains = attention_weights[layer_index]
        (
            weight_sets,
            places,
            scaled_a,
            inverse_a,
            plane_normed_a,
            queries,
            pairs_all,
            attended,
            scaled_b,
            inverse_b,
            plane_rows,
            gates_all,
            weighted_places,
            kept_sets,
            returned,
        ) = stored_all[layer_index]
        plane_grads = head_gather((valid_column * grad_hidden).astype(jnp.bfloat16))
        queue_grads = mm("tr,td->rd", weighted_places, plane_grads).astype(jnp.bfloat16)
        own_grad, shared_grad = to_experts(queue_grads)
        grad_in_sets = []
        grad_weight_sets = []
        for grad_produced, weights, kept in zip(
            [own_grad, shared_grad] if owned else [shared_grad], weight_sets, kept_sets
        ):
            grad_incoming, grad_weights = experts_backward(grad_produced, weights, kept)
            grad_in_sets.append(grad_incoming)
            grad_weight_sets.append(grad_weights)
        grad_rows = from_experts(*(grad_in_sets if owned else [None] + grad_in_sets))
        grad_normed_b = head_scatter(mm("tr,rd->td", places, grad_rows))
        pair_dots = mm("td,rd->tr", plane_grads, returned) * places
        plane_grad_gates = mm("er,tr->et", spread.astype(jnp.float32), pair_dots)
        grad_gates = (
            lax.all_to_all(
                jnp.broadcast_to(plane_grad_gates[None], (heads_count, experts_local, all_tokens)),
                "head",
                0,
                0,
                tiled=True,
            )
            .reshape(EXPERTS, all_tokens)
            .T
        )
        grad_logits = gates_all * (
            grad_gates - jnp.sum(gates_all * grad_gates, axis=-1, keepdims=True)
        )
        plane_width = width // heads_count
        grad_router = mm(
            "td,te->de",
            lax.dynamic_slice_in_dim(plane_rows, head_index * plane_width, plane_width, 1),
            grad_logits.astype(jnp.bfloat16),
        )
        own_logits = lax.dynamic_slice_in_dim(grad_logits, head_index * slot_rows, slot_rows, 0)
        grad_normed_b = grad_normed_b + mm(
            "te,de->td", own_logits.astype(jnp.bfloat16), router_full
        )
        grad_norm_b, grad_gain_b = norm_back(grad_normed_b, scaled_b, inverse_b, gains[1:])
        grad_middle = grad_hidden + grad_norm_b
        plane_branch = head_gather((valid_column * grad_middle).astype(jnp.bfloat16))
        grad_out_w = mm("tf,td->fd", attended, plane_branch)
        grad_attended = by_slot(mm("td,fd->tf", plane_branch, out_full).astype(jnp.bfloat16))
        grad_queries, grad_pairs = attention_call(
            functools.partial(
                attend_back_kernel, heads_count, blocks_count, resident, group, kv_local
            ),
            info,
            [queries, pairs_all, grad_attended],
            [
                jax.ShapeDtypeStruct(queries.shape, jnp.bfloat16),
                jax.ShapeDtypeStruct(pairs_all.shape, jnp.bfloat16),
            ],
            [pltpu.VMEM((keys_total, pair_columns), jnp.float32)],
            10 * rows_local * keys_total * query_columns,
            "attend_back",
        )
        grad_pairs = (
            grad_pairs.reshape(SEQUENCE_SLOTS, heads_count, blocks_count, resident, pair_columns)
            .transpose(2, 1, 0, 3, 4)
            .reshape(blocks_count, all_tokens, pair_columns)
        )
        grad_pairs = lax.all_to_all(grad_pairs, "blk", 0, 0, tiled=True)
        grad_pairs = jnp.sum(grad_pairs.astype(jnp.float32), axis=0)
        grad_pairs = grad_pairs.astype(jnp.bfloat16).astype(jnp.float32)
        grad_pairs = grad_pairs.reshape(all_tokens, kv_local, 2, HEAD_SIZE)
        grad_keys = rotate(grad_pairs[:, :, 0].reshape(all_tokens, -1), cosine, -sine)
        grad_projected = jnp.concatenate(
            [
                rotate(by_head(grad_queries).astype(jnp.float32), cosine, -sine),
                jnp.stack(
                    [grad_keys.reshape(all_tokens, kv_local, HEAD_SIZE), grad_pairs[:, :, 1]],
                    axis=2,
                ).reshape(all_tokens, pair_columns),
            ],
            axis=-1,
        ).astype(jnp.bfloat16)
        grad_qkv = mm("td,te->de", plane_normed_a, grad_projected)
        grad_normed_a = head_scatter(mm("te,de->td", grad_projected, qkv_full))
        grad_norm_a, grad_gain_a = norm_back(grad_normed_a, scaled_a, inverse_a, gains[:1])
        grad_hidden = grad_middle + grad_norm_a

        grad_out_w = jnp.concatenate(
            [grad_out_w, jnp.pad(grad_router, ((0, 0), (0, small_columns - EXPERTS)))], axis=1
        ).astype(jnp.bfloat16)
        grad_out_w = lax.psum_scatter(grad_out_w, "blk", scatter_dimension=0, tiled=True)
        out_list[layer_index] = grad_out_w[:, :width].astype(jnp.float32)
        router_list[layer_index] = grad_out_w[:, width : width + EXPERTS].astype(jnp.float32)
        grad_qkv = (
            grad_qkv.astype(jnp.bfloat16)
            .reshape(heads_count, blocks_count, weight_rows, -1)
            .transpose(1, 0, 2, 3)
            .reshape(width, -1)
        )
        grad_qkv = lax.psum_scatter(grad_qkv, "blk", scatter_dimension=0, tiled=True)
        grad_qkv = lax.all_to_all(
            grad_qkv.reshape(heads_count, weight_rows, -1), "head", 0, 0, tiled=True
        ).transpose(1, 0, 2)
        qkv_list[layer_index] = jnp.concatenate(
            [
                grad_qkv[..., :query_columns].reshape(weight_rows, -1),
                grad_qkv[..., query_columns:].reshape(weight_rows, -1),
            ],
            axis=1,
        ).astype(jnp.float32)
        gains_list[layer_index] = jnp.stack([grad_gain_a, grad_gain_b])
        own_and_shared = []
        if owned:
            own_and_shared.append(
                tuple(
                    rows_from_owner(term, blocks_count, owned, blk_index)
                    for term in grad_weight_sets[0]
                )
            )
        if owned_total < experts_local:
            own_and_shared.append(
                tuple(
                    lax.psum_scatter(term, "blk", scatter_dimension=1, tiled=True)
                    for term in grad_weight_sets[-1]
                )
            )
        expert_list[layer_index] = tuple(
            jnp.concatenate(terms, axis=0).astype(jnp.float32) for terms in zip(*own_and_shared)
        )
    devices = heads_count * blocks_count
    grad_gains = jnp.stack(gains_list).reshape(2 * DECODER_LAYERS, devices, weight_rows)
    grad_gains = lax.all_to_all(
        grad_gains.transpose(1, 0, 2).reshape(devices, -1), ("head", "blk"), 0, 0, tiled=True
    )
    grad_gains = jnp.sum(grad_gains, axis=0).reshape(DECODER_LAYERS, 2, weight_rows)
    return (
        result,
        grad_hidden.reshape(tokens.shape),
        jnp.stack(qkv_list),
        jnp.stack(out_list),
        jnp.stack(router_list),
        grad_gains[:, 0],
        grad_gains[:, 1],
        jnp.stack([terms[0] for terms in expert_list]),
        jnp.stack([terms[1] for terms in expert_list]),
    )


def solution(mesh):
    in_specs = (
        P(None, ("head", "blk"), None),
        P(),
        P(None, None, ("head", "blk"), None),
        P(None, None, ("head", "blk"), None),
        P(None, ("head", "blk"), None),
        P(None, ("head", "blk"), None),
        P(None, ("head", "blk"), None),
        P(None, None, ("head", "blk")),
        P(None, "head", "blk", None),
        P(None, "head", "blk", None),
        P(None, ("head", "blk"), None),
    )
    out_specs = (
        P(None, ("head", "blk"), None),
        P(None, ("head", "blk"), None),
        P(None, ("head", "blk"), None),
        P(None, ("head", "blk"), None),
        P(None, ("head", "blk"), None),
        P(None, ("head", "blk")),
        P(None, ("head", "blk")),
        P(None, "head", "blk", None),
        P(None, "head", "blk", None),
    )
    return jax.shard_map(shards, mesh=mesh, in_specs=in_specs, out_specs=out_specs, check_vma=False)
```

time: 3160 us -> 1760 us (0.56)
  waiting for transfers between devices: 1380 us -> 676 us
  blocking collectives: 448 us -> 72.6 us
  other arithmetic: 396 us -> 78.4 us
  Pallas kernels: 0 us -> 288 us
  matrix products: 419 us -> 188 us
  local copies, waits for them, and re-layouts: 317 us -> 189 us
  starting transfers between devices: 160 us -> 241 us
    reduce_scatter x6 -> x4, waiting for transfers between devices: 502 us -> 0.06 us  [the longest x2 0.04 us: shards(): lax.psum_scatter(grad_out_w, 'blk', scatter_dimension=0, tiled=True)]
    pallas_call x0 -> x12, Pallas kernels: none -> 288 us  [the longest x8 241 us: head_gather(): pl.pallas_call(functools.partial(head_gather_kernel, heads), out_shape=ja...]
    unnamed x28 -> x16, waiting for transfers between devices: 271 us -> 1.3 us
    all_gather x4 -> x0, blocking collectives: 264 us -> none  [the longest x2 154 us: shards(): lax.all_gather(router[layer_index], ('head', 'blk'), axis=0, tiled=True)]
    dot_general x110 -> x56, matrix products: 415 us -> 188 us  [mm(): return jnp.einsum(spec, left, right, preferred_element_type=jnp.float32)]
    unnamed x12 -> x1, other arithmetic: 221 us -> 0.01 us
    reduce_scatter x4, waiting for transfers between devices: 145 us -> 0.04 us  [shards(): lax.psum_scatter(term, 'blk', scatter_dimension=1, tiled=True)]
    all_to_all x4 -> x8, waiting for transfers between devices: 93.7 us -> 207 us  [head_scatter(): parts = lax.all_to_all(parts, 'head', 0, 0, tiled=True)]
  transfers between devices with their start and end apart: 103 -> 96, of which waited for: 52 -> 47; matrix products, arithmetic and copies ran while one was open for 24% -> 22% of each run, Pallas kernels for 0% -> 14%
where the time goes in v2:
time: 1760 us; the launch traced here: 1750 us
  waiting for transfers between devices  676 us (38%)
  Pallas kernels  288 us (16%)
  starting transfers between devices  241 us (14%)
  local copies, waits for them, and re-layouts  189 us (11%)
  matrix products  188 us (11%)
  other arithmetic  78.4 us (4%)
  blocking collectives  72.6 us (4%)
    pallas_call x8, Pallas kernels, head_gather(): pl.pallas_call(functools.partial(head_gather_kernel, heads), out_shape=ja...  241 us
    all_to_all x8, waiting for transfers between devices, head_scatter(): parts = lax.all_to_all(parts, 'head', 0, 0, tiled=True)  207 us
    dot_general x56, matrix products, mm(): return jnp.einsum(spec, left, right, preferred_element_type=jnp.float32)  188 us
    ppermute x28, waiting for transfers between devices, rows_from_owner(): piece = lax.ppermute(piece, 'blk', ring(blocks_count, offset))  174 us
    ppermute x28, waiting for transfers between devices, rows_to_owner(): piece = lax.ppermute(piece, 'blk', ring(blocks_count, offset))  125 us
    all_to_all x4, waiting for transfers between devices, from_experts(): own = lax.all_to_all(own, 'blk', 0, 0, tiled=True)  66.2 us
    all_to_all x8, starting transfers between devices, head_scatter(): parts = lax.all_to_all(parts, 'head', 0, 0, tiled=True)  61.1 us
    pallas_call x4, Pallas kernels, attention_call(): pl.pallas_call(kernel, grid_spec=pltpu.PrefetchScalarGridSpec(num_scalar_...  46.8 us
  transfers between devices with their start and end apart: 96, of which 47 were waited for; matrix products, arithmetic and copies ran while one was open for 22% of the time, Pallas kernels for 14%

profile of v2, /device:TPU:0, one launch (start us, length us, event | category | flops | bytes accessed | tf_op | source)
XLA Modules:
  0.0 1748.8 jit_solution(7061245406853938376)
XLA Ops:
  11.1 22.0 %all_to_all.135 = bf16[4,2,48,768]{3,2,1,0:T(8,128)(2,1)S(1)} all-to-all(bf16[4,2,48,768]{3,2,1,0:T(8,128)(2,1)S(1)} %copy.231), channel_id=1, replica_groups=mesh['head'=4,'blk'=8] {'head'}, dimensions={0} | all-to-all | bytes 1179648 | tf_op jit(solution)/shard_map/all_to_all | solution.py:463
  72.9 28.8 %head_gather.8 = bf16[4,128,1536]{2,1,0:T(8,128)(2,1)} custom-call(bf16[128,1536]{1,0:T(8,128)(2,1)} %bitcast.656), custom_call_target="tpu_custom_call" | custom-call | tf_op jit(solution)/shard_map/head_gather/pallas_call | solution.py:121
  142.1 37.5 %collective-permute-done.8 = bf16[1,64,1536]{2,1,0:T(8,128)(2,1)S(1)} collective-permute-done((bf16[1,64,1536]{2,1,0:T(8,128)(2,1)S(1)}, bf16[1,64,1536]{2,1,0:T(8,128)(2,1)S(1)}, u32[]{:S(2)}, u32[]{:S(2)}) %collective-permute-start.8) | collective-permute-done | bytes 196640 | tf_op jit(solution)/shard_map/ppermute | solution.py:74
  231.1 17.4 all-to-all-done.2
  250.6 30.2 %head_gather.9 = bf16[4,128,1536]{2,1,0:T(8,128)(2,1)} custom-call(bf16[128,1536]{1,0:T(8,128)(2,1)} %get-tuple-element.97.own_ref), custom_call_target="tpu_custom_call" | custom-call | tf_op jit(solution)/shard_map/head_gather/pallas_call | solution.py:121
  304.6 31.5 %collective-permute-done.2 = bf16[1,192,1024]{2,1,0:T(8,128)(2,1)S(1)} collective-permute-done((bf16[1,192,1024]{2,1,0:T(8,128)(2,1)}, bf16[1,192,1024]{2,1,0:T(8,128)(2,1)S(1)}, u32[]{:S(2)}, u32[]{:S(2)}) %collective-permute-start.2) | collective-permute-done | bytes 393248 | tf_op jit(solution)/shard_map/ppermute | solution.py:74
  358.5 17.6 %all-to-all-start.4 = ((bf16[8,112,1536]{2,1,0:T(8,128)(2,1)}), bf16[8,112,1536]{2,1,0:T(8,128)(2,1)}, u32[]{:S(2)}, u32[]{:S(2)}) async-start(bf16[8,112,1536]{2,1,0:T(8,128)(2,1)} %bitcast.702), calls=%async_computation.4 | async-start | bytes 5505024 | tf_op jit(solution)/shard_map/all_to_all | solution.py:382
  389.4 22.2 %all-to-all-done.4 = bf16[8,112,1536]{2,1,0:T(8,128)(2,1)} async-done(((bf16[8,112,1536]{2,1,0:T(8,128)(2,1)}), bf16[8,112,1536]{2,1,0:T(8,128)(2,1)}, u32[]{:S(2)}, u32[]{:S(2)}) %all-to-all-start.4) | async-done | bytes 2752544 | tf_op jit(solution)/shard_map/all_to_all | solution.py:382
  435.6 29.0 %all-to-all-done.5 = bf16[4,128,1536]{2,1,0:T(8,128)(2,1)} async-done(((bf16[4,128,1536]{2,1,0:T(8,128)(2,1)}), bf16[4,128,1536]{2,1,0:T(8,128)(2,1)}, u32[]{:S(2)}, u32[]{:S(2)}) %all-to-all-start.5) | async-done | bytes 1572896 | tf_op jit(solution)/shard_map/all_to_all | solution.py:140
  469.7 29.3 %head_gather.10 = bf16[4,128,1536]{2,1,0:T(8,128)(2,1)} custom-call(bf16[128,1536]{1,0:T(8,128)(2,1)} %get-tuple-element.95.own_ref), custom_call_target="tpu_custom_call" | custom-call | tf_op jit(solution)/shard_map/head_gather/pallas_call | solution.py:121
  514.7 23.0 %all-to-all-done.6 = bf16[8,512,256]{2,1,0:T(8,128)(2,1)} async-done(((bf16[8,512,256]{2,1,0:T(8,128)(2,1)}), bf16[8,512,256]{2,1,0:T(8,128)(2,1)}, u32[]{:S(2)}, u32[]{:S(2)}) %all-to-all-start.6) | async-done | bytes 2097184 | tf_op jit(solution)/shard_map/all_to_all | solution.py:493
  566.7 33.1 %all-to-all-done.7 = bf16[4,128,1536]{2,1,0:T(8,128)(2,1)} async-done(((bf16[4,128,1536]{2,1,0:T(8,128)(2,1)}), bf16[4,128,1536]{2,1,0:T(8,128)(2,1)}, u32[]{:S(2)}, u32[]{:S(2)}) %all-to-all-start.7) | async-done | bytes 1572896 | tf_op jit(solution)/shard_map/all_to_all | solution.py:140
  603.3 29.3 %head_gather.11 = bf16[4,128,1536]{2,1,0:T(8,128)(2,1)} custom-call(bf16[128,1536]{1,0:T(8,128)(2,1)} %get-tuple-element.93.own_ref), custom_call_target="tpu_custom_call" | custom-call | tf_op jit(solution)/shard_map/head_gather/pallas_call | solution.py:121
  654.5 36.4 %collective-permute-done.14 = bf16[1,192,1024]{2,1,0:T(8,128)(2,1)} collective-permute-done((bf16[1,192,1024]{2,1,0:T(8,128)(2,1)}, bf16[1,192,1024]{2,1,0:T(8,128)(2,1)}, u32[]{:S(2)}, u32[]{:S(2)}) %collective-permute-start.14) | collective-permute-done | bytes 393248 | tf_op jit(solution)/shard_map/ppermute | solution.py:74
  741.9 35.7 %head_gather.12 = bf16[4,128,1536]{2,1,0:T(8,128)(2,1)} custom-call(bf16[128,1536]{1,0:T(8,128)(2,1)} %get-tuple-element.213.own_ref), custom_call_target="tpu_custom_call" | custom-call | tf_op jit(solution)/shard_map/head_gather/pallas_call | solution.py:121
  819.2 37.5 %all_to_all.136 = bf16[8,112,1536]{2,1,0:T(8,128)(2,1)S(1)} all-to-all(bf16[8,112,1536]{2,1,0:T(8,128)(2,1)S(1)} %bitcast.666), channel_id=1, replica_groups=mesh['head'=4,'blk'=8] {'blk'}, dimensions={0} | all-to-all | bytes 5505024 | tf_op jit(solution)/shard_map/all_to_all | solution.py:372
  881.7 25.0 %all-to-all-done.12 = bf16[8,112,1536]{2,1,0:T(8,128)(2,1)} async-done(((bf16[8,112,1536]{2,1,0:T(8,128)(2,1)}), bf16[8,112,1536]{2,1,0:T(8,128)(2,1)}, u32[]{:S(2)}, u32[]{:S(2)}) %all-to-all-start.12) | async-done | bytes 2752544 | tf_op jit(solution)/shard_map/all_to_all | solution.py:382
  917.1 34.3 %all-to-all-done.13 = bf16[4,128,1536]{2,1,0:T(8,128)(2,1)} async-done(((bf16[4,128,1536]{2,1,0:T(8,128)(2,1)}), bf16[4,128,1536]{2,1,0:T(8,128)(2,1)}, u32[]{:S(2)}, u32[]{:S(2)}) %all-to-all-start.13) | async-done | bytes 1572896 | tf_op jit(solution)/shard_map/all_to_all | solution.py:140
  956.5 29.3 %head_gather.13 = bf16[4,128,1536]{2,1,0:T(8,128)(2,1)} custom-call(bf16[128,1536]{1,0:T(8,128)(2,1)} %get-tuple-element.89.own_ref), custom_call_target="tpu_custom_call" | custom-call | tf_op jit(solution)/shard_map/head_gather/pallas_call | solution.py:121
  1018.7 20.9 %all-to-all-done.15 = bf16[8,512,256]{2,1,0:T(8,128)(2,1)S(1)} async-done(((bf16[8,512,256]{2,1,0:T(8,128)(2,1)}), bf16[8,512,256]{2,1,0:T(8,128)(2,1)S(1)}, u32[]{:S(2)}, u32[]{:S(2)}) %all-to-all-start.15) | async-done | bytes 2097184 | tf_op jit(solution)/shard_map/all_to_all | solution.py:646
  1095.0 29.7 %all-to-all-done.16 = bf16[4,128,1536]{2,1,0:T(8,128)(2,1)} async-done(((bf16[4,128,1536]{2,1,0:T(8,128)(2,1)}), bf16[4,128,1536]{2,1,0:T(8,128)(2,1)}, u32[]{:S(2)}, u32[]{:S(2)}) %all-to-all-start.16) | async-done | bytes 1572896 | tf_op jit(solution)/shard_map/all_to_all | solution.py:140
  1130.6 29.3 %head_gather.14 = bf16[4,128,1536]{2,1,0:T(8,128)(2,1)} custom-call(bf16[128,1536]{1,0:T(8,128)(2,1)} %get-tuple-element.87.own_ref), custom_call_target="tpu_custom_call" | custom-call | tf_op jit(solution)/shard_map/head_gather/pallas_call | solution.py:121
  1174.4 30.6 %all-to-all-done.17 = bf16[8,112,1536]{2,1,0:T(8,128)(2,1)} async-done(((bf16[8,112,1536]{2,1,0:T(8,128)(2,1)}), bf16[8,112,1536]{2,1,0:T(8,128)(2,1)}, u32[]{:S(2)}, u32[]{:S(2)}) %all-to-all-start.17) | async-done | bytes 2752544 | tf_op jit(solution)/shard_map/all_to_all | solution.py:372
  1238.5 19.0 %all-to-all-done.18 = bf16[8,112,1536]{2,1,0:T(8,128)(2,1)} async-done(((bf16[8,112,1536]{2,1,0:T(8,128)(2,1)}), bf16[8,112,1536]{2,1,0:T(8,128)(2,1)}, u32[]{:S(2)}, u32[]{:S(2)}) %all-to-all-start.18) | async-done | bytes 2752544 | tf_op jit(solution)/shard_map/all_to_all | solution.py:382
  1280.3 32.4 %all-to-all-done.19 = bf16[4,128,1536]{2,1,0:T(8,128)(2,1)} async-done(((bf16[4,128,1536]{2,1,0:T(8,128)(2,1)}), bf16[4,128,1536]{2,1,0:T(8,128)(2,1)}, u32[]{:S(2)}, u32[]{:S(2)}) %all-to-all-start.19) | async-done | bytes 1572896 | tf_op jit(solution)/shard_map/all_to_all | solution.py:140
  1317.8 29.3 %head_gather.15 = bf16[4,128,1536]{2,1,0:T(8,128)(2,1)} custom-call(bf16[128,1536]{1,0:T(8,128)(2,1)} %get-tuple-element.85.own_ref), custom_call_target="tpu_custom_call" | custom-call | tf_op jit(solution)/shard_map/head_gather/pallas_call | solution.py:121
  1373.7 15.2 collective-permute-done.49
  1468.1 17.5 %all-to-all-start.24 = ((bf16[4,48,640]{2,1,0:T(8,128)(2,1)}), bf16[4,48,640]{2,1,0:T(8,128)(2,1)S(1)}, u32[]{:S(2)}, u32[]{:S(2)}) async-start(bf16[4,48,640]{2,1,0:T(8,128)(2,1)} %bitcast.778), calls=%async_computation.26 | async-start | bytes 491520 | tf_op jit(solution)/shard_map/all_to_all | solution.py:679
  1538.2 26.4 %collective-permute-done.44 = bf16[1,64,1536]{2,1,0:T(8,128)(2,1)S(1)} collective-permute-done((bf16[1,64,1536]{2,1,0:T(8,128)(2,1)S(1)}, bf16[1,64,1536]{2,1,0:T(8,128)(2,1)S(1)}, u32[]{:S(2)}, u32[]{:S(2)}) %collective-permute-start.44) | collective-permute-done | bytes 196640 | tf_op jit(solution)/shard_map/ppermute | solution.py:87
  1594.1 14.9 attend_back.3
  1625.0 25.6 %collective-permute-done.33 = bf16[1,192,1024]{2,1,0:T(8,128)(2,1)S(1)} collective-permute-done((bf16[1,192,1024]{2,1,0:T(8,128)(2,1)}, bf16[1,192,1024]{2,1,0:T(8,128)(2,1)S(1)}, u32[]{:S(2)}, u32[]{:S(2)}) %collective-permute-start.33) | collective-permute-done | bytes 393248 | tf_op jit(solution)/shard_map/ppermute | solution.py:87
  1697.0 17.0 all-to-all-done.22
  (840 shorter events, 874.6 us)
Async XLA Ops:
  7.2 115.8 %all-gather.17.cloned.1.call-start = ((), (), s32[]{:S(2)}) async-start(), calls=%async_computation.42 | async-start | bytes 2654208 | tf_op jit(solution)/shard_map/all_gather | solution.py:466
  34.7 164.4 %all-gather.19.cloned.1.call-start = ((), (), s32[]{:S(2)}) async-start(), calls=%async_computation.43 | async-start | bytes 1327104 | tf_op jit(solution)/shard_map/all_gather | solution.py:467
  35.6 346.3 %all-gather.21.cloned.1.call-start = ((), (), s32[]{:S(2)}) async-start(), calls=%async_computation.44 | async-start | bytes 7077888 | tf_op jit(solution)/shard_map/all_gather | solution.py:398
  38.3 348.5 %all-gather.23.cloned.1.call-start = ((), (), s32[]{:S(2)}) async-start(), calls=%async_computation.45 | async-start | bytes 3538944 | tf_op jit(solution)/shard_map/all_gather | solution.py:398
  43.8 77.5 %collective-permute-start.21 = (bf16[1,64,1536]{2,1,0:T(8,128)(2,1)S(1)}, bf16[1,64,1536]{2,1,0:T(8,128)(2,1)}, u32[]{:S(2)}, u32[]{:S(2)}) collective-permute-start(bf16[1,64,1536]{2,1,0:T(8,128)(2,1)S(1)} %get-tuple-element.159), channel_id=1, source_target_pairs={{0,1},{1,2},{2,3},{3,4},{4,5},{5,6},{6,7},{7,0},{8,9},{9,10},{10,1... | collective-permute-start | bytes 589832 | tf_op jit(solution)/shard_map/ppermute | solution.py:74
  43.8 96.7 %collective-permute-start.22 = (bf16[1,64,1536]{2,1,0:T(8,128)(2,1)}, bf16[1,64,1536]{2,1,0:T(8,128)(2,1)}, u32[]{:S(2)}, u32[]{:S(2)}) collective-permute-start(bf16[1,64,1536]{2,1,0:T(8,128)(2,1)} %get-tuple-element.158), channel_id=1, source_target_pairs={{0,2},{1,3},{2,4},{3,5},{4,6},{5,7},{6,0},{7,1},{8,10},{9,11},{10,... | collective-permute-start | bytes 589832 | tf_op jit(solution)/shard_map/ppermute | solution.py:74
  45.4 135.0 %collective-permute-start.23 = (bf16[1,64,1536]{2,1,0:T(8,128)(2,1)}, bf16[1,64,1536]{2,1,0:T(8,128)(2,1)}, u32[]{:S(2)}, u32[]{:S(2)}) collective-permute-start(bf16[1,64,1536]{2,1,0:T(8,128)(2,1)} %get-tuple-element.157), channel_id=1, source_target_pairs={{0,3},{1,4},{2,5},{3,6},{4,7},{5,0},{6,1},{7,2},{8,11},{9,12},{10,... | collective-permute-start | bytes 589832 | tf_op jit(solution)/shard_map/ppermute | solution.py:74
  47.7 165.5 %collective-permute-start.24 = (bf16[1,64,1536]{2,1,0:T(8,128)(2,1)}, bf16[1,64,1536]{2,1,0:T(8,128)(2,1)}, u32[]{:S(2)}, u32[]{:S(2)}) collective-permute-start(bf16[1,64,1536]{2,1,0:T(8,128)(2,1)} %get-tuple-element.156), channel_id=1, source_target_pairs={{0,4},{1,5},{2,6},{3,7},{4,0},{5,1},{6,2},{7,3},{8,12},{9,13},{10,... | collective-permute-start | bytes 589832 | tf_op jit(solution)/shard_map/ppermute | solution.py:74
  48.3 171.7 %collective-permute-start.25 = (bf16[1,64,1536]{2,1,0:T(8,128)(2,1)}, bf16[1,64,1536]{2,1,0:T(8,128)(2,1)}, u32[]{:S(2)}, u32[]{:S(2)}) collective-permute-start(bf16[1,64,1536]{2,1,0:T(8,128)(2,1)} %get-tuple-element.155), channel_id=1, source_target_pairs={{0,5},{1,6},{2,7},{3,0},{4,1},{5,2},{6,3},{7,4},{8,13},{9,14},{10,... | collective-permute-start | bytes 589832 | tf_op jit(solution)/shard_map/ppermute | solution.py:74
  136.9 86.0 %collective-permute-start.26 = (bf16[1,64,1536]{2,1,0:T(8,128)(2,1)}, bf16[1,64,1536]{2,1,0:T(8,128)(2,1)}, u32[]{:S(2)}, u32[]{:S(2)}) collective-permute-start(bf16[1,64,1536]{2,1,0:T(8,128)(2,1)} %get-tuple-element.154), channel_id=1, source_target_pairs={{0,6},{1,7},{2,0},{3,1},{4,2},{5,3},{6,4},{7,5},{8,14},{9,15},{10,... | collective-permute-start | bytes 589832 | tf_op jit(solution)/shard_map/ppermute | solution.py:74
  179.7 115.0 %collective-permute-start.27 = (bf16[1,64,1536]{2,1,0:T(8,128)(2,1)}, bf16[1,64,1536]{2,1,0:T(8,128)(2,1)}, u32[]{:S(2)}, u32[]{:S(2)}) collective-permute-start(bf16[1,64,1536]{2,1,0:T(8,128)(2,1)} %get-tuple-element.153), channel_id=1, source_target_pairs={{0,7},{1,0},{2,1},{3,2},{4,3},{5,4},{6,5},{7,6},{8,15},{9,8},{10,9... | collective-permute-start | bytes 589832 | tf_op jit(solution)/shard_map/ppermute | solution.py:74
  210.2 221.1 %all-gather.25.cloned.1.call-start = ((), (), s32[]{:S(2)}) async-start(), calls=%async_computation.46 | async-start | bytes 2654208 | tf_op jit(solution)/shard_map/all_gather | solution.py:466
  218.0 73.4 %collective-permute-start.12 = (bf16[1,64,1536]{2,1,0:T(8,128)(2,1)}, bf16[1,64,1536]{2,1,0:T(8,128)(2,1)}, u32[]{:S(2)}, u32[]{:S(2)}) collective-permute-start(bf16[1,64,1536]{2,1,0:T(8,128)(2,1)} %get-tuple-element.161), channel_id=1, source_target_pairs={{0,6},{1,7},{2,0},{3,1},{4,2},{5,3},{6,4},{7,5},{8,14},{9,15},{10,... | collective-permute-start | bytes 589832 | tf_op jit(solution)/shard_map/ppermute | solution.py:74
  220.0 76.2 %collective-permute-start.13 = (bf16[1,64,1536]{2,1,0:T(8,128)(2,1)}, bf16[1,64,1536]{2,1,0:T(8,128)(2,1)}, u32[]{:S(2)}, u32[]{:S(2)}) collective-permute-start(bf16[1,64,1536]{2,1,0:T(8,128)(2,1)} %get-tuple-element.160), channel_id=1, source_target_pairs={{0,7},{1,0},{2,1},{3,2},{4,3},{5,4},{6,5},{7,6},{8,15},{9,8},{10,9... | collective-permute-start | bytes 589832 | tf_op jit(solution)/shard_map/ppermute | solution.py:74
  221.9 76.4 %collective-permute-start = (bf16[1,192,1024]{2,1,0:T(8,128)(2,1)}, bf16[1,192,1024]{2,1,0:T(8,128)(2,1)}, u32[]{:S(2)}, u32[]{:S(2)}) collective-permute-start(bf16[1,192,1024]{2,1,0:T(8,128)(2,1)} %get-tuple-element.138), channel_id=1, source_target_pairs={{0,1},{1,2},{2,3},{3,4},{4,5},{5,6},{6,7},{7,0},{8,9},{9,10},{10,1... | collective-permute-start | bytes 1179656 | tf_op jit(solution)/shard_map/ppermute | solution.py:74
  222.8 78.7 %collective-permute-start.1 = (bf16[1,192,1024]{2,1,0:T(8,128)(2,1)}, bf16[1,192,1024]{2,1,0:T(8,128)(2,1)}, u32[]{:S(2)}, u32[]{:S(2)}) collective-permute-start(bf16[1,192,1024]{2,1,0:T(8,128)(2,1)} %get-tuple-element.137), channel_id=1, source_target_pairs={{0,2},{1,3},{2,4},{3,5},{4,6},{5,7},{6,0},{7,1},{8,10},{9,11},{10,... | collective-permute-start | bytes 1179656 | tf_op jit(solution)/shard_map/ppermute | solution.py:74
  376.1 174.3 %all-gather.27.cloned.1.call-start = ((), (), s32[]{:S(2)}) async-start(), calls=%async_computation.47 | async-start | bytes 1327104 | tf_op jit(solution)/shard_map/all_gather | solution.py:467
  430.6 347.1 %all-gather.29.cloned.1.call-start = ((), (), s32[]{:S(2)}) async-start(), calls=%async_computation.48 | async-start | bytes 7077888 | tf_op jit(solution)/shard_map/all_gather | solution.py:398
  638.7 84.6 %all-to-all-start.8 = ((bf16[8,112,1536]{2,1,0:T(8,128)(2,1)}), bf16[8,112,1536]{2,1,0:T(8,128)(2,1)}, u32[]{:S(2)}, u32[]{:S(2)}) async-start(bf16[8,112,1536]{2,1,0:T(8,128)(2,1)} %bitcast.663), calls=%async_computation.8 | async-start | bytes 5505024 | tf_op jit(solution)/shard_map/all_to_all | solution.py:372
  643.9 138.7 %all-gather.31.cloned.1.call-start = ((), (), s32[]{:S(2)}) async-start(), calls=%async_computation.49 | async-start | bytes 3538944 | tf_op jit(solution)/shard_map/all_gather | solution.py:398
  1049.6 412.3 %reduce-scatter.15.cloned.1.call-start = ((), (), s32[]{:S(2)}) async-start(), calls=%async_computation.37 | async-start | bytes 1437696 | tf_op jit(solution)/shard_map/reduce_scatter | solution.py:669
  1088.2 379.8 %reduce-scatter.11.cloned.1.call-start = ((), (), s32[]{:S(2)}) async-start(), calls=%async_computation.35 | async-start | bytes 2211840 | tf_op jit(solution)/shard_map/reduce_scatter | solution.py:678
  1171.2 509.3 %reduce-scatter.23.cloned.1.call-start = ((), (), s32[]{:S(2)}) async-start(), calls=%async_computation.41 | async-start | bytes 3538944 | tf_op jit(solution)/shard_map/reduce_scatter | solution.py:701
  1219.6 460.9 %reduce-scatter.21.cloned.1.call-start = ((), (), s32[]{:S(2)}) async-start(), calls=%async_computation.40 | async-start | bytes 3538944 | tf_op jit(solution)/shard_map/reduce_scatter | solution.py:701
  1278.6 407.0 %reduce-scatter.13.cloned.1.call-start = ((), (), s32[]{:S(2)}) async-start(), calls=%async_computation.36 | async-start | bytes 1437696 | tf_op jit(solution)/shard_map/reduce_scatter | solution.py:669
  1350.6 338.3 %reduce-scatter.19.cloned.1.call-start = ((), (), s32[]{:S(2)}) async-start(), calls=%async_computation.39 | async-start | bytes 7077888 | tf_op jit(solution)/shard_map/reduce_scatter | solution.py:701
  1355.2 333.7 %reduce-scatter.17.cloned.1.call-start = ((), (), s32[]{:S(2)}) async-start(), calls=%async_computation.38 | async-start | bytes 7077888 | tf_op jit(solution)/shard_map/reduce_scatter | solution.py:701
  1362.6 73.7 %collective-permute-start.36 = (bf16[1,192,1024]{2,1,0:T(8,128)(2,1)S(1)}, bf16[1,192,1024]{2,1,0:T(8,128)(2,1)S(1)}, u32[]{:S(2)}, u32[]{:S(2)}) collective-permute-start(bf16[1,192,1024]{2,1,0:T(8,128)(2,1)S(1)} %get-tuple-element.123), channel_id=1, source_target_pairs={{0,2},{1,3},{2,4},{3,5},{4,6},{5,7},{6,0},{7,1},{8,10},{9,11},{10,... | collective-permute-start | bytes 1179656 | tf_op jit(solution)/shard_map/ppermute | solution.py:87
  1503.6 113.0 %collective-permute-start.28 = (bf16[1,192,1024]{2,1,0:T(8,128)(2,1)}, bf16[1,192,1024]{2,1,0:T(8,128)(2,1)}, u32[]{:S(2)}, u32[]{:S(2)}) collective-permute-start(bf16[1,192,1024]{2,1,0:T(8,128)(2,1)} %get-tuple-element.117), channel_id=1, source_target_pairs={{0,1},{1,2},{2,3},{3,4},{4,5},{5,6},{6,7},{7,0},{8,9},{9,10},{10,1... | collective-permute-start | bytes 1179656 | tf_op jit(solution)/shard_map/ppermute | solution.py:87
  1503.6 116.9 %collective-permute-start.29 = (bf16[1,192,1024]{2,1,0:T(8,128)(2,1)}, bf16[1,192,1024]{2,1,0:T(8,128)(2,1)}, u32[]{:S(2)}, u32[]{:S(2)}) collective-permute-start(bf16[1,192,1024]{2,1,0:T(8,128)(2,1)} %get-tuple-element.116), channel_id=1, source_target_pairs={{0,2},{1,3},{2,4},{3,5},{4,6},{5,7},{6,0},{7,1},{8,10},{9,11},{10,... | collective-permute-start | bytes 1179656 | tf_op jit(solution)/shard_map/ppermute | solution.py:87
  1504.1 117.7 %collective-permute-start.30 = (bf16[1,192,1024]{2,1,0:T(8,128)(2,1)}, bf16[1,192,1024]{2,1,0:T(8,128)(2,1)}, u32[]{:S(2)}, u32[]{:S(2)}) collective-permute-start(bf16[1,192,1024]{2,1,0:T(8,128)(2,1)} %get-tuple-element.115), channel_id=1, source_target_pairs={{0,3},{1,4},{2,5},{3,6},{4,7},{5,0},{6,1},{7,2},{8,11},{9,12},{10,... | collective-permute-start | bytes 1179656 | tf_op jit(solution)/shard_map/ppermute | solution.py:87
  1505.7 117.2 %collective-permute-start.31 = (bf16[1,192,1024]{2,1,0:T(8,128)(2,1)}, bf16[1,192,1024]{2,1,0:T(8,128)(2,1)}, u32[]{:S(2)}, u32[]{:S(2)}) collective-permute-start(bf16[1,192,1024]{2,1,0:T(8,128)(2,1)} %get-tuple-element.114), channel_id=1, source_target_pairs={{0,4},{1,5},{2,6},{3,7},{4,0},{5,1},{6,2},{7,3},{8,12},{9,13},{10,... | collective-permute-start | bytes 1179656 | tf_op jit(solution)/shard_map/ppermute | solution.py:87
  (208 other events, 5203.7 us)
Sparse Core Ops, SparseCore 0:
  34.9 38.0 all-gather.16
  74.8 22.3 all-gather.18
  99.2 51.2 all-gather.20
  152.2 39.7 all-gather.22
  231.3 31.5 all-gather.24
  378.5 37.6 all-gather.26
  433.9 45.4 all-gather.28
  646.6 70.6 all-gather.30
  1061.7 36.4 reduce-scatter.14
  1101.8 40.2 reduce-scatter.10
  1175.4 61.4 reduce-scatter.22
  1241.1 48.6 reduce-scatter.20
  1350.7 62.5 reduce-scatter.12
  1417.5 81.0 reduce-scatter.18
  1501.8 80.2 reduce-scatter.16
  1680.6 41.7 reduce-scatter.8

commit v3 on v2

--- a/solution.py
+++ b/solution.py
@@ -59,85 +59,642 @@
     return (grad_hidden, grad_gain)
 
 
-def ring(count, offset):
-    return [(i, (i + offset) % count) for i in range(count)]
-
-
-def rows_to_owner(matrices, blocks_count, owned, blk_index):
-    rows, columns = matrices.shape[1:]
-    whole = jnp.zeros((owned, blocks_count * rows, columns), matrices.dtype)
-    for offset in range(blocks_count):
-        target = (blk_index + offset) % blocks_count
-        origin = (blk_index - offset) % blocks_count
-        piece = lax.dynamic_slice_in_dim(matrices, target * owned, owned, 0)
-        if offset:
-            piece = lax.ppermute(piece, "blk", ring(blocks_count, offset))
-        whole = lax.dynamic_update_slice_in_dim(whole, piece, origin * rows, 1)
-    return whole
-
-
-def rows_from_owner(whole, blocks_count, owned, blk_index):
-    rows = whole.shape[1] // blocks_count
-    matrices = jnp.zeros((owned * blocks_count, rows, whole.shape[2]), whole.dtype)
-    for offset in range(blocks_count):
-        target = (blk_index + offset) % blocks_count
-        origin = (blk_index - offset) % blocks_count
-        piece = lax.dynamic_slice_in_dim(whole, target * rows, rows, 1)
-        if offset:
-            piece = lax.ppermute(piece, "blk", ring(blocks_count, offset))
-        matrices = lax.dynamic_update_slice_in_dim(matrices, piece, origin * owned, 0)
-    return matrices
-
-
-def head_gather_kernel(heads, own_ref, all_ref, send_sems, recv_sems, local_sem):
+def exchange_kernel(heads, blocks, items, waited, *refs):
+    count = len(items)
+    sources = refs[:count]
+    targets = refs[count + waited : 2 * count + waited]
+    send_sems, recv_sems, local_sems = refs[2 * count + waited :]
     head = lax.axis_index("head")
     blk = lax.axis_index("blk")
-    peers = [lax.rem(head + step, heads) for step in range(1, heads)]
+    chips = blocks // 2
+    chip, core = blk // 2, lax.rem(blk, 2)
+    sibling = chip * 2 + 1 - core
+    kinds = {kind for kind, _ in items}
+    head_peers = [(lax.rem(head + step, heads), blk) for step in range(1, heads)]
+    blk_peers = [(head, lax.rem(blk + step, blocks)) for step in range(1, blocks)]
+    pair_peers = [
+        (head, lax.rem(chip + step, chips) * 2 + core) for step in range(1, chips)
+    ] + [(head, sibling)]
+    greeted = []
+    if kinds & {"head_gather", "head_swap"}:
+        greeted += head_peers
+    if "blk_swap" in kinds:
+        greeted += blk_peers
+    elif "blk_pairs" in kinds:
+        greeted += pair_peers
+    barrier = pltpu.get_barrier_semaphore()
+    for peer in greeted:
+        pl.semaphore_signal(barrier, inc=1, device_id=peer, device_id_type=MESH)
+    pl.semaphore_wait(barrier, len(greeted))
+    used = 0
+    copies = []
+    forwards = []
+
+    def send(source, target, peer):
+        nonlocal used
+        copy = pltpu.make_async_remote_copy(
+            src_ref=source,
+            dst_ref=target,
+            send_sem=send_sems.at[used],
+            recv_sem=recv_sems.at[used],
+            device_id=peer,
+            device_id_type=MESH,
+        )
+        copy.start()
+        used += 1
+        return copy
+
+    locals_started = []
+    for number, (kind, layer) in enumerate(items):
+        source, target = sources[number], targets[number]
+
+        def piece(index, source=source, layer=layer):
+            return source.at[index] if layer is None else source.at[layer, index]
+
+        if kind == "head_gather":
+            mine, place = source, head
+            copies += [send(source, target.at[head], peer) for peer in head_peers]
+        elif kind == "head_swap":
+            mine, place = piece(head), head
+            copies += [send(piece(peer[0]), target.at[head], peer) for peer in head_peers]
+        elif kind == "blk_swap":
+            mine, place = piece(blk), blk
+            copies += [send(piece(peer[1]), target.at[blk], peer) for peer in blk_peers]
+        else:
+            mine, place = source, blk
+            sent = [send(source, target.at[blk], peer) for peer in pair_peers]
+            copies += sent[-1:]
+            forwards.append((sent[:-1], target))
+        local = pltpu.make_async_copy(mine, target.at[place], local_sems.at[number])
+        local.start()
+        locals_started.append(local)
+    for sent, target in forwards:
+        for step, copy in enumerate(sent, start=1):
+            copy.wait_recv()
+            origin = lax.rem(chip + chips - step, chips) * 2 + core
+            copies.append(send(target.at[origin], target.at[origin], (head, sibling)))
+    for sent, _ in forwards:
+        for copy in sent:
+            copy.wait_send()
+    for local in locals_started:
+        local.wait()
+    for copy in copies:
+        copy.wait()
+
+
+kernel_numbers = {}
+
+
+def kernel_number(*key):
+    return kernel_numbers.setdefault(key, 1 + len(kernel_numbers))
+
+
+def exchange(*items, after=()):
+    heads, blocks = lax.axis_size("head"), lax.axis_size("blk")
+    arrays = [item[1] for item in items]
+    plan = [(item[0], item[2] if len(item) > 2 else None) for item in items]
+    outs = []
+    total = 0
+    for (kind, layer), array in zip(plan, arrays):
+        group = heads if kind.startswith("head") else blocks
+        tail = array.shape
+        if kind.endswith("swap"):
+            tail = tail[1:] if layer is None else tail[2:]
+        outs.append(jax.ShapeDtypeStruct((group,) + tail, array.dtype))
+        total += group - 1
+    collective_id = kernel_number(
+        "exchange", tuple(plan), *((array.shape, str(array.dtype)) for array in (*arrays, *after))
+    )
+    results = pl.pallas_call(
+        functools.partial(exchange_kernel, heads, blocks, plan, len(after)),
+        out_shape=outs,
+        in_specs=[pl.BlockSpec(memory_space=pl.ANY)] * (len(arrays) + len(after)),
+        out_specs=[pl.BlockSpec(memory_space=pl.ANY)] * len(arrays),
+        scratch_shapes=[
+            pltpu.SemaphoreType.DMA((total,)),
+            pltpu.SemaphoreType.DMA((total,)),
+            pltpu.SemaphoreType.DMA((len(arrays),)),
+        ],
+        compiler_params=pltpu.CompilerParams(collective_id=collective_id, has_side_effects=True),
+        cost_estimate=pl.CostEstimate(flops=0, bytes_accessed=110 << 20, transcendentals=0),
+        name="exchange",
+    )(*arrays, *after)
+    return results
+
+
+def greet(peers):
     barrier = pltpu.get_barrier_semaphore()
     for peer in peers:
-        pl.semaphore_signal(barrier, inc=1, device_id=(peer, blk), device_id_type=MESH)
-    pl.semaphore_wait(barrier, heads - 1)
-    copies = []
-    for step, peer in enumerate(peers):
-        copy = pltpu.make_async_remote_copy(
-            src_ref=own_ref,
-            dst_ref=all_ref.at[head],
-            send_sem=send_sems.at[step],
-            recv_sem=recv_sems.at[step],
-            device_id=(peer, blk),
-            device_id_type=MESH,
-        )
-        copy.start()
-        copies.append(copy)
-    local = pltpu.make_async_copy(own_ref, all_ref.at[head], local_sem)
-    local.start()
-    local.wait()
-    for copy in copies:
+        pl.semaphore_signal(barrier, inc=1, device_id=peer, device_id_type=MESH)
+    pl.semaphore_wait(barrier, len(peers))
+
+
+def plane_peers(heads, blocks):
+    head = lax.axis_index("head")
+    blk = lax.axis_index("blk")
+    head_peers = [(lax.rem(head + step, heads), blk) for step in range(1, heads)]
+    blk_peers = [(head, lax.rem(blk + step, blocks)) for step in range(1, blocks)]
+    return head, blk, head_peers, blk_peers
+
+
+def remote(source, target, sems, index, peer, landing=None):
+    return pltpu.make_async_remote_copy(
+        src_ref=source,
+        dst_ref=target,
+        send_sem=sems[0].at[index],
+        recv_sem=sems[1].at[index if landing is None else landing],
+        device_id=peer,
+        device_id_type=MESH,
+    )
+
+
+def started(copy):
+    copy.start()
+    return copy
+
+
+def weight_part(ref, columns, by_columns):
+    return ref[:, columns] if by_columns else ref[columns, :]
+
+
+def meet(left, part, by_columns):
+    return (
+        dot_last(left, part)
+        if by_columns
+        else jnp.dot(left, part, preferred_element_type=jnp.float32)
+    )
+
+
+def dispatch_kernel(
+    heads,
+    blocks,
+    pieces,
+    window,
+    by_columns,
+    own_ref,
+    place_ref,
+    weight_ref,
+    shared_weight_ref,
+    plane_ref,
+    queue_ref,
+    shared_ref,
+    out_ref,
+    shared_out_ref,
+    send_ref,
+    held_ref,
+    shared_held_ref,
+    head_send,
+    head_recv,
+    blk_send,
+    blk_recv,
+    local_sems,
+):
+    head, blk, head_peers, blk_peers = plane_peers(heads, blocks)
+    rows, width = own_ref.shape
+    slot = queue_ref.shape[1]
+    shared = shared_ref.shape[0]
+    step_width = width // pieces
+    outputs = out_ref.shape[1]
+    tile = 256
+    greet(head_peers + blk_peers)
+    loads = [
+        pltpu.make_async_copy(weight_ref, held_ref, local_sems.at[0]),
+        pltpu.make_async_copy(shared_weight_ref, shared_held_ref, local_sems.at[1]),
+    ]
+    for load in loads:
+        load.start()
+    head_copies = []
+    blk_copies = []
+
+    def far(peer):
+        return jnp.abs(peer[0] - head) == heads - 1
+
+    relay = heads == 4
+    inner = jnp.logical_and(head > 0, head < heads - 1)
+    relayed = []
+
+    def spread(piece):
+        columns = pl.ds(piece * step_width, step_width)
+        copies = []
+        for number, peer in enumerate(head_peers):
+            copy = remote(
+                own_ref.at[:, columns],
+                plane_ref.at[head, :, columns],
+                (head_send, head_recv),
+                piece * heads + number,
+                peer,
+            )
+            copies.append(copy)
+            if relay and number != 1:
+                pl.when(jnp.logical_not(far(peer)))(copy.start)
+            else:
+                copy.start()
+        head_copies.append(copies)
+
+    def pass_on(piece):
+        columns = pl.ds(piece * step_width, step_width)
+        origin = lax.rem(head + 2, heads)
+        rows_there = plane_ref.at[origin, :, columns]
+        copy = remote(
+            rows_there,
+            rows_there,
+            (head_send, head_recv),
+            piece * heads + heads - 1,
+            ((head - 1) * (heads - 1), blk),
+            piece * heads + jnp.where(head == 1, 0, heads - 2),
+        )
+        relayed.append(copy)
+        pl.when(inner)(copy.start)
+
+    for piece in range(min(window, pieces)):
+        spread(piece)
+    plane_ref[head] = own_ref[...]
+
+    def consume(piece):
+        columns = pl.ds(piece * step_width, step_width)
+        for copy in blk_copies[piece]:
+            copy.wait_recv()
+        queue = queue_ref[:, :, columns].reshape(blocks * slot, step_width)
+
+        def one_tile(index, carry):
+            lanes = pl.ds(pl.multiple_of(index * tile, tile), tile)
+            if by_columns:
+                product = dot_last(queue, held_ref[lanes, columns])
+            else:
+                product = jnp.dot(
+                    queue, held_ref[columns, lanes], preferred_element_type=jnp.float32
+                )
+            if piece:
+                product = product + out_ref[:, lanes]
+            out_ref[:, lanes] = product
+            return carry
+
+        lax.fori_loop(0, outputs // tile, one_tile, 0)
+
+    for piece in range(pieces):
+        columns = pl.ds(piece * step_width, step_width)
+        if relay:
+            head_copies[piece][1].wait_recv()
+            pass_on(piece)
+        for number, copy in enumerate(head_copies[piece]):
+            if not relay or number != 1:
+                copy.wait_recv()
+        if piece + window < pieces:
+            spread(piece + window)
+        plane = plane_ref[:, :, columns].reshape(heads * rows, step_width)
+
+        def fill(expert, carry):
+            start = pl.multiple_of(expert * slot, 16)
+            send_ref[expert, :, columns] = jnp.dot(
+                place_ref[pl.ds(start, slot), :], plane, preferred_element_type=jnp.float32
+            ).astype(send_ref.dtype)
+            return carry
+
+        lax.fori_loop(0, blocks, fill, 0)
+        blk_copies.append(
+            [
+                started(
+                    remote(
+                        send_ref.at[peer[1], :, columns],
+                        queue_ref.at[blk, :, columns],
+                        (blk_send, blk_recv),
+                        piece * (blocks - 1) + number,
+                        peer,
+                    )
+                )
+                for number, peer in enumerate(blk_peers)
+            ]
+        )
+        queue_ref[blk, :, columns] = send_ref[blk, :, columns]
+        if not piece:
+            for load in loads:
+                load.wait()
+        for expert in range(shared):
+            taken = jnp.dot(
+                place_ref[pl.ds((blocks + expert) * slot, slot), :],
+                plane,
+                preferred_element_type=jnp.float32,
+            ).astype(shared_ref.dtype)
+            shared_ref[expert, :, columns] = taken
+            product = meet(
+                taken, weight_part(shared_held_ref.at[expert], columns, by_columns), by_columns
+            )
+            if piece:
+                product = product + shared_out_ref[expert]
+            shared_out_ref[expert] = product
+        if piece:
+            consume(piece - 1)
+    consume(pieces - 1)
+    for copies in head_copies:
+        for number, copy in enumerate(copies):
+            if relay and number != 1:
+                pl.when(jnp.logical_not(far(head_peers[number])))(copy.wait_send)
+            else:
+                copy.wait_send()
+    for copy in relayed:
+        pl.when(inner)(copy.wait_send)
+    for copies in blk_copies:
+        for copy in copies:
+            copy.wait_send()
+
+
+def dispatch(rows, places, weights, by_columns, pieces=6, window=2):
+    heads, blocks = lax.axis_size("head"), lax.axis_size("blk")
+    count, width = rows.shape
+    (own_weight, shared_weight) = weights
+    shared = shared_weight.shape[0]
+    slot = places.shape[0] // (blocks + shared)
+    outputs = own_weight.shape[0 if by_columns else 1]
+    outs = [
+        jax.ShapeDtypeStruct((heads, count, width), jnp.bfloat16),
+        jax.ShapeDtypeStruct((blocks, slot, width), jnp.bfloat16),
+        jax.ShapeDtypeStruct((shared, slot, width), jnp.bfloat16),
+        jax.ShapeDtypeStruct((blocks * slot, outputs), jnp.float32),
+        jax.ShapeDtypeStruct((shared, slot, outputs), jnp.float32),
+    ]
+    vmem = pl.BlockSpec(memory_space=pltpu.VMEM)
+    anywhere = pl.BlockSpec(memory_space=pl.ANY)
+    return pl.pallas_call(
+        functools.partial(dispatch_kernel, heads, blocks, pieces, window, by_columns),
+        out_shape=outs,
+        in_specs=[vmem, vmem, anywhere, anywhere],
+        out_specs=[vmem] * 5,
+        scratch_shapes=[
+            pltpu.VMEM((blocks, slot, width), jnp.bfloat16),
+            pltpu.VMEM(own_weight.shape, jnp.bfloat16),
+            pltpu.VMEM(shared_weight.shape, jnp.bfloat16),
+            pltpu.SemaphoreType.DMA((pieces * heads,)),
+            pltpu.SemaphoreType.DMA((pieces * heads,)),
+            pltpu.SemaphoreType.DMA((pieces * (blocks - 1),)),
+            pltpu.SemaphoreType.DMA((pieces * (blocks - 1),)),
+            pltpu.SemaphoreType.DMA((2,)),
+        ],
+        compiler_params=pltpu.CompilerParams(
+            collective_id=kernel_number("dispatch", by_columns),
+            has_side_effects=True,
+            vmem_limit_bytes=56 * 1024 * 1024,
+        ),
+        cost_estimate=pl.CostEstimate(flops=0, bytes_accessed=170 << 20, transcendentals=0),
+        name="dispatch",
+    )(rows, places, own_weight, shared_weight)
+
+
+def combine_kernel(
+    heads,
+    blocks,
+    pieces,
+    by_columns,
+    extra,
+    units_ref,
+    shared_units_ref,
+    place_ref,
+    weight_ref,
+    shared_weight_ref,
+    *refs,
+):
+    extra_ref, *refs = refs if extra else (None, *refs)
+    out_ref, returned_ref, *refs = refs
+    extra_out_ref, *refs = refs if extra else (None, *refs)
+    (
+    made_ref,
+    part_ref,
+    landed_ref,
+    relay_ref,
+    held_ref,
+    shared_held_ref,
+    head_send,
+    head_recv,
+    blk_send,
+    blk_recv,
+    local_sems,
+    ) = refs
+    head, blk, head_peers, blk_peers = plane_peers(heads, blocks)
+    rows, width = out_ref.shape
+    slot = returned_ref.shape[1]
+    shared = shared_units_ref.shape[0]
+    step_width = width // pieces
+    relay = heads == 4
+    inner = jnp.logical_and(head > 0, head < heads - 1)
+    greet(head_peers + blk_peers)
+    loads = [
+        pltpu.make_async_copy(weight_ref, held_ref, local_sems.at[0]),
+        pltpu.make_async_copy(shared_weight_ref, shared_held_ref, local_sems.at[1]),
+    ]
+    for load in loads:
+        load.start()
+    extra_copies = []
+    if extra:
+        loads.append(
+            pltpu.make_async_copy(extra_ref, extra_out_ref.at[head], local_sems.at[2])
+        )
+        loads[-1].start()
+        extra_copies = [
+            started(
+                remote(
+                    extra_ref,
+                    extra_out_ref.at[head],
+                    (head_send, head_recv),
+                    pieces * heads + number,
+                    peer,
+                )
+            )
+            for number, peer in enumerate(head_peers)
+        ]
+    for load in loads:
+        load.wait()
+    head_copies = []
+    blk_copies = []
+
+    def produce(piece):
+        columns = pl.ds(piece * step_width, step_width)
+
+        def make(block, carry):
+            start = pl.multiple_of(block * slot, 16)
+            made_ref[block, :, columns] = meet(
+                units_ref[pl.ds(start, slot), :],
+                weight_part(held_ref, columns, not by_columns),
+                by_columns,
+            ).astype(made_ref.dtype)
+            return carry
+
+        lax.fori_loop(0, blocks, make, 0)
+        blk_copies.append(
+            [
+                started(
+                    remote(
+                        made_ref.at[peer[1], :, columns],
+                        returned_ref.at[blk, :, columns],
+                        (blk_send, blk_recv),
+                        piece * (blocks - 1) + number,
+                        peer,
+                    )
+                )
+                for number, peer in enumerate(blk_peers)
+            ]
+        )
+        returned_ref[blk, :, columns] = made_ref[blk, :, columns]
+        for expert in range(shared):
+            returned_ref[blocks + expert, :, columns] = meet(
+                shared_units_ref[expert],
+                weight_part(shared_held_ref.at[expert], columns, not by_columns),
+                by_columns,
+            ).astype(returned_ref.dtype)
+
+    def gather(piece):
+        columns = pl.ds(piece * step_width, step_width)
+        for copy in blk_copies[piece]:
+            copy.wait_recv()
+        returned = returned_ref[:, :, columns].reshape((blocks + shared) * slot, step_width)
+
+        def part(owner):
+            start = pl.multiple_of(owner * rows, 16)
+            return jnp.dot(
+                place_ref[pl.ds(start, rows), :], returned, preferred_element_type=jnp.float32
+            )
+
+        sent = []
+        for number, peer in enumerate(head_peers):
+            part_ref[peer[0], :, columns] = part(peer[0]).astype(part_ref.dtype)
+            copy = remote(
+                part_ref.at[peer[0], :, columns],
+                landed_ref.at[head, :, columns],
+                (head_send, head_recv),
+                piece * heads + number,
+                peer,
+            )
+            sent.append(copy)
+            if not relay:
+                copy.start()
+            elif number == 1:
+                pl.when(jnp.logical_not(inner))(copy.start)
+            else:
+                distant = far(peer)
+                pl.when(jnp.logical_not(distant))(copy.start)
+                through = through_copy(piece, peer)
+                pl.when(distant)(through.start)
+        head_copies.append(sent)
+        out_ref[:, columns] = part(head)
+
+    def far(peer):
+        return jnp.abs(peer[0] - head) == heads - 1
+
+    def through_copy(piece, peer):
+        columns = pl.ds(piece * step_width, step_width)
+        return remote(
+            part_ref.at[peer[0], :, columns],
+            relay_ref.at[:, columns],
+            (head_send, head_recv),
+            piece * heads + heads - 1,
+            (jnp.where(head == 0, 1, heads - 2), blk),
+        )
+
+    def pass_on(piece):
+        columns = pl.ds(piece * step_width, step_width)
+        target = lax.rem(head + 2, heads)
+
+        @pl.when(inner)
+        def _():
+            through_copy(piece, (target, blk)).wait_recv()
+            part_ref[target, :, columns] = (
+                part_ref[target, :, columns].astype(jnp.float32)
+                + relay_ref[:, columns].astype(jnp.float32)
+            ).astype(part_ref.dtype)
+            head_copies[piece][1].start()
+
+    def finish(piece):
+        columns = pl.ds(piece * step_width, step_width)
+        for number, peer in enumerate(head_peers):
+            copy = head_copies[piece][number]
+
+            def add(copy=copy, peer=peer):
+                copy.wait_recv()
+                out_ref[:, columns] += landed_ref[peer_origin(peer), :, columns].astype(
+                    jnp.float32
+                )
+
+            if relay and number != 1:
+                pl.when(jnp.logical_not(far((peer_origin(peer), blk))))(add)
+            else:
+                add()
+
+    def peer_origin(peer):
+        return lax.rem(2 * head + heads - peer[0], heads)
+
+    lag = 3 if relay else 2
+    for step in range(pieces + lag):
+        if step < pieces:
+            produce(step)
+        if 0 < step <= pieces:
+            gather(step - 1)
+        if relay and 1 < step <= pieces + 1:
+            pass_on(step - 2)
+        if step >= lag:
+            finish(step - lag)
+    for piece, copies in enumerate(head_copies):
+        for number, copy in enumerate(copies):
+            if relay and number != 1:
+                distant = far(head_peers[number])
+                pl.when(jnp.logical_not(distant))(copy.wait_send)
+                pl.when(distant)(through_copy(piece, head_peers[number]).wait_send)
+            else:
+                copy.wait_send()
+    for copy in extra_copies:
         copy.wait()
-
-
-def head_gather(rows):
+    for copies in blk_copies:
+        for copy in copies:
+            copy.wait_send()
+
+
+def combine(
+    units, shared_units, places, weights, by_columns, extra=None, pieces=6
+):
+    heads, blocks = lax.axis_size("head"), lax.axis_size("blk")
+    (own_weight, shared_weight) = weights
+    shared, slot = shared_units.shape[:2]
+    count = places.shape[0] // heads
+    width = own_weight.shape[0 if by_columns else 1]
+    outs = [
+        jax.ShapeDtypeStruct((count, width), jnp.float32),
+        jax.ShapeDtypeStruct((blocks + shared, slot, width), jnp.bfloat16),
+    ]
+    vmem = pl.BlockSpec(memory_space=pltpu.VMEM)
+    anywhere = pl.BlockSpec(memory_space=pl.ANY)
+    extras = [] if extra is None else [extra]
+    outs += [jax.ShapeDtypeStruct((heads,) + array.shape, array.dtype) for array in extras]
+    return pl.pallas_call(
+        functools.partial(combine_kernel, heads, blocks, pieces, by_columns, bool(extras)),
+        out_shape=outs,
+        in_specs=[vmem, vmem, vmem, anywhere, anywhere] + [anywhere] * len(extras),
+        out_specs=[vmem] * 2 + [anywhere] * len(extras),
+        scratch_shapes=[
+            pltpu.VMEM((blocks, slot, width), jnp.bfloat16),
+            pltpu.VMEM((heads, count, width), jnp.bfloat16),
+            pltpu.VMEM((heads, count, width), jnp.bfloat16),
+            pltpu.VMEM((count, width), jnp.bfloat16),
+            pltpu.VMEM(own_weight.shape, jnp.bfloat16),
+            pltpu.VMEM(shared_weight.shape, jnp.bfloat16),
+            pltpu.SemaphoreType.DMA(((pieces + 1) * heads,)),
+            pltpu.SemaphoreType.DMA(((pieces + 1) * heads,)),
+            pltpu.SemaphoreType.DMA((pieces * (blocks - 1),)),
+            pltpu.SemaphoreType.DMA((pieces * (blocks - 1),)),
+            pltpu.SemaphoreType.DMA((3,)),
+        ],
+        compiler_params=pltpu.CompilerParams(
+            collective_id=kernel_number("combine", by_columns),
+            has_side_effects=True,
+            vmem_limit_bytes=56 * 1024 * 1024,
+        ),
+        cost_estimate=pl.CostEstimate(flops=0, bytes_accessed=170 << 20, transcendentals=0),
+        name="combine",
+    )(units, shared_units, places, own_weight, shared_weight, *extras)
+
+
+def head_parts(partial):
     heads = lax.axis_size("head")
-    gathered = pl.pallas_call(
-        functools.partial(head_gather_kernel, heads),
-        out_shape=jax.ShapeDtypeStruct((heads,) + rows.shape, rows.dtype),
-        in_specs=[pl.BlockSpec(memory_space=pl.ANY)],
-        out_specs=pl.BlockSpec(memory_space=pl.ANY),
-        scratch_shapes=[
-            pltpu.SemaphoreType.DMA((heads - 1,)),
-            pltpu.SemaphoreType.DMA((heads - 1,)),
-            pltpu.SemaphoreType.DMA,
-        ],
-        compiler_params=pltpu.CompilerParams(collective_id=1, has_side_effects=True),
-        name="head_gather",
-    )(rows)
-    return gathered.reshape(-1, rows.shape[-1])
-
-
-def head_scatter(partial):
-    heads = lax.axis_size("head")
-    parts = partial.astype(jnp.bfloat16).reshape(heads, -1, partial.shape[-1])
-    parts = lax.all_to_all(parts, "head", 0, 0, tiled=True)
+    return partial.astype(jnp.bfloat16).reshape(heads, -1, partial.shape[-1])
+
+
+def head_sum(parts):
     return jnp.sum(parts.astype(jnp.float32), axis=0)
 
 
@@ -302,6 +859,7 @@
     w_down,
     cotangent,
 ):
+    kernel_numbers.clear()
     heads_count = lax.axis_size("head")
     blocks_count = lax.axis_size("blk")
     head_index = lax.axis_index("head")
@@ -339,9 +897,6 @@
     sine = jnp.sin(angles)
     info = jnp.concatenate([blk_index[None].astype(jnp.int32), lengths])
 
-    plan = lax.all_gather(
-        jnp.stack([routes, queue_ranks]).reshape(2, DECODER_LAYERS, slot_rows, TOP), "head", axis=0
-    )
     expert_ids = jnp.arange(EXPERTS, dtype=jnp.int32)
     row_ids = jnp.arange(experts_local * slot, dtype=jnp.int32)
     spread = (
@@ -383,47 +938,99 @@
             parts = [own.reshape(owned_total, slot, width), shared]
         return jnp.concatenate(parts, axis=0).reshape(experts_local * slot, width)
 
-    def expert_weights(layer_index):
-        sets = []
-        if owned:
-            sets.append(
-                tuple(
-                    rows_to_owner(matrix[layer_index, :owned_total], blocks_count, owned, blk_index)
-                    for matrix in (w_in, w_down)
-                )
-            )
-        if owned_total < experts_local:
-            sets.append(
-                tuple(
-                    lax.all_gather(matrix[layer_index, owned_total:], "blk", axis=1, tiled=True)
-                    for matrix in (w_in, w_down)
-                )
-            )
-        return sets
-
-    def experts_forward(incoming, weights):
-        gate_up = mm("erd,edf->erf", incoming, weights[0])
-        units = (jax.nn.silu(gate_up[..., :FF]) * gate_up[..., FF:]).astype(jnp.bfloat16)
-        produced = mm("erf,efd->erd", units, weights[1]).astype(jnp.bfloat16)
-        return (produced, (incoming, gate_up, units))
-
-    def experts_backward(grad_produced, weights, kept):
-        incoming, gate_up, units = kept
-        grad_units = mm("erd,efd->erf", grad_produced, weights[1])
-        grad_down = mm("erf,erd->efd", units, grad_produced).astype(jnp.bfloat16)
+    def shared_weights(layer_index):
+        if owned_total == experts_local:
+            return []
+        return [
+            tuple(
+                lax.all_gather(matrix[layer_index, owned_total:], "blk", axis=1, tiled=True)
+                for matrix in (w_in, w_down)
+            )
+        ]
+
+    def to_owner(matrix, layer_index):
+        if not owned:
+            return []
+        if owned == 1:
+            return [("blk_swap", matrix, layer_index)]
+        pieces = matrix[layer_index, :owned_total]
+        return [("blk_swap", pieces.reshape((blocks_count, owned) + pieces.shape[1:]))]
+
+    def owned_matrix(received):
+        if not owned:
+            return None
+        columns = received.shape[-1]
+        pieces = received.reshape(blocks_count, owned, -1, columns)
+        return pieces.transpose(1, 0, 2, 3).reshape(owned, -1, columns)
+
+    def from_owner(term):
+        if not owned:
+            return []
+        columns = term.shape[-1]
+        pieces = term.reshape(owned, blocks_count, -1, columns).transpose(1, 0, 2, 3)
+        return [("blk_swap", pieces)]
+
+    def owned_rows(received):
+        if not owned:
+            return []
+        return [received.reshape(owned_total, -1, received.shape[-1])]
+
+    def moe_in(rows, turned_places, sets, which):
+        if owned == 1 and owned_total < experts_local:
+            own_weight, shared_weight = (matrices[which] for matrices in sets)
+            plane, own, shared, own_out, shared_out = dispatch(
+                rows, turned_places, (own_weight[0], shared_weight), which == 1
+            )
+            return (
+                plane.reshape(all_tokens, width),
+                [own.reshape(1, -1, width), shared],
+                [own_out[None], shared_out],
+            )
+        (plane,) = exchange(("head_gather", rows))
+        plane = plane.reshape(all_tokens, width)
+        queues = [
+            part
+            for part in to_experts(mm("rt,td->rd", turned_places, plane).astype(jnp.bfloat16))
+            if part is not None
+        ]
+        spec = ("erd,edf->erf", "erd,efd->erf")[which]
+        return (plane, queues, [mm(spec, rows, mats[which]) for rows, mats in zip(queues, sets)])
+
+    def moe_out(units, places, sets, which, extra=None):
+        if owned == 1 and owned_total < experts_local:
+            own_weight, shared_weight = (matrices[which] for matrices in sets)
+            total, returned, *extras = combine(
+                units[0][0],
+                units[1],
+                places,
+                (own_weight[0], shared_weight),
+                which == 0,
+                extra,
+            )
+            return (total, returned.reshape(-1, width), *extras)
+        spec = ("erf,edf->erd", "erf,efd->erd")[which]
+        made = [mm(spec, part, mats[which]).astype(jnp.bfloat16) for part, mats in zip(units, sets)]
+        returned = from_experts(*(made if owned else [None] + made))
+        parts, *extras = exchange(
+            ("head_swap", head_parts(mm("tr,rd->td", places, returned))),
+            *([] if extra is None else [("head_gather", extra)]),
+        )
+        return (head_sum(parts), returned, *extras)
+
+    def gated(gate_up):
+        return (jax.nn.silu(gate_up[..., :FF]) * gate_up[..., FF:]).astype(jnp.bfloat16)
+
+    def gated_back(gate_up, grad_units):
         gate_part = gate_up[..., :FF]
         up_part = gate_up[..., FF:]
         sigmoid_part = jax.nn.sigmoid(gate_part)
-        grad_gate_up = jnp.concatenate(
+        return jnp.concatenate(
             [
                 grad_units * up_part * sigmoid_part * (1.0 + gate_part * (1.0 - sigmoid_part)),
                 grad_units * gate_part * sigmoid_part,
             ],
             axis=-1,
         ).astype(jnp.bfloat16)
-        grad_in = mm("erd,erf->edf", incoming, grad_gate_up).astype(jnp.bfloat16)
-        grad_incoming = mm("erf,edf->erd", grad_gate_up, weights[0]).astype(jnp.bfloat16)
-        return (grad_incoming, (grad_in, grad_down))
 
     def by_slot(rows):
         return (
@@ -460,26 +1067,41 @@
                 axis=-1,
             )
         )
-    send = lax.all_to_all(jnp.stack(send, axis=1), "head", 0, 0, tiled=True)
-    attention_weights = []
-    for layer_index in range(DECODER_LAYERS):
-        wide = lax.all_gather(send[:, layer_index], "blk", axis=1, tiled=True).reshape(width, -1)
-        out_full = lax.all_gather(w_out[layer_index], "blk", axis=0, tiled=True)
+    plan = jnp.stack([routes, queue_ranks]).reshape(2 * DECODER_LAYERS, slot_rows * TOP)
+    plan, plane_tokens, first_send, first_out, *own_in_next = exchange(
+        ("head_gather", plan),
+        ("head_gather", tokens.reshape(slot_rows, width)),
+        ("head_swap", send[0]),
+        ("blk_pairs", w_out[0]),
+        *to_owner(w_in, 0),
+    )
+    plan = plan.reshape(heads_count, 2, DECODER_LAYERS, slot_rows, TOP)
+    plane_tokens = plane_tokens.reshape(all_tokens, width)
+
+    def attention_set(wide, out_full):
+        wide = wide.transpose(1, 0, 2, 3).reshape(width, -1)
         columns = query_columns + pair_columns
         small = wide[:, columns:]
         gains = small.T[EXPERTS : EXPERTS + 2].astype(jnp.float32)
-        attention_weights.append((wide[:, :columns], out_full, small[:, :EXPERTS], gains))
+        return (wide[:, :columns], out_full.reshape(-1, width), small[:, :EXPERTS], gains)
+
+    (wide,) = exchange(("blk_pairs", first_send))
+    attention_weights = [
+        attention_set(wide, first_out),
+    ]
 
     hidden = tokens.reshape(slot_rows, width).astype(jnp.float32)
-    plane_tokens = head_gather(tokens.reshape(slot_rows, width))
     stored_all = []
     for layer_index in range(DECODER_LAYERS):
         qkv_full, out_full, router_full, gains = attention_weights[layer_index]
-        weight_sets = expert_weights(layer_index)
         chosen, places = layer_plan(layer_index)
         scaled_a, inverse_a = norm_rows(hidden)
         if layer_index:
-            plane_normed_a = head_gather((scaled_a * gains[:1]).astype(jnp.bfloat16))
+            plane_normed_a, *own_in_next = exchange(
+                ("head_gather", (scaled_a * gains[:1]).astype(jnp.bfloat16)),
+                *to_owner(w_in, layer_index),
+            )
+            plane_normed_a = plane_normed_a.reshape(all_tokens, width)
         else:
             plane_normed_a = (
                 norm_rows(plane_tokens.astype(jnp.float32))[0] * gains[:1]
@@ -490,9 +1112,18 @@
         keys = rotate(pairs[:, :, 0].reshape(all_tokens, -1), cosine, sine)
         pairs = jnp.stack([keys.reshape(all_tokens, kv_local, HEAD_SIZE), pairs[:, :, 1]], axis=2)
         pairs = pairs.reshape(all_tokens, pair_columns).astype(jnp.bfloat16)
-        pairs = lax.all_to_all(
-            jnp.broadcast_to(pairs[None], (blocks_count,) + pairs.shape), "blk", 0, 0, tiled=True
-        )
+        if layer_index + 1 < DECODER_LAYERS:
+            pairs, next_send = exchange(
+                ("blk_pairs", pairs), ("head_swap", send[layer_index + 1])
+            )
+            attention_weights.append(
+                attention_set(
+                    lax.all_gather(next_send, "blk", axis=0),
+                    lax.all_gather(w_out[layer_index + 1], "blk", axis=0),
+                )
+            )
+        else:
+            (pairs,) = exchange(("blk_pairs", pairs))
         pairs_all = (
             pairs.reshape(blocks_count, heads_count, SEQUENCE_SLOTS, resident, pair_columns)
             .transpose(2, 1, 0, 3, 4)
@@ -510,10 +1141,20 @@
             "attend",
         )
         attended = by_head(attended)
-        middle = hidden + valid_column * head_scatter(mm("tf,fd->td", attended, out_full))
+        branch, *own_down_next = exchange(
+            ("head_swap", head_parts(mm("tf,fd->td", attended, out_full))),
+            *to_owner(w_down, layer_index),
+        )
+        weight_sets = shared_weights(layer_index)
+        if owned:
+            weight_sets = [
+                (owned_matrix(own_in_next[0]), owned_matrix(own_down_next[0]))
+            ] + weight_sets
+        middle = hidden + valid_column * head_sum(branch)
         scaled_b, inverse_b = norm_rows(middle)
         normed_b = (scaled_b * gains[1:]).astype(jnp.bfloat16)
-        plane_rows = head_gather(normed_b)
+        plane_rows, incoming, gate_up = moe_in(normed_b, places.T, weight_sets, 0)
+        units = [gated(part) for part in gate_up]
         logits = mm("td,de->te", plane_rows, router_full)
         peaks = jnp.max(jnp.where(chosen, logits, negative), axis=-1, keepdims=True)
         lifted = jnp.where(chosen, jnp.exp(logits - peaks), 0.0)
@@ -524,16 +1165,7 @@
         weighted_places = (
             mm("te,er->tr", plane_gates.astype(jnp.bfloat16), spread).astype(jnp.bfloat16) * places
         )
-        queues = mm("tr,td->rd", places, plane_rows).astype(jnp.bfloat16)
-        own_in, shared_in = to_experts(queues)
-        kept_sets = []
-        produced = []
-        for incoming, weights in zip([own_in, shared_in] if owned else [shared_in], weight_sets):
-            made, kept = experts_forward(incoming, weights)
-            produced.append(made)
-            kept_sets.append(kept)
-        returned = from_experts(*(produced if owned else [None] + produced))
-        mixture = head_scatter(mm("tr,rd->td", weighted_places, returned))
+        mixture, returned = moe_out(units, weighted_places, weight_sets, 1)
         stored_all.append(
             (
                 weight_sets,
@@ -549,7 +1181,9 @@
                 plane_rows,
                 gates_all,
                 weighted_places,
-                kept_sets,
+                incoming,
+                gate_up,
+                units,
                 returned,
             )
         )
@@ -561,6 +1195,7 @@
     router_list = [None] * DECODER_LAYERS
     gains_list = [None] * DECODER_LAYERS
     expert_list = [None] * DECODER_LAYERS
+    pending = []
     for layer_index in reversed(range(DECODER_LAYERS)):
         qkv_full, out_full, router_full, gains = attention_weights[layer_index]
         (
@@ -577,35 +1212,31 @@
             plane_rows,
             gates_all,
             weighted_places,
-            kept_sets,
+            incoming,
+            gate_up,
+            units,
             returned,
         ) = stored_all[layer_index]
-        plane_grads = head_gather((valid_column * grad_hidden).astype(jnp.bfloat16))
-        queue_grads = mm("tr,td->rd", weighted_places, plane_grads).astype(jnp.bfloat16)
-        own_grad, shared_grad = to_experts(queue_grads)
-        grad_in_sets = []
-        grad_weight_sets = []
-        for grad_produced, weights, kept in zip(
-            [own_grad, shared_grad] if owned else [shared_grad], weight_sets, kept_sets
-        ):
-            grad_incoming, grad_weights = experts_backward(grad_produced, weights, kept)
-            grad_in_sets.append(grad_incoming)
-            grad_weight_sets.append(grad_weights)
-        grad_rows = from_experts(*(grad_in_sets if owned else [None] + grad_in_sets))
-        grad_normed_b = head_scatter(mm("tr,rd->td", places, grad_rows))
-        pair_dots = mm("td,rd->tr", plane_grads, returned) * places
-        plane_grad_gates = mm("er,tr->et", spread.astype(jnp.float32), pair_dots)
-        grad_gates = (
-            lax.all_to_all(
-                jnp.broadcast_to(plane_grad_gates[None], (heads_count, experts_local, all_tokens)),
-                "head",
-                0,
-                0,
-                tiled=True,
-            )
-            .reshape(EXPERTS, all_tokens)
-            .T
-        )
+        plane_grads, grad_produced, grad_units = moe_in(
+            (valid_column * grad_hidden).astype(jnp.bfloat16),
+            weighted_places.T,
+            weight_sets,
+            1,
+        )
+        grad_gate_up = [gated_back(*parts) for parts in zip(gate_up, grad_units)]
+        pair_dots = (mm("td,rd->tr", plane_grads, returned) * places).astype(jnp.bfloat16)
+        plane_grad_gates = mm("tr,er->te", pair_dots, spread).T
+        grad_normed_b, _, grad_gates = moe_out(
+            grad_gate_up, places, weight_sets, 0, plane_grad_gates
+        )
+        grad_gates = grad_gates.reshape(EXPERTS, all_tokens).T
+        grad_weight_sets = [
+            (
+                mm("erd,erf->edf", rows, grads).astype(jnp.bfloat16),
+                mm("erf,erd->efd", inner, out_grads).astype(jnp.bfloat16),
+            )
+            for rows, grads, inner, out_grads in zip(incoming, grad_gate_up, units, grad_produced)
+        ]
         grad_logits = gates_all * (
             grad_gates - jnp.sum(gates_all * grad_gates, axis=-1, keepdims=True)
         )
@@ -621,7 +1252,19 @@
         )
         grad_norm_b, grad_gain_b = norm_back(grad_normed_b, scaled_b, inverse_b, gains[1:])
         grad_middle = grad_hidden + grad_norm_b
-        plane_branch = head_gather((valid_column * grad_middle).astype(jnp.bfloat16))
+        plane_branch, *own_grad_in = exchange(
+            ("head_gather", (valid_column * grad_middle).astype(jnp.bfloat16)),
+            *(from_owner(grad_weight_sets[0][0]) if owned else []),
+            after=[*pending, *(grad_weight_sets[-1] if owned_total < experts_local else ())],
+        )
+        pending = []
+        shared_terms = []
+        if owned_total < experts_local:
+            shared_terms = [
+                lax.psum_scatter(term, "blk", scatter_dimension=1, tiled=True)
+                for term in grad_weight_sets[-1]
+            ]
+        plane_branch = plane_branch.reshape(all_tokens, width)
         grad_out_w = mm("tf,td->fd", attended, plane_branch)
         grad_attended = by_slot(mm("td,fd->tf", plane_branch, out_full).astype(jnp.bfloat16))
         grad_queries, grad_pairs = attention_call(
@@ -643,7 +1286,7 @@
             .transpose(2, 1, 0, 3, 4)
             .reshape(blocks_count, all_tokens, pair_columns)
         )
-        grad_pairs = lax.all_to_all(grad_pairs, "blk", 0, 0, tiled=True)
+        (grad_pairs,) = exchange(("blk_swap", grad_pairs))
         grad_pairs = jnp.sum(grad_pairs.astype(jnp.float32), axis=0)
         grad_pairs = grad_pairs.astype(jnp.bfloat16).astype(jnp.float32)
         grad_pairs = grad_pairs.reshape(all_tokens, kv_local, 2, HEAD_SIZE)
@@ -659,23 +1302,37 @@
             axis=-1,
         ).astype(jnp.bfloat16)
         grad_qkv = mm("td,te->de", plane_normed_a, grad_projected)
-        grad_normed_a = head_scatter(mm("te,de->td", grad_projected, qkv_full))
-        grad_norm_a, grad_gain_a = norm_back(grad_normed_a, scaled_a, inverse_a, gains[:1])
-        grad_hidden = grad_middle + grad_norm_a
-
         grad_out_w = jnp.concatenate(
             [grad_out_w, jnp.pad(grad_router, ((0, 0), (0, small_columns - EXPERTS)))], axis=1
         ).astype(jnp.bfloat16)
-        grad_out_w = lax.psum_scatter(grad_out_w, "blk", scatter_dimension=0, tiled=True)
-        out_list[layer_index] = grad_out_w[:, :width].astype(jnp.float32)
-        router_list[layer_index] = grad_out_w[:, width : width + EXPERTS].astype(jnp.float32)
         grad_qkv = (
             grad_qkv.astype(jnp.bfloat16)
             .reshape(heads_count, blocks_count, weight_rows, -1)
             .transpose(1, 0, 2, 3)
-            .reshape(width, -1)
-        )
-        grad_qkv = lax.psum_scatter(grad_qkv, "blk", scatter_dimension=0, tiled=True)
+        )
+        grad_normed_a, grad_out_w, *others = exchange(
+            ("head_swap", head_parts(mm("te,de->td", grad_projected, qkv_full))),
+            ("blk_swap", grad_out_w.reshape(blocks_count, weight_rows, -1)),
+            *([] if layer_index else [("blk_swap", grad_qkv)]),
+            *(from_owner(grad_weight_sets[0][1]) if owned else []),
+            after=shared_terms,
+        )
+        if layer_index:
+            own_grad_down = others
+            grad_qkv = lax.psum_scatter(
+                grad_qkv.reshape(width, -1), "blk", scatter_dimension=0, tiled=True
+            )
+            pending.append(grad_qkv)
+        else:
+            grad_qkv, *own_grad_down = others
+            grad_qkv = jnp.sum(grad_qkv.astype(jnp.float32), axis=0).astype(jnp.bfloat16)
+        grad_out_w = jnp.sum(grad_out_w.astype(jnp.float32), axis=0)
+        grad_normed_a = head_sum(grad_normed_a)
+        grad_norm_a, grad_gain_a = norm_back(grad_normed_a, scaled_a, inverse_a, gains[:1])
+        grad_hidden = grad_middle + grad_norm_a
+
+        out_list[layer_index] = grad_out_w[:, :width]
+        router_list[layer_index] = grad_out_w[:, width : width + EXPERTS]
         grad_qkv = lax.all_to_all(
             grad_qkv.reshape(heads_count, weight_rows, -1), "head", 0, 0, tiled=True
         ).transpose(1, 0, 2)
@@ -687,24 +1344,13 @@
             axis=1,
         ).astype(jnp.float32)
         gains_list[layer_index] = jnp.stack([grad_gain_a, grad_gain_b])
-        own_and_shared = []
-        if owned:
-            own_and_shared.append(
-                tuple(
-                    rows_from_owner(term, blocks_count, owned, blk_index)
-                    for term in grad_weight_sets[0]
-                )
-            )
-        if owned_total < experts_local:
-            own_and_shared.append(
-                tuple(
-                    lax.psum_scatter(term, "blk", scatter_dimension=1, tiled=True)
-                    for term in grad_weight_sets[-1]
-                )
-            )
-        expert_list[layer_index] = tuple(
-            jnp.concatenate(terms, axis=0).astype(jnp.float32) for terms in zip(*own_and_shared)
-        )
+        terms = []
+        for number, received in enumerate((own_grad_in, own_grad_down)):
+            parts = owned_rows(received[0]) if owned else []
+            if owned_total < experts_local:
+                parts.append(shared_terms[number])
+            terms.append(jnp.concatenate(parts, axis=0).astype(jnp.float32))
+        expert_list[layer_index] = tuple(terms)
     devices = heads_count * blocks_count
     grad_gains = jnp.stack(gains_list).reshape(2 * DECODER_LAYERS, devices, weight_rows)
     grad_gains = lax.all_to_all(

time: 1760 us -> 1280 us (0.73)
  Pallas kernels: 288 us -> 952 us
  waiting for transfers between devices: 676 us -> 23.5 us
  starting transfers between devices: 241 us -> 13.5 us
  matrix products: 188 us -> 91.1 us
  local copies, waits for them, and re-layouts: 189 us -> 94.1 us
  blocking collectives: 72.6 us -> 0 us
    pallas_call x8 -> x21, Pallas kernels: 241 us -> 905 us  [the longest x13 434 us: exchange(): pl.pallas_call(functools.partial(exchange_kernel, heads, blocks, plan, le...]
    all_to_all x21 -> x0, waiting for transfers between devices: 353 us -> none  [the longest x8 207 us: head_scatter(): parts = lax.all_to_all(parts, 'head', 0, 0, tiled=True)]
    ppermute x56 -> x0, waiting for transfers between devices: 299 us -> none  [the longest x28 174 us: rows_from_owner(): piece = lax.ppermute(piece, 'blk', ring(blocks_count, offset))]
    all_to_all x21 -> x0, starting transfers between devices: 148 us -> none  [the longest x8 61.1 us: head_scatter(): parts = lax.all_to_all(parts, 'head', 0, 0, tiled=True)]
    dot_general x56 -> x32, matrix products: 188 us -> 91.1 us  [mm(): return jnp.einsum(spec, left, right, preferred_element_type=jnp.float32)]
    ppermute x56 -> x0, starting transfers between devices: 67 us -> none  [the longest x28 43.8 us: rows_to_owner(): piece = lax.ppermute(piece, 'blk', ring(blocks_count, offset))]
    all_to_all x2 -> x0, blocking collectives: 59.5 us -> none  [the longest x1 37.5 us: to_experts(): own = lax.all_to_all(own, 'blk', 0, 0, tiled=True)]
    dynamic_update_slice x63 -> x0, local copies, waits for them, and re-layouts: 52.9 us -> none  [the longest x31 35.7 us: rows_to_owner(): whole = lax.dynamic_update_slice_in_dim(whole, piece, origin * rows, 1)]
  transfers between devices with their start and end apart: 96 -> 14, of which waited for: 47 -> 3; matrix products, arithmetic and copies ran while one was open for 22% -> 18% of each run, Pallas kernels for 14% -> 60%
where the time goes in v3:
time: 1280 us; the launch traced here: 1270 us
  Pallas kernels  952 us (74%)
  local copies, waits for them, and re-layouts  94.1 us (7%)
  matrix products  91.1 us (7%)
  other arithmetic  79.4 us (6%)
  waiting for transfers between devices  23.5 us (2%)
  between operations  16.5 us (1%)
  starting transfers between devices  13.5 us (1%)
    pallas_call x13, Pallas kernels, exchange(): pl.pallas_call(functools.partial(exchange_kernel, heads, blocks, plan, le...  434 us
    pallas_call x4, Pallas kernels, combine(): pl.pallas_call(functools.partial(combine_kernel, heads, blocks, pieces, b...  239 us
    pallas_call x4, Pallas kernels, dispatch(): pl.pallas_call(functools.partial(dispatch_kernel, heads, blocks, pieces,...  232 us
    dot_general x32, matrix products, mm(): return jnp.einsum(spec, left, right, preferred_element_type=jnp.float32)  91.1 us
    pallas_call x4, Pallas kernels, attention_call(): pl.pallas_call(kernel, grid_spec=pltpu.PrefetchScalarGridSpec(num_scalar_...  47.1 us
  transfers between devices with their start and end apart: 14, of which 3 were waited for; matrix products, arithmetic and copies ran while one was open for 18% of the time, Pallas kernels for 60%

profile of v3, /device:TPU:0, one launch (start us, length us, event | category | flops | bytes accessed | tf_op | source)
XLA Modules:
  0.0 1269.9 jit_solution(10870530954563720103)
XLA Ops:
  11.1 48.7 %exchange.13 = (s32[4,4,1024]{2,1,0:T(4,128)}, bf16[4,128,1536]{2,1,0:T(8,128)(2,1)}, bf16[4,48,768]{2,1,0:T(8,128)(2,1)}, bf16[8,48,1536]{2,1,0:T(8,128)(2,1)}, bf16[8,192,1024]{2,1,0:T(8,128)(2,1)}) custom-call(s32[4,1024]{1,0:T(4,128)} %reshape.877.refs_0_, bf16[128,1536]{1,0:T(8,128)(2,1)} %bitcast.389, bf16[4,48,768]{2,1,0:T(8,128)(2,1)} %pad_maximum_fusion.17.refs_2_, ...), custom_call_target="tpu_custom_call" | custom-call | bytes 115343360 | tf_op jit(solution)/shard_map/exchange/pallas_call | solution.py:168
  61.6 17.8 %exchange.14 = bf16[8,4,48,768]{3,2,1,0:T(8,128)(2,1)} custom-call(bf16[4,48,768]{2,1,0:T(8,128)(2,1)} %get-tuple-element.66.refs_0_), custom_call_target="tpu_custom_call" | custom-call | bytes 115343360 | tf_op jit(solution)/shard_map/exchange/pallas_call | solution.py:168
  88.0 18.2 %exchange.15 = (bf16[8,512,256]{2,1,0:T(8,128)(2,1)}, bf16[4,48,768]{2,1,0:T(8,128)(2,1)}) custom-call(bf16[512,256]{1,0:T(8,128)(2,1)} %copy.291.refs_0_, bf16[4,48,768]{2,1,0:T(8,128)(2,1)} %pad_maximum_fusion.18.refs_1_), custom_call_target="tpu_custom_call" | custom-call | bytes 115343360 | tf_op jit(solution)/shard_map/exchange/pallas_call | solution.py:168
  123.8 8.6 attend.2
  136.4 30.3 %exchange.16 = (bf16[4,128,1536]{2,1,0:T(8,128)(2,1)}, bf16[8,64,1536]{2,1,0:T(8,128)(2,1)}) custom-call(bf16[4,128,1536]{2,1,0:T(8,128)(2,1)} %bitcast.401, bf16[2,10,64,1536]{3,2,1,0:T(8,128)(2,1)} %refs_1_.5), custom_call_target="tpu_custom_call" | custom-call | bytes 115343360 | tf_op jit(solution)/shard_map/exchange/pallas_call | solution.py:168
  183.5 6.7 all-gather.14.cloned.1.call-done
  190.2 64.7 %dispatch.4 = (bf16[4,128,1536]{2,1,0:T(8,128)(2,1)}, bf16[8,112,1536]{2,1,0:T(8,128)(2,1)}, bf16[2,112,1536]{2,1,0:T(8,128)(2,1)}, f32[896,1024]{1,0:T(8,128)}, f32[2,112,1024]{2,1,0:T(8,128)}) custom-call(bf16[128,1536]{1,0:T(8,128)(2,1)} %get-tuple-element.199.own_ref, bf16[1120,512]{1,0:T(8,128)(2,1)} %copy.298.place_ref, bf16[1536,1024]{1,0:T(8,128)(2,1)} %bitcast.385, ...), custom_call_target="tpu_custom_call" | custom-call | bytes 178257920 | tf_op jit(solution)/shard_map/dispatch/pallas_call | solution.py:417
  261.6 59.4 %combine.4 = (f32[128,1536]{1,0:T(8,128)}, bf16[10,112,1536]{2,1,0:T(8,128)(2,1)}) custom-call(bf16[896,512]{1,0:T(8,128)(2,1)} %fusion.36.units_ref, bf16[2,112,512]{2,1,0:T(8,128)(2,1)} %multiply_convert_fusion.14.shared_units_ref, bf16[512,1120]{1,0:T(8,128)(2,1)} %get-tuple-element.265.place_ref, bf16[512,1536]{1,0:T(8,128)(2,1)} %bitcast.397, ...), custom_call_target="tpu_custom_call" | custom-call | bytes 178257920 | tf_op jit(solution)/shard_map/combine/pallas_call | solution.py:664
  323.4 41.0 %exchange.17 = (bf16[4,128,1536]{2,1,0:T(8,128)(2,1)}, bf16[8,192,1024]{2,1,0:T(8,128)(2,1)}) custom-call(bf16[128,1536]{1,0:T(8,128)(2,1)} %multiply_convert_fusion.7.refs_0_, bf16[2,10,192,1024]{3,2,1,0:T(8,128)(2,1)} %refs_1_.4), custom_call_target="tpu_custom_call" | custom-call | bytes 115343360 | tf_op jit(solution)/shard_map/exchange/pallas_call | solution.py:168
  382.7 18.2 %exchange.18 = bf16[8,512,256]{2,1,0:T(8,128)(2,1)} custom-call(bf16[512,256]{1,0:T(8,128)(2,1)} %copy.307.refs_0_), custom_call_target="tpu_custom_call" | custom-call | bytes 115343360 | tf_op jit(solution)/shard_map/exchange/pallas_call | solution.py:168
  404.1 8.5 attend.3
  417.2 31.2 %exchange.19 = (bf16[4,128,1536]{2,1,0:T(8,128)(2,1)}, bf16[8,64,1536]{2,1,0:T(8,128)(2,1)}) custom-call(bf16[4,128,1536]{2,1,0:T(8,128)(2,1)} %bitcast.402, bf16[2,10,64,1536]{3,2,1,0:T(8,128)(2,1)} %refs_1_.5), custom_call_target="tpu_custom_call" | custom-call | bytes 115343360 | tf_op jit(solution)/shard_map/exchange/pallas_call | solution.py:168
  452.2 61.5 %dispatch.5 = (bf16[4,128,1536]{2,1,0:T(8,128)(2,1)}, bf16[8,112,1536]{2,1,0:T(8,128)(2,1)}, bf16[2,112,1536]{2,1,0:T(8,128)(2,1)}, f32[896,1024]{1,0:T(8,128)}, f32[2,112,1024]{2,1,0:T(8,128)}) custom-call(bf16[128,1536]{1,0:T(8,128)(2,1)} %multiply_convert_fusion.6.own_ref, bf16[1120,512]{1,0:T(8,128)(2,1)} %copy.314.place_ref, ...), custom_call_target="tpu_custom_call" | custom-call | bytes 178257920 | tf_op jit(solution)/shard_map/dispatch/pallas_call | solution.py:417
  521.3 52.7 %dispatch.6 = (bf16[4,128,1536]{2,1,0:T(8,128)(2,1)}, bf16[8,112,1536]{2,1,0:T(8,128)(2,1)}, bf16[2,112,1536]{2,1,0:T(8,128)(2,1)}, f32[896,512]{1,0:T(8,128)}, f32[2,112,512]{2,1,0:T(8,128)}) custom-call(bf16[128,1536]{1,0:T(8,128)(2,1)} %get-tuple-element.261.own_ref, bf16[1120,512]{1,0:T(8,128)(2,1)} %copy.316.place_ref, bf16[512,1536]{1,0:T(8,128)(2,1)} %bitcast.399, ...), custom_call_target="tpu_custom_call" | custom-call | bytes 178257920 | tf_op jit(solution)/shard_map/dispatch/pallas_call | solution.py:417
  579.8 5.8 convolution_convert_fusion.1.refs_2_
  600.2 56.2 %combine.5 = (f32[128,1536]{1,0:T(8,128)}, bf16[10,112,1536]{2,1,0:T(8,128)(2,1)}) custom-call(bf16[896,512]{1,0:T(8,128)(2,1)} %get-tuple-element.209.units_ref, bf16[2,112,512]{2,1,0:T(8,128)(2,1)} %copy-done.38, bf16[512,1120]{1,0:T(8,128)(2,1)} %fusion.29.place_ref, bf16[512,1536]{1,0:T(8,128)(2,1)} %bitcast.400, bf16[2,512,1536]{2,1,0:T(8,128)(2,1)} %bitcast.383), custom_call_target="tpu_custom_call" | custom-call | bytes 178257920 | tf_op jit(solution)/shard_map/combine/pallas_call | solution.py:664
  658.7 6.0 fusion.31.refs_0_
  664.7 67.1 %combine.6 = (f32[128,1536]{1,0:T(8,128)}, bf16[10,112,1536]{2,1,0:T(8,128)(2,1)}, f32[4,10,512]{2,1,0:T(8,128)}) custom-call(bf16[896,1024]{1,0:T(8,128)(2,1)} %pad_maximum_fusion.units_ref, bf16[2,112,1024]{2,1,0:T(8,128)(2,1)} %pad_maximum_fusion.7.shared_units_ref, bf16[512,1120]{1,0:T(8,128)(2,1)} %get-tuple-element.249.place_ref, ...), custom_call_target="tpu_custom_call" | custom-call | bytes 178257920 | tf_op jit(solution)/shard_map/combine/pallas_call | solution.py:664
  741.4 37.0 %exchange.20 = (bf16[4,128,1536]{2,1,0:T(8,128)(2,1)}, bf16[8,1,192,1024]{3,2,1,0:T(8,128)(2,1)}) custom-call(bf16[128,1536]{1,0:T(8,128)(2,1)} %get-tuple-element.193.refs_0_, bf16[8,1,192,1024]{3,2,1,0:T(8,128)(2,1)} %bitcast.429, bf16[2,1536,1024]{2,1,0:T(8,128)(2,1)} %convolution_convert_fusion.1.refs_2_, ...), custom_call_target="tpu_custom_call" | custom-call | bytes 115343360 | tf_op jit(solution)/shard_map/exchange/pallas_call | solution.py:168
  781.6 15.1 %attend_back.2 = (bf16[2,256,384]{2,1,0:T(8,128)(2,1)}, bf16[2,2048,256]{2,1,0:T(8,128)(2,1)}) custom-call(s32[3]{0:T(128)} %pad_add_fusion.1.info_ref, bf16[2,256,384]{2,1,0:T(8,128)(2,1)} %bitcast.502, bf16[2,2048,256]{2,1,0:T(8,128)(2,1)} %bitcast.442, bf16[2,256,384]{2,1,0:T(8,128)(2,1)} %bitcast.490), custom_call_target="tpu_custom_call" | custom-call | flops 2013265920 | bytes 8388608 | tf_op jit(solution)/shard_map/attend_back/pallas_call | solution.py:831
  799.9 26.0 %exchange.21 = bf16[8,512,256]{2,1,0:T(8,128)(2,1)} custom-call(bf16[8,512,256]{2,1,0:T(8,128)(2,1)} %bitcast.392), custom_call_target="tpu_custom_call" | custom-call | bytes 115343360 | tf_op jit(solution)/shard_map/exchange/pallas_call | solution.py:168
  851.1 42.6 %exchange.22 = (bf16[4,128,1536]{2,1,0:T(8,128)(2,1)}, bf16[8,48,1664]{2,1,0:T(8,128)(2,1)}, bf16[8,1,64,1536]{3,2,1,0:T(8,128)(2,1)}) custom-call(bf16[4,128,1536]{2,1,0:T(8,128)(2,1)} %bitcast.454, bf16[8,48,1664]{2,1,0:T(8,128)(2,1)} %pad_maximum_fusion.2.refs_1_, bf16[8,1,64,1536]{3,2,1,0:T(8,128)(2,1)} %bitcast.405, ...), custom_call_target="tpu_custom_call" | custom-call | bytes 115343360 | tf_op jit(solution)/shard_map/exchange/pallas_call | solution.py:168
  897.1 52.8 %dispatch.7 = (bf16[4,128,1536]{2,1,0:T(8,128)(2,1)}, bf16[8,112,1536]{2,1,0:T(8,128)(2,1)}, bf16[2,112,1536]{2,1,0:T(8,128)(2,1)}, f32[896,512]{1,0:T(8,128)}, f32[2,112,512]{2,1,0:T(8,128)}) custom-call(bf16[128,1536]{1,0:T(8,128)(2,1)} %get-tuple-element.191.own_ref, bf16[1120,512]{1,0:T(8,128)(2,1)} %copy.327.place_ref, bf16[512,1536]{1,0:T(8,128)(2,1)} %bitcast.398, ...), custom_call_target="tpu_custom_call" | custom-call | bytes 178257920 | tf_op jit(solution)/shard_map/dispatch/pallas_call | solution.py:417
  966.8 7.7 all-to-all-done.1
  982.7 6.0 fusion.30.refs_0_
  988.7 55.9 %combine.7 = (f32[128,1536]{1,0:T(8,128)}, bf16[10,112,1536]{2,1,0:T(8,128)(2,1)}, f32[4,10,512]{2,1,0:T(8,128)}) custom-call(bf16[896,1024]{1,0:T(8,128)(2,1)} %pad_maximum_fusion.1.units_ref, bf16[2,112,1024]{2,1,0:T(8,128)(2,1)} %pad_maximum_fusion.8.shared_units_ref, bf16[512,1120]{1,0:T(8,128)(2,1)} %get-tuple-element.248.place_ref, ...), custom_call_target="tpu_custom_call" | custom-call | bytes 178257920 | tf_op jit(solution)/shard_map/combine/pallas_call | solution.py:664
  1058.8 40.5 %exchange.23 = (bf16[4,128,1536]{2,1,0:T(8,128)(2,1)}, bf16[8,1,192,1024]{3,2,1,0:T(8,128)(2,1)}) custom-call(bf16[128,1536]{1,0:T(8,128)(2,1)} %get-tuple-element.189.refs_0_, bf16[8,1,192,1024]{3,2,1,0:T(8,128)(2,1)} %bitcast.428, bf16[192,640]{1,0:T(8,128)(2,1)} %reduce-scatter.10.cloned.1.call-done.refs_2_, ...), custom_call_target="tpu_custom_call" | custom-call | bytes 115343360 | tf_op jit(solution)/shard_map/exchange/pallas_call | solution.py:168
  1102.5 14.9 %attend_back.3 = (bf16[2,256,384]{2,1,0:T(8,128)(2,1)}, bf16[2,2048,256]{2,1,0:T(8,128)(2,1)}) custom-call(s32[3]{0:T(128)} %pad_add_fusion.1.info_ref, bf16[2,256,384]{2,1,0:T(8,128)(2,1)} %bitcast.500, bf16[2,2048,256]{2,1,0:T(8,128)(2,1)} %bitcast.440, bf16[2,256,384]{2,1,0:T(8,128)(2,1)} %bitcast.489), custom_call_target="tpu_custom_call" | custom-call | flops 2013265920 | bytes 8388608 | tf_op jit(solution)/shard_map/attend_back/pallas_call | solution.py:831
  1120.6 26.4 %exchange.24 = bf16[8,512,256]{2,1,0:T(8,128)(2,1)} custom-call(bf16[8,512,256]{2,1,0:T(8,128)(2,1)} %bitcast.393), custom_call_target="tpu_custom_call" | custom-call | bytes 115343360 | tf_op jit(solution)/shard_map/exchange/pallas_call | solution.py:168
  1166.9 56.3 %exchange.25 = (bf16[4,128,1536]{2,1,0:T(8,128)(2,1)}, bf16[8,48,1664]{2,1,0:T(8,128)(2,1)}, bf16[8,4,48,640]{3,2,1,0:T(8,128)(2,1)}, bf16[8,1,64,1536]{3,2,1,0:T(8,128)(2,1)}) custom-call(bf16[4,128,1536]{2,1,0:T(8,128)(2,1)} %bitcast.457, bf16[8,48,1664]{2,1,0:T(8,128)(2,1)} %pad_maximum_fusion.3.refs_1_, bf16[8,4,48,640]{3,2,1,0:T(8,128)(2,1)} %bitcast.395, ...), custom_call_target="tpu_custom_call" | custom-call | bytes 115343360 | tf_op jit(solution)/shard_map/exchange/pallas_call | solution.py:168
  1240.1 6.0 maximum_convert_fusion
  1254.2 7.3 all-to-all-done
  (533 shorter events, 256.2 us)
Async XLA Ops:
  7.2 172.1 %all-gather.18.cloned.1.call-start = ((), (), s32[]{:S(2)}) async-start(), calls=%async_computation.16 | async-start | bytes 2654208 | tf_op jit(solution)/shard_map/all_gather | solution.py:1121
  82.3 96.1 %copy-start.81 = (f32[1536]{0:T(1024)}, f32[1536]{0:T(1024)S(1)}, u32[]{:S(2)}) copy-start(f32[1536]{0:T(1024)S(1)} %get-tuple-element.183) | copy-start | bytes 18436
  86.2 741.9 %copy-start.12 = (f32[512,32]{0,1:T(8,128)}, f32[512,32]{0,1:T(8,128)S(1)}, u32[]{:S(2)}) copy-start(f32[512,32]{0,1:T(8,128)S(1)} %get-tuple-element.256) | copy-start | bytes 196612
  86.2 741.9 %copy-start.42 = (f32[512,32]{0,1:T(8,128)}, f32[512,32]{0,1:T(8,128)S(1)}, u32[]{:S(2)}) copy-start(f32[512,32]{0,1:T(8,128)S(1)} %get-tuple-element.254) | copy-start | bytes 196612
  106.1 84.1 %all-gather.14.cloned.1.call-start = ((), (), s32[]{:S(2)}) async-start(), calls=%async_computation.14 | async-start | bytes 7077888 | tf_op jit(solution)/shard_map/all_gather | solution.py:946
  108.9 152.8 %all-gather.16.cloned.1.call-start = ((), (), s32[]{:S(2)}) async-start(), calls=%async_computation.15 | async-start | bytes 3538944 | tf_op jit(solution)/shard_map/all_gather | solution.py:946
  111.0 302.7 %all-gather.12.cloned.1.call-start = ((), (), s32[]{:S(2)}) async-start(), calls=%async_computation.8 | async-start | bytes 1327104 | tf_op jit(solution)/shard_map/all_gather | solution.py:1122
  111.6 340.6 %all-gather.20.cloned.1.call-start = ((), (), s32[]{:S(2)}) async-start(), calls=%async_computation.17 | async-start | bytes 7077888 | tf_op jit(solution)/shard_map/all_gather | solution.py:946
  112.2 409.2 %all-gather.22.cloned.1.call-start = ((), (), s32[]{:S(2)}) async-start(), calls=%async_computation.18 | async-start | bytes 3538944 | tf_op jit(solution)/shard_map/all_gather | solution.py:946
  112.7 738.4 %reduce-scatter.8.cloned.1.call-start = ((), (), s32[]{:S(2)}) async-start(), calls=%async_computation.10 | async-start | bytes 3538944 | tf_op jit(solution)/shard_map/reduce_scatter | solution.py:1264
  113.4 144.6 %copy-start.75 = (s32[1120]{0:T(1024)}, s32[1120]{0:T(1024)S(1)}, u32[]{:S(2)}) copy-start(s32[1120]{0:T(1024)S(1)} %add_select_fusion) | copy-start | bytes 13444
  170.3 87.7 %copy-start.9 = (pred[512,1120]{1,0:T(32,128)(4,1)}, pred[512,1120]{1,0:T(32,128)(4,1)S(1)}, u32[]{:S(2)}) copy-start(pred[512,1120]{1,0:T(32,128)(4,1)S(1)} %fusion.2) | copy-start | bytes 1720324
  183.5 139.0 %copy-start.83 = (f32[1536]{0:T(1024)}, f32[1536]{0:T(1024)S(1)}, u32[]{:S(2)}) copy-start(f32[1536]{0:T(1024)S(1)} %get-tuple-element.182) | copy-start | bytes 18436
  183.5 267.8 %copy-start.85 = (f32[1536]{0:T(1024)}, f32[1536]{0:T(1024)S(1)}, u32[]{:S(2)}) copy-start(f32[1536]{0:T(1024)S(1)} %get-tuple-element.181) | copy-start | bytes 18436
  190.2 64.7 %copy-start.70 = (pred[512,40]{0,1:T(8,128)(4,1)S(1)}, pred[512,40]{0,1:T(8,128)(4,1)}, u32[]{:S(2)}) copy-start(pred[512,40]{0,1:T(8,128)(4,1)} %fusion.54) | copy-start | bytes 61444
  261.6 59.4 %copy-start.103 = (f32[128]{0:T(128)S(1)}, f32[128]{0:T(128)}, u32[]{:S(2)}) copy-start(f32[128]{0:T(128)} %reshape.940) | copy-start | bytes 1540
  451.3 62.4 %copy-start.113 = (f32[128]{0:T(128)}, f32[128]{0:T(128)S(1)}, u32[]{:S(2)}) copy-start(f32[128]{0:T(128)S(1)} %add_rsqrt_fusion.2) | copy-start | bytes 1540
  452.2 61.5 %copy-start.69 = (pred[512,40]{0,1:T(8,128)(4,1)S(1)}, pred[512,40]{0,1:T(8,128)(4,1)}, u32[]{:S(2)}) copy-start(pred[512,40]{0,1:T(8,128)(4,1)} %fusion.52) | copy-start | bytes 61444
  579.7 271.4 %reduce-scatter.6.cloned.1.call-start = ((), (), s32[]{:S(2)}) async-start(), calls=%async_computation.9 | async-start | bytes 7077888 | tf_op jit(solution)/shard_map/reduce_scatter | solution.py:1264
  585.5 375.3 %reduce-scatter.10.cloned.1.call-start = ((), (), s32[]{:S(2)}) async-start(), calls=%async_computation.11 | async-start | bytes 2211840 | tf_op jit(solution)/shard_map/reduce_scatter | solution.py:1322
  598.5 58.8 %copy-start.20 = (bf16[896,512]{1,0:T(8,128)(2,1)}, bf16[896,512]{1,0:T(8,128)(2,1)S(1)}, u32[]{:S(2)}) copy-start(bf16[896,512]{1,0:T(8,128)(2,1)S(1)} %get-tuple-element.205) | copy-start | bytes 2752516
  598.5 58.8 %copy-start.22 = (bf16[896,512]{1,0:T(8,128)(2,1)}, bf16[896,512]{1,0:T(8,128)(2,1)S(1)}, u32[]{:S(2)}) copy-start(bf16[896,512]{1,0:T(8,128)(2,1)S(1)} %get-tuple-element.206) | copy-start | bytes 2752516
  664.7 68.2 %copy-start.86 = (f32[1536]{0:T(1024)S(1)}, f32[1536]{0:T(1024)}, u32[]{:S(2)}) copy-start(f32[1536]{0:T(1024)} %copy-done.85) | copy-start | bytes 18436
  664.7 68.2 %copy-start.114 = (f32[128]{0:T(128)S(1)}, f32[128]{0:T(128)}, u32[]{:S(2)}) copy-start(f32[128]{0:T(128)} %copy-done.113) | copy-start | bytes 1540
  839.0 327.9 %reduce-scatter.14.cloned.1.call-start = ((), (), s32[]{:S(2)}) async-start(), calls=%async_computation.13 | async-start | bytes 3538944 | tf_op jit(solution)/shard_map/reduce_scatter | solution.py:1264
  953.8 213.1 %reduce-scatter.12.cloned.1.call-start = ((), (), s32[]{:S(2)}) async-start(), calls=%async_computation.12 | async-start | bytes 7077888 | tf_op jit(solution)/shard_map/reduce_scatter | solution.py:1264
  960.8 13.6 %all-to-all-start.1 = ((bf16[4,48,640]{2,1,0:T(8,128)(2,1)}), bf16[4,48,640]{2,1,0:T(8,128)(2,1)S(1)}, u32[]{:S(2)}, u32[]{:S(2)}) async-start(bf16[4,48,640]{2,1,0:T(8,128)(2,1)} %bitcast.470), calls=%async_computation.6 | async-start | bytes 491520 | tf_op jit(solution)/shard_map/all_to_all | solution.py:1336
  988.7 56.8 %copy-start.59 = (f32[512,40]{0,1:T(8,128)S(1)}, f32[512,40]{0,1:T(8,128)}, u32[]{:S(2)}) copy-start(f32[512,40]{0,1:T(8,128)} %copy-done.58) | copy-start | bytes 245764
  988.7 56.9 %copy-start.82 = (f32[1536]{0:T(1024)S(1)}, f32[1536]{0:T(1024)}, u32[]{:S(2)}) copy-start(f32[1536]{0:T(1024)} %copy-done.81) | copy-start | bytes 18436
  988.7 56.9 %copy-start.110 = (f32[128]{0:T(128)S(1)}, f32[128]{0:T(128)}, u32[]{:S(2)}) copy-start(f32[128]{0:T(128)} %copy-done.109) | copy-start | bytes 1540
  1227.0 20.8 %all-to-all-start.2 = ((f32[32,1,192]{2,1,0:T(1,128)}), f32[32,1,192]{2,1,0:T(1,128)S(1)}, u32[]{:S(2)}, u32[]{:S(2)}) async-start(f32[32,1,192]{2,1,0:T(1,128)} %all_to_all.16), calls=%async_computation.7 | async-start | bytes 65536 | tf_op jit(solution)/shard_map/all_to_all | solution.py:1356
  1247.8 13.8 %all-to-all-start = ((bf16[4,48,640]{2,1,0:T(8,128)(2,1)}), bf16[4,48,640]{2,1,0:T(8,128)(2,1)S(1)}, u32[]{:S(2)}, u32[]{:S(2)}) async-start(bf16[4,48,640]{2,1,0:T(8,128)(2,1)} %reduce_sum.297), calls=%async_computation.5 | async-start | bytes 491520 | tf_op jit(solution)/shard_map/all_to_all | solution.py:1336
  (107 other events, 755.0 us)
Sparse Core Ops, SparseCore 0:
  106.3 27.2 all-gather.17
  136.0 54.1 all-gather.13
  192.1 53.4 all-gather.15
  247.4 23.1 all-gather.11
  272.9 77.7 all-gather.19
  352.4 34.4 all-gather.21
  579.8 54.6 reduce-scatter.7
  638.8 81.9 reduce-scatter.5
  839.1 55.4 reduce-scatter.9
  953.9 44.2 reduce-scatter.13
  1002.1 64.9 reduce-scatter.11

commit v4 on v3

--- a/solution.py
+++ b/solution.py
@@ -225,30 +225,32 @@
     )
 
 
-def dispatch_kernel(
-    heads,
-    blocks,
-    pieces,
-    window,
-    by_columns,
-    own_ref,
-    place_ref,
-    weight_ref,
-    shared_weight_ref,
-    plane_ref,
-    queue_ref,
-    shared_ref,
-    out_ref,
-    shared_out_ref,
-    send_ref,
-    held_ref,
-    shared_held_ref,
-    head_send,
-    head_recv,
-    blk_send,
-    blk_recv,
-    local_sems,
-):
+DISPATCH_PIECES, DISPATCH_WINDOW, DISPATCH_LAG = 6, 3, 2
+COMBINE_PIECES = 6
+
+
+def dispatch_stages(heads, blocks, by_columns, refs):
+    (
+        own_ref,
+        place_ref,
+        scale_ref,
+        weight_ref,
+        shared_weight_ref,
+        plane_ref,
+        queue_ref,
+        shared_ref,
+        out_ref,
+        shared_out_ref,
+        send_ref,
+        held_ref,
+        shared_held_ref,
+        head_send,
+        head_recv,
+        blk_send,
+        blk_recv,
+        local_sems,
+    ) = refs
+    pieces, window, lag = DISPATCH_PIECES, DISPATCH_WINDOW, DISPATCH_LAG
     head, blk, head_peers, blk_peers = plane_peers(heads, blocks)
     rows, width = own_ref.shape
     slot = queue_ref.shape[1]
@@ -256,22 +258,18 @@
     step_width = width // pieces
     outputs = out_ref.shape[1]
     tile = 256
-    greet(head_peers + blk_peers)
+    relay = heads == 4
+    inner = jnp.logical_and(head > 0, head < heads - 1)
     loads = [
         pltpu.make_async_copy(weight_ref, held_ref, local_sems.at[0]),
         pltpu.make_async_copy(shared_weight_ref, shared_held_ref, local_sems.at[1]),
     ]
-    for load in loads:
-        load.start()
     head_copies = []
     blk_copies = []
+    relayed = []
 
     def far(peer):
         return jnp.abs(peer[0] - head) == heads - 1
-
-    relay = heads == 4
-    inner = jnp.logical_and(head > 0, head < heads - 1)
-    relayed = []
 
     def spread(piece):
         columns = pl.ds(piece * step_width, step_width)
@@ -306,9 +304,17 @@
         relayed.append(copy)
         pl.when(inner)(copy.start)
 
-    for piece in range(min(window, pieces)):
-        spread(piece)
-    plane_ref[head] = own_ref[...]
+    def scaled(values, start):
+        if scale_ref is not None:
+            values = values * scale_ref[pl.ds(start, slot), :]
+        return values.astype(queue_ref.dtype)
+
+    def begin():
+        for load in loads:
+            load.start()
+        for piece in range(min(window, pieces)):
+            spread(piece)
+        plane_ref[head] = own_ref[...]
 
     def consume(piece):
         columns = pl.ds(piece * step_width, step_width)
@@ -331,11 +337,12 @@
 
         lax.fori_loop(0, outputs // tile, one_tile, 0)
 
-    for piece in range(pieces):
+    def take(piece):
         columns = pl.ds(piece * step_width, step_width)
         if relay:
-            head_copies[piece][1].wait_recv()
-            pass_on(piece)
+            for later in range(piece + 1 if piece else 0, min(piece + 2, pieces)):
+                head_copies[later][1].wait_recv()
+                pass_on(later)
         for number, copy in enumerate(head_copies[piece]):
             if not relay or number != 1:
                 copy.wait_recv()
@@ -345,9 +352,10 @@
 
         def fill(expert, carry):
             start = pl.multiple_of(expert * slot, 16)
-            send_ref[expert, :, columns] = jnp.dot(
+            taken = jnp.dot(
                 place_ref[pl.ds(start, slot), :], plane, preferred_element_type=jnp.float32
-            ).astype(send_ref.dtype)
+            )
+            send_ref[expert, :, columns] = scaled(taken, start)
             return carry
 
         lax.fori_loop(0, blocks, fill, 0)
@@ -370,11 +378,11 @@
             for load in loads:
                 load.wait()
         for expert in range(shared):
+            start = (blocks + expert) * slot
             taken = jnp.dot(
-                place_ref[pl.ds((blocks + expert) * slot, slot), :],
-                plane,
-                preferred_element_type=jnp.float32,
-            ).astype(shared_ref.dtype)
+                place_ref[pl.ds(start, slot), :], plane, preferred_element_type=jnp.float32
+            )
+            taken = scaled(taken, start)
             shared_ref[expert, :, columns] = taken
             product = meet(
                 taken, weight_part(shared_held_ref.at[expert], columns, by_columns), by_columns
@@ -382,44 +390,53 @@
             if piece:
                 product = product + shared_out_ref[expert]
             shared_out_ref[expert] = product
-        if piece:
-            consume(piece - 1)
-    consume(pieces - 1)
-    for copies in head_copies:
-        for number, copy in enumerate(copies):
-            if relay and number != 1:
-                pl.when(jnp.logical_not(far(head_peers[number])))(copy.wait_send)
-            else:
+
+    def step(number):
+        if number < pieces:
+            take(number)
+        if number >= lag:
+            consume(number - lag)
+
+    def end():
+        for copies in head_copies:
+            for number, copy in enumerate(copies):
+                if relay and number != 1:
+                    pl.when(jnp.logical_not(far(head_peers[number])))(copy.wait_send)
+                else:
+                    copy.wait_send()
+        for copy in relayed:
+            pl.when(inner)(copy.wait_send)
+        for copies in blk_copies:
+            for copy in copies:
                 copy.wait_send()
-    for copy in relayed:
-        pl.when(inner)(copy.wait_send)
-    for copies in blk_copies:
-        for copy in copies:
-            copy.wait_send()
-
-
-def dispatch(rows, places, weights, by_columns, pieces=6, window=2):
+
+    steps = [functools.partial(step, number) for number in range(pieces + lag)]
+    return [begin, *steps, end]
+
+
+def dispatch_plan(rows, places, scale, weights, by_columns):
     heads, blocks = lax.axis_size("head"), lax.axis_size("blk")
     count, width = rows.shape
     (own_weight, shared_weight) = weights
     shared = shared_weight.shape[0]
     slot = places.shape[0] // (blocks + shared)
     outputs = own_weight.shape[0 if by_columns else 1]
-    outs = [
-        jax.ShapeDtypeStruct((heads, count, width), jnp.bfloat16),
-        jax.ShapeDtypeStruct((blocks, slot, width), jnp.bfloat16),
-        jax.ShapeDtypeStruct((shared, slot, width), jnp.bfloat16),
-        jax.ShapeDtypeStruct((blocks * slot, outputs), jnp.float32),
-        jax.ShapeDtypeStruct((shared, slot, outputs), jnp.float32),
-    ]
+    pieces = DISPATCH_PIECES
     vmem = pl.BlockSpec(memory_space=pltpu.VMEM)
     anywhere = pl.BlockSpec(memory_space=pl.ANY)
-    return pl.pallas_call(
-        functools.partial(dispatch_kernel, heads, blocks, pieces, window, by_columns),
-        out_shape=outs,
-        in_specs=[vmem, vmem, anywhere, anywhere],
-        out_specs=[vmem] * 5,
-        scratch_shapes=[
+    scales = [] if scale is None else [scale]
+    return (
+        [rows, places, *scales, own_weight, shared_weight],
+        [vmem, vmem, *([vmem] * len(scales)), anywhere, anywhere],
+        [
+            jax.ShapeDtypeStruct((heads, count, width), jnp.bfloat16),
+            jax.ShapeDtypeStruct((blocks, slot, width), jnp.bfloat16),
+            jax.ShapeDtypeStruct((shared, slot, width), jnp.bfloat16),
+            jax.ShapeDtypeStruct((blocks * slot, outputs), jnp.float32),
+            jax.ShapeDtypeStruct((shared, slot, outputs), jnp.float32),
+        ],
+        [vmem] * 5,
+        [
             pltpu.VMEM((blocks, slot, width), jnp.bfloat16),
             pltpu.VMEM(own_weight.shape, jnp.bfloat16),
             pltpu.VMEM(shared_weight.shape, jnp.bfloat16),
@@ -429,45 +446,610 @@
             pltpu.SemaphoreType.DMA((pieces * (blocks - 1),)),
             pltpu.SemaphoreType.DMA((2,)),
         ],
+    )
+
+
+def staged_call(plans, name, millions):
+    heads, blocks = lax.axis_size("head"), lax.axis_size("blk")
+    inputs = [len(plan[2]) for plan in plans]
+    outputs = [len(plan[4]) for plan in plans]
+    scratches = [len(plan[6]) for plan in plans]
+
+    def kernel(*refs):
+        _, _, head_peers, blk_peers = plane_peers(heads, blocks)
+        greet(head_peers + blk_peers)
+        lists = []
+        for number, plan in enumerate(plans):
+            first = sum(inputs[:number])
+            given = list(refs[first : first + inputs[number]])
+            if not plan[7]:
+                given.insert(2 if plan[0][0] == "dispatch" else 3, None)
+            first = sum(inputs) + sum(outputs[:number])
+            given += refs[first : first + outputs[number]]
+            first = sum(inputs) + sum(outputs) + sum(scratches[:number])
+            given += refs[first : first + scratches[number]]
+            lists.append(plan[1](given))
+        for index in range(max(len(stages) for stages in lists)):
+            for stages in lists:
+                if index < len(stages):
+                    stages[index]()
+
+    arrays = [array for plan in plans for array in plan[2]]
+    results = pl.pallas_call(
+        kernel,
+        out_shape=[out for plan in plans for out in plan[4]],
+        in_specs=[spec for plan in plans for spec in plan[3]],
+        out_specs=[spec for plan in plans for spec in plan[5]],
+        scratch_shapes=[scratch for plan in plans for scratch in plan[6]],
         compiler_params=pltpu.CompilerParams(
-            collective_id=kernel_number("dispatch", by_columns),
+            collective_id=kernel_number(*(plan[0] for plan in plans)),
+            has_side_effects=True,
+            vmem_limit_bytes=60 * 1024 * 1024,
+        ),
+        cost_estimate=pl.CostEstimate(
+            flops=0, bytes_accessed=millions << 20, transcendentals=0
+        ),
+        name=name,
+    )(*arrays)
+    return [
+        results[sum(outputs[:number]) : sum(outputs[: number + 1])] for number in range(len(plans))
+    ]
+
+
+def dispatch_call(rows, places, scale, weights, by_columns):
+    heads, blocks = lax.axis_size("head"), lax.axis_size("blk")
+    return (
+        ("dispatch", by_columns, scale is not None),
+        functools.partial(dispatch_stages, heads, blocks, by_columns),
+        *dispatch_plan(rows, places, scale, weights, by_columns),
+        scale is not None,
+    )
+
+
+def turn_heads(values, cosine, sine):
+    lane = lax.broadcasted_iota(jnp.int32, values.shape, 1) % HEAD_SIZE
+    half = HEAD_SIZE // 2
+    width = values.shape[1]
+    swapped = jnp.where(
+        lane < half, pltpu.roll(values, width - half, 1), pltpu.roll(values, half, 1)
+    )
+    return values * cosine + swapped * sine
+
+
+def project_kernel(
+    heads,
+    blocks,
+    pieces,
+    layer,
+    own_ref,
+    weight_ref,
+    cosine_ref,
+    sine_ref,
+    moved_ref,
+    plane_ref,
+    query_ref,
+    pair_ref,
+    moved_out_ref,
+    head_send,
+    head_recv,
+    pair_send,
+    pair_recv,
+    moved_send,
+    moved_recv,
+    local_sem,
+):
+    head, blk, head_peers, blk_peers = plane_peers(heads, blocks)
+    chips = blocks // 2
+    chip, core = blk // 2, lax.rem(blk, 2)
+    sibling = (head, chip * 2 + 1 - core)
+    rows, width = own_ref.shape
+    count = rows // pieces
+    slots, _, _, resident, pair_columns = pair_ref.shape
+    query_columns = query_ref.shape[2]
+    inner = jnp.logical_and(head > 0, head < heads - 1)
+    greet(head_peers + blk_peers)
+
+    def far(peer):
+        return jnp.abs(peer[0] - head) == heads - 1
+
+    def place(piece):
+        return piece * count // resident, pl.ds(piece * count % resident, count)
+
+    head_copies = []
+    relayed = []
+    for piece in range(pieces):
+        part = pl.ds(piece * count, count)
+        copies = []
+        for number, peer in enumerate(head_peers):
+            copy = remote(
+                own_ref.at[part],
+                plane_ref.at[head, part],
+                (head_send, head_recv),
+                piece * heads + number,
+                peer,
+            )
+            copies.append(copy)
+            if number != 1:
+                pl.when(jnp.logical_not(far(peer)))(copy.start)
+            else:
+                copy.start()
+        head_copies.append(copies)
+    moved = []
+    if layer is not None:
+        moved = [
+            started(
+                remote(
+                    moved_ref.at[layer, peer[1]],
+                    moved_out_ref.at[blk],
+                    (moved_send, moved_recv),
+                    number,
+                    peer,
+                )
+            )
+            for number, peer in enumerate(blk_peers)
+        ]
+        local = pltpu.make_async_copy(moved_ref.at[layer, blk], moved_out_ref.at[blk], local_sem)
+        local.start()
+    plane_ref[head] = own_ref[...]
+
+    def pass_on(piece):
+        head_copies[piece][1].wait_recv()
+        part = pl.ds(piece * count, count)
+        rows_there = plane_ref.at[lax.rem(head + 2, heads), part]
+        copy = remote(
+            rows_there,
+            rows_there,
+            (head_send, head_recv),
+            piece * heads + heads - 1,
+            ((head - 1) * (heads - 1), blk),
+            piece * heads + jnp.where(head == 1, 0, heads - 2),
+        )
+        relayed.append(copy)
+        pl.when(inner)(copy.start)
+
+    pair_copies = []
+    forwards = []
+
+    def forward(piece):
+        slot, part = place(piece)
+        for step in range(1, chips):
+            pair_copies[piece][step - 1].wait_recv()
+            origin = lax.rem(chip + chips - step, chips) * 2 + core
+            there = pair_ref.at[slot, :, origin, part]
+            forwards.append(
+                started(
+                    remote(
+                        there,
+                        there,
+                        (pair_send, pair_recv),
+                        piece * blocks + chips - 1 + step,
+                        sibling,
+                    )
+                )
+            )
+
+    tile = 2 * HEAD_SIZE
+    for piece in range(pieces):
+        for later in range(piece + 1 if piece else 0, min(piece + 2, pieces)):
+            pass_on(later)
+        for number in range(heads - 1):
+            if number != 1:
+                head_copies[piece][number].wait_recv()
+        part = pl.ds(piece * count, count)
+        slot, inside = place(piece)
+        projected = jnp.dot(
+            plane_ref[:, part, :].reshape(heads * count, width),
+            weight_ref[...],
+            preferred_element_type=jnp.float32,
+        )
+        cosine = cosine_ref[:, part, :].reshape(heads * count, tile)
+        sine = sine_ref[:, part, :].reshape(heads * count, tile)
+        turned = jnp.concatenate(
+            [
+                turn_heads(projected[:, start : start + tile], cosine, sine)
+                for start in range(0, query_columns, tile)
+            ],
+            axis=1,
+        ).astype(query_ref.dtype)
+        is_key = lax.broadcasted_iota(jnp.int32, cosine.shape, 1) < HEAD_SIZE
+        key_cosine = jnp.where(is_key, cosine, 1.0)
+        key_sine = jnp.where(is_key, sine, 0.0)
+        pairs = jnp.concatenate(
+            [
+                turn_heads(projected[:, start : start + tile], key_cosine, key_sine)
+                for start in range(query_columns, query_columns + pair_columns, tile)
+            ],
+            axis=1,
+        ).astype(pair_ref.dtype)
+        for there in range(heads):
+            taken = slice(there * count, (there + 1) * count)
+            query_ref[slot, pl.ds(there * resident + piece * count % resident, count), :] = turned[
+                taken
+            ]
+            pair_ref[slot, there, blk, inside, :] = pairs[taken]
+        mine = pair_ref.at[slot, :, blk, inside]
+        targets = [
+            (head, lax.rem(chip + step, chips) * 2 + core) for step in range(1, chips)
+        ] + [sibling]
+        pair_copies.append(
+            [
+                started(
+                    remote(mine, mine, (pair_send, pair_recv), piece * blocks + number, peer)
+                )
+                for number, peer in enumerate(targets)
+            ]
+        )
+        if piece:
+            forward(piece - 1)
+    forward(pieces - 1)
+    for copies in pair_copies:
+        for copy in copies[:-1]:
+            copy.wait_send()
+        copies[-1].wait()
+    for copy in forwards:
+        copy.wait()
+    for copies in head_copies:
+        for number, copy in enumerate(copies):
+            if number != 1:
+                pl.when(jnp.logical_not(far(head_peers[number])))(copy.wait_send)
+            else:
+                copy.wait_send()
+    for copy in relayed:
+        pl.when(inner)(copy.wait_send)
+    for copy in moved:
+        copy.wait()
+    if moved:
+        local.wait()
+
+
+def project(rows, weight, cosine, sine, moved, layer, pair_columns, resident, pieces=4):
+    heads, blocks = lax.axis_size("head"), lax.axis_size("blk")
+    count, width = rows.shape
+    slots = count // resident
+    outs = [
+        jax.ShapeDtypeStruct((heads, count, width), jnp.bfloat16),
+        jax.ShapeDtypeStruct(
+            (slots, heads * resident, weight.shape[1] - pair_columns), jnp.bfloat16
+        ),
+        jax.ShapeDtypeStruct((slots, heads, blocks, resident, pair_columns), jnp.bfloat16),
+        jax.ShapeDtypeStruct((blocks,) + moved.shape[2:], moved.dtype),
+    ]
+    vmem = pl.BlockSpec(memory_space=pltpu.VMEM)
+    anywhere = pl.BlockSpec(memory_space=pl.ANY)
+    return pl.pallas_call(
+        functools.partial(project_kernel, heads, blocks, pieces, layer),
+        out_shape=outs,
+        in_specs=[vmem] * 4 + [anywhere],
+        out_specs=[vmem] * 3 + [anywhere],
+        scratch_shapes=[
+            pltpu.SemaphoreType.DMA((pieces * heads,)),
+            pltpu.SemaphoreType.DMA((pieces * heads,)),
+            pltpu.SemaphoreType.DMA((pieces * blocks,)),
+            pltpu.SemaphoreType.DMA((pieces * blocks,)),
+            pltpu.SemaphoreType.DMA((blocks,)),
+            pltpu.SemaphoreType.DMA((blocks,)),
+            pltpu.SemaphoreType.DMA,
+        ],
+        compiler_params=pltpu.CompilerParams(
+            collective_id=kernel_number("project", layer),
             has_side_effects=True,
             vmem_limit_bytes=56 * 1024 * 1024,
         ),
-        cost_estimate=pl.CostEstimate(flops=0, bytes_accessed=170 << 20, transcendentals=0),
-        name="dispatch",
-    )(rows, places, own_weight, shared_weight)
-
-
-def combine_kernel(
+        cost_estimate=pl.CostEstimate(flops=0, bytes_accessed=130 << 20, transcendentals=0),
+        name="project",
+    )(rows, weight, cosine, sine, moved)
+
+
+def unproject_kernel(
     heads,
     blocks,
     pieces,
-    by_columns,
-    extra,
-    units_ref,
-    shared_units_ref,
-    place_ref,
+    items,
+    grad_query_ref,
+    grad_pair_ref,
     weight_ref,
-    shared_weight_ref,
+    cosine_ref,
+    sine_ref,
     *refs,
 ):
+    moved_refs = refs[:items]
+    grad_ref, out_ref = refs[items : items + 2]
+    moved_out_refs = refs[items + 2 : 2 * items + 2]
+    (
+        near_ref,
+        sum_ref,
+        far_ref,
+        product_ref,
+        part_ref,
+        landed_ref,
+        relay_ref,
+        near_send,
+        near_recv,
+        chip_send,
+        chip_recv,
+        head_send,
+        head_recv,
+        moved_send,
+        moved_recv,
+        local_sems,
+    ) = refs[2 * items + 2 :]
+    head, blk, head_peers, blk_peers = plane_peers(heads, blocks)
+    chips = blocks // 2
+    chip, core = blk // 2, lax.rem(blk, 2)
+    sibling = (head, chip * 2 + 1 - core)
+    rows, width = out_ref.shape
+    count = rows // pieces
+    resident, pair_columns = grad_pair_ref.shape[4:]
+    query_columns = grad_query_ref.shape[2]
+    inner = jnp.logical_and(head > 0, head < heads - 1)
+    chip_peers = [(head, lax.rem(chip + step, chips) * 2 + core) for step in range(1, chips)]
+    greet(head_peers + blk_peers)
+
+    def far(peer):
+        return jnp.abs(peer[0] - head) == heads - 1
+
+    def peer_origin(peer):
+        return lax.rem(2 * head + heads - peer[0], heads)
+
+    def place(piece):
+        return piece * count // resident, pl.ds(piece * count % resident, count)
+
+    near_copies = []
+    for piece in range(pieces):
+        slot, inside = place(piece)
+        near_copies.append(
+            started(
+                remote(
+                    grad_pair_ref.at[slot, :, :, 1 - core, inside],
+                    near_ref.at[piece],
+                    (near_send, near_recv),
+                    piece,
+                    sibling,
+                )
+            )
+        )
+    chip_copies = []
+    head_copies = []
+    moved = []
+
+    def add_cores(piece):
+        slot, inside = place(piece)
+        near_copies[piece].wait_recv()
+        sum_ref[piece] = (
+            grad_pair_ref[slot, :, :, core, inside, :].astype(jnp.float32)
+            + near_ref[piece].astype(jnp.float32)
+        ).astype(sum_ref.dtype)
+        chip_copies.append(
+            [
+                started(
+                    remote(
+                        sum_ref.at[piece, :, peer[1] // 2],
+                        far_ref.at[piece, chip],
+                        (chip_send, chip_recv),
+                        piece * chips + number,
+                        peer,
+                    )
+                )
+                for number, peer in enumerate(chip_peers)
+            ]
+        )
+
+    def through_copy(piece, peer):
+        part = pl.ds(piece * count, count)
+        return remote(
+            part_ref.at[peer[0], part],
+            relay_ref.at[part],
+            (head_send, head_recv),
+            piece * heads + heads - 1,
+            (jnp.where(head == 0, 1, heads - 2), blk),
+        )
+
+    tile = 2 * HEAD_SIZE
+
+    def multiply(piece):
+        slot, inside = place(piece)
+        part = pl.ds(piece * count, count)
+        for copy in chip_copies[piece]:
+            copy.wait_recv()
+        pairs = sum_ref[piece, :, chip].astype(jnp.float32)
+        for peer in chip_peers:
+            pairs = pairs + far_ref[piece, peer[1] // 2].astype(jnp.float32)
+        pairs = pairs.reshape(heads * count, pair_columns)
+        pairs = pairs.astype(jnp.bfloat16).astype(jnp.float32)
+        queries = jnp.concatenate(
+            [
+                grad_query_ref[
+                    slot, pl.ds(there * resident + piece * count % resident, count), :
+                ]
+                for there in range(heads)
+            ],
+            axis=0,
+        ).astype(jnp.float32)
+        cosine = cosine_ref[:, part, :].reshape(heads * count, tile)
+        sine = -sine_ref[:, part, :].reshape(heads * count, tile)
+        is_key = lax.broadcasted_iota(jnp.int32, cosine.shape, 1) < HEAD_SIZE
+        key_cosine = jnp.where(is_key, cosine, 1.0)
+        key_sine = jnp.where(is_key, sine, 0.0)
+        turned = jnp.concatenate(
+            [
+                turn_heads(queries[:, start : start + tile], cosine, sine)
+                for start in range(0, query_columns, tile)
+            ]
+            + [
+                turn_heads(pairs[:, start : start + tile], key_cosine, key_sine)
+                for start in range(0, pair_columns, tile)
+            ],
+            axis=1,
+        ).astype(grad_ref.dtype)
+        grad_ref[:, part, :] = turned.reshape(heads, count, query_columns + pair_columns)
+        product_ref[...] = dot_last(turned, weight_ref[...]).reshape(heads, count, width)
+        sent = []
+        for number, peer in enumerate(head_peers):
+            part_ref[peer[0], part, :] = product_ref[peer[0]].astype(part_ref.dtype)
+            copy = remote(
+                part_ref.at[peer[0], part],
+                landed_ref.at[head, part],
+                (head_send, head_recv),
+                piece * heads + number,
+                peer,
+            )
+            sent.append(copy)
+            if number == 1:
+                pl.when(jnp.logical_not(inner))(copy.start)
+            else:
+                distant = far(peer)
+                pl.when(jnp.logical_not(distant))(copy.start)
+                pl.when(distant)(through_copy(piece, peer).start)
+        head_copies.append(sent)
+        out_ref[part, :] = product_ref[head]
+
+    def pass_on(piece):
+        part = pl.ds(piece * count, count)
+        target = lax.rem(head + 2, heads)
+
+        @pl.when(inner)
+        def _():
+            through_copy(piece, (target, blk)).wait_recv()
+            part_ref[target, part, :] = (
+                part_ref[target, part, :].astype(jnp.float32)
+                + relay_ref[part, :].astype(jnp.float32)
+            ).astype(part_ref.dtype)
+            head_copies[piece][1].start()
+
+    def finish(piece):
+        part = pl.ds(piece * count, count)
+        for number, peer in enumerate(head_peers):
+            copy = head_copies[piece][number]
+
+            def add(copy=copy, peer=peer):
+                copy.wait_recv()
+                out_ref[part, :] += landed_ref[peer_origin(peer), part, :].astype(jnp.float32)
+
+            if number != 1:
+                pl.when(jnp.logical_not(far((peer_origin(peer), blk))))(add)
+            else:
+                add()
+
+    for step in range(pieces + 3):
+        if step < pieces:
+            add_cores(step)
+        if step == pieces - 1:
+            for item in range(items):
+                source, target = moved_refs[item], moved_out_refs[item]
+                moved += [
+                    started(
+                        remote(
+                            source.at[peer[1]],
+                            target.at[blk],
+                            (moved_send, moved_recv),
+                            item * blocks + number,
+                            peer,
+                        )
+                    )
+                    for number, peer in enumerate(blk_peers)
+                ]
+                local = pltpu.make_async_copy(
+                    source.at[blk], target.at[blk], local_sems.at[item]
+                )
+                moved.append(started(local))
+        if 0 < step <= pieces:
+            multiply(step - 1)
+        if 1 < step <= pieces + 1:
+            pass_on(step - 2)
+        if step > 2:
+            finish(step - 3)
+    for copy in near_copies:
+        copy.wait_send()
+    for copies in chip_copies:
+        for copy in copies:
+            copy.wait_send()
+    for piece, copies in enumerate(head_copies):
+        for number, copy in enumerate(copies):
+            if number != 1:
+                distant = far(head_peers[number])
+                pl.when(jnp.logical_not(distant))(copy.wait_send)
+                pl.when(distant)(through_copy(piece, head_peers[number]).wait_send)
+            else:
+                copy.wait_send()
+    for copy in moved:
+        copy.wait()
+
+
+def unproject(grad_queries, grad_pairs, weight, cosine, sine, moved, after, pieces=4):
+    heads, blocks = lax.axis_size("head"), lax.axis_size("blk")
+    chips = blocks // 2
+    slots, _, _, _, resident, pair_columns = grad_pairs.shape
+    rows = slots * resident
+    count = rows // pieces
+    width, columns = weight.shape
+    outs = [
+        jax.ShapeDtypeStruct((heads, rows, columns), jnp.bfloat16),
+        jax.ShapeDtypeStruct((rows, width), jnp.float32),
+    ] + [jax.ShapeDtypeStruct(array.shape, array.dtype) for array in moved]
+    vmem = pl.BlockSpec(memory_space=pltpu.VMEM)
+    anywhere = pl.BlockSpec(memory_space=pl.ANY)
+    items = len(moved)
+
+    def kernel(*refs):
+        given = refs[: 5 + items]
+        unproject_kernel(
+            heads, blocks, pieces, items, *given, *refs[5 + items + len(after) :]
+        )
+
+    return pl.pallas_call(
+        kernel,
+        out_shape=outs,
+        in_specs=[vmem] * 5 + [anywhere] * (items + len(after)),
+        out_specs=[vmem] * 2 + [anywhere] * items,
+        scratch_shapes=[
+            pltpu.VMEM((pieces, heads, chips, count, pair_columns), jnp.bfloat16),
+            pltpu.VMEM((pieces, heads, chips, count, pair_columns), jnp.bfloat16),
+            pltpu.VMEM((pieces, chips, heads, count, pair_columns), jnp.bfloat16),
+            pltpu.VMEM((heads, count, width), jnp.float32),
+            pltpu.VMEM((heads, rows, width), jnp.bfloat16),
+            pltpu.VMEM((heads, rows, width), jnp.bfloat16),
+            pltpu.VMEM((rows, width), jnp.bfloat16),
+            pltpu.SemaphoreType.DMA((pieces,)),
+            pltpu.SemaphoreType.DMA((pieces,)),
+            pltpu.SemaphoreType.DMA((pieces * chips,)),
+            pltpu.SemaphoreType.DMA((pieces * chips,)),
+            pltpu.SemaphoreType.DMA((pieces * heads,)),
+            pltpu.SemaphoreType.DMA((pieces * heads,)),
+            pltpu.SemaphoreType.DMA((items * blocks,)),
+            pltpu.SemaphoreType.DMA((items * blocks,)),
+            pltpu.SemaphoreType.DMA((items,)),
+        ],
+        compiler_params=pltpu.CompilerParams(
+            collective_id=kernel_number(
+                "unproject", *(array.shape for array in (*moved, *after))
+            ),
+            has_side_effects=True,
+            vmem_limit_bytes=56 * 1024 * 1024,
+        ),
+        cost_estimate=pl.CostEstimate(flops=0, bytes_accessed=150 << 20, transcendentals=0),
+        name="unproject",
+    )(grad_queries, grad_pairs, weight, cosine, sine, *moved, *after)
+
+
+def combine_stages(heads, blocks, by_columns, extra, refs):
+    units_ref, shared_units_ref, place_ref, scale_ref, weight_ref, shared_weight_ref, *refs = refs
     extra_ref, *refs = refs if extra else (None, *refs)
     out_ref, returned_ref, *refs = refs
     extra_out_ref, *refs = refs if extra else (None, *refs)
     (
-    made_ref,
-    part_ref,
-    landed_ref,
-    relay_ref,
-    held_ref,
-    shared_held_ref,
-    head_send,
-    head_recv,
-    blk_send,
-    blk_recv,
-    local_sems,
+        made_ref,
+        part_ref,
+        landed_ref,
+        relay_ref,
+        held_ref,
+        shared_held_ref,
+        head_send,
+        head_recv,
+        blk_send,
+        blk_recv,
+        local_sems,
     ) = refs
+    pieces = COMBINE_PIECES
     head, blk, head_peers, blk_peers = plane_peers(heads, blocks)
     rows, width = out_ref.shape
     slot = returned_ref.shape[1]
@@ -475,35 +1057,36 @@
     step_width = width // pieces
     relay = heads == 4
     inner = jnp.logical_and(head > 0, head < heads - 1)
-    greet(head_peers + blk_peers)
     loads = [
         pltpu.make_async_copy(weight_ref, held_ref, local_sems.at[0]),
         pltpu.make_async_copy(shared_weight_ref, shared_held_ref, local_sems.at[1]),
     ]
-    for load in loads:
-        load.start()
     extra_copies = []
-    if extra:
-        loads.append(
-            pltpu.make_async_copy(extra_ref, extra_out_ref.at[head], local_sems.at[2])
-        )
-        loads[-1].start()
-        extra_copies = [
-            started(
-                remote(
-                    extra_ref,
-                    extra_out_ref.at[head],
-                    (head_send, head_recv),
-                    pieces * heads + number,
-                    peer,
-                )
-            )
-            for number, peer in enumerate(head_peers)
-        ]
-    for load in loads:
-        load.wait()
     head_copies = []
     blk_copies = []
+
+    def begin():
+        if extra:
+            loads.append(
+                pltpu.make_async_copy(extra_ref, extra_out_ref.at[head], local_sems.at[2])
+            )
+        for load in loads:
+            load.start()
+        if extra:
+            extra_copies.extend(
+                started(
+                    remote(
+                        extra_ref,
+                        extra_out_ref.at[head],
+                        (head_send, head_recv),
+                        pieces * heads + number,
+                        peer,
+                    )
+                )
+                for number, peer in enumerate(head_peers)
+            )
+        for load in loads:
+            load.wait()
 
     def produce(piece):
         columns = pl.ds(piece * step_width, step_width)
@@ -540,11 +1123,29 @@
                 by_columns,
             ).astype(returned_ref.dtype)
 
+    def far(peer):
+        return jnp.abs(peer[0] - head) == heads - 1
+
+    def peer_origin(peer):
+        return lax.rem(2 * head + heads - peer[0], heads)
+
+    def through_copy(piece, peer):
+        columns = pl.ds(piece * step_width, step_width)
+        return remote(
+            part_ref.at[peer[0], :, columns],
+            relay_ref.at[:, columns],
+            (head_send, head_recv),
+            piece * heads + heads - 1,
+            (jnp.where(head == 0, 1, heads - 2), blk),
+        )
+
     def gather(piece):
         columns = pl.ds(piece * step_width, step_width)
         for copy in blk_copies[piece]:
             copy.wait_recv()
         returned = returned_ref[:, :, columns].reshape((blocks + shared) * slot, step_width)
+        if scale_ref is not None:
+            returned = (returned.astype(jnp.float32) * scale_ref[...]).astype(returned_ref.dtype)
 
         def part(owner):
             start = pl.multiple_of(owner * rows, 16)
@@ -570,23 +1171,9 @@
             else:
                 distant = far(peer)
                 pl.when(jnp.logical_not(distant))(copy.start)
-                through = through_copy(piece, peer)
-                pl.when(distant)(through.start)
+                pl.when(distant)(through_copy(piece, peer).start)
         head_copies.append(sent)
         out_ref[:, columns] = part(head)
-
-    def far(peer):
-        return jnp.abs(peer[0] - head) == heads - 1
-
-    def through_copy(piece, peer):
-        columns = pl.ds(piece * step_width, step_width)
-        return remote(
-            part_ref.at[peer[0], :, columns],
-            relay_ref.at[:, columns],
-            (head_send, head_recv),
-            piece * heads + heads - 1,
-            (jnp.where(head == 0, 1, heads - 2), blk),
-        )
 
     def pass_on(piece):
         columns = pl.ds(piece * step_width, step_width)
@@ -617,56 +1204,60 @@
             else:
                 add()
 
-    def peer_origin(peer):
-        return lax.rem(2 * head + heads - peer[0], heads)
-
     lag = 3 if relay else 2
-    for step in range(pieces + lag):
-        if step < pieces:
-            produce(step)
-        if 0 < step <= pieces:
-            gather(step - 1)
-        if relay and 1 < step <= pieces + 1:
-            pass_on(step - 2)
-        if step >= lag:
-            finish(step - lag)
-    for piece, copies in enumerate(head_copies):
-        for number, copy in enumerate(copies):
-            if relay and number != 1:
-                distant = far(head_peers[number])
-                pl.when(jnp.logical_not(distant))(copy.wait_send)
-                pl.when(distant)(through_copy(piece, head_peers[number]).wait_send)
-            else:
+
+    def step(number):
+        if number < pieces:
+            produce(number)
+        if 0 < number <= pieces:
+            gather(number - 1)
+        if relay and 1 < number <= pieces + 1:
+            pass_on(number - 2)
+        if number >= lag:
+            finish(number - lag)
+
+    def end():
+        for piece, copies in enumerate(head_copies):
+            for number, copy in enumerate(copies):
+                if relay and number != 1:
+                    distant = far(head_peers[number])
+                    pl.when(jnp.logical_not(distant))(copy.wait_send)
+                    pl.when(distant)(through_copy(piece, head_peers[number]).wait_send)
+                else:
+                    copy.wait_send()
+        for copy in extra_copies:
+            copy.wait()
+        for copies in blk_copies:
+            for copy in copies:
                 copy.wait_send()
-    for copy in extra_copies:
-        copy.wait()
-    for copies in blk_copies:
-        for copy in copies:
-            copy.wait_send()
-
-
-def combine(
-    units, shared_units, places, weights, by_columns, extra=None, pieces=6
-):
+
+    steps = [functools.partial(step, number) for number in range(pieces + lag)]
+    return [begin, *steps, end]
+
+
+def combine_call(units, shared_units, places, scale, weights, by_columns, extra=None):
     heads, blocks = lax.axis_size("head"), lax.axis_size("blk")
     (own_weight, shared_weight) = weights
     shared, slot = shared_units.shape[:2]
     count = places.shape[0] // heads
     width = own_weight.shape[0 if by_columns else 1]
-    outs = [
-        jax.ShapeDtypeStruct((count, width), jnp.float32),
-        jax.ShapeDtypeStruct((blocks + shared, slot, width), jnp.bfloat16),
-    ]
+    pieces = COMBINE_PIECES
     vmem = pl.BlockSpec(memory_space=pltpu.VMEM)
     anywhere = pl.BlockSpec(memory_space=pl.ANY)
+    scales = [] if scale is None else [scale]
     extras = [] if extra is None else [extra]
-    outs += [jax.ShapeDtypeStruct((heads,) + array.shape, array.dtype) for array in extras]
-    return pl.pallas_call(
-        functools.partial(combine_kernel, heads, blocks, pieces, by_columns, bool(extras)),
-        out_shape=outs,
-        in_specs=[vmem, vmem, vmem, anywhere, anywhere] + [anywhere] * len(extras),
-        out_specs=[vmem] * 2 + [anywhere] * len(extras),
-        scratch_shapes=[
+    return (
+        ("combine", by_columns, scale is not None, extra is not None),
+        functools.partial(combine_stages, heads, blocks, by_columns, bool(extras)),
+        [units, shared_units, places, *scales, own_weight, shared_weight, *extras],
+        [vmem] * (3 + len(scales)) + [anywhere] * (2 + len(extras)),
+        [
+            jax.ShapeDtypeStruct((count, width), jnp.float32),
+            jax.ShapeDtypeStruct((blocks + shared, slot, width), jnp.bfloat16),
+            *(jax.ShapeDtypeStruct((heads,) + array.shape, array.dtype) for array in extras),
+        ],
+        [vmem] * 2 + [anywhere] * len(extras),
+        [
             pltpu.VMEM((blocks, slot, width), jnp.bfloat16),
             pltpu.VMEM((heads, count, width), jnp.bfloat16),
             pltpu.VMEM((heads, count, width), jnp.bfloat16),
@@ -679,14 +1270,8 @@
             pltpu.SemaphoreType.DMA((pieces * (blocks - 1),)),
             pltpu.SemaphoreType.DMA((3,)),
         ],
-        compiler_params=pltpu.CompilerParams(
-            collective_id=kernel_number("combine", by_columns),
-            has_side_effects=True,
-            vmem_limit_bytes=56 * 1024 * 1024,
-        ),
-        cost_estimate=pl.CostEstimate(flops=0, bytes_accessed=170 << 20, transcendentals=0),
-        name="combine",
-    )(units, shared_units, places, own_weight, shared_weight, *extras)
+        scale is not None,
+    )
 
 
 def head_parts(partial):
@@ -895,6 +1480,10 @@
     angles = plane_places[:, None] * frequency[None, :]
     cosine = jnp.cos(angles)
     sine = jnp.sin(angles)
+    repeats = 2 * HEAD_SIZE // half
+    tile_cosine = jnp.concatenate([cosine] * repeats, axis=1).reshape(heads_count, slot_rows, -1)
+    tile_sine = jnp.concatenate([-sine, sine] * (repeats // 2), axis=1)
+    tile_sine = tile_sine.reshape(heads_count, slot_rows, -1)
     info = jnp.concatenate([blk_index[None].astype(jnp.int32), lengths])
 
     expert_ids = jnp.arange(EXPERTS, dtype=jnp.int32)
@@ -975,47 +1564,66 @@
             return []
         return [received.reshape(owned_total, -1, received.shape[-1])]
 
-    def moe_in(rows, turned_places, sets, which):
-        if owned == 1 and owned_total < experts_local:
-            own_weight, shared_weight = (matrices[which] for matrices in sets)
-            plane, own, shared, own_out, shared_out = dispatch(
-                rows, turned_places, (own_weight[0], shared_weight), which == 1
-            )
-            return (
-                plane.reshape(all_tokens, width),
-                [own.reshape(1, -1, width), shared],
-                [own_out[None], shared_out],
-            )
+    staged = owned == 1 and owned_total < experts_local
+
+    def matrices(sets, which):
+        own_weight, shared_weight = (mats[which] for mats in sets)
+        return (own_weight[0], shared_weight)
+
+    def unpack_in(results):
+        plane, own, shared, own_out, shared_out = results
+        return (
+            plane.reshape(all_tokens, width),
+            [own.reshape(1, -1, width), shared],
+            [own_out[None], shared_out],
+        )
+
+    def unpack_out(results):
+        total, returned, *extras = results
+        return (total, returned.reshape(-1, width), *extras)
+
+    def moe_in(rows, turned_places, scale, sets, which):
+        if staged:
+            plan = dispatch_call(rows, turned_places, scale, matrices(sets, which), which == 1)
+            return unpack_in(staged_call([plan], "dispatch", 170)[0])
         (plane,) = exchange(("head_gather", rows))
         plane = plane.reshape(all_tokens, width)
-        queues = [
-            part
-            for part in to_experts(mm("rt,td->rd", turned_places, plane).astype(jnp.bfloat16))
-            if part is not None
-        ]
+        queues = mm("rt,td->rd", turned_places, plane)
+        if scale is not None:
+            queues = queues * scale
+        queues = [part for part in to_experts(queues.astype(jnp.bfloat16)) if part is not None]
         spec = ("erd,edf->erf", "erd,efd->erf")[which]
         return (plane, queues, [mm(spec, rows, mats[which]) for rows, mats in zip(queues, sets)])
 
-    def moe_out(units, places, sets, which, extra=None):
-        if owned == 1 and owned_total < experts_local:
-            own_weight, shared_weight = (matrices[which] for matrices in sets)
-            total, returned, *extras = combine(
-                units[0][0],
-                units[1],
-                places,
-                (own_weight[0], shared_weight),
-                which == 0,
-                extra,
-            )
-            return (total, returned.reshape(-1, width), *extras)
+    def moe_out(units, places, scale, sets, which, extra=None):
+        if staged:
+            plan = combine_call(
+                units[0][0], units[1], places, scale, matrices(sets, which), which == 0, extra
+            )
+            return unpack_out(staged_call([plan], "combine", 170)[0])
         spec = ("erf,edf->erd", "erf,efd->erd")[which]
         made = [mm(spec, part, mats[which]).astype(jnp.bfloat16) for part, mats in zip(units, sets)]
         returned = from_experts(*(made if owned else [None] + made))
+        rows = returned
+        if scale is not None:
+            rows = (returned.astype(jnp.float32) * scale).astype(jnp.bfloat16)
         parts, *extras = exchange(
-            ("head_swap", head_parts(mm("tr,rd->td", places, returned))),
+            ("head_swap", head_parts(mm("tr,rd->td", places, rows))),
             *([] if extra is None else [("head_gather", extra)]),
         )
         return (head_sum(parts), returned, *extras)
+
+    def moe_turn(units, places, turned_places, scale, grad_rows, sets):
+        if not staged:
+            return (
+                moe_out(units, places, scale, sets, 1),
+                moe_in(grad_rows, turned_places, scale, sets, 1),
+            )
+        weights = matrices(sets, 1)
+        out_plan = combine_call(units[0][0], units[1], places, scale, weights, False)
+        in_plan = dispatch_call(grad_rows, turned_places, scale, weights, True)
+        out_results, in_results = staged_call([out_plan, in_plan], "turn", 260)
+        return (unpack_out(out_results), unpack_in(in_results))
 
     def gated(gate_up):
         return (jax.nn.silu(gate_up[..., :FF]) * gate_up[..., FF:]).astype(jnp.bfloat16)
@@ -1068,15 +1676,8 @@
             )
         )
     plan = jnp.stack([routes, queue_ranks]).reshape(2 * DECODER_LAYERS, slot_rows * TOP)
-    plan, plane_tokens, first_send, first_out, *own_in_next = exchange(
-        ("head_gather", plan),
-        ("head_gather", tokens.reshape(slot_rows, width)),
-        ("head_swap", send[0]),
-        ("blk_pairs", w_out[0]),
-        *to_owner(w_in, 0),
-    )
+    plan, first_send = exchange(("head_gather", plan), ("head_swap", send[0]))
     plan = plan.reshape(heads_count, 2, DECODER_LAYERS, slot_rows, TOP)
-    plane_tokens = plane_tokens.reshape(all_tokens, width)
 
     def attention_set(wide, out_full):
         wide = wide.transpose(1, 0, 2, 3).reshape(width, -1)
@@ -1085,7 +1686,7 @@
         gains = small.T[EXPERTS : EXPERTS + 2].astype(jnp.float32)
         return (wide[:, :columns], out_full.reshape(-1, width), small[:, :EXPERTS], gains)
 
-    (wide,) = exchange(("blk_pairs", first_send))
+    wide, first_out = exchange(("blk_pairs", first_send), ("blk_pairs", w_out[0]))
     attention_weights = [
         attention_set(wide, first_out),
     ]
@@ -1096,39 +1697,42 @@
         qkv_full, out_full, router_full, gains = attention_weights[layer_index]
         chosen, places = layer_plan(layer_index)
         scaled_a, inverse_a = norm_rows(hidden)
-        if layer_index:
-            plane_normed_a, *own_in_next = exchange(
-                ("head_gather", (scaled_a * gains[:1]).astype(jnp.bfloat16)),
-                *to_owner(w_in, layer_index),
+        normed_a = (scaled_a * gains[:1]).astype(jnp.bfloat16)
+        next_layer = layer_index + 1 < DECODER_LAYERS
+        fused = owned == 1 and heads_count == 4
+        if fused:
+            plane_normed_a, queries, pairs_all, own_down = project(
+                normed_a,
+                qkv_full,
+                tile_cosine,
+                tile_sine,
+                w_down,
+                layer_index,
+                pair_columns,
+                resident,
             )
             plane_normed_a = plane_normed_a.reshape(all_tokens, width)
+            own_down_next = [own_down]
         else:
-            plane_normed_a = (
-                norm_rows(plane_tokens.astype(jnp.float32))[0] * gains[:1]
-            ).astype(jnp.bfloat16)
-        projected = mm("td,de->te", plane_normed_a, qkv_full)
-        queries = by_slot(rotate(projected[:, :query_columns], cosine, sine).astype(jnp.bfloat16))
-        pairs = projected[:, query_columns:].reshape(all_tokens, kv_local, 2, HEAD_SIZE)
-        keys = rotate(pairs[:, :, 0].reshape(all_tokens, -1), cosine, sine)
-        pairs = jnp.stack([keys.reshape(all_tokens, kv_local, HEAD_SIZE), pairs[:, :, 1]], axis=2)
-        pairs = pairs.reshape(all_tokens, pair_columns).astype(jnp.bfloat16)
-        if layer_index + 1 < DECODER_LAYERS:
-            pairs, next_send = exchange(
-                ("blk_pairs", pairs), ("head_swap", send[layer_index + 1])
-            )
-            attention_weights.append(
-                attention_set(
-                    lax.all_gather(next_send, "blk", axis=0),
-                    lax.all_gather(w_out[layer_index + 1], "blk", axis=0),
-                )
-            )
-        else:
+            plane_normed_a, *own_down_next = exchange(
+                ("head_gather", normed_a), *to_owner(w_down, layer_index)
+            )
+            plane_normed_a = plane_normed_a.reshape(all_tokens, width)
+            projected = mm("td,de->te", plane_normed_a, qkv_full)
+            queries = by_slot(
+                rotate(projected[:, :query_columns], cosine, sine).astype(jnp.bfloat16)
+            )
+            pairs = projected[:, query_columns:].reshape(all_tokens, kv_local, 2, HEAD_SIZE)
+            keys = rotate(pairs[:, :, 0].reshape(all_tokens, -1), cosine, sine)
+            pairs = jnp.stack(
+                [keys.reshape(all_tokens, kv_local, HEAD_SIZE), pairs[:, :, 1]], axis=2
+            )
+            pairs = pairs.reshape(all_tokens, pair_columns).astype(jnp.bfloat16)
             (pairs,) = exchange(("blk_pairs", pairs))
-        pairs_all = (
-            pairs.reshape(blocks_count, heads_count, SEQUENCE_SLOTS, resident, pair_columns)
-            .transpose(2, 1, 0, 3, 4)
-            .reshape(SEQUENCE_SLOTS, keys_total, pair_columns)
-        )
+            pairs_all = pairs.reshape(
+                blocks_count, heads_count, SEQUENCE_SLOTS, resident, pair_columns
+            ).transpose(2, 1, 0, 3, 4)
+        pairs_all = pairs_all.reshape(SEQUENCE_SLOTS, keys_total, pair_columns)
         (attended,) = attention_call(
             functools.partial(
                 attend_kernel, heads_count, blocks_count, resident, group, kv_local
@@ -1141,11 +1745,22 @@
             "attend",
         )
         attended = by_head(attended)
-        branch, *own_down_next = exchange(
+        weight_sets = shared_weights(layer_index)
+        branch, *others = exchange(
             ("head_swap", head_parts(mm("tf,fd->td", attended, out_full))),
-            *to_owner(w_down, layer_index),
-        )
-        weight_sets = shared_weights(layer_index)
+            *([("head_swap", send[layer_index + 1])] if next_layer else []),
+            *to_owner(w_in, layer_index),
+            after=weight_sets[0] if weight_sets else (),
+        )
+        if next_layer:
+            next_send, *others = others
+            attention_weights.append(
+                attention_set(
+                    lax.all_gather(next_send, "blk", axis=0),
+                    lax.all_gather(w_out[layer_index + 1], "blk", axis=0),
+                )
+            )
+        own_in_next = others
         if owned:
             weight_sets = [
                 (owned_matrix(own_in_next[0]), owned_matrix(own_down_next[0]))
@@ -1153,7 +1768,8 @@
         middle = hidden + valid_column * head_sum(branch)
         scaled_b, inverse_b = norm_rows(middle)
         normed_b = (scaled_b * gains[1:]).astype(jnp.bfloat16)
-        plane_rows, incoming, gate_up = moe_in(normed_b, places.T, weight_sets, 0)
+        turned_places = places.T
+        plane_rows, incoming, gate_up = moe_in(normed_b, turned_places, None, weight_sets, 0)
         units = [gated(part) for part in gate_up]
         logits = mm("td,de->te", plane_rows, router_full)
         peaks = jnp.max(jnp.where(chosen, logits, negative), axis=-1, keepdims=True)
@@ -1162,10 +1778,19 @@
         plane_gates = lax.dynamic_slice_in_dim(
             gates_all, head_index * experts_local, experts_local, 1
         )
-        weighted_places = (
-            mm("te,er->tr", plane_gates.astype(jnp.bfloat16), spread).astype(jnp.bfloat16) * places
-        )
-        mixture, returned = moe_out(units, weighted_places, weight_sets, 1)
+        row_gates = mm("rt,te->re", turned_places, plane_gates.astype(jnp.bfloat16))
+        row_gates = jnp.sum(row_gates * spread.T.astype(jnp.float32), axis=1, keepdims=True)
+        if next_layer:
+            mixture, returned = moe_out(units, places, row_gates, weight_sets, 1)
+        else:
+            (mixture, returned), turned = moe_turn(
+                units,
+                places,
+                turned_places,
+                row_gates,
+                (valid_column * cotangent.reshape(slot_rows, width)).astype(jnp.bfloat16),
+                weight_sets,
+            )
         stored_all.append(
             (
                 weight_sets,
@@ -1180,7 +1805,8 @@
                 inverse_b,
                 plane_rows,
                 gates_all,
-                weighted_places,
+                turned_places,
+                row_gates,
                 incoming,
                 gate_up,
                 units,
@@ -1211,23 +1837,27 @@
             inverse_b,
             plane_rows,
             gates_all,
-            weighted_places,
+            turned_places,
+            row_gates,
             incoming,
             gate_up,
             units,
             returned,
         ) = stored_all[layer_index]
-        plane_grads, grad_produced, grad_units = moe_in(
-            (valid_column * grad_hidden).astype(jnp.bfloat16),
-            weighted_places.T,
-            weight_sets,
-            1,
-        )
+        if layer_index + 1 < DECODER_LAYERS:
+            turned = moe_in(
+                (valid_column * grad_hidden).astype(jnp.bfloat16),
+                turned_places,
+                row_gates,
+                weight_sets,
+                1,
+            )
+        plane_grads, grad_produced, grad_units = turned
         grad_gate_up = [gated_back(*parts) for parts in zip(gate_up, grad_units)]
         pair_dots = (mm("td,rd->tr", plane_grads, returned) * places).astype(jnp.bfloat16)
         plane_grad_gates = mm("tr,er->te", pair_dots, spread).T
         grad_normed_b, _, grad_gates = moe_out(
-            grad_gate_up, places, weight_sets, 0, plane_grad_gates
+            grad_gate_up, places, None, weight_sets, 0, plane_grad_gates
         )
         grad_gates = grad_gates.reshape(EXPERTS, all_tokens).T
         grad_weight_sets = [
@@ -1281,53 +1911,69 @@
             10 * rows_local * keys_total * query_columns,
             "attend_back",
         )
-        grad_pairs = (
-            grad_pairs.reshape(SEQUENCE_SLOTS, heads_count, blocks_count, resident, pair_columns)
-            .transpose(2, 1, 0, 3, 4)
-            .reshape(blocks_count, all_tokens, pair_columns)
-        )
-        (grad_pairs,) = exchange(("blk_swap", grad_pairs))
-        grad_pairs = jnp.sum(grad_pairs.astype(jnp.float32), axis=0)
-        grad_pairs = grad_pairs.astype(jnp.bfloat16).astype(jnp.float32)
-        grad_pairs = grad_pairs.reshape(all_tokens, kv_local, 2, HEAD_SIZE)
-        grad_keys = rotate(grad_pairs[:, :, 0].reshape(all_tokens, -1), cosine, -sine)
-        grad_projected = jnp.concatenate(
-            [
-                rotate(by_head(grad_queries).astype(jnp.float32), cosine, -sine),
-                jnp.stack(
-                    [grad_keys.reshape(all_tokens, kv_local, HEAD_SIZE), grad_pairs[:, :, 1]],
-                    axis=2,
-                ).reshape(all_tokens, pair_columns),
-            ],
-            axis=-1,
-        ).astype(jnp.bfloat16)
-        grad_qkv = mm("td,te->de", plane_normed_a, grad_projected)
         grad_out_w = jnp.concatenate(
             [grad_out_w, jnp.pad(grad_router, ((0, 0), (0, small_columns - EXPERTS)))], axis=1
         ).astype(jnp.bfloat16)
+        swapped = [("blk_swap", grad_out_w.reshape(blocks_count, weight_rows, -1))]
+        if owned:
+            swapped += from_owner(grad_weight_sets[0][1])
+        if fused:
+            grad_projected, grad_normed_a, grad_out_w, *own_grad_down = unproject(
+                grad_queries,
+                grad_pairs.reshape(
+                    SEQUENCE_SLOTS, heads_count, blocks_count // 2, 2, resident, pair_columns
+                ),
+                qkv_full,
+                tile_cosine,
+                tile_sine,
+                [array for _, array in swapped],
+                shared_terms,
+            )
+            grad_projected = grad_projected.reshape(all_tokens, -1)
+        else:
+            grad_pairs = (
+                grad_pairs.reshape(
+                    SEQUENCE_SLOTS, heads_count, blocks_count, resident, pair_columns
+                )
+                .transpose(2, 1, 0, 3, 4)
+                .reshape(blocks_count, all_tokens, pair_columns)
+            )
+            (grad_pairs,) = exchange(("blk_swap", grad_pairs))
+            grad_pairs = jnp.sum(grad_pairs.astype(jnp.float32), axis=0)
+            grad_pairs = grad_pairs.astype(jnp.bfloat16).astype(jnp.float32)
+            grad_pairs = grad_pairs.reshape(all_tokens, kv_local, 2, HEAD_SIZE)
+            grad_keys = rotate(grad_pairs[:, :, 0].reshape(all_tokens, -1), cosine, -sine)
+            grad_projected = jnp.concatenate(
+                [
+                    rotate(by_head(grad_queries).astype(jnp.float32), cosine, -sine),
+                    jnp.stack(
+                        [grad_keys.reshape(all_tokens, kv_local, HEAD_SIZE), grad_pairs[:, :, 1]],
+                        axis=2,
+                    ).reshape(all_tokens, pair_columns),
+                ],
+                axis=-1,
+            ).astype(jnp.bfloat16)
+            grad_normed_a, grad_out_w, *own_grad_down = exchange(
+                ("head_swap", head_parts(mm("te,de->td", grad_projected, qkv_full))),
+                *swapped,
+                after=shared_terms,
+            )
+            grad_normed_a = head_sum(grad_normed_a)
+        grad_out_w = jnp.sum(grad_out_w.astype(jnp.float32), axis=0)
         grad_qkv = (
-            grad_qkv.astype(jnp.bfloat16)
+            mm("td,te->de", plane_normed_a, grad_projected)
+            .astype(jnp.bfloat16)
             .reshape(heads_count, blocks_count, weight_rows, -1)
             .transpose(1, 0, 2, 3)
         )
-        grad_normed_a, grad_out_w, *others = exchange(
-            ("head_swap", head_parts(mm("te,de->td", grad_projected, qkv_full))),
-            ("blk_swap", grad_out_w.reshape(blocks_count, weight_rows, -1)),
-            *([] if layer_index else [("blk_swap", grad_qkv)]),
-            *(from_owner(grad_weight_sets[0][1]) if owned else []),
-            after=shared_terms,
-        )
         if layer_index:
-            own_grad_down = others
             grad_qkv = lax.psum_scatter(
                 grad_qkv.reshape(width, -1), "blk", scatter_dimension=0, tiled=True
             )
             pending.append(grad_qkv)
         else:
-            grad_qkv, *own_grad_down = others
+            (grad_qkv,) = exchange(("blk_swap", grad_qkv))
             grad_qkv = jnp.sum(grad_qkv.astype(jnp.float32), axis=0).astype(jnp.bfloat16)
-        grad_out_w = jnp.sum(grad_out_w.astype(jnp.float32), axis=0)
-        grad_normed_a = head_sum(grad_normed_a)
         grad_norm_a, grad_gain_a = norm_back(grad_normed_a, scaled_a, inverse_a, gains[:1])
         grad_hidden = grad_middle + grad_norm_a
 

time: 1280 us -> 1220 us (0.953)
  local copies, waits for them, and re-layouts: 94.1 us -> 61.6 us
  waiting for transfers between devices: 23.5 us -> 9.76 us
    pallas_call x13 -> x7, Pallas kernels: 434 us -> 245 us  [exchange(): pl.pallas_call(functools.partial(exchange_kernel, heads, blocks, plan, le...]
    pallas_call x8 -> x11, Pallas kernels: 470 us -> 641 us  [the longest x7 446 us: staged_call(): pl.pallas_call(kernel, out_shape=[out for plan in plans for out in plan[4...]
    convert_element_type x8 -> x0, local copies, waits for them, and re-layouts: 13.5 us -> none  [the longest x4 8.05 us: shards(): by_head(grad_queries).astype(jnp.float32)]
    dot_general x32 -> x28, matrix products: 91.1 us -> 85.9 us  [mm(): return jnp.einsum(spec, left, right, preferred_element_type=jnp.float32)]
  transfers between devices with their start and end apart: 14 -> 14, of which waited for: 3 -> 1; matrix products, arithmetic and copies ran while one was open for 18% -> 16% of each run, Pallas kernels for 60% -> 51%
where the time goes in v4:
time: 1220 us; the launch traced here: 1210 us
  Pallas kernels  940 us (77%)
  matrix products  85.9 us (7%)
  other arithmetic  79 us (6%)
  local copies, waits for them, and re-layouts  61.6 us (5%)
  starting transfers between devices  19.3 us (2%)
  between operations  15.9 us (1%)
    pallas_call x7, Pallas kernels, staged_call(): pl.pallas_call(kernel, out_shape=[out for plan in plans for out in plan[4...  446 us
    pallas_call x7, Pallas kernels, exchange(): pl.pallas_call(functools.partial(exchange_kernel, heads, blocks, plan, le...  245 us
    pallas_call x2, Pallas kernels, unproject(): pl.pallas_call(kernel, out_shape=outs, in_specs=[vmem] * 5 + [anywhere] *...  103 us
    pallas_call x2, Pallas kernels, project(): pl.pallas_call(functools.partial(project_kernel, heads, blocks, pieces, l...  92.1 us
    dot_general x28, matrix products, mm(): return jnp.einsum(spec, left, right, preferred_element_type=jnp.float32)  85.9 us
    pallas_call x4, Pallas kernels, attention_call(): pl.pallas_call(kernel, grid_spec=pltpu.PrefetchScalarGridSpec(num_scalar_...  53.9 us
  transfers between devices with their start and end apart: 14, of which 1 were waited for; matrix products, arithmetic and copies ran while one was open for 16% of the time, Pallas kernels for 51%

profile of v4, /device:TPU:0, one launch (start us, length us, event | category | flops | bytes accessed | tf_op | source)
XLA Modules:
  0.0 1211.2 jit_solution(966171529181402891)
XLA Ops:
  14.6 12.7 %exchange.7 = (s32[4,4,1024]{2,1,0:T(4,128)}, bf16[4,48,768]{2,1,0:T(8,128)(2,1)}) custom-call(s32[4,1024]{1,0:T(4,128)} %reshape.769.refs_0_, bf16[4,48,768]{2,1,0:T(8,128)(2,1)} %pad_maximum_fusion.7.refs_1_), custom_call_target="tpu_custom_call" | custom-call | bytes 115343360 | tf_op jit(solution)/shard_map/exchange/pallas_call | solution.py:168
  28.1 32.8 %exchange.8 = (bf16[8,4,48,768]{3,2,1,0:T(8,128)(2,1)}, bf16[8,48,1536]{2,1,0:T(8,128)(2,1)}) custom-call(bf16[4,48,768]{2,1,0:T(8,128)(2,1)} %get-tuple-element.70.refs_0_, bf16[48,1536]{1,0:T(8,128)(2,1)} %get-tuple-element.240.refs_1_), custom_call_target="tpu_custom_call" | custom-call | bytes 115343360 | tf_op jit(solution)/shard_map/exchange/pallas_call | solution.py:168
  69.1 50.1 %project.2 = (bf16[4,128,1536]{2,1,0:T(8,128)(2,1)}, bf16[2,256,384]{2,1,0:T(8,128)(2,1)}, bf16[2,4,8,64,256]{4,3,2,1,0:T(8,128)(2,1)}, bf16[8,64,1536]{2,1,0:T(8,128)(2,1)}) custom-call(bf16[128,1536]{1,0:T(8,128)(2,1)} %fusion.38.own_ref, bf16[1536,640]{1,0:T(8,128)(2,1)} %slice.219.weight_ref.refs_2_, ...), custom_call_target="tpu_custom_call" | custom-call | bytes 136314880 | tf_op jit(solution)/shard_map/project/pallas_call | solution.py:719
  119.8 9.6 attend.2
  134.7 44.3 %exchange.9 = (bf16[4,128,1536]{2,1,0:T(8,128)(2,1)}, bf16[4,48,768]{2,1,0:T(8,128)(2,1)}, bf16[8,192,1024]{2,1,0:T(8,128)(2,1)}) custom-call(bf16[4,128,1536]{2,1,0:T(8,128)(2,1)} %bitcast.332, bf16[4,48,768]{2,1,0:T(8,128)(2,1)} %pad_maximum_fusion.8.refs_1_, bf16[2,10,192,1024]{3,2,1,0:T(8,128)(2,1)} %refs_1_.1, bf16[2,1536,1024]{2,1,0:T(8,128)(2,1)} %bitcast.299, ...), custom_call_target="tpu_custom_call" | custom-call | bytes 115343360 | tf_op jit(solution)/shard_map/exchange/pallas_call | solution.py:168
  206.2 57.7 %dispatch.3 = (bf16[4,128,1536]{2,1,0:T(8,128)(2,1)}, bf16[8,112,1536]{2,1,0:T(8,128)(2,1)}, bf16[2,112,1536]{2,1,0:T(8,128)(2,1)}, f32[896,1024]{1,0:T(8,128)}, f32[2,112,1024]{2,1,0:T(8,128)}) custom-call(bf16[128,1536]{1,0:T(8,128)(2,1)} %get-tuple-element.216.refs_0_, bf16[1120,512]{1,0:T(8,128)(2,1)} %copy.250.refs_1_, bf16[1536,1024]{1,0:T(8,128)(2,1)} %bitcast.323, ...), custom_call_target="tpu_custom_call" | custom-call | bytes 178257920 | tf_op jit(solution)/shard_map/dispatch/pallas_call | solution.py:478
  270.4 63.0 %combine.3 = (f32[128,1536]{1,0:T(8,128)}, bf16[10,112,1536]{2,1,0:T(8,128)(2,1)}) custom-call(bf16[896,512]{1,0:T(8,128)(2,1)} %fusion.28.refs_0_, bf16[2,112,512]{2,1,0:T(8,128)(2,1)} %multiply_convert_fusion.14.refs_1_, bf16[512,1120]{1,0:T(8,128)(2,1)} %get-tuple-element.244.refs_2_, f32[1120,1]{1,0:T(8,128)} %broadcast_in_dim.101.refs_3_.refs_2_, ...), custom_call_target="tpu_custom_call" | custom-call | bytes 178257920 | tf_op jit(solution)/shard_map/combine/pallas_call | solution.py:478
  341.6 42.0 %project.3 = (bf16[4,128,1536]{2,1,0:T(8,128)(2,1)}, bf16[2,256,384]{2,1,0:T(8,128)(2,1)}, bf16[2,4,8,64,256]{4,3,2,1,0:T(8,128)(2,1)}, bf16[8,64,1536]{2,1,0:T(8,128)(2,1)}) custom-call(bf16[128,1536]{1,0:T(8,128)(2,1)} %multiply_convert_fusion.7.own_ref, bf16[1536,640]{1,0:T(8,128)(2,1)} %slice.231.weight_ref.refs_2_, ...), custom_call_target="tpu_custom_call" | custom-call | bytes 136314880 | tf_op jit(solution)/shard_map/project/pallas_call | solution.py:719
  383.7 9.7 attend.3
  398.7 39.1 %exchange.10 = (bf16[4,128,1536]{2,1,0:T(8,128)(2,1)}, bf16[8,192,1024]{2,1,0:T(8,128)(2,1)}) custom-call(bf16[4,128,1536]{2,1,0:T(8,128)(2,1)} %bitcast.333, bf16[2,10,192,1024]{3,2,1,0:T(8,128)(2,1)} %refs_1_.1, bf16[2,1536,1024]{2,1,0:T(8,128)(2,1)} %bitcast.302, bf16[2,512,1536]{2,1,0:T(8,128)(2,1)} %bitcast.305), custom_call_target="tpu_custom_call" | custom-call | bytes 115343360 | tf_op jit(solution)/shard_map/exchange/pallas_call | solution.py:168
  442.4 53.6 %dispatch.4 = (bf16[4,128,1536]{2,1,0:T(8,128)(2,1)}, bf16[8,112,1536]{2,1,0:T(8,128)(2,1)}, bf16[2,112,1536]{2,1,0:T(8,128)(2,1)}, f32[896,1024]{1,0:T(8,128)}, f32[2,112,1024]{2,1,0:T(8,128)}) custom-call(bf16[128,1536]{1,0:T(8,128)(2,1)} %multiply_convert_fusion.6.refs_0_, bf16[1120,512]{1,0:T(8,128)(2,1)} %copy.258.refs_1_.refs_7_, ...), custom_call_target="tpu_custom_call" | custom-call | bytes 178257920 | tf_op jit(solution)/shard_map/dispatch/pallas_call | solution.py:478
  503.5 87.8 %turn.1 = (f32[128,1536]{1,0:T(8,128)}, bf16[10,112,1536]{2,1,0:T(8,128)(2,1)}, bf16[4,128,1536]{2,1,0:T(8,128)(2,1)}, bf16[8,112,1536]{2,1,0:T(8,128)(2,1)}, bf...) custom-call(bf16[896,512]{1,0:T(8,128)(2,1)} %fusion.29.refs_0_, ...), custom_call_target="tpu_custom_call" | custom-call | bytes 272629760 | tf_op jit(solution)/shard_map/turn/pallas_call | solution.py:478
  610.2 6.1 fusion.19.refs_5_
  616.3 59.6 %combine.4 = (f32[128,1536]{1,0:T(8,128)}, bf16[10,112,1536]{2,1,0:T(8,128)(2,1)}, f32[4,10,512]{2,1,0:T(8,128)}) custom-call(bf16[896,1024]{1,0:T(8,128)(2,1)} %pad_maximum_fusion.refs_0_, bf16[2,112,1024]{2,1,0:T(8,128)(2,1)} %pad_maximum_fusion.5.refs_1_, bf16[512,1120]{1,0:T(8,128)(2,1)} %get-tuple-element.243.refs_2_, bf16[1536,1024]{1,0:T(8,128)(2,1)} %bitcast.326, ...), custom_call_target="tpu_custom_call" | custom-call | bytes 178257920 | tf_op jit(solution)/shard_map/combine/pallas_call | solution.py:478
  691.7 4.9 convolution_convert_fusion.5
  696.7 46.8 %exchange.11 = (bf16[4,128,1536]{2,1,0:T(8,128)(2,1)}, bf16[8,1,192,1024]{3,2,1,0:T(8,128)(2,1)}) custom-call(bf16[128,1536]{1,0:T(8,128)(2,1)} %get-tuple-element.210.refs_0_, bf16[8,1,192,1024]{3,2,1,0:T(8,128)(2,1)} %bitcast.345, bf16[2,1536,1024]{2,1,0:T(8,128)(2,1)} %convolution_convert_fusion.1.refs_2_, ...), custom_call_target="tpu_custom_call" | custom-call | bytes 115343360 | tf_op jit(solution)/shard_map/exchange/pallas_call | solution.py:168
  747.0 17.5 %attend_back.2 = (bf16[2,256,384]{2,1,0:T(8,128)(2,1)}, bf16[2,2048,256]{2,1,0:T(8,128)(2,1)}) custom-call(s32[3]{0:T(128)} %pad_add_fusion.1.info_ref, bf16[2,256,384]{2,1,0:T(8,128)(2,1)} %get-tuple-element.84.query_ref, bf16[2,2048,256]{2,1,0:T(8,128)(2,1)} %bitcast.410, bf16[2,256,384]{2,1,0:T(8,128)(2,1)} %bitcast.387), custom_call_target="tpu_custom_call" | custom-call | flops 2013265920 | bytes 8388608 | tf_op jit(solution)/shard_map/attend_back/pallas_call | solution.py:1416
  770.2 50.8 %unproject.2 = (bf16[4,128,640]{2,1,0:T(8,128)(2,1)}, f32[128,1536]{1,0:T(8,128)}, bf16[8,48,1664]{2,1,0:T(8,128)(2,1)}, bf16[8,1,64,1536]{3,2,1,0:T(8,128)(2,1)}) custom-call(bf16[2,256,384]{2,1,0:T(8,128)(2,1)} %get-tuple-element.103.refs_0_, bf16[2,4,4,2,64,256]{5,4,3,2,1,0:T(8,128)(2,1)} %bitcast.357, bf16[1536,640]{1,0:T(8,128)(2,1)} %slice.231.weight_ref.refs_2_, ...), custom_call_target="tpu_custom_call" | custom-call | bytes 157286400 | tf_op jit(solution)/shard_map/unproject/pallas_call | solution.py:999
  829.2 63.6 %dispatch.5 = (bf16[4,128,1536]{2,1,0:T(8,128)(2,1)}, bf16[8,112,1536]{2,1,0:T(8,128)(2,1)}, bf16[2,112,1536]{2,1,0:T(8,128)(2,1)}, f32[896,512]{1,0:T(8,128)}, f32[2,112,512]{2,1,0:T(8,128)}) custom-call(bf16[128,1536]{1,0:T(8,128)(2,1)} %get-tuple-element.208.refs_0_, bf16[1120,512]{1,0:T(8,128)(2,1)} %copy.250.refs_1_, ...), custom_call_target="tpu_custom_call" | custom-call | bytes 178257920 | tf_op jit(solution)/shard_map/dispatch/pallas_call | solution.py:478
  898.8 5.6 convolution_convert_fusion.refs_3_
  914.5 5.9 fusion.18.refs_5_
  920.4 60.9 %combine.5 = (f32[128,1536]{1,0:T(8,128)}, bf16[10,112,1536]{2,1,0:T(8,128)(2,1)}, f32[4,10,512]{2,1,0:T(8,128)}) custom-call(bf16[896,1024]{1,0:T(8,128)(2,1)} %pad_maximum_fusion.1.refs_0_, bf16[2,112,1024]{2,1,0:T(8,128)(2,1)} %pad_maximum_fusion.6.refs_1_, bf16[512,1120]{1,0:T(8,128)(2,1)} %get-tuple-element.244.refs_2_, bf16[1536,1024]{1,0:T(8,128)(2,1)} %bitcast.324, ...), custom_call_target="tpu_custom_call" | custom-call | bytes 178257920 | tf_op jit(solution)/shard_map/combine/pallas_call | solution.py:478
  998.4 4.9 convolution_convert_fusion.4
  1003.3 44.5 %exchange.12 = (bf16[4,128,1536]{2,1,0:T(8,128)(2,1)}, bf16[8,1,192,1024]{3,2,1,0:T(8,128)(2,1)}) custom-call(bf16[128,1536]{1,0:T(8,128)(2,1)} %get-tuple-element.206.refs_0_, bf16[8,1,192,1024]{3,2,1,0:T(8,128)(2,1)} %bitcast.344, bf16[192,640]{1,0:T(8,128)(2,1)} %reduce-scatter.10.cloned.1.call-done.refs_2_, ...), custom_call_target="tpu_custom_call" | custom-call | bytes 115343360 | tf_op jit(solution)/shard_map/exchange/pallas_call | solution.py:168
  1051.1 4.8 all-to-all-start.1
  1058.1 17.1 %attend_back.3 = (bf16[2,256,384]{2,1,0:T(8,128)(2,1)}, bf16[2,2048,256]{2,1,0:T(8,128)(2,1)}) custom-call(s32[3]{0:T(128)} %pad_add_fusion.1.info_ref, bf16[2,256,384]{2,1,0:T(8,128)(2,1)} %get-tuple-element.72.query_ref, bf16[2,2048,256]{2,1,0:T(8,128)(2,1)} %bitcast.408, bf16[2,256,384]{2,1,0:T(8,128)(2,1)} %bitcast.386), custom_call_target="tpu_custom_call" | custom-call | flops 2013265920 | bytes 8388608 | tf_op jit(solution)/shard_map/attend_back/pallas_call | solution.py:1416
  1076.7 51.9 %unproject.3 = (bf16[4,128,640]{2,1,0:T(8,128)(2,1)}, f32[128,1536]{1,0:T(8,128)}, bf16[8,48,1664]{2,1,0:T(8,128)(2,1)}, bf16[8,1,64,1536]{3,2,1,0:T(8,128)(2,1)}) custom-call(bf16[2,256,384]{2,1,0:T(8,128)(2,1)} %get-tuple-element.119.refs_0_, bf16[2,4,4,2,64,256]{5,4,3,2,1,0:T(8,128)(2,1)} %bitcast.356, bf16[1536,640]{1,0:T(8,128)(2,1)} %slice.219.weight_ref.refs_2_, ...), custom_call_target="tpu_custom_call" | custom-call | bytes 157286400 | tf_op jit(solution)/shard_map/unproject/pallas_call | solution.py:999
  1131.5 9.2 all-to-all-start.2
  1153.2 6.0 maximum_convert_fusion
  1161.4 24.7 %exchange.13 = bf16[8,4,48,640]{3,2,1,0:T(8,128)(2,1)} custom-call(bf16[8,4,48,640]{3,2,1,0:T(8,128)(2,1)} %bitcast.328), custom_call_target="tpu_custom_call" | custom-call | bytes 115343360 | tf_op jit(solution)/shard_map/exchange/pallas_call | solution.py:168
  1188.7 4.6 all-to-all-start
  1194.9 8.0 all-to-all-done
  (436 shorter events, 195.3 us)
Async XLA Ops:
  7.2 127.5 %all-gather.16.cloned.1.call-start = ((), (), s32[]{:S(2)}) async-start(), calls=%async_computation.15 | async-start | bytes 3538944 | tf_op jit(solution)/shard_map/all_gather | solution.py:1535
  9.3 125.4 %all-gather.14.cloned.1.call-start = ((), (), s32[]{:S(2)}) async-start(), calls=%async_computation.14 | async-start | bytes 7077888 | tf_op jit(solution)/shard_map/all_gather | solution.py:1535
  12.1 323.5 %all-gather.18.cloned.1.call-start = ((), (), s32[]{:S(2)}) async-start(), calls=%async_computation.16 | async-start | bytes 2654208 | tf_op jit(solution)/shard_map/all_gather | solution.py:1759
  12.2 15.2 %copy-start.59 = (bf16[2,48,1536]{2,1,0:T(8,128)(2,1)S(1)}, bf16[2,48,1536]{2,1,0:T(8,128)(2,1)}, u32[]{:S(2)}) copy-start(bf16[2,48,1536]{2,1,0:T(8,128)(2,1)} %param.16) | copy-start | bytes 884740
  68.2 51.0 %copy-start.62 = (f32[1536]{0:T(1024)}, f32[1536]{0:T(1024)S(1)}, u32[]{:S(2)}) copy-start(f32[1536]{0:T(1024)S(1)} %get-tuple-element.205) | copy-start | bytes 18436
  69.1 50.1 %copy-start.102 = (s32[2]{0:T(128)S(1)}, s32[2]{0:T(128)}, u32[]{:S(2)}) copy-start(s32[2]{0:T(128)} %param.12) | copy-start | bytes 28
  134.7 47.1 %copy-start.67 = (s32[4,4,1024]{2,1,0:T(4,128)S(1)}, s32[4,4,1024]{2,1,0:T(4,128)}, u32[]{:S(2)}) copy-start(s32[4,4,1024]{2,1,0:T(4,128)} %get-tuple-element.76) | copy-start | bytes 196612
  179.1 216.1 %all-gather.12.cloned.1.call-start = ((), (), s32[]{:S(2)}) async-start(), calls=%async_computation.8 | async-start | bytes 1327104 | tf_op jit(solution)/shard_map/all_gather | solution.py:1760
  179.7 219.1 %all-gather.22.cloned.1.call-start = ((), (), s32[]{:S(2)}) async-start(), calls=%async_computation.18 | async-start | bytes 3538944 | tf_op jit(solution)/shard_map/all_gather | solution.py:1535
  180.2 218.5 %all-gather.20.cloned.1.call-start = ((), (), s32[]{:S(2)}) async-start(), calls=%async_computation.17 | async-start | bytes 7077888 | tf_op jit(solution)/shard_map/all_gather | solution.py:1535
  180.8 589.3 %reduce-scatter.8.cloned.1.call-start = ((), (), s32[]{:S(2)}) async-start(), calls=%async_computation.10 | async-start | bytes 3538944 | tf_op jit(solution)/shard_map/reduce_scatter | solution.py:1894
  190.3 9.1 copy-start.49
  205.0 59.0 %copy-start.92 = (f32[128]{0:T(128)}, f32[128]{0:T(128)S(1)}, u32[]{:S(2)}) copy-start(f32[128]{0:T(128)S(1)} %rsqrt.41) | copy-start | bytes 1540
  206.2 57.8 %copy-start.58 = (pred[512,40]{0,1:T(8,128)(4,1)S(1)}, pred[512,40]{0,1:T(8,128)(4,1)}, u32[]{:S(2)}) copy-start(pred[512,40]{0,1:T(8,128)(4,1)} %fusion.49) | copy-start | bytes 61444
  442.4 53.6 %copy-start.57 = (pred[512,40]{0,1:T(8,128)(4,1)S(1)}, pred[512,40]{0,1:T(8,128)(4,1)}, u32[]{:S(2)}) copy-start(pred[512,40]{0,1:T(8,128)(4,1)} %fusion.47) | copy-start | bytes 61444
  503.5 87.8 %copy-start.31 = (bf16[2,112,512]{2,1,0:T(8,128)(2,1)S(1)}, bf16[2,112,512]{2,1,0:T(8,128)(2,1)}, u32[]{:S(2)}) copy-start(bf16[2,112,512]{2,1,0:T(8,128)(2,1)} %multiply_convert_fusion.13.refs_1_) | copy-start | bytes 688132
  595.2 174.9 %reduce-scatter.6.cloned.1.call-start = ((), (), s32[]{:S(2)}) async-start(), calls=%async_computation.9 | async-start | bytes 7077888 | tf_op jit(solution)/shard_map/reduce_scatter | solution.py:1894
  602.2 401.1 %reduce-scatter.10.cloned.1.call-start = ((), (), s32[]{:S(2)}) async-start(), calls=%async_computation.11 | async-start | bytes 2211840 | tf_op jit(solution)/shard_map/reduce_scatter | solution.py:1970
  747.0 17.5 %copy-start.56 = (bf16[384,512]{1,0:T(8,128)(2,1)S(1)}, bf16[384,512]{1,0:T(8,128)(2,1)}, u32[]{:S(2)}) copy-start(bf16[384,512]{1,0:T(8,128)(2,1)} %copy.264) | copy-start | bytes 1179652
  747.0 17.5 %copy-start.106 = (bf16[4,128,1536]{2,1,0:T(8,128)(2,1)S(1)}, bf16[4,128,1536]{2,1,0:T(8,128)(2,1)}, u32[]{:S(2)}) copy-start(bf16[4,128,1536]{2,1,0:T(8,128)(2,1)} %get-tuple-element.102) | copy-start | bytes 4718596
  770.2 50.8 %copy-start.105 = (bf16[4,128,1536]{2,1,0:T(8,128)(2,1)S(1)}, bf16[4,128,1536]{2,1,0:T(8,128)(2,1)}, u32[]{:S(2)}) copy-start(bf16[4,128,1536]{2,1,0:T(8,128)(2,1)} %get-tuple-element.114) | copy-start | bytes 4718596
  825.0 251.7 %reduce-scatter.14.cloned.1.call-start = ((), (), s32[]{:S(2)}) async-start(), calls=%async_computation.13 | async-start | bytes 3538944 | tf_op jit(solution)/shard_map/reduce_scatter | solution.py:1894
  829.2 63.6 %copy-start.35 = (bf16[2,112,512]{2,1,0:T(8,128)(2,1)S(1)}, bf16[2,112,512]{2,1,0:T(8,128)(2,1)}, u32[]{:S(2)}) copy-start(bf16[2,112,512]{2,1,0:T(8,128)(2,1)} %multiply_convert_fusion.14.refs_1_) | copy-start | bytes 688132
  896.5 180.1 %reduce-scatter.12.cloned.1.call-start = ((), (), s32[]{:S(2)}) async-start(), calls=%async_computation.12 | async-start | bytes 7077888 | tf_op jit(solution)/shard_map/reduce_scatter | solution.py:1894
  981.3 9.0 copy-start.6
  1003.3 44.5 %copy-start.44 = (bf16[8,48,1536]{2,1,0:T(8,128)(2,1)S(1)}, bf16[8,48,1536]{2,1,0:T(8,128)(2,1)}, u32[]{:S(2)}) copy-start(bf16[8,48,1536]{2,1,0:T(8,128)(2,1)} %get-tuple-element.74) | copy-start | bytes 3538948
  1047.8 8.0 copy-start.55
  1051.1 25.2 %all-to-all-start.1 = ((bf16[4,48,640]{2,1,0:T(8,128)(2,1)}), bf16[4,48,640]{2,1,0:T(8,128)(2,1)S(1)}, u32[]{:S(2)}, u32[]{:S(2)}) async-start(bf16[4,48,640]{2,1,0:T(8,128)(2,1)} %bitcast.111), calls=%async_computation.6 | async-start | bytes 491520 | tf_op jit(solution)/shard_map/all_to_all | solution.py:1982
  1058.1 17.1 %copy-start.53 = (bf16[384,128]{1,0:T(8,128)(2,1)S(1)}, bf16[384,128]{1,0:T(8,128)(2,1)}, u32[]{:S(2)}) copy-start(bf16[384,128]{1,0:T(8,128)(2,1)} %pad.19.clone) | copy-start | bytes 294916
  1131.5 57.2 %all-to-all-start.2 = ((f32[32,1,192]{2,1,0:T(1,128)}), f32[32,1,192]{2,1,0:T(1,128)S(1)}, u32[]{:S(2)}, u32[]{:S(2)}) async-start(f32[32,1,192]{2,1,0:T(1,128)} %all_to_all.16), calls=%async_computation.7 | async-start | bytes 65536 | tf_op jit(solution)/shard_map/all_to_all | solution.py:2002
  1153.2 6.7 copy-start.36
  1188.7 14.2 %all-to-all-start = ((bf16[4,48,640]{2,1,0:T(8,128)(2,1)}), bf16[4,48,640]{2,1,0:T(8,128)(2,1)S(1)}, u32[]{:S(2)}, u32[]{:S(2)}) async-start(bf16[4,48,640]{2,1,0:T(8,128)(2,1)} %reduce_sum.258), calls=%async_computation.5 | async-start | bytes 491520 | tf_op jit(solution)/shard_map/all_to_all | solution.py:1982
  (89 other events, 228.8 us)
Sparse Core Ops, SparseCore 0:
  10.5 49.5 all-gather.15
  62.6 66.6 all-gather.13
  179.2 28.4 all-gather.17
  209.4 31.2 all-gather.11
  242.5 35.6 all-gather.21
  280.5 60.3 all-gather.19
  595.3 54.3 reduce-scatter.7
  654.1 83.4 reduce-scatter.5
  825.1 58.8 reduce-scatter.9
  896.7 53.5 reduce-scatter.13
  954.2 86.9 reduce-scatter.11

commit v5 on v4

--- a/solution.py
+++ b/solution.py
@@ -57,6 +57,46 @@
         grad_scaled - scaled * jnp.mean(grad_scaled * scaled, axis=-1, keepdims=True)
     )
     return (grad_hidden, grad_gain)
+
+
+RELAY_PIECES = 4
+
+
+def relayed_gather(heads, head, blk, head_peers, source, target, sems, first):
+    count = source.shape[0] // RELAY_PIECES
+    inner = jnp.logical_and(head > 0, head < heads - 1)
+    rounds = []
+    for piece in range(RELAY_PIECES):
+        part = pl.ds(piece * count, count)
+        index = first + piece * heads
+        copies = []
+        for number, peer in enumerate(head_peers):
+            copy = remote(source.at[part], target.at[head, part], sems, index + number, peer)
+            near = jnp.abs(peer[0] - head) < heads - 1
+            copies.append((copy, near))
+            pl.when(near)(copy.start)
+        rounds.append(copies)
+    passed = []
+    for piece, copies in enumerate(rounds):
+        copies[1][0].wait_recv()
+        there = target.at[lax.rem(head + 2, heads), pl.ds(piece * count, count)]
+        index = first + piece * heads
+        copy = remote(
+            there,
+            there,
+            sems,
+            index + heads - 1,
+            ((head - 1) * (heads - 1), blk),
+            index + jnp.where(head == 1, 0, heads - 2),
+        )
+        pl.when(inner)(copy.start)
+        passed.append(copy)
+    for copies, copy in zip(rounds, passed):
+        copies[0][0].wait_recv()
+        copies[2][0].wait_recv()
+        for sent, near in copies:
+            pl.when(near)(sent.wait_send)
+        pl.when(inner)(copy.wait_send)
 
 
 def exchange_kernel(heads, blocks, items, waited, *refs):
@@ -105,13 +145,17 @@
         return copy
 
     locals_started = []
+    gathers = []
     for number, (kind, layer) in enumerate(items):
         source, target = sources[number], targets[number]
 
         def piece(index, source=source, layer=layer):
             return source.at[index] if layer is None else source.at[layer, index]
 
-        if kind == "head_gather":
+        if kind == "head_gather" and heads == 4 and source.shape[0] % 64 == 0:
+            mine, place = source, head
+            gathers.append((source, target))
+        elif kind == "head_gather":
             mine, place = source, head
             copies += [send(source, target.at[head], peer) for peer in head_peers]
         elif kind == "head_swap":
@@ -128,6 +172,9 @@
         local = pltpu.make_async_copy(mine, target.at[place], local_sems.at[number])
         local.start()
         locals_started.append(local)
+    for source, target in gathers:
+        relayed_gather(heads, head, blk, head_peers, source, target, (send_sems, recv_sems), used)
+        used += RELAY_PIECES * heads
     for sent, target in forwards:
         for step, copy in enumerate(sent, start=1):
             copy.wait_recv()
@@ -161,7 +208,7 @@
         if kind.endswith("swap"):
             tail = tail[1:] if layer is None else tail[2:]
         outs.append(jax.ShapeDtypeStruct((group,) + tail, array.dtype))
-        total += group - 1
+        total += RELAY_PIECES * group
     collective_id = kernel_number(
         "exchange", tuple(plan), *((array.shape, str(array.dtype)) for array in (*arrays, *after))
     )
@@ -225,6 +272,7 @@
     )
 
 
+STORED_TURNED, STORED_GATES = 12, 13
 DISPATCH_PIECES, DISPATCH_WINDOW, DISPATCH_LAG = 6, 3, 2
 COMBINE_PIECES = 6
 
@@ -260,10 +308,9 @@
     tile = 256
     relay = heads == 4
     inner = jnp.logical_and(head > 0, head < heads - 1)
-    loads = [
-        pltpu.make_async_copy(weight_ref, held_ref, local_sems.at[0]),
-        pltpu.make_async_copy(shared_weight_ref, shared_held_ref, local_sems.at[1]),
-    ]
+    loads = [pltpu.make_async_copy(shared_weight_ref, shared_held_ref, local_sems.at[1])]
+    if weight_ref is not None:
+        loads.append(pltpu.make_async_copy(weight_ref, held_ref, local_sems.at[0]))
     head_copies = []
     blk_copies = []
     relayed = []
@@ -449,7 +496,7 @@
     )
 
 
-def staged_call(plans, name, millions):
+def staged_call(plans, name, millions, after=()):
     heads, blocks = lax.axis_size("head"), lax.axis_size("blk")
     inputs = [len(plan[2]) for plan in plans]
     outputs = [len(plan[4]) for plan in plans]
@@ -459,6 +506,7 @@
         _, _, head_peers, blk_peers = plane_peers(heads, blocks)
         greet(head_peers + blk_peers)
         lists = []
+        refs = refs[: sum(inputs)] + refs[sum(inputs) + len(after) :]
         for number, plan in enumerate(plans):
             first = sum(inputs[:number])
             given = list(refs[first : first + inputs[number]])
@@ -478,11 +526,14 @@
     results = pl.pallas_call(
         kernel,
         out_shape=[out for plan in plans for out in plan[4]],
-        in_specs=[spec for plan in plans for spec in plan[3]],
+        in_specs=[spec for plan in plans for spec in plan[3]]
+        + [pl.BlockSpec(memory_space=pl.ANY)] * len(after),
         out_specs=[spec for plan in plans for spec in plan[5]],
         scratch_shapes=[scratch for plan in plans for scratch in plan[6]],
         compiler_params=pltpu.CompilerParams(
-            collective_id=kernel_number(*(plan[0] for plan in plans)),
+            collective_id=kernel_number(
+                *(plan[0] for plan in plans), *(array.shape for array in after)
+            ),
             has_side_effects=True,
             vmem_limit_bytes=60 * 1024 * 1024,
         ),
@@ -490,7 +541,7 @@
             flops=0, bytes_accessed=millions << 20, transcendentals=0
         ),
         name=name,
-    )(*arrays)
+    )(*arrays, *after)
     return [
         results[sum(outputs[:number]) : sum(outputs[: number + 1])] for number in range(len(plans))
     ]
@@ -506,6 +557,259 @@
     )
 
 
+def enter_kernel(heads, blocks, layer, swaps, *refs):
+    attended_ref, out_weight_ref, hidden_ref, valid_ref, gain_ref, place_ref, *refs = refs
+    moved_ref, shared_weight_ref, *refs = refs
+    swap_refs, refs = refs[:swaps], refs[swaps:]
+    middle_ref, scaled_ref, inverse_ref, plane_ref, queue_ref, shared_ref, *refs = refs
+    out_ref, shared_out_ref, matrix_ref, *refs = refs
+    swap_out_refs, refs = refs[:swaps], refs[swaps:]
+    own_ref, part_ref, landed_ref, relay_ref, sum_send, sum_recv, *refs = refs
+    moved_send, moved_recv, swap_send, swap_recv, side_sems, *refs = refs
+    send_ref, held_ref, shared_held_ref, head_send, head_recv, blk_send, blk_recv, local_sems = refs
+    head, blk, head_peers, blk_peers = plane_peers(heads, blocks)
+    rows, width = middle_ref.shape
+    pieces = COMBINE_PIECES
+    step_width = width // pieces
+    matrix_rows = moved_ref.shape[2]
+    inner = jnp.logical_and(head > 0, head < heads - 1)
+    greet(head_peers + blk_peers)
+
+    def far(peer):
+        return jnp.abs(peer[0] - head) == heads - 1
+
+    def peer_origin(peer):
+        return lax.rem(2 * head + heads - peer[0], heads)
+
+    sent = []
+
+    def through_copy(piece, peer):
+        columns = pl.ds(piece * step_width, step_width)
+        return remote(
+            part_ref.at[peer[0], :, columns],
+            relay_ref.at[:, columns],
+            (sum_send, sum_recv),
+            piece * heads + heads - 1,
+            (jnp.where(head == 0, 1, heads - 2), blk),
+        )
+
+    def spread(piece):
+        columns = pl.ds(piece * step_width, step_width)
+        weight = out_weight_ref[:, columns]
+
+        def part(owner):
+            start = pl.multiple_of(owner * rows, 16)
+            return jnp.dot(
+                attended_ref[pl.ds(start, rows), :], weight, preferred_element_type=jnp.float32
+            )
+
+        copies = []
+        for number, peer in enumerate(head_peers):
+            part_ref[peer[0], :, columns] = part(peer[0]).astype(part_ref.dtype)
+            copy = remote(
+                part_ref.at[peer[0], :, columns],
+                landed_ref.at[head, :, columns],
+                (sum_send, sum_recv),
+                piece * heads + number,
+                peer,
+            )
+            copies.append(copy)
+            if number == 1:
+                pl.when(jnp.logical_not(inner))(copy.start)
+            else:
+                distant = far(peer)
+                pl.when(jnp.logical_not(distant))(copy.start)
+                pl.when(distant)(through_copy(piece, peer).start)
+        sent.append(copies)
+        middle_ref[:, columns] = part(head)
+
+    def pass_on(piece):
+        columns = pl.ds(piece * step_width, step_width)
+        target = lax.rem(head + 2, heads)
+
+        @pl.when(inner)
+        def _():
+            through_copy(piece, (target, blk)).wait_recv()
+            part_ref[target, :, columns] = (
+                part_ref[target, :, columns].astype(jnp.float32)
+                + relay_ref[:, columns].astype(jnp.float32)
+            ).astype(part_ref.dtype)
+            sent[piece][1].start()
+
+    def finish(piece):
+        columns = pl.ds(piece * step_width, step_width)
+        for number, peer in enumerate(head_peers):
+            copy = sent[piece][number]
+
+            def add(copy=copy, peer=peer):
+                copy.wait_recv()
+                middle_ref[:, columns] += landed_ref[peer_origin(peer), :, columns].astype(
+                    jnp.float32
+                )
+
+            if number != 1:
+                pl.when(jnp.logical_not(far((peer_origin(peer), blk))))(add)
+            else:
+                add()
+
+    moved = []
+
+    def move():
+        for number, peer in enumerate(blk_peers):
+            place = pl.ds(pl.multiple_of(blk * matrix_rows, 16), matrix_rows)
+            moved.append(
+                started(
+                    remote(
+                        moved_ref.at[layer, peer[1]],
+                        held_ref.at[place],
+                        (moved_send, moved_recv),
+                        number,
+                        peer,
+                    )
+                )
+            )
+        place = pl.ds(pl.multiple_of(blk * matrix_rows, 16), matrix_rows)
+        moved.append(
+            started(
+                pltpu.make_async_copy(
+                    moved_ref.at[layer, blk], held_ref.at[place], side_sems.at[0]
+                )
+            )
+        )
+        for item in range(swaps):
+            for number, peer in enumerate(head_peers):
+                swapped.append(
+                    started(
+                        remote(
+                            swap_refs[item].at[peer[0]],
+                            swap_out_refs[item].at[head],
+                            (swap_send, swap_recv),
+                            item * heads + number,
+                            peer,
+                        )
+                    )
+                )
+            swapped.append(
+                started(
+                    pltpu.make_async_copy(
+                        swap_refs[item].at[head], swap_out_refs[item].at[head], side_sems.at[2]
+                    )
+                )
+            )
+
+    swapped = []
+    lag = 2
+    for step in range(pieces + lag):
+        if step < pieces:
+            spread(step)
+        if not step:
+            move()
+        if 0 < step <= pieces:
+            pass_on(step - 1)
+        if step >= lag:
+            finish(step - lag)
+    middle = hidden_ref[...] + valid_ref[...] * middle_ref[...]
+    inverse = lax.rsqrt(jnp.mean(middle * middle, axis=1, keepdims=True) + epsilon)
+    scaled = middle * inverse
+    middle_ref[...] = middle
+    scaled_ref[...] = scaled
+    inverse_ref[...] = jnp.broadcast_to(inverse, inverse_ref.shape)
+    own_ref[...] = (scaled * gain_ref[...]).astype(own_ref.dtype)
+    stages = dispatch_stages(
+        heads,
+        blocks,
+        False,
+        (
+            own_ref,
+            place_ref,
+            None,
+            None,
+            shared_weight_ref,
+            plane_ref,
+            queue_ref,
+            shared_ref,
+            out_ref,
+            shared_out_ref,
+            send_ref,
+            held_ref,
+            shared_held_ref,
+            head_send,
+            head_recv,
+            blk_send,
+            blk_recv,
+            local_sems,
+        ),
+    )
+    stages[0]()
+    for copy in moved:
+        if hasattr(copy, "wait_recv") and copy is not moved[-1]:
+            copy.wait_recv()
+        else:
+            copy.wait()
+    saved = pltpu.make_async_copy(held_ref, matrix_ref, side_sems.at[1])
+    saved.start()
+    for stage in stages[1:]:
+        stage()
+    saved.wait()
+    for copy in moved[:-1]:
+        copy.wait_send()
+    for copy in swapped:
+        copy.wait()
+    for piece, copies in enumerate(sent):
+        for number, copy in enumerate(copies):
+            if number != 1:
+                distant = far(head_peers[number])
+                pl.when(jnp.logical_not(distant))(copy.wait_send)
+                pl.when(distant)(through_copy(piece, head_peers[number]).wait_send)
+            else:
+                copy.wait_send()
+
+
+def enter(attended, out_weight, hidden, valid, gain, places, moved, layer, shared_weight, swaps):
+    heads, blocks = lax.axis_size("head"), lax.axis_size("blk")
+    count, width = hidden.shape
+    matrix = jax.ShapeDtypeStruct((blocks * moved.shape[2], moved.shape[3]), moved.dtype)
+    rows = jax.ShapeDtypeStruct((count, width), jnp.bfloat16)
+    _, _, outs, _, scratch = dispatch_plan(rows, places, None, (matrix, shared_weight), False)
+    vmem = pl.BlockSpec(memory_space=pltpu.VMEM)
+    anywhere = pl.BlockSpec(memory_space=pl.ANY)
+    pieces = COMBINE_PIECES
+    return pl.pallas_call(
+        functools.partial(enter_kernel, heads, blocks, layer, len(swaps)),
+        out_shape=[
+            jax.ShapeDtypeStruct((count, width), jnp.float32),
+            jax.ShapeDtypeStruct((count, width), jnp.float32),
+            jax.ShapeDtypeStruct((count, 128), jnp.float32),
+            *outs,
+            matrix,
+            *(jax.ShapeDtypeStruct(array.shape, array.dtype) for array in swaps),
+        ],
+        in_specs=[vmem] * 6 + [anywhere] * (2 + len(swaps)),
+        out_specs=[vmem] * (3 + len(outs)) + [anywhere] * (1 + len(swaps)),
+        scratch_shapes=[
+            pltpu.VMEM((count, width), jnp.bfloat16),
+            pltpu.VMEM((heads, count, width), jnp.bfloat16),
+            pltpu.VMEM((heads, count, width), jnp.bfloat16),
+            pltpu.VMEM((count, width), jnp.bfloat16),
+            pltpu.SemaphoreType.DMA((pieces * heads,)),
+            pltpu.SemaphoreType.DMA((pieces * heads,)),
+            pltpu.SemaphoreType.DMA((blocks,)),
+            pltpu.SemaphoreType.DMA((blocks,)),
+            pltpu.SemaphoreType.DMA((max(1, len(swaps)) * heads,)),
+            pltpu.SemaphoreType.DMA((max(1, len(swaps)) * heads,)),
+            pltpu.SemaphoreType.DMA((3,)),
+            *scratch,
+        ],
+        compiler_params=pltpu.CompilerParams(
+            collective_id=kernel_number("enter", layer, len(swaps)),
+            has_side_effects=True,
+            vmem_limit_bytes=60 * 1024 * 1024,
+        ),
+        cost_estimate=pl.CostEstimate(flops=0, bytes_accessed=270 << 20, transcendentals=0),
+        name="enter",
+    )(attended, out_weight, hidden, valid, gain, places, moved, shared_weight, *swaps)
+
+
 def turn_heads(values, cosine, sine):
     lane = lax.broadcasted_iota(jnp.int32, values.shape, 1) % HEAD_SIZE
     half = HEAD_SIZE // 2
@@ -521,6 +825,7 @@
     blocks,
     pieces,
     layer,
+    greeted,
     own_ref,
     weight_ref,
     cosine_ref,
@@ -547,7 +852,8 @@
     slots, _, _, resident, pair_columns = pair_ref.shape
     query_columns = query_ref.shape[2]
     inner = jnp.logical_and(head > 0, head < heads - 1)
-    greet(head_peers + blk_peers)
+    if not greeted:
+        greet(head_peers + blk_peers)
 
     def far(peer):
         return jnp.abs(peer[0] - head) == heads - 1
@@ -702,26 +1008,27 @@
         local.wait()
 
 
-def project(rows, weight, cosine, sine, moved, layer, pair_columns, resident, pieces=4):
+PROJECT_PIECES = 4
+
+
+def project_plan(count, width, weight, moved, layer, pair_columns, resident):
     heads, blocks = lax.axis_size("head"), lax.axis_size("blk")
-    count, width = rows.shape
+    pieces = PROJECT_PIECES
     slots = count // resident
-    outs = [
-        jax.ShapeDtypeStruct((heads, count, width), jnp.bfloat16),
-        jax.ShapeDtypeStruct(
-            (slots, heads * resident, weight.shape[1] - pair_columns), jnp.bfloat16
-        ),
-        jax.ShapeDtypeStruct((slots, heads, blocks, resident, pair_columns), jnp.bfloat16),
-        jax.ShapeDtypeStruct((blocks,) + moved.shape[2:], moved.dtype),
-    ]
+    moves = [] if layer is None else [moved]
     vmem = pl.BlockSpec(memory_space=pltpu.VMEM)
     anywhere = pl.BlockSpec(memory_space=pl.ANY)
-    return pl.pallas_call(
-        functools.partial(project_kernel, heads, blocks, pieces, layer),
-        out_shape=outs,
-        in_specs=[vmem] * 4 + [anywhere],
-        out_specs=[vmem] * 3 + [anywhere],
-        scratch_shapes=[
+    return (
+        [
+            jax.ShapeDtypeStruct((heads, count, width), jnp.bfloat16),
+            jax.ShapeDtypeStruct(
+                (slots, heads * resident, weight.shape[1] - pair_columns), jnp.bfloat16
+            ),
+            jax.ShapeDtypeStruct((slots, heads, blocks, resident, pair_columns), jnp.bfloat16),
+            *(jax.ShapeDtypeStruct((blocks,) + array.shape[2:], array.dtype) for array in moves),
+        ],
+        [vmem] * 3 + [anywhere] * len(moves),
+        [
             pltpu.SemaphoreType.DMA((pieces * heads,)),
             pltpu.SemaphoreType.DMA((pieces * heads,)),
             pltpu.SemaphoreType.DMA((pieces * blocks,)),
@@ -730,6 +1037,23 @@
             pltpu.SemaphoreType.DMA((blocks,)),
             pltpu.SemaphoreType.DMA,
         ],
+    )
+
+
+def project(rows, weight, cosine, sine, moved, layer, pair_columns, resident):
+    heads, blocks = lax.axis_size("head"), lax.axis_size("blk")
+    outs, out_specs, scratch = project_plan(
+        *rows.shape, weight, moved, layer, pair_columns, resident
+    )
+    moves = [] if layer is None else [moved]
+    vmem = pl.BlockSpec(memory_space=pltpu.VMEM)
+    anywhere = pl.BlockSpec(memory_space=pl.ANY)
+    return pl.pallas_call(
+        functools.partial(project_kernel, heads, blocks, PROJECT_PIECES, layer, False),
+        out_shape=outs,
+        in_specs=[vmem] * 4 + [anywhere] * len(moves),
+        out_specs=out_specs,
+        scratch_shapes=scratch,
         compiler_params=pltpu.CompilerParams(
             collective_id=kernel_number("project", layer),
             has_side_effects=True,
@@ -737,7 +1061,78 @@
         ),
         cost_estimate=pl.CostEstimate(flops=0, bytes_accessed=130 << 20, transcendentals=0),
         name="project",
-    )(rows, weight, cosine, sine, moved)
+    )(rows, weight, cosine, sine, *moves)
+
+
+def cross(plan, middle, valid, gain, weight, cosine, sine, moved, layer, pair_columns, resident):
+    heads, blocks = lax.axis_size("head"), lax.axis_size("blk")
+    key, maker, arrays, specs, outs, out_specs, scratch, scaled_rows = plan
+    count, width = middle.shape
+    more_outs, more_specs, more_scratch = project_plan(
+        count, width, weight, moved, layer, pair_columns, resident
+    )
+    inputs, results, temps = len(arrays), len(outs), len(scratch)
+    vmem = pl.BlockSpec(memory_space=pltpu.VMEM)
+    anywhere = pl.BlockSpec(memory_space=pl.ANY)
+    norm_outs = [
+        jax.ShapeDtypeStruct((count, width), jnp.float32),
+        jax.ShapeDtypeStruct((count, width), jnp.float32),
+        jax.ShapeDtypeStruct((count, 128), jnp.float32),
+    ]
+
+    def kernel(*refs):
+        _, _, head_peers, blk_peers = plane_peers(heads, blocks)
+        greet(head_peers + blk_peers)
+        given, refs = list(refs[:inputs]), refs[inputs:]
+        middle_ref, valid_ref, gain_ref, weight_ref, cosine_ref, sine_ref, *refs = refs
+        moved_ref, *refs = refs
+        given += refs[:results]
+        sum_ref, refs = refs[0], refs[results:]
+        hidden_ref, scaled_ref, inverse_ref, *refs = refs
+        made, refs = refs[: len(more_outs)], refs[len(more_outs) :]
+        given += refs[:temps]
+        own_ref, *rest = refs[temps:]
+        if not scaled_rows:
+            given.insert(3, None)
+        for stage in maker(given):
+            stage()
+        hidden = middle_ref[...] + valid_ref[...] * sum_ref[...]
+        inverse = lax.rsqrt(jnp.mean(hidden * hidden, axis=1, keepdims=True) + epsilon)
+        scaled = hidden * inverse
+        hidden_ref[...] = hidden
+        scaled_ref[...] = scaled
+        inverse_ref[...] = jnp.broadcast_to(inverse, inverse_ref.shape)
+        own_ref[...] = (scaled * gain_ref[...]).astype(own_ref.dtype)
+        project_kernel(
+            heads,
+            blocks,
+            PROJECT_PIECES,
+            layer,
+            True,
+            own_ref,
+            weight_ref,
+            cosine_ref,
+            sine_ref,
+            moved_ref,
+            *made,
+            *rest,
+        )
+
+    values = pl.pallas_call(
+        kernel,
+        out_shape=[*outs, *norm_outs, *more_outs],
+        in_specs=[*specs, *([vmem] * 6), anywhere],
+        out_specs=[*out_specs, *([vmem] * 3), *more_specs],
+        scratch_shapes=[*scratch, pltpu.VMEM((count, width), jnp.bfloat16), *more_scratch],
+        compiler_params=pltpu.CompilerParams(
+            collective_id=kernel_number("cross", key, layer),
+            has_side_effects=True,
+            vmem_limit_bytes=60 * 1024 * 1024,
+        ),
+        cost_estimate=pl.CostEstimate(flops=0, bytes_accessed=290 << 20, transcendentals=0),
+        name="cross",
+    )(*arrays, middle, valid, gain, weight, cosine, sine, moved)
+    return values[:results], values[results : results + 3], values[results + 3 :]
 
 
 def unproject_kernel(
@@ -975,33 +1370,28 @@
         copy.wait()
 
 
-def unproject(grad_queries, grad_pairs, weight, cosine, sine, moved, after, pieces=4):
+UNPROJECT_PIECES = 4
+
+
+def unproject_plan(grad_pairs, weight, moved):
     heads, blocks = lax.axis_size("head"), lax.axis_size("blk")
     chips = blocks // 2
+    pieces = UNPROJECT_PIECES
     slots, _, _, _, resident, pair_columns = grad_pairs.shape
     rows = slots * resident
     count = rows // pieces
     width, columns = weight.shape
-    outs = [
-        jax.ShapeDtypeStruct((heads, rows, columns), jnp.bfloat16),
-        jax.ShapeDtypeStruct((rows, width), jnp.float32),
-    ] + [jax.ShapeDtypeStruct(array.shape, array.dtype) for array in moved]
+    items = len(moved)
     vmem = pl.BlockSpec(memory_space=pltpu.VMEM)
     anywhere = pl.BlockSpec(memory_space=pl.ANY)
-    items = len(moved)
-
-    def kernel(*refs):
-        given = refs[: 5 + items]
-        unproject_kernel(
-            heads, blocks, pieces, items, *given, *refs[5 + items + len(after) :]
-        )
-
-    return pl.pallas_call(
-        kernel,
-        out_shape=outs,
-        in_specs=[vmem] * 5 + [anywhere] * (items + len(after)),
-        out_specs=[vmem] * 2 + [anywhere] * items,
-        scratch_shapes=[
+    return (
+        [
+            jax.ShapeDtypeStruct((heads, rows, columns), jnp.bfloat16),
+            jax.ShapeDtypeStruct((rows, width), jnp.float32),
+            *(jax.ShapeDtypeStruct(array.shape, array.dtype) for array in moved),
+        ],
+        [vmem] * 2 + [anywhere] * items,
+        [
             pltpu.VMEM((pieces, heads, chips, count, pair_columns), jnp.bfloat16),
             pltpu.VMEM((pieces, heads, chips, count, pair_columns), jnp.bfloat16),
             pltpu.VMEM((pieces, chips, heads, count, pair_columns), jnp.bfloat16),
@@ -1019,23 +1409,95 @@
             pltpu.SemaphoreType.DMA((items * blocks,)),
             pltpu.SemaphoreType.DMA((items,)),
         ],
+    )
+
+
+def unproject(grad_queries, grad_pairs, weight, cosine, sine, moved, after, onward=None):
+    heads, blocks = lax.axis_size("head"), lax.axis_size("blk")
+    outs, out_specs, scratch = unproject_plan(grad_pairs, weight, moved)
+    results, temps = len(outs), len(scratch)
+    items = len(moved)
+    vmem = pl.BlockSpec(memory_space=pltpu.VMEM)
+    anywhere = pl.BlockSpec(memory_space=pl.ANY)
+    norm_arrays, arrays, specs, more_outs, more_specs, more_scratch = [], [], [], [], [], []
+    if onward is not None:
+        *norm_arrays, (places, scale, matrices) = onward
+        rows, width = norm_arrays[0].shape
+        arrays, specs, more_outs, more_specs, more_scratch = dispatch_plan(
+            jax.ShapeDtypeStruct((rows, width), jnp.bfloat16), places, scale, matrices, True
+        )
+        arrays, specs = arrays[1:], specs[1:]
+        more_outs = [
+            jax.ShapeDtypeStruct((rows, width), jnp.float32),
+            jax.ShapeDtypeStruct((1, width), jnp.float32),
+            *more_outs,
+        ]
+        more_specs = [vmem, vmem, *more_specs]
+        more_scratch = [pltpu.VMEM((rows, width), jnp.bfloat16), *more_scratch]
+
+    def kernel(*refs):
+        given, refs = refs[: 5 + items], refs[5 + items + len(after) :]
+        norm_refs, refs = refs[: len(norm_arrays)], refs[len(norm_arrays) :]
+        dispatch_refs, refs = list(refs[: len(arrays)]), refs[len(arrays) :]
+        made, refs = refs[:results], refs[results:]
+        more, refs = refs[: len(more_outs)], refs[len(more_outs) :]
+        unproject_kernel(heads, blocks, UNPROJECT_PIECES, items, *given, *made, *refs[:temps])
+        if onward is None:
+            return
+        refs = refs[temps:]
+        other_ref, valid_ref, gain_ref, scaled_ref, inverse_ref = norm_refs
+        hidden_ref, grad_gain_ref, *more = more
+        own_ref, *rest = refs
+        grad = made[1][...]
+        scaled = scaled_ref[...]
+        grad_gain_ref[...] = jnp.sum(grad * scaled, axis=0, keepdims=True)
+        grad = grad * gain_ref[...]
+        grad = inverse_ref[:, :1] * (
+            grad - scaled * jnp.mean(grad * scaled, axis=1, keepdims=True)
+        )
+        hidden = other_ref[...] + grad
+        hidden_ref[...] = hidden
+        own_ref[...] = (valid_ref[...] * hidden).astype(own_ref.dtype)
+        for stage in dispatch_stages(
+            heads, blocks, True, (own_ref, *dispatch_refs, *more, *rest)
+        ):
+            stage()
+
+    values = pl.pallas_call(
+        kernel,
+        out_shape=[*outs, *more_outs],
+        in_specs=[vmem] * 5
+        + [anywhere] * (items + len(after))
+        + [vmem] * len(norm_arrays)
+        + specs,
+        out_specs=[*out_specs, *more_specs],
+        scratch_shapes=[*scratch, *more_scratch],
         compiler_params=pltpu.CompilerParams(
             collective_id=kernel_number(
-                "unproject", *(array.shape for array in (*moved, *after))
+                "unproject", onward is None, *(array.shape for array in (*moved, *after))
             ),
             has_side_effects=True,
-            vmem_limit_bytes=56 * 1024 * 1024,
+            vmem_limit_bytes=60 * 1024 * 1024,
         ),
-        cost_estimate=pl.CostEstimate(flops=0, bytes_accessed=150 << 20, transcendentals=0),
+        cost_estimate=pl.CostEstimate(
+            flops=0, bytes_accessed=(150 if onward is None else 320) << 20, transcendentals=0
+        ),
         name="unproject",
-    )(grad_queries, grad_pairs, weight, cosine, sine, *moved, *after)
-
-
-def combine_stages(heads, blocks, by_columns, extra, refs):
+    )(grad_queries, grad_pairs, weight, cosine, sine, *moved, *after, *norm_arrays, *arrays)
+    return values[:results], values[results:]
+
+
+def combine_stages(heads, blocks, by_columns, backward, refs):
     units_ref, shared_units_ref, place_ref, scale_ref, weight_ref, shared_weight_ref, *refs = refs
-    extra_ref, *refs = refs if extra else (None, *refs)
+    if backward:
+        gate_up_ref, grad_units_ref = units_ref, refs[0]
+        sources, refs = refs[1:6], refs[6:]
     out_ref, returned_ref, *refs = refs
-    extra_out_ref, *refs = refs if extra else (None, *refs)
+    if backward:
+        grad_in_ref, grad_down_ref, gates_ref, *refs = refs
+        units_ref, dots_ref, gate_part_ref, *held = refs[-10:]
+        queue_ref, inner_ref, made_grad_ref, plane_ref, came_ref, late_sems, _ = held
+        refs = refs[:-10]
     (
         made_ref,
         part_ref,
@@ -1061,32 +1523,86 @@
         pltpu.make_async_copy(weight_ref, held_ref, local_sems.at[0]),
         pltpu.make_async_copy(shared_weight_ref, shared_held_ref, local_sems.at[1]),
     ]
-    extra_copies = []
+    gate_copies = []
     head_copies = []
     blk_copies = []
+    late = []
+    if backward:
+        late = [
+            pltpu.make_async_copy(source, target, late_sems.at[number])
+            for number, (source, target) in enumerate(
+                zip(sources, (queue_ref, inner_ref, made_grad_ref, plane_ref, came_ref))
+            )
+        ]
 
     def begin():
-        if extra:
-            loads.append(
-                pltpu.make_async_copy(extra_ref, extra_out_ref.at[head], local_sems.at[2])
-            )
+        for load in loads + late:
+            load.start()
+        if backward:
+            half = grad_units_ref.shape[1]
+
+            def turn(block, carry):
+                rows_here = pl.ds(pl.multiple_of(block * slot, 16), slot)
+                gate = gate_up_ref[rows_here, pl.ds(0, half)]
+                up = gate_up_ref[rows_here, pl.ds(half, half)]
+                grad = grad_units_ref[rows_here, :]
+                share = 1.0 / (1.0 + jnp.exp(-gate))
+                units_ref[rows_here, pl.ds(0, half)] = (
+                    grad * up * share * (1.0 + gate * (1.0 - share))
+                ).astype(units_ref.dtype)
+                units_ref[rows_here, pl.ds(half, half)] = (grad * gate * share).astype(
+                    units_ref.dtype
+                )
+                return carry
+
+            lax.fori_loop(0, blocks, turn, 0)
         for load in loads:
-            load.start()
-        if extra:
-            extra_copies.extend(
+            load.wait()
+
+    def fill(number):
+        if number == 1:
+            for load in late:
+                load.wait()
+        piece = number - 1
+        columns = pl.ds(piece * step_width, step_width)
+        if 0 <= piece < pieces:
+            grad_in_ref[columns, :] = dot_first(queue_ref[:, columns], units_ref[...]).astype(
+                grad_in_ref.dtype
+            )
+            dots = dot_last(plane_ref[:, columns], came_ref[:, columns])
+            if piece:
+                dots = dots + dots_ref[...]
+            dots_ref[...] = dots
+        tile = 128
+        if 0 <= piece < inner_ref.shape[1] // tile:
+            lanes = pl.ds(piece * tile, tile)
+            grad_down_ref[lanes, :] = dot_first(inner_ref[:, lanes], made_grad_ref[...]).astype(
+                grad_down_ref.dtype
+            )
+        if piece == pieces:
+            count = dots_ref.shape[1]
+            shape = (gate_part_ref.shape[0], count)
+            spread = jnp.where(
+                lax.broadcasted_iota(jnp.int32, shape, 1) // slot
+                == lax.broadcasted_iota(jnp.int32, shape, 0),
+                1.0,
+                0.0,
+            ).astype(jnp.bfloat16)
+            dots = dots_ref[...].astype(jnp.bfloat16) * place_ref[...]
+            gate_part_ref[...] = dot_last(spread, dots)
+            gates_ref[head] = gate_part_ref[...]
+            gate_copies.extend(
                 started(
                     remote(
-                        extra_ref,
-                        extra_out_ref.at[head],
+                        gate_part_ref,
+                        gates_ref.at[head],
                         (head_send, head_recv),
-                        pieces * heads + number,
+                        pieces * heads + index,
                         peer,
                     )
                 )
-                for number, peer in enumerate(head_peers)
-            )
-        for load in loads:
-            load.wait()
+                for index, peer in enumerate(head_peers)
+            )
 
     def produce(piece):
         columns = pl.ds(piece * step_width, step_width)
@@ -1209,6 +1725,8 @@
     def step(number):
         if number < pieces:
             produce(number)
+        if backward:
+            fill(number)
         if 0 < number <= pieces:
             gather(number - 1)
         if relay and 1 < number <= pieces + 1:
@@ -1225,7 +1743,7 @@
                     pl.when(distant)(through_copy(piece, head_peers[number]).wait_send)
                 else:
                     copy.wait_send()
-        for copy in extra_copies:
+        for copy in gate_copies:
             copy.wait()
         for copies in blk_copies:
             for copy in copies:
@@ -1235,7 +1753,7 @@
     return [begin, *steps, end]
 
 
-def combine_call(units, shared_units, places, scale, weights, by_columns, extra=None):
+def combine_call(units, shared_units, places, scale, weights, by_columns, backward=None):
     heads, blocks = lax.axis_size("head"), lax.axis_size("blk")
     (own_weight, shared_weight) = weights
     shared, slot = shared_units.shape[:2]
@@ -1245,31 +1763,52 @@
     vmem = pl.BlockSpec(memory_space=pltpu.VMEM)
     anywhere = pl.BlockSpec(memory_space=pl.ANY)
     scales = [] if scale is None else [scale]
-    extras = [] if extra is None else [extra]
+    outs = [
+        jax.ShapeDtypeStruct((count, width), jnp.float32),
+        jax.ShapeDtypeStruct((blocks + shared, slot, width), jnp.bfloat16),
+    ]
+    scratch = [
+        pltpu.VMEM((blocks, slot, width), jnp.bfloat16),
+        pltpu.VMEM((heads, count, width), jnp.bfloat16),
+        pltpu.VMEM((heads, count, width), jnp.bfloat16),
+        pltpu.VMEM((count, width), jnp.bfloat16),
+        pltpu.VMEM(own_weight.shape, jnp.bfloat16),
+        pltpu.VMEM(shared_weight.shape, jnp.bfloat16),
+        pltpu.SemaphoreType.DMA(((pieces + 1) * heads,)),
+        pltpu.SemaphoreType.DMA(((pieces + 1) * heads,)),
+        pltpu.SemaphoreType.DMA((pieces * (blocks - 1),)),
+        pltpu.SemaphoreType.DMA((pieces * (blocks - 1),)),
+        pltpu.SemaphoreType.DMA((2,)),
+    ]
+    arrays = [units, shared_units, places, *scales, own_weight, shared_weight]
+    specs = [vmem] * (3 + len(scales)) + [anywhere] * 2
+    if backward is not None:
+        grad_units, *late = backward
+        arrays += [grad_units, *late]
+        specs += [vmem] + [anywhere] * len(late)
+        inner = late[1].shape[1]
+        gate_rows = -(-(blocks + shared) // 8) * 8
+        outs += [
+            jax.ShapeDtypeStruct((width, units.shape[1]), jnp.bfloat16),
+            jax.ShapeDtypeStruct((inner, width), jnp.bfloat16),
+            jax.ShapeDtypeStruct((heads, gate_rows, places.shape[0]), jnp.float32),
+        ]
+        scratch += [
+            pltpu.VMEM(units.shape, jnp.bfloat16),
+            pltpu.VMEM(places.shape, jnp.float32),
+            pltpu.VMEM((gate_rows, places.shape[0]), jnp.float32),
+            *(pltpu.VMEM(array.shape, array.dtype) for array in late),
+            pltpu.SemaphoreType.DMA((len(late),)),
+            pltpu.SemaphoreType.DMA,
+        ]
     return (
-        ("combine", by_columns, scale is not None, extra is not None),
-        functools.partial(combine_stages, heads, blocks, by_columns, bool(extras)),
-        [units, shared_units, places, *scales, own_weight, shared_weight, *extras],
-        [vmem] * (3 + len(scales)) + [anywhere] * (2 + len(extras)),
-        [
-            jax.ShapeDtypeStruct((count, width), jnp.float32),
-            jax.ShapeDtypeStruct((blocks + shared, slot, width), jnp.bfloat16),
-            *(jax.ShapeDtypeStruct((heads,) + array.shape, array.dtype) for array in extras),
-        ],
-        [vmem] * 2 + [anywhere] * len(extras),
-        [
-            pltpu.VMEM((blocks, slot, width), jnp.bfloat16),
-            pltpu.VMEM((heads, count, width), jnp.bfloat16),
-            pltpu.VMEM((heads, count, width), jnp.bfloat16),
-            pltpu.VMEM((count, width), jnp.bfloat16),
-            pltpu.VMEM(own_weight.shape, jnp.bfloat16),
-            pltpu.VMEM(shared_weight.shape, jnp.bfloat16),
-            pltpu.SemaphoreType.DMA(((pieces + 1) * heads,)),
-            pltpu.SemaphoreType.DMA(((pieces + 1) * heads,)),
-            pltpu.SemaphoreType.DMA((pieces * (blocks - 1),)),
-            pltpu.SemaphoreType.DMA((pieces * (blocks - 1),)),
-            pltpu.SemaphoreType.DMA((3,)),
-        ],
+        ("combine", by_columns, scale is not None, backward is not None),
+        functools.partial(combine_stages, heads, blocks, by_columns, backward is not None),
+        arrays,
+        specs,
+        outs,
+        [vmem] * len(outs),
+        scratch,
         scale is not None,
     )
 
@@ -1342,13 +1881,13 @@
                 weighted = weighted / totals
                 for member in range(group):
                     start = (kv_head * group + member) * HEAD_SIZE
-                    out_ref[0, rows, start : start + HEAD_SIZE] = weighted[
+                    out_ref[head, 0, :, start : start + HEAD_SIZE] = weighted[
                         member * resident : (member + 1) * resident, HEAD_SIZE:
                     ].astype(out_ref.dtype)
 
         @pl.when(jnp.logical_not(live))
-        def _(rows=rows):
-            out_ref[0, rows, :] = jnp.zeros((resident, out_ref.shape[2]), out_ref.dtype)
+        def _(head=head):
+            out_ref[head, 0] = jnp.zeros(out_ref.shape[2:], out_ref.dtype)
 
 
 def attend_back_kernel(
@@ -1408,9 +1947,97 @@
     grad_pair_ref[0] = total_ref[...].astype(grad_pair_ref.dtype)
 
 
+def plan_kernel(heads, experts_local, slot, info_ref, routes_ref, ranks_ref, chosen_ref, place_ref, turned_ref):
+    routes = routes_ref[0]
+    ranks = ranks_ref[0]
+    tokens = routes.shape[1]
+    count = place_ref.shape[2]
+    first = info_ref[0] * experts_local
+    lanes = 128
+    named = [
+        jnp.max(jnp.where(routes == expert, 1, 0), axis=0, keepdims=True)
+        for expert in range(EXPERTS)
+    ]
+    named.append(jnp.zeros((lanes - EXPERTS, tokens), jnp.int32))
+    chosen_ref[0] = jnp.concatenate(named, axis=0).astype(jnp.float32).T
+    marks = [
+        jnp.sum(
+            jnp.where((routes == first + expert) & (ranks < CAP), ranks + 1, 0),
+            axis=0,
+            keepdims=True,
+        )
+        for expert in range(experts_local)
+    ]
+    marks.append(jnp.zeros((lanes - experts_local, tokens), jnp.int32))
+    marks = jnp.concatenate(marks, axis=0).astype(jnp.float32)
+    slot_rows = tokens // heads
+
+    def fits(shape, row_axis, wide):
+        row = lax.broadcasted_iota(jnp.int32, shape, row_axis)
+        token = lax.broadcasted_iota(jnp.int32, shape, 1 - row_axis)
+        inside = row % slot
+        same = (inside // CAP == token // slot_rows) & (wide.astype(jnp.int32) == inside % CAP + 1)
+        return jnp.where(same, 1.0, 0.0).astype(jnp.bfloat16)
+
+    def spread(shape, row_axis):
+        row = lax.broadcasted_iota(jnp.int32, shape, row_axis)
+        expert = lax.broadcasted_iota(jnp.int32, shape, 1 - row_axis)
+        return jnp.where(row // slot == expert, 1.0, 0.0).astype(jnp.bfloat16)
+
+    place_ref[0] = fits(
+        (tokens, count),
+        1,
+        jnp.dot(
+            marks.T.astype(jnp.bfloat16),
+            spread((lanes, count), 1),
+            preferred_element_type=jnp.float32,
+        ),
+    )
+    turned_ref[0] = fits(
+        (count, tokens),
+        0,
+        jnp.dot(
+            spread((count, lanes), 0),
+            marks.astype(jnp.bfloat16),
+            preferred_element_type=jnp.float32,
+        ),
+    )
+
+
+def plans(heads, experts_local, slot, head_index, routes, ranks):
+    layers, top, tokens = routes.shape
+    count = experts_local * slot
+
+    def spec(*shape):
+        return pl.BlockSpec((1,) + shape, lambda layer, info: (layer, 0, 0))
+
+    chosen, places, turned = pl.pallas_call(
+        functools.partial(plan_kernel, heads, experts_local, slot),
+        grid_spec=pltpu.PrefetchScalarGridSpec(
+            num_scalar_prefetch=1,
+            grid=(layers,),
+            in_specs=[spec(top, tokens)] * 2,
+            out_specs=[spec(tokens, 128), spec(tokens, count), spec(count, tokens)],
+        ),
+        out_shape=[
+            jax.ShapeDtypeStruct((layers, tokens, 128), jnp.float32),
+            jax.ShapeDtypeStruct((layers, tokens, count), jnp.bfloat16),
+            jax.ShapeDtypeStruct((layers, count, tokens), jnp.bfloat16),
+        ],
+        compiler_params=pltpu.CompilerParams(vmem_limit_bytes=40 * 1024 * 1024),
+        cost_estimate=pl.CostEstimate(flops=0, bytes_accessed=16 << 20, transcendentals=0),
+        name="plans",
+    )(head_index[None].astype(jnp.int32), routes, ranks)
+    return chosen[:, :, :EXPERTS] > 0.0, places, turned
+
+
 def attention_call(kernel, info, arrays, outs, scratch, flops, name):
     def spec(array):
         shape = array.shape
+        if len(shape) == 4:
+            return pl.BlockSpec(
+                (shape[0], 1) + shape[2:], lambda slot, info: (0, slot, 0, 0)
+            )
         return pl.BlockSpec((1,) + shape[1:], lambda slot, info: (slot, 0, 0))
 
     return pl.pallas_call(
@@ -1486,28 +2113,10 @@
     tile_sine = tile_sine.reshape(heads_count, slot_rows, -1)
     info = jnp.concatenate([blk_index[None].astype(jnp.int32), lengths])
 
-    expert_ids = jnp.arange(EXPERTS, dtype=jnp.int32)
     row_ids = jnp.arange(experts_local * slot, dtype=jnp.int32)
     spread = (
         row_ids[None, :] // slot == jnp.arange(experts_local, dtype=jnp.int32)[:, None]
     ).astype(jnp.bfloat16)
-    token_head = plane_ids[:, None] // slot_rows
-    row_head = row_ids[None, :] % slot // CAP
-    row_rank = (row_ids % slot % CAP).astype(jnp.float32)[None, :]
-
-    def layer_plan(layer_index):
-        plan_routes = plan[:, 0, layer_index].reshape(all_tokens, TOP)
-        plan_ranks = plan[:, 1, layer_index].reshape(all_tokens, TOP)
-        named = plan_routes[:, :, None] == expert_ids
-        chosen = jnp.any(named, axis=1)
-        marks = jnp.sum(
-            jnp.where(named & (plan_ranks < CAP)[:, :, None], plan_ranks[:, :, None] + 1, 0), axis=1
-        )
-        marks = lax.dynamic_slice_in_dim(marks, head_index * experts_local, experts_local, 1)
-        wide = mm("te,er->tr", marks.astype(jnp.bfloat16), spread) - 1.0
-        places = ((wide == row_rank) & (token_head == row_head)).astype(jnp.bfloat16)
-        return (chosen, places)
-
     def to_experts(rows):
         rows = rows.reshape(experts_local, slot, width)
         own = None
@@ -1527,15 +2136,12 @@
             parts = [own.reshape(owned_total, slot, width), shared]
         return jnp.concatenate(parts, axis=0).reshape(experts_local * slot, width)
 
-    def shared_weights(layer_index):
+    def shared_weights(layer_index, reached):
         if owned_total == experts_local:
             return []
-        return [
-            tuple(
-                lax.all_gather(matrix[layer_index, owned_total:], "blk", axis=1, tiled=True)
-                for matrix in (w_in, w_down)
-            )
-        ]
+        parts = tuple(matrix[layer_index, owned_total:] for matrix in (w_in, w_down))
+        parts, _ = lax.optimization_barrier((parts, reached))
+        return [tuple(lax.all_gather(part, "blk", axis=1, tiled=True) for part in parts)]
 
     def to_owner(matrix, layer_index):
         if not owned:
@@ -1582,10 +2188,10 @@
         total, returned, *extras = results
         return (total, returned.reshape(-1, width), *extras)
 
-    def moe_in(rows, turned_places, scale, sets, which):
+    def moe_in(rows, turned_places, scale, sets, which, after=()):
         if staged:
             plan = dispatch_call(rows, turned_places, scale, matrices(sets, which), which == 1)
-            return unpack_in(staged_call([plan], "dispatch", 170)[0])
+            return unpack_in(staged_call([plan], "dispatch", 170, after)[0])
         (plane,) = exchange(("head_gather", rows))
         plane = plane.reshape(all_tokens, width)
         queues = mm("rt,td->rd", turned_places, plane)
@@ -1595,28 +2201,64 @@
         spec = ("erd,edf->erf", "erd,efd->erf")[which]
         return (plane, queues, [mm(spec, rows, mats[which]) for rows, mats in zip(queues, sets)])
 
-    def moe_out(units, places, scale, sets, which, extra=None):
+    def moe_out(units, places, scale, sets):
         if staged:
             plan = combine_call(
-                units[0][0], units[1], places, scale, matrices(sets, which), which == 0, extra
+                units[0][0], units[1], places, scale, matrices(sets, 1), False
             )
             return unpack_out(staged_call([plan], "combine", 170)[0])
-        spec = ("erf,edf->erd", "erf,efd->erd")[which]
-        made = [mm(spec, part, mats[which]).astype(jnp.bfloat16) for part, mats in zip(units, sets)]
+        made = [
+            mm("erf,efd->erd", part, mats[1]).astype(jnp.bfloat16)
+            for part, mats in zip(units, sets)
+        ]
         returned = from_experts(*(made if owned else [None] + made))
-        rows = returned
-        if scale is not None:
-            rows = (returned.astype(jnp.float32) * scale).astype(jnp.bfloat16)
-        parts, *extras = exchange(
-            ("head_swap", head_parts(mm("tr,rd->td", places, rows))),
-            *([] if extra is None else [("head_gather", extra)]),
-        )
-        return (head_sum(parts), returned, *extras)
+        rows = (returned.astype(jnp.float32) * scale).astype(jnp.bfloat16)
+        (parts,) = exchange(("head_swap", head_parts(mm("tr,rd->td", places, rows))))
+        return (head_sum(parts), returned)
+
+    def moe_back(places, sets, gate_up, grad_units, incoming, units, grad_rows, plane_grads, came):
+        grad_gate_up = [
+            gated_back(*parts) if number or not staged else None
+            for number, parts in enumerate(zip(gate_up, grad_units))
+        ]
+        grad_weights = [
+            (
+                mm("erd,erf->edf", rows, grads).astype(jnp.bfloat16),
+                mm("erf,erd->efd", inner, out_grads).astype(jnp.bfloat16),
+            )
+            if grads is not None
+            else None
+            for rows, grads, inner, out_grads in zip(incoming, grad_gate_up, units, grad_rows)
+        ]
+        if staged:
+            plan = combine_call(
+                gate_up[0][0],
+                grad_gate_up[1],
+                places,
+                None,
+                matrices(sets, 0),
+                True,
+                [grad_units[0][0], incoming[0][0], units[0][0], grad_rows[0][0], plane_grads, came],
+            )
+            total, _, grad_in, grad_down, gates = staged_call([plan], "combine_back", 170)[0]
+            grad_weights[0] = (grad_in[None], grad_down[None])
+            return (total, gates[:, :experts_local].reshape(EXPERTS, all_tokens), grad_weights)
+        pair_dots = (mm("td,rd->tr", plane_grads, came) * places).astype(jnp.bfloat16)
+        made = [
+            mm("erf,edf->erd", part, mats[0]).astype(jnp.bfloat16)
+            for part, mats in zip(grad_gate_up, sets)
+        ]
+        returned = from_experts(*(made if owned else [None] + made))
+        parts, gates = exchange(
+            ("head_swap", head_parts(mm("tr,rd->td", places, returned))),
+            ("head_gather", mm("tr,er->te", pair_dots, spread).T),
+        )
+        return (head_sum(parts), gates.reshape(EXPERTS, all_tokens), grad_weights)
 
     def moe_turn(units, places, turned_places, scale, grad_rows, sets):
         if not staged:
             return (
-                moe_out(units, places, scale, sets, 1),
+                moe_out(units, places, scale, sets),
                 moe_in(grad_rows, turned_places, scale, sets, 1),
             )
         weights = matrices(sets, 1)
@@ -1675,9 +2317,14 @@
                 axis=-1,
             )
         )
-    plan = jnp.stack([routes, queue_ranks]).reshape(2 * DECODER_LAYERS, slot_rows * TOP)
+    plan = jnp.stack([routes, queue_ranks]).reshape(2 * DECODER_LAYERS, slot_rows, TOP)
+    plan = plan.transpose(0, 2, 1).reshape(2 * DECODER_LAYERS * TOP, slot_rows)
     plan, first_send = exchange(("head_gather", plan), ("head_swap", send[0]))
-    plan = plan.reshape(heads_count, 2, DECODER_LAYERS, slot_rows, TOP)
+    plan = plan.reshape(heads_count, 2, DECODER_LAYERS, TOP, slot_rows)
+    plan = plan.transpose(1, 2, 3, 0, 4).reshape(2, DECODER_LAYERS, TOP, all_tokens)
+    chosen_all, places_all, turned_all = plans(
+        heads_count, experts_local, slot, head_index, plan[0], plan[1]
+    )
 
     def attention_set(wide, out_full):
         wide = wide.transpose(1, 0, 2, 3).reshape(width, -1)
@@ -1686,21 +2333,38 @@
         gains = small.T[EXPERTS : EXPERTS + 2].astype(jnp.float32)
         return (wide[:, :columns], out_full.reshape(-1, width), small[:, :EXPERTS], gains)
 
-    wide, first_out = exchange(("blk_pairs", first_send), ("blk_pairs", w_out[0]))
+    wide, first_out, *next_sends = exchange(
+        ("blk_pairs", first_send),
+        ("blk_pairs", w_out[0]),
+        *(("head_swap", array) for array in send[1:]),
+    )
     attention_weights = [
         attention_set(wide, first_out),
     ]
+    for layer_index, array in enumerate(next_sends, start=1):
+        attention_weights.append(
+            attention_set(
+                lax.all_gather(array, "blk", axis=0),
+                lax.all_gather(w_out[layer_index], "blk", axis=0),
+            )
+        )
 
     hidden = tokens.reshape(slot_rows, width).astype(jnp.float32)
     stored_all = []
     for layer_index in range(DECODER_LAYERS):
         qkv_full, out_full, router_full, gains = attention_weights[layer_index]
-        chosen, places = layer_plan(layer_index)
-        scaled_a, inverse_a = norm_rows(hidden)
-        normed_a = (scaled_a * gains[:1]).astype(jnp.bfloat16)
+        chosen, places, turned_places = (
+            part[layer_index] for part in (chosen_all, places_all, turned_all)
+        )
         next_layer = layer_index + 1 < DECODER_LAYERS
-        fused = owned == 1 and heads_count == 4
-        if fused:
+        fused = staged and heads_count == 4
+        if not fused or not layer_index:
+            scaled_a, inverse_a = norm_rows(hidden)
+            normed_a = (scaled_a * gains[:1]).astype(jnp.bfloat16)
+        if fused and layer_index:
+            plane_normed_a, queries, pairs_all, *own_down_next = crossed
+            plane_normed_a = plane_normed_a.reshape(all_tokens, width)
+        elif fused:
             plane_normed_a, queries, pairs_all, own_down = project(
                 normed_a,
                 qkv_full,
@@ -1739,37 +2403,49 @@
             ),
             info,
             [queries, pairs_all],
-            [jax.ShapeDtypeStruct(queries.shape, jnp.bfloat16)],
+            [
+                jax.ShapeDtypeStruct(
+                    (heads_count, SEQUENCE_SLOTS, resident, query_columns), jnp.bfloat16
+                )
+            ],
             [],
             4 * rows_local * keys_total * query_columns,
             "attend",
         )
-        attended = by_head(attended)
-        weight_sets = shared_weights(layer_index)
-        branch, *others = exchange(
-            ("head_swap", head_parts(mm("tf,fd->td", attended, out_full))),
-            *([("head_swap", send[layer_index + 1])] if next_layer else []),
-            *to_owner(w_in, layer_index),
-            after=weight_sets[0] if weight_sets else (),
-        )
-        if next_layer:
-            next_send, *others = others
-            attention_weights.append(
-                attention_set(
-                    lax.all_gather(next_send, "blk", axis=0),
-                    lax.all_gather(w_out[layer_index + 1], "blk", axis=0),
-                )
-            )
-        own_in_next = others
-        if owned:
-            weight_sets = [
-                (owned_matrix(own_in_next[0]), owned_matrix(own_down_next[0]))
-            ] + weight_sets
-        middle = hidden + valid_column * head_sum(branch)
-        scaled_b, inverse_b = norm_rows(middle)
-        normed_b = (scaled_b * gains[1:]).astype(jnp.bfloat16)
-        turned_places = places.T
-        plane_rows, incoming, gate_up = moe_in(normed_b, turned_places, None, weight_sets, 0)
+        attended = attended.reshape(all_tokens, query_columns)
+        weight_sets = shared_weights(layer_index, middle if layer_index else wide)
+        swaps = []
+        if fused and staged:
+            middle, scaled_b, inverse_b, *results = enter(
+                attended,
+                out_full,
+                hidden,
+                valid_column,
+                gains[1:],
+                turned_places,
+                w_in,
+                layer_index,
+                weight_sets[0][0],
+                swaps,
+            )
+            inverse_b = inverse_b[:, :1]
+            results, own_in = results[:5], results[5]
+            plane_rows, incoming, gate_up = unpack_in(results)
+            weight_sets = [(own_in[None], owned_matrix(own_down_next[0]))] + weight_sets
+        else:
+            branch, *others = exchange(
+                ("head_swap", head_parts(mm("tf,fd->td", attended, out_full))),
+                *to_owner(w_in, layer_index),
+            )
+            own_in_next = others
+            if owned:
+                weight_sets = [
+                    (owned_matrix(own_in_next[0]), owned_matrix(own_down_next[0]))
+                ] + weight_sets
+            middle = hidden + valid_column * head_sum(branch)
+            scaled_b, inverse_b = norm_rows(middle)
+            normed_b = (scaled_b * gains[1:]).astype(jnp.bfloat16)
+            plane_rows, incoming, gate_up = moe_in(normed_b, turned_places, None, weight_sets, 0)
         units = [gated(part) for part in gate_up]
         logits = mm("td,de->te", plane_rows, router_full)
         peaks = jnp.max(jnp.where(chosen, logits, negative), axis=-1, keepdims=True)
@@ -1780,8 +2456,26 @@
         )
         row_gates = mm("rt,te->re", turned_places, plane_gates.astype(jnp.bfloat16))
         row_gates = jnp.sum(row_gates * spread.T.astype(jnp.float32), axis=1, keepdims=True)
-        if next_layer:
-            mixture, returned = moe_out(units, places, row_gates, weight_sets, 1)
+        if next_layer and fused:
+            next_weights = attention_weights[layer_index + 1]
+            (_, returned), norms, crossed = cross(
+                combine_call(
+                    units[0][0], units[1], places, row_gates, matrices(weight_sets, 1), False
+                ),
+                middle,
+                valid_column,
+                next_weights[3][:1],
+                next_weights[0],
+                tile_cosine,
+                tile_sine,
+                w_down,
+                layer_index + 1,
+                pair_columns,
+                resident,
+            )
+            returned = returned.reshape(-1, width)
+        elif next_layer:
+            mixture, returned = moe_out(units, places, row_gates, weight_sets)
         else:
             (mixture, returned), turned = moe_turn(
                 units,
@@ -1813,7 +2507,11 @@
                 returned,
             )
         )
-        hidden = middle + valid_column * mixture
+        if next_layer and fused:
+            hidden, scaled_a, inverse_a = norms
+            inverse_a = inverse_a[:, :1]
+        else:
+            hidden = middle + valid_column * mixture
     result = (valid_column * hidden).astype(jnp.bfloat16).reshape(tokens.shape)
     grad_hidden = valid_column * cotangent.reshape(slot_rows, width).astype(jnp.float32)
     qkv_list = [None] * DECODER_LAYERS
@@ -1822,6 +2520,7 @@
     gains_list = [None] * DECODER_LAYERS
     expert_list = [None] * DECODER_LAYERS
     pending = []
+    waiting = []
     for layer_index in reversed(range(DECODER_LAYERS)):
         qkv_full, out_full, router_full, gains = attention_weights[layer_index]
         (
@@ -1844,29 +2543,28 @@
             units,
             returned,
         ) = stored_all[layer_index]
-        if layer_index + 1 < DECODER_LAYERS:
+        if layer_index + 1 < DECODER_LAYERS and not fused:
             turned = moe_in(
                 (valid_column * grad_hidden).astype(jnp.bfloat16),
                 turned_places,
                 row_gates,
                 weight_sets,
                 1,
+                waiting,
             )
         plane_grads, grad_produced, grad_units = turned
-        grad_gate_up = [gated_back(*parts) for parts in zip(gate_up, grad_units)]
-        pair_dots = (mm("td,rd->tr", plane_grads, returned) * places).astype(jnp.bfloat16)
-        plane_grad_gates = mm("tr,er->te", pair_dots, spread).T
-        grad_normed_b, _, grad_gates = moe_out(
-            grad_gate_up, places, None, weight_sets, 0, plane_grad_gates
-        )
-        grad_gates = grad_gates.reshape(EXPERTS, all_tokens).T
-        grad_weight_sets = [
-            (
-                mm("erd,erf->edf", rows, grads).astype(jnp.bfloat16),
-                mm("erf,erd->efd", inner, out_grads).astype(jnp.bfloat16),
-            )
-            for rows, grads, inner, out_grads in zip(incoming, grad_gate_up, units, grad_produced)
-        ]
+        grad_normed_b, grad_gates, grad_weight_sets = moe_back(
+            places,
+            weight_sets,
+            gate_up,
+            grad_units,
+            incoming,
+            units,
+            grad_produced,
+            plane_grads,
+            returned,
+        )
+        grad_gates = grad_gates.T
         grad_logits = gates_all * (
             grad_gates - jnp.sum(gates_all * grad_gates, axis=-1, keepdims=True)
         )
@@ -1885,7 +2583,11 @@
         plane_branch, *own_grad_in = exchange(
             ("head_gather", (valid_column * grad_middle).astype(jnp.bfloat16)),
             *(from_owner(grad_weight_sets[0][0]) if owned else []),
-            after=[*pending, *(grad_weight_sets[-1] if owned_total < experts_local else ())],
+            after=[
+                *pending,
+                *(waiting if fused else ()),
+                *(grad_weight_sets[-1] if owned_total < experts_local else ()),
+            ],
         )
         pending = []
         shared_terms = []
@@ -1918,7 +2620,18 @@
         if owned:
             swapped += from_owner(grad_weight_sets[0][1])
         if fused:
-            grad_projected, grad_normed_a, grad_out_w, *own_grad_down = unproject(
+            onward = None
+            if layer_index:
+                before = stored_all[layer_index - 1]
+                onward = (
+                    grad_middle,
+                    valid_column,
+                    gains[:1],
+                    scaled_a,
+                    jnp.broadcast_to(inverse_a, (slot_rows, 128)),
+                    (before[STORED_TURNED], before[STORED_GATES], matrices(before[0], 1)),
+                )
+            (grad_projected, grad_normed_a, grad_out_w, *own_grad_down), further = unproject(
                 grad_queries,
                 grad_pairs.reshape(
                     SEQUENCE_SLOTS, heads_count, blocks_count // 2, 2, resident, pair_columns
@@ -1927,8 +2640,10 @@
                 tile_cosine,
                 tile_sine,
                 [array for _, array in swapped],
-                shared_terms,
-            )
+                shared_terms if layer_index else [],
+                onward,
+            )
+            waiting = [] if layer_index else shared_terms
             grad_projected = grad_projected.reshape(all_tokens, -1)
         else:
             grad_pairs = (
@@ -1960,6 +2675,13 @@
             )
             grad_normed_a = head_sum(grad_normed_a)
         grad_out_w = jnp.sum(grad_out_w.astype(jnp.float32), axis=0)
+        if fused and layer_index:
+            grad_hidden, grad_gain_a, *further = further
+            grad_gain_a = grad_gain_a[0]
+            turned = unpack_in(further)
+        else:
+            grad_norm_a, grad_gain_a = norm_back(grad_normed_a, scaled_a, inverse_a, gains[:1])
+            grad_hidden = grad_middle + grad_norm_a
         grad_qkv = (
             mm("td,te->de", plane_normed_a, grad_projected)
             .astype(jnp.bfloat16)
@@ -1971,25 +2693,45 @@
                 grad_qkv.reshape(width, -1), "blk", scatter_dimension=0, tiled=True
             )
             pending.append(grad_qkv)
+            qkv_list[layer_index] = grad_qkv
+            gains_list[layer_index] = jnp.stack([grad_gain_a, grad_gain_b])
         else:
-            (grad_qkv,) = exchange(("blk_swap", grad_qkv))
+            gains_list[0] = jnp.stack([grad_gain_a, grad_gain_b])
+            grad_gains = (
+                jnp.stack(gains_list)
+                .reshape(2 * DECODER_LAYERS, heads_count, blocks_count, weight_rows)
+                .transpose(1, 2, 0, 3)
+                .reshape(heads_count, -1)
+            )
+            grad_qkv, grad_gains = exchange(
+                ("blk_swap", grad_qkv),
+                ("head_swap", grad_gains[:, None]),
+                after=waiting,
+            )
             grad_qkv = jnp.sum(grad_qkv.astype(jnp.float32), axis=0).astype(jnp.bfloat16)
-        grad_norm_a, grad_gain_a = norm_back(grad_normed_a, scaled_a, inverse_a, gains[:1])
-        grad_hidden = grad_middle + grad_norm_a
+            grad_gains = jnp.sum(grad_gains, axis=0).reshape(blocks_count, 1, -1)
+            qkv_list[0] = grad_qkv
+            *qkv_list, grad_gains = exchange(
+                *(
+                    ("head_swap", term.reshape(heads_count, weight_rows, -1))
+                    for term in qkv_list
+                ),
+                ("blk_swap", grad_gains),
+            )
+            qkv_list = [
+                jnp.concatenate(
+                    [
+                        term[..., :query_columns].transpose(1, 0, 2).reshape(weight_rows, -1),
+                        term[..., query_columns:].transpose(1, 0, 2).reshape(weight_rows, -1),
+                    ],
+                    axis=1,
+                ).astype(jnp.float32)
+                for term in qkv_list
+            ]
+            grad_gains = jnp.sum(grad_gains, axis=0).reshape(DECODER_LAYERS, 2, weight_rows)
 
         out_list[layer_index] = grad_out_w[:, :width]
         router_list[layer_index] = grad_out_w[:, width : width + EXPERTS]
-        grad_qkv = lax.all_to_all(
-            grad_qkv.reshape(heads_count, weight_rows, -1), "head", 0, 0, tiled=True
-        ).transpose(1, 0, 2)
-        qkv_list[layer_index] = jnp.concatenate(
-            [
-                grad_qkv[..., :query_columns].reshape(weight_rows, -1),
-                grad_qkv[..., query_columns:].reshape(weight_rows, -1),
-            ],
-            axis=1,
-        ).astype(jnp.float32)
-        gains_list[layer_index] = jnp.stack([grad_gain_a, grad_gain_b])
         terms = []
         for number, received in enumerate((own_grad_in, own_grad_down)):
             parts = owned_rows(received[0]) if owned else []
@@ -1997,12 +2739,6 @@
                 parts.append(shared_terms[number])
             terms.append(jnp.concatenate(parts, axis=0).astype(jnp.float32))
         expert_list[layer_index] = tuple(terms)
-    devices = heads_count * blocks_count
-    grad_gains = jnp.stack(gains_list).reshape(2 * DECODER_LAYERS, devices, weight_rows)
-    grad_gains = lax.all_to_all(
-        grad_gains.transpose(1, 0, 2).reshape(devices, -1), ("head", "blk"), 0, 0, tiled=True
-    )
-    grad_gains = jnp.sum(grad_gains, axis=0).reshape(DECODER_LAYERS, 2, weight_rows)
     return (
         result,
         grad_hidden.reshape(tokens.shape),

time: 1220 us -> 1140 us (0.934)
  matrix products: 85.9 us -> 37.7 us
  other arithmetic: 79 us -> 49.9 us
  Pallas kernels: 940 us -> 968 us
  starting transfers between devices: 19.3 us -> 0.83 us
    pallas_call x4 -> x7, Pallas kernels: 195 us -> 511 us  [the longest x2 179 us: enter(): pl.pallas_call(functools.partial(enter_kernel, heads, blocks, layer, len(...]
    pallas_call x7 -> x3, Pallas kernels: 446 us -> 228 us  [staged_call(): pl.pallas_call(kernel, out_shape=[out for plan in plans for out in plan[4...]
    pallas_call x7 -> x6, Pallas kernels: 245 us -> 182 us  [exchange(): pl.pallas_call(functools.partial(exchange_kernel, heads, blocks, plan, le...]
    dot_general x28 -> x18, matrix products: 85.9 us -> 37.7 us  [mm(): return jnp.einsum(spec, left, right, preferred_element_type=jnp.float32)]
    all_to_all x3 -> x0, starting transfers between devices: 18.7 us -> none  [the longest x2 9.42 us: shards(): lax.all_to_all(grad_qkv.reshape(heads_count, weight_rows, -1), 'head', 0,...]
    concatenate x6 -> x2, other arithmetic: 14.9 us -> 1.66 us  [gated_back(): jnp.concatenate([grad_units * up_part * sigmoid_part * (1.0 + gate_part *...]
  transfers between devices with their start and end apart: 14 -> 11, of which waited for: 1 -> 0; matrix products, arithmetic and copies ran while one was open for 16% -> 9% of each run, Pallas kernels for 51% -> 61%
where the time goes in v5:
time: 1140 us; the launch traced here: 1130 us
  Pallas kernels  968 us (85%)
  local copies, waits for them, and re-layouts  58.8 us (5%)
  other arithmetic  49.9 us (4%)
  matrix products  37.7 us (3%)
  between operations  15.2 us (1%)
    pallas_call x3, Pallas kernels, staged_call(): pl.pallas_call(kernel, out_shape=[out for plan in plans for out in plan[4...  228 us
    pallas_call x6, Pallas kernels, exchange(): pl.pallas_call(functools.partial(exchange_kernel, heads, blocks, plan, le...  182 us
    pallas_call x2, Pallas kernels, enter(): pl.pallas_call(functools.partial(enter_kernel, heads, blocks, layer, len(...  179 us
    pallas_call x2, Pallas kernels, unproject(): pl.pallas_call(kernel, out_shape=[*outs, *more_outs], in_specs=[vmem] * 5...  158 us
    pallas_call x1, Pallas kernels, cross(): pl.pallas_call(kernel, out_shape=[*outs, *norm_outs, *more_outs], in_spec...  113 us
    pallas_call x1, Pallas kernels, project(): pl.pallas_call(functools.partial(project_kernel, heads, blocks, PROJECT_P...  56.2 us
    pallas_call x4, Pallas kernels, attention_call(): pl.pallas_call(kernel, grid_spec=pltpu.PrefetchScalarGridSpec(num_scalar_...  47.3 us
    dot_general x18, matrix products, mm(): return jnp.einsum(spec, left, right, preferred_element_type=jnp.float32)  37.7 us
  transfers between devices with their start and end apart: 11, of which 0 were waited for; matrix products, arithmetic and copies ran while one was open for 9% of the time, Pallas kernels for 61%

profile of v5, /device:TPU:0, one launch (start us, length us, event | category | flops | bytes accessed | tf_op | source)
XLA Modules:
  0.0 1132.8 jit_solution(1922541505283961437)
XLA Ops:
  12.4 2.6 slice_bitcast_fusion.4
  15.8 13.2 %exchange.6 = (s32[4,32,128]{2,1,0:T(8,128)}, bf16[4,48,768]{2,1,0:T(8,128)(2,1)}) custom-call(s32[32,128]{1,0:T(8,128)} %bitcast.338, bf16[4,48,768]{2,1,0:T(8,128)(2,1)} %pad_maximum_fusion.5.refs_1_), custom_call_target="tpu_custom_call" | custom-call | bytes 115343360 | tf_op jit(solution)/shard_map/exchange/pallas_call | solution.py:215
  29.7 26.2 %exchange.7 = (bf16[8,4,48,768]{3,2,1,0:T(8,128)(2,1)}, bf16[8,48,1536]{2,1,0:T(8,128)(2,1)}, bf16[4,48,768]{2,1,0:T(8,128)(2,1)}) custom-call(bf16[4,48,768]{2,1,0:T(8,128)(2,1)} %get-tuple-element.93.refs_0_, bf16[48,1536]{1,0:T(8,128)(2,1)} %get-tuple-element.241.refs_1_, bf16[4,48,768]{2,1,0:T(8,128)(2,1)} %pad_maximum_fusion.6.refs_2_), custom_call_target="tpu_custom_call" | custom-call | bytes 115343360 | tf_op jit(solution)/shard_map/exchange/pallas_call | solution.py:215
  65.7 5.1 plans.1
  75.4 56.2 %project.1 = (bf16[4,128,1536]{2,1,0:T(8,128)(2,1)}, bf16[2,256,384]{2,1,0:T(8,128)(2,1)}, bf16[2,4,8,64,256]{4,3,2,1,0:T(8,128)(2,1)}, bf16[8,64,1536]{2,1,0:T(8,128)(2,1)}) custom-call(bf16[128,1536]{1,0:T(8,128)(2,1)} %multiply_convert_fusion.3.own_ref, bf16[1536,640]{1,0:T(8,128)(2,1)} %slice.259.weight_ref.refs_2_, ...), custom_call_target="tpu_custom_call" | custom-call | bytes 136314880 | tf_op jit(solution)/shard_map/project/pallas_call | solution.py:1051
  132.2 8.5 attend.2
  143.2 94.8 %enter.2 = (f32[128,1536]{1,0:T(8,128)}, f32[128,1536]{1,0:T(8,128)}, f32[128,128]{1,0:T(8,128)}, bf16[4,128,1536]{2,1,0:T(8,128)(2,1)}, bf16[8,112,1536]{2,1,0:...) custom-call(bf16[512,384]{1,0:T(8,128)(2,1)} %bitcast.300, ...), custom_call_target="tpu_custom_call" | custom-call | bytes 283115520 | tf_op jit(solution)/shard_map/enter/pallas_call | solution.py:777
  240.7 3.2 slice_bitcast_fusion
  258.4 113.1 %cross.1 = (f32[128,1536]{1,0:T(8,128)}, bf16[10,112,1536]{2,1,0:T(8,128)(2,1)}, f32[128,1536]{1,0:T(8,128)}, f32[128,1536]{1,0:T(8,128)}, f32[128,128]{1,0:T(8,...) custom-call(bf16[896,512]{1,0:T(8,128)(2,1)} %fusion.4.refs_0_.refs_, ...), custom_call_target="tpu_custom_call" | custom-call | bytes 304087040 | tf_op jit(solution)/shard_map/cross/pallas_call | solution.py:1121
  371.5 8.5 attend.3
  380.1 84.6 %enter.3 = (f32[128,1536]{1,0:T(8,128)}, f32[128,1536]{1,0:T(8,128)}, f32[128,128]{1,0:T(8,128)}, bf16[4,128,1536]{2,1,0:T(8,128)(2,1)}, bf16[8,112,1536]{2,1,0:...) custom-call(bf16[512,384]{1,0:T(8,128)(2,1)} %bitcast.302, ...), custom_call_target="tpu_custom_call" | custom-call | bytes 283115520 | tf_op jit(solution)/shard_map/enter/pallas_call | solution.py:777
  471.2 86.8 %turn.1 = (f32[128,1536]{1,0:T(8,128)}, bf16[10,112,1536]{2,1,0:T(8,128)(2,1)}, bf16[4,128,1536]{2,1,0:T(8,128)(2,1)}, bf16[8,112,1536]{2,1,0:T(8,128)(2,1)}, bf...) custom-call(bf16[896,512]{1,0:T(8,128)(2,1)} %fusion.5.refs_0_.refs_7_, ...), custom_call_target="tpu_custom_call" | custom-call | bytes 272629760 | tf_op jit(solution)/shard_map/turn/pallas_call | solution.py:526
  558.0 3.8 convolution_convert_fusion.3.refs_3_
  564.3 4.5 convolution_convert_fusion.1.refs_2_
  571.7 75.8 %combine_back.2 = (f32[128,1536]{1,0:T(8,128)}, bf16[10,112,1536]{2,1,0:T(8,128)(2,1)}, bf16[1536,1024]{1,0:T(8,128)(2,1)}, bf16[512,1536]{1,0:T(8,128)(2,1)}, f32[4,16,512]{2,1,0:T(8,128)}) custom-call(f32[896,1024]{1,0:T(8,128)} %get-tuple-element.115.refs_0_, bf16[2,112,1024]{2,1,0:T(8,128)(2,1)} %pad_maximum_fusion.3.refs_1_, ...), custom_call_target="tpu_custom_call" | custom-call | bytes 178257920 | tf_op jit(solution)/shard_map/combine_back/pallas_call | solution.py:526
  653.5 53.8 %exchange.8 = (bf16[4,128,1536]{2,1,0:T(8,128)(2,1)}, bf16[8,1,192,1024]{3,2,1,0:T(8,128)(2,1)}) custom-call(bf16[128,1536]{1,0:T(8,128)(2,1)} %get-tuple-element.223.refs_0_, bf16[8,1,192,1024]{3,2,1,0:T(8,128)(2,1)} %bitcast.281, bf16[2,1536,1024]{2,1,0:T(8,128)(2,1)} %convolution_convert_fusion.1.refs_2_, ...), custom_call_target="tpu_custom_call" | custom-call | bytes 115343360 | tf_op jit(solution)/shard_map/exchange/pallas_call | solution.py:215
  710.5 15.0 %attend_back.2 = (bf16[2,256,384]{2,1,0:T(8,128)(2,1)}, bf16[2,2048,256]{2,1,0:T(8,128)(2,1)}) custom-call(s32[3]{0:T(128)} %pad_add_fusion.1.info_ref, bf16[2,256,384]{2,1,0:T(8,128)(2,1)} %get-tuple-element.110.query_ref, bf16[2,2048,256]{2,1,0:T(8,128)(2,1)} %bitcast.347, bf16[2,256,384]{2,1,0:T(8,128)(2,1)} %bitcast.323), custom_call_target="tpu_custom_call" | custom-call | flops 2013265920 | bytes 8388608 | tf_op jit(solution)/shard_map/attend_back/pallas_call | solution.py:2043
  728.2 106.0 %unproject.2 = (bf16[4,128,640]{2,1,0:T(8,128)(2,1)}, f32[128,1536]{1,0:T(8,128)}, bf16[8,48,1664]{2,1,0:T(8,128)(2,1)}, bf16[8,1,64,1536]{3,2,1,0:T(8,128)(2,1)...) custom-call(bf16[2,256,384]{2,1,0:T(8,128)(2,1)} %get-tuple-element., ...), custom_call_target="tpu_custom_call" | custom-call | bytes 335544320 | tf_op jit(solution)/shard_map/unproject/pallas_call | solution.py:1466
  834.2 2.5 bitcast_convert_fusion.1
  839.4 2.7 convolution_convert_fusion.2.refs_4_
  843.7 4.5 convolution_convert_fusion.refs_3_
  851.7 65.1 %combine_back.3 = (f32[128,1536]{1,0:T(8,128)}, bf16[10,112,1536]{2,1,0:T(8,128)(2,1)}, bf16[1536,1024]{1,0:T(8,128)(2,1)}, bf16[512,1536]{1,0:T(8,128)(2,1)}, f32[4,16,512]{2,1,0:T(8,128)}) custom-call(f32[896,1024]{1,0:T(8,128)} %get-tuple-element.101.refs_0_, bf16[2,112,1024]{2,1,0:T(8,128)(2,1)} %pad_maximum_fusion.4.refs_1_, ...), custom_call_target="tpu_custom_call" | custom-call | bytes 178257920 | tf_op jit(solution)/shard_map/combine_back/pallas_call | solution.py:526
  924.6 2.8 multiply_convert_fusion
  927.4 42.9 %exchange.9 = (bf16[4,128,1536]{2,1,0:T(8,128)(2,1)}, bf16[8,1,192,1024]{3,2,1,0:T(8,128)(2,1)}) custom-call(bf16[128,1536]{1,0:T(8,128)(2,1)} %get-tuple-element.221.refs_0_, bf16[8,1,192,1024]{3,2,1,0:T(8,128)(2,1)} %bitcast.280, bf16[192,640]{1,0:T(8,128)(2,1)} %reduce-scatter.10.cloned.1.call-done.refs_2_, ...), custom_call_target="tpu_custom_call" | custom-call | bytes 115343360 | tf_op jit(solution)/shard_map/exchange/pallas_call | solution.py:215
  973.5 15.2 %attend_back.3 = (bf16[2,256,384]{2,1,0:T(8,128)(2,1)}, bf16[2,2048,256]{2,1,0:T(8,128)(2,1)}) custom-call(s32[3]{0:T(128)} %pad_add_fusion.1.info_ref, bf16[2,256,384]{2,1,0:T(8,128)(2,1)} %get-tuple-element.95.query_ref, bf16[2,2048,256]{2,1,0:T(8,128)(2,1)} %bitcast.345, bf16[2,256,384]{2,1,0:T(8,128)(2,1)} %bitcast.322), custom_call_target="tpu_custom_call" | custom-call | flops 2013265920 | bytes 8388608 | tf_op jit(solution)/shard_map/attend_back/pallas_call | solution.py:2043
  990.6 51.6 %unproject.3 = (bf16[4,128,640]{2,1,0:T(8,128)(2,1)}, f32[128,1536]{1,0:T(8,128)}, bf16[8,48,1664]{2,1,0:T(8,128)(2,1)}, bf16[8,1,64,1536]{3,2,1,0:T(8,128)(2,1)}) custom-call(bf16[2,256,384]{2,1,0:T(8,128)(2,1)} %get-tuple-element.159.refs_0_, bf16[2,4,4,2,64,256]{5,4,3,2,1,0:T(8,128)(2,1)} %bitcast.291, bf16[1536,640]{1,0:T(8,128)(2,1)} %slice.259.weight_ref.refs_2_, ...), custom_call_target="tpu_custom_call" | custom-call | bytes 157286400 | tf_op jit(solution)/shard_map/unproject/pallas_call | solution.py:1466
  1042.2 2.5 bitcast_convert_fusion
  1057.2 4.9 maximum_convert_fusion.1
  1062.2 28.3 %exchange.10 = (bf16[8,4,48,640]{3,2,1,0:T(8,128)(2,1)}, f32[4,1,1536]{2,1,0:T(1,128)}) custom-call(bf16[8,4,48,640]{3,2,1,0:T(8,128)(2,1)} %bitcast.271, f32[4,1,1536]{2,1,0:T(1,128)} %broadcast_in_dim_reshape.3.refs_1_, bf16[2,192,1024]{2,1,0:T(8,128)(2,1)} %reduce-scatter.12.cloned.1.call-done.refs_2_, ...), custom_call_target="tpu_custom_call" | custom-call | bytes 115343360 | tf_op jit(solution)/shard_map/exchange/pallas_call | solution.py:215
  1090.5 2.6 reduce_sum.178.refs_0_
  1093.7 17.2 %exchange.11 = (bf16[4,48,640]{2,1,0:T(8,128)(2,1)}, bf16[4,48,640]{2,1,0:T(8,128)(2,1)}, f32[8,1,192]{2,1,0:T(1,128)}) custom-call(bf16[4,48,640]{2,1,0:T(8,128)(2,1)} %reduce_sum.178.refs_0_, bf16[4,48,640]{2,1,0:T(8,128)(2,1)} %bitcast.310, f32[8,1,192]{2,1,0:T(1,128)} %reshape.617.refs_2_), custom_call_target="tpu_custom_call" | custom-call | bytes 115343360 | tf_op jit(solution)/shard_map/exchange/pallas_call | solution.py:215
  1117.7 8.4 maximum_convert_fusion
  (298 shorter events, 104.7 us)
Async XLA Ops:
  7.2 135.9 %all-gather.8.cloned.1.call-start = ((), (), s32[]{:S(2)}) async-start(), calls=%async_computation.5 | async-start | bytes 7077888 | tf_op jit(solution)/shard_map/all_gather | solution.py:2144
  56.0 188.0 %all-gather.18.cloned.1.call-start = ((), (), s32[]{:S(2)}) async-start(), calls=%async_computation.15 | async-start | bytes 2654208 | tf_op jit(solution)/shard_map/all_gather | solution.py:2347
  56.7 201.7 %all-gather.10.cloned.1.call-start = ((), (), s32[]{:S(2)}) async-start(), calls=%async_computation.6 | async-start | bytes 3538944 | tf_op jit(solution)/shard_map/all_gather | solution.py:2144
  57.5 322.6 %all-gather.12.cloned.1.call-start = ((), (), s32[]{:S(2)}) async-start(), calls=%async_computation.7 | async-start | bytes 1327104 | tf_op jit(solution)/shard_map/all_gather | solution.py:2348
  58.0 322.0 %all-gather.14.cloned.1.call-start = ((), (), s32[]{:S(2)}) async-start(), calls=%async_computation.8 | async-start | bytes 7077888 | tf_op jit(solution)/shard_map/all_gather | solution.py:2144
  63.1 11.4 %copy-start.47 = (f32[128]{0:T(128)}, f32[128]{0:T(128)S(1)}, u32[]{:S(2)}) copy-start(f32[128]{0:T(128)S(1)} %rsqrt.12) | copy-start | bytes 1540
  238.0 233.2 %all-gather.16.cloned.1.call-start = ((), (), s32[]{:S(2)}) async-start(), calls=%async_computation.9 | async-start | bytes 3538944 | tf_op jit(solution)/shard_map/all_gather | solution.py:2144
  238.6 489.0 %reduce-scatter.8.cloned.1.call-start = ((), (), s32[]{:S(2)}) async-start(), calls=%async_computation.11 | async-start | bytes 3538944 | tf_op jit(solution)/shard_map/reduce_scatter | solution.py:2596
  238.7 413.4 %copy-start.49 = (f32[128]{0:T(128)}, f32[128]{0:T(128)S(1)}, u32[]{:S(2)}) copy-start(f32[128]{0:T(128)S(1)} %reshape.619) | copy-start | bytes 1540
  238.8 14.4 %copy-start.25 = (pred[2,512,40]{2,1,0:T(32,128)(4,1)}, pred[2,512,40]{2,1,0:T(32,128)(4,1)S(1)}, u32[]{:S(2)}) copy-start(pred[2,512,40]{2,1,0:T(32,128)(4,1)S(1)} %slice_compare_fusion) | copy-start | bytes 122884
  251.0 5.1 copy-start.6
  380.0 84.6 %copy-start.26 = (pred[2,512,40]{2,1,0:T(32,128)(4,1)S(1)}, pred[2,512,40]{2,1,0:T(32,128)(4,1)}, u32[]{:S(2)}) copy-start(pred[2,512,40]{2,1,0:T(32,128)(4,1)} %copy-done.25) | copy-start | bytes 122884
  464.7 4.2 copy-start.8
  471.2 86.8 %copy-start.15 = (bf16[2,112,512]{2,1,0:T(8,128)(2,1)S(1)}, bf16[2,112,512]{2,1,0:T(8,128)(2,1)}, u32[]{:S(2)}) copy-start(bf16[2,112,512]{2,1,0:T(8,128)(2,1)} %multiply_convert_fusion.8.refs_1_) | copy-start | bytes 688132
  561.8 165.7 %reduce-scatter.6.cloned.1.call-start = ((), (), s32[]{:S(2)}) async-start(), calls=%async_computation.10 | async-start | bytes 7077888 | tf_op jit(solution)/shard_map/reduce_scatter | solution.py:2596
  568.8 358.5 %reduce-scatter.10.cloned.1.call-start = ((), (), s32[]{:S(2)}) async-start(), calls=%async_computation.12 | async-start | bytes 2211840 | tf_op jit(solution)/shard_map/reduce_scatter | solution.py:2692
  653.5 53.8 %copy-start.24 = (bf16[8,48,1536]{2,1,0:T(8,128)(2,1)S(1)}, bf16[8,48,1536]{2,1,0:T(8,128)(2,1)}, u32[]{:S(2)}) copy-start(bf16[8,48,1536]{2,1,0:T(8,128)(2,1)} %all-gather.12.cloned.1.call-done) | copy-start | bytes 3538948
  710.5 15.0 %copy-start.34 = (bf16[384,512]{1,0:T(8,128)(2,1)S(1)}, bf16[384,512]{1,0:T(8,128)(2,1)}, u32[]{:S(2)}) copy-start(bf16[384,512]{1,0:T(8,128)(2,1)} %copy.156) | copy-start | bytes 1179652
  710.5 15.1 %copy-start.57 = (bf16[4,128,1536]{2,1,0:T(8,128)(2,1)S(1)}, bf16[4,128,1536]{2,1,0:T(8,128)(2,1)}, u32[]{:S(2)}) copy-start(bf16[4,128,1536]{2,1,0:T(8,128)(2,1)} %get-tuple-element.135) | copy-start | bytes 4718596
  728.2 106.0 %copy-start.55 = (bf16[4,128,1536]{2,1,0:T(8,128)(2,1)S(1)}, bf16[4,128,1536]{2,1,0:T(8,128)(2,1)}, u32[]{:S(2)}) copy-start(bf16[4,128,1536]{2,1,0:T(8,128)(2,1)} %get-tuple-element.154) | copy-start | bytes 4718596
  838.2 219.0 %reduce-scatter.14.cloned.1.call-start = ((), (), s32[]{:S(2)}) async-start(), calls=%async_computation.14 | async-start | bytes 3538944 | tf_op jit(solution)/shard_map/reduce_scatter | solution.py:2596
  842.2 220.0 %reduce-scatter.12.cloned.1.call-start = ((), (), s32[]{:S(2)}) async-start(), calls=%async_computation.13 | async-start | bytes 7077888 | tf_op jit(solution)/shard_map/reduce_scatter | solution.py:2596
  918.3 5.0 copy-start.46
  919.8 4.8 copy-start.50
  919.8 4.8 copy-start.51
  927.4 42.9 %copy-start.23 = (bf16[8,48,1536]{2,1,0:T(8,128)(2,1)S(1)}, bf16[8,48,1536]{2,1,0:T(8,128)(2,1)}, u32[]{:S(2)}) copy-start(bf16[8,48,1536]{2,1,0:T(8,128)(2,1)} %get-tuple-element.97) | copy-start | bytes 3538948
  973.5 15.2 %copy-start.33 = (bf16[384,512]{1,0:T(8,128)(2,1)S(1)}, bf16[384,512]{1,0:T(8,128)(2,1)}, u32[]{:S(2)}) copy-start(bf16[384,512]{1,0:T(8,128)(2,1)} %copy.164) | copy-start | bytes 1179652
  973.5 15.2 %copy-start.56 = (bf16[4,128,1536]{2,1,0:T(8,128)(2,1)S(1)}, bf16[4,128,1536]{2,1,0:T(8,128)(2,1)}, u32[]{:S(2)}) copy-start(bf16[4,128,1536]{2,1,0:T(8,128)(2,1)} %get-tuple-element.158) | copy-start | bytes 4718596
  990.6 51.6 %copy-start.54 = (bf16[4,128,1536]{2,1,0:T(8,128)(2,1)S(1)}, bf16[4,128,1536]{2,1,0:T(8,128)(2,1)}, u32[]{:S(2)}) copy-start(bf16[4,128,1536]{2,1,0:T(8,128)(2,1)} %get-tuple-element.163) | copy-start | bytes 4718596
  1044.8 7.1 copy-start.21
  1112.8 4.9 copy-start.10
  1112.8 4.9 copy-start.11
  (37 other events, 68.0 us)
Sparse Core Ops, SparseCore 0:
  56.1 69.2 all-gather.7
  127.3 43.4 all-gather.17
  172.7 48.0 all-gather.9
  222.5 26.7 all-gather.11
  251.1 67.3 all-gather.13
  320.2 49.8 all-gather.15
  561.9 67.6 reduce-scatter.7
  633.9 91.8 reduce-scatter.5
  838.4 43.3 reduce-scatter.9
  886.0 46.4 reduce-scatter.13
  936.4 66.9 reduce-scatter.11

commit v6 on v5

--- a/solution.py
+++ b/solution.py
@@ -945,7 +945,7 @@
         slot, inside = place(piece)
         projected = jnp.dot(
             plane_ref[:, part, :].reshape(heads * count, width),
-            weight_ref[...],
+            weight_ref[:, : query_columns + pair_columns],
             preferred_element_type=jnp.float32,
         )
         cosine = cosine_ref[:, part, :].reshape(heads * count, tile)
@@ -1011,7 +1011,7 @@
 PROJECT_PIECES = 4
 
 
-def project_plan(count, width, weight, moved, layer, pair_columns, resident):
+def project_plan(count, width, moved, layer, query_columns, pair_columns, resident):
     heads, blocks = lax.axis_size("head"), lax.axis_size("blk")
     pieces = PROJECT_PIECES
     slots = count // resident
@@ -1022,7 +1022,7 @@
         [
             jax.ShapeDtypeStruct((heads, count, width), jnp.bfloat16),
             jax.ShapeDtypeStruct(
-                (slots, heads * resident, weight.shape[1] - pair_columns), jnp.bfloat16
+                (slots, heads * resident, query_columns), jnp.bfloat16
             ),
             jax.ShapeDtypeStruct((slots, heads, blocks, resident, pair_columns), jnp.bfloat16),
             *(jax.ShapeDtypeStruct((blocks,) + array.shape[2:], array.dtype) for array in moves),
@@ -1040,10 +1040,10 @@
     )
 
 
-def project(rows, weight, cosine, sine, moved, layer, pair_columns, resident):
+def project(rows, weight, cosine, sine, moved, layer, query_columns, pair_columns, resident):
     heads, blocks = lax.axis_size("head"), lax.axis_size("blk")
     outs, out_specs, scratch = project_plan(
-        *rows.shape, weight, moved, layer, pair_columns, resident
+        *rows.shape, moved, layer, query_columns, pair_columns, resident
     )
     moves = [] if layer is None else [moved]
     vmem = pl.BlockSpec(memory_space=pltpu.VMEM)
@@ -1064,12 +1064,12 @@
     )(rows, weight, cosine, sine, *moves)
 
 
-def cross(plan, middle, valid, gain, weight, cosine, sine, moved, layer, pair_columns, resident):
+def cross(plan, middle, valid, gain, weight, cosine, sine, moved, layer, *sizes):
     heads, blocks = lax.axis_size("head"), lax.axis_size("blk")
     key, maker, arrays, specs, outs, out_specs, scratch, scaled_rows = plan
     count, width = middle.shape
     more_outs, more_specs, more_scratch = project_plan(
-        count, width, weight, moved, layer, pair_columns, resident
+        count, width, moved, layer, *sizes
     )
     inputs, results, temps = len(arrays), len(outs), len(scratch)
     vmem = pl.BlockSpec(memory_space=pltpu.VMEM)
@@ -1277,7 +1277,8 @@
             axis=1,
         ).astype(grad_ref.dtype)
         grad_ref[:, part, :] = turned.reshape(heads, count, query_columns + pair_columns)
-        product_ref[...] = dot_last(turned, weight_ref[...]).reshape(heads, count, width)
+        weight = weight_ref[:, : query_columns + pair_columns]
+        product_ref[...] = dot_last(turned, weight).reshape(heads, count, width)
         sent = []
         for number, peer in enumerate(head_peers):
             part_ref[peer[0], part, :] = product_ref[peer[0]].astype(part_ref.dtype)
@@ -1373,20 +1374,22 @@
 UNPROJECT_PIECES = 4
 
 
-def unproject_plan(grad_pairs, weight, moved):
+def unproject_plan(grad_queries, grad_pairs, weight, moved):
     heads, blocks = lax.axis_size("head"), lax.axis_size("blk")
     chips = blocks // 2
     pieces = UNPROJECT_PIECES
     slots, _, _, _, resident, pair_columns = grad_pairs.shape
     rows = slots * resident
     count = rows // pieces
-    width, columns = weight.shape
+    width = weight.shape[0]
     items = len(moved)
     vmem = pl.BlockSpec(memory_space=pltpu.VMEM)
     anywhere = pl.BlockSpec(memory_space=pl.ANY)
     return (
         [
-            jax.ShapeDtypeStruct((heads, rows, columns), jnp.bfloat16),
+            jax.ShapeDtypeStruct(
+                (heads, rows, grad_queries.shape[2] + pair_columns), jnp.bfloat16
+            ),
             jax.ShapeDtypeStruct((rows, width), jnp.float32),
             *(jax.ShapeDtypeStruct(array.shape, array.dtype) for array in moved),
         ],
@@ -1414,7 +1417,7 @@
 
 def unproject(grad_queries, grad_pairs, weight, cosine, sine, moved, after, onward=None):
     heads, blocks = lax.axis_size("head"), lax.axis_size("blk")
-    outs, out_specs, scratch = unproject_plan(grad_pairs, weight, moved)
+    outs, out_specs, scratch = unproject_plan(grad_queries, grad_pairs, weight, moved)
     results, temps = len(outs), len(scratch)
     items = len(moved)
     vmem = pl.BlockSpec(memory_space=pltpu.VMEM)
@@ -1813,6 +1816,106 @@
     )
 
 
+def depart(plan, other, valid, gain, scaled, inverse, gates, router, after):
+    heads, blocks = lax.axis_size("head"), lax.axis_size("blk")
+    key, maker, arrays, specs, outs, out_specs, scratch, _ = plan
+    count, width = other.shape
+    matrix = outs[2]
+    matrix_rows = matrix.shape[0] // blocks
+    inputs, results, temps = len(arrays), len(outs), len(scratch)
+    vmem = pl.BlockSpec(memory_space=pltpu.VMEM)
+    anywhere = pl.BlockSpec(memory_space=pl.ANY)
+    more_outs = [
+        jax.ShapeDtypeStruct((count, width), jnp.float32),
+        jax.ShapeDtypeStruct((1, width), jnp.float32),
+        jax.ShapeDtypeStruct((heads, count, width), jnp.bfloat16),
+        jax.ShapeDtypeStruct((blocks, matrix_rows, matrix.shape[1]), matrix.dtype),
+    ]
+
+    def kernel(*refs):
+        head, blk, head_peers, blk_peers = plane_peers(heads, blocks)
+        greet(head_peers + blk_peers)
+        given, refs = list(refs[:inputs]), refs[inputs:]
+        other_ref, valid_ref, gain_ref, scaled_ref, inverse_ref, gates_ref, *refs = refs
+        router_ref, *refs = refs
+        refs = refs[len(after) :]
+        made, refs = refs[:results], refs[results:]
+        total_ref, _, matrix_ref, _, came_gates_ref = made
+        middle_ref, grad_gain_ref, plane_ref, moved_ref, *refs = refs
+        temp, refs = refs[:temps], refs[temps:]
+        own_ref, row_send, row_recv, moved_send, moved_recv, moved_sem = refs
+        given.insert(3, None)
+        moved = []
+        for number, stage in enumerate(maker([*given, *made, *temp])):
+            stage()
+            if number == COMBINE_PIECES + 1:
+                moved = [
+                    started(
+                        remote(
+                            matrix_ref.at[
+                                pl.ds(pl.multiple_of(peer[1] * matrix_rows, 16), matrix_rows)
+                            ],
+                            moved_ref.at[blk],
+                            (moved_send, moved_recv),
+                            index,
+                            peer,
+                        )
+                    )
+                    for index, peer in enumerate(blk_peers)
+                ]
+                place = pl.ds(pl.multiple_of(blk * matrix_rows, 16), matrix_rows)
+                moved.append(
+                    started(
+                        pltpu.make_async_copy(matrix_ref.at[place], moved_ref.at[blk], moved_sem)
+                    )
+                )
+        mine = pl.ds(pl.multiple_of(head * count, 128), count)
+        grad_gates = came_gates_ref[:, :, mine].reshape(-1, count).T
+        shares = gates_ref[...]
+        grad_logits = shares * (
+            grad_gates - jnp.sum(shares * grad_gates, axis=1, keepdims=True)
+        )
+        grad = total_ref[...] + dot_last(grad_logits.astype(jnp.bfloat16), router_ref[...])
+        scaled = scaled_ref[...]
+        grad_gain_ref[...] = jnp.sum(grad * scaled, axis=0, keepdims=True)
+        grad = grad * gain_ref[...]
+        grad = inverse_ref[:, :1] * (
+            grad - scaled * jnp.mean(grad * scaled, axis=1, keepdims=True)
+        )
+        middle = other_ref[...] + grad
+        middle_ref[...] = middle
+        own = (valid_ref[...] * middle).astype(own_ref.dtype)
+        own_ref[...] = own
+        plane_ref[head] = own
+        relayed_gather(heads, head, blk, head_peers, own_ref, plane_ref, (row_send, row_recv), 0)
+        for copy in moved:
+            copy.wait()
+
+    values = pl.pallas_call(
+        kernel,
+        out_shape=[*outs, *more_outs],
+        in_specs=[*specs, *([vmem] * 7), *([anywhere] * len(after))],
+        out_specs=[*out_specs, *([vmem] * 3), anywhere],
+        scratch_shapes=[
+            *scratch,
+            pltpu.VMEM((count, width), jnp.bfloat16),
+            pltpu.SemaphoreType.DMA((RELAY_PIECES * heads,)),
+            pltpu.SemaphoreType.DMA((RELAY_PIECES * heads,)),
+            pltpu.SemaphoreType.DMA((blocks,)),
+            pltpu.SemaphoreType.DMA((blocks,)),
+            pltpu.SemaphoreType.DMA,
+        ],
+        compiler_params=pltpu.CompilerParams(
+            collective_id=kernel_number("depart", key, *(array.shape for array in after)),
+            has_side_effects=True,
+            vmem_limit_bytes=60 * 1024 * 1024,
+        ),
+        cost_estimate=pl.CostEstimate(flops=0, bytes_accessed=330 << 20, transcendentals=0),
+        name="depart",
+    )(*arrays, other, valid, gain, scaled, inverse, gates, router, *after)
+    return values[:results], values[results:]
+
+
 def head_parts(partial):
     heads = lax.axis_size("head")
     return partial.astype(jnp.bfloat16).reshape(heads, -1, partial.shape[-1])
@@ -1954,11 +2057,15 @@
     count = place_ref.shape[2]
     first = info_ref[0] * experts_local
     lanes = 128
-    named = [
-        jnp.max(jnp.where(routes == expert, 1, 0), axis=0, keepdims=True)
-        for expert in range(EXPERTS)
-    ]
-    named.append(jnp.zeros((lanes - EXPERTS, tokens), jnp.int32))
+    room = -(-experts_local // 8) * 8
+    named = []
+    for lane in range(lanes):
+        plane, expert = lane // room, lane % room
+        if plane < heads and expert < experts_local:
+            hit = jnp.where(routes == plane * experts_local + expert, 1, 0)
+            named.append(jnp.max(hit, axis=0, keepdims=True))
+        else:
+            named.append(jnp.zeros((1, tokens), jnp.int32))
     chosen_ref[0] = jnp.concatenate(named, axis=0).astype(jnp.float32).T
     marks = [
         jnp.sum(
@@ -2028,7 +2135,8 @@
         cost_estimate=pl.CostEstimate(flops=0, bytes_accessed=16 << 20, transcendentals=0),
         name="plans",
     )(head_index[None].astype(jnp.int32), routes, ranks)
-    return chosen[:, :, :EXPERTS] > 0.0, places, turned
+    gate_lanes = heads * -(-experts_local // 8) * 8
+    return chosen[0, :, :gate_lanes] > 0.0, places[0], turned[0]
 
 
 def attention_call(kernel, info, arrays, outs, scratch, flops, name):
@@ -2216,7 +2324,9 @@
         (parts,) = exchange(("head_swap", head_parts(mm("tr,rd->td", places, rows))))
         return (head_sum(parts), returned)
 
-    def moe_back(places, sets, gate_up, grad_units, incoming, units, grad_rows, plane_grads, came):
+    def moe_back(
+        places, sets, gate_up, grad_units, incoming, units, grad_rows, plane_grads, came, onward
+    ):
         grad_gate_up = [
             gated_back(*parts) if number or not staged else None
             for number, parts in enumerate(zip(gate_up, grad_units))
@@ -2240,9 +2350,16 @@
                 True,
                 [grad_units[0][0], incoming[0][0], units[0][0], grad_rows[0][0], plane_grads, came],
             )
-            total, _, grad_in, grad_down, gates = staged_call([plan], "combine_back", 170)[0]
+            further = []
+            if fused:
+                (total, _, grad_in, grad_down, gates), further = depart(
+                    plan, *onward, grad_weights[1]
+                )
+            else:
+                total, _, grad_in, grad_down, gates = staged_call([plan], "combine_back", 170)[0]
             grad_weights[0] = (grad_in[None], grad_down[None])
-            return (total, gates[:, :experts_local].reshape(EXPERTS, all_tokens), grad_weights)
+            gates = gates.reshape(gate_lanes, all_tokens)
+            return (total, gates, grad_weights, further)
         pair_dots = (mm("td,rd->tr", plane_grads, came) * places).astype(jnp.bfloat16)
         made = [
             mm("erf,edf->erd", part, mats[0]).astype(jnp.bfloat16)
@@ -2253,7 +2370,8 @@
             ("head_swap", head_parts(mm("tr,rd->td", places, returned))),
             ("head_gather", mm("tr,er->te", pair_dots, spread).T),
         )
-        return (head_sum(parts), gates.reshape(EXPERTS, all_tokens), grad_weights)
+        gates = by_plane(gates.reshape(EXPERTS, all_tokens), 0)
+        return (head_sum(parts), gates, grad_weights, [])
 
     def moe_turn(units, places, turned_places, scale, grad_rows, sets):
         if not staged:
@@ -2297,11 +2415,23 @@
         )
 
     small_columns = 128
+    room = -(-experts_local // 8) * 8
+    gate_lanes = heads_count * room
+
+    def by_plane(values, axis):
+        shape = values.shape
+        values = values.reshape(shape[:axis] + (heads_count, experts_local) + shape[axis + 1 :])
+        pads = [(0, 0)] * values.ndim
+        pads[axis + 1] = (0, room - experts_local)
+        return jnp.pad(values, pads).reshape(shape[:axis] + (gate_lanes,) + shape[axis + 1 :])
+
     send = []
     for layer_index in range(DECODER_LAYERS):
         weight = query_key_value_weight[layer_index]
         split = QUERY_HEAD_COUNT * HEAD_SIZE
-        small = jnp.concatenate([router[layer_index], norm_gains[layer_index].T], axis=1)
+        small = jnp.concatenate(
+            [by_plane(router[layer_index], 1), norm_gains[layer_index].T], axis=1
+        )
         small = jnp.pad(small, ((0, 0), (0, small_columns - small.shape[1])))
         send.append(
             jnp.concatenate(
@@ -2322,16 +2452,12 @@
     plan, first_send = exchange(("head_gather", plan), ("head_swap", send[0]))
     plan = plan.reshape(heads_count, 2, DECODER_LAYERS, TOP, slot_rows)
     plan = plan.transpose(1, 2, 3, 0, 4).reshape(2, DECODER_LAYERS, TOP, all_tokens)
-    chosen_all, places_all, turned_all = plans(
-        heads_count, experts_local, slot, head_index, plan[0], plan[1]
-    )
 
     def attention_set(wide, out_full):
         wide = wide.transpose(1, 0, 2, 3).reshape(width, -1)
-        columns = query_columns + pair_columns
-        small = wide[:, columns:]
-        gains = small.T[EXPERTS : EXPERTS + 2].astype(jnp.float32)
-        return (wide[:, :columns], out_full.reshape(-1, width), small[:, :EXPERTS], gains)
+        small = wide[:, query_columns + pair_columns :]
+        gains = small.T[gate_lanes : gate_lanes + 2].astype(jnp.float32)
+        return (wide, out_full.reshape(-1, width), small[:, :gate_lanes], gains)
 
     wide, first_out, *next_sends = exchange(
         ("blk_pairs", first_send),
@@ -2353,8 +2479,9 @@
     stored_all = []
     for layer_index in range(DECODER_LAYERS):
         qkv_full, out_full, router_full, gains = attention_weights[layer_index]
-        chosen, places, turned_places = (
-            part[layer_index] for part in (chosen_all, places_all, turned_all)
+        layer = slice(layer_index, layer_index + 1)
+        chosen, places, turned_places = plans(
+            heads_count, experts_local, slot, head_index, plan[0, layer], plan[1, layer]
         )
         next_layer = layer_index + 1 < DECODER_LAYERS
         fused = staged and heads_count == 4
@@ -2372,6 +2499,7 @@
                 tile_sine,
                 w_down,
                 layer_index,
+                query_columns,
                 pair_columns,
                 resident,
             )
@@ -2382,7 +2510,8 @@
                 ("head_gather", normed_a), *to_owner(w_down, layer_index)
             )
             plane_normed_a = plane_normed_a.reshape(all_tokens, width)
-            projected = mm("td,de->te", plane_normed_a, qkv_full)
+            narrow = qkv_full[:, : query_columns + pair_columns]
+            projected = mm("td,de->te", plane_normed_a, narrow)
             queries = by_slot(
                 rotate(projected[:, :query_columns], cosine, sine).astype(jnp.bfloat16)
             )
@@ -2452,7 +2581,7 @@
         lifted = jnp.where(chosen, jnp.exp(logits - peaks), 0.0)
         gates_all = lifted / jnp.sum(lifted, axis=-1, keepdims=True)
         plane_gates = lax.dynamic_slice_in_dim(
-            gates_all, head_index * experts_local, experts_local, 1
+            gates_all, head_index * room, experts_local, 1
         )
         row_gates = mm("rt,te->re", turned_places, plane_gates.astype(jnp.bfloat16))
         row_gates = jnp.sum(row_gates * spread.T.astype(jnp.float32), axis=1, keepdims=True)
@@ -2470,6 +2599,7 @@
                 tile_sine,
                 w_down,
                 layer_index + 1,
+                query_columns,
                 pair_columns,
                 resident,
             )
@@ -2553,7 +2683,16 @@
                 waiting,
             )
         plane_grads, grad_produced, grad_units = turned
-        grad_normed_b, grad_gates, grad_weight_sets = moe_back(
+        onward = (
+            grad_hidden,
+            valid_column,
+            gains[1:],
+            scaled_b,
+            jnp.broadcast_to(inverse_b, (slot_rows, 128)),
+            lax.dynamic_slice_in_dim(gates_all, head_index * slot_rows, slot_rows, 0),
+            router_full,
+        )
+        grad_normed_b, grad_gates, grad_weight_sets, departed = moe_back(
             places,
             weight_sets,
             gate_up,
@@ -2563,6 +2702,7 @@
             grad_produced,
             plane_grads,
             returned,
+            onward,
         )
         grad_gates = grad_gates.T
         grad_logits = gates_all * (
@@ -2574,21 +2714,26 @@
             lax.dynamic_slice_in_dim(plane_rows, head_index * plane_width, plane_width, 1),
             grad_logits.astype(jnp.bfloat16),
         )
-        own_logits = lax.dynamic_slice_in_dim(grad_logits, head_index * slot_rows, slot_rows, 0)
-        grad_normed_b = grad_normed_b + mm(
-            "te,de->td", own_logits.astype(jnp.bfloat16), router_full
-        )
-        grad_norm_b, grad_gain_b = norm_back(grad_normed_b, scaled_b, inverse_b, gains[1:])
-        grad_middle = grad_hidden + grad_norm_b
-        plane_branch, *own_grad_in = exchange(
-            ("head_gather", (valid_column * grad_middle).astype(jnp.bfloat16)),
-            *(from_owner(grad_weight_sets[0][0]) if owned else []),
-            after=[
-                *pending,
-                *(waiting if fused else ()),
-                *(grad_weight_sets[-1] if owned_total < experts_local else ()),
-            ],
-        )
+        if fused:
+            grad_middle, grad_gain_b, plane_branch, *own_grad_in = departed
+            grad_gain_b = grad_gain_b[0]
+            reached_terms = pending
+        else:
+            own_logits = lax.dynamic_slice_in_dim(
+                grad_logits, head_index * slot_rows, slot_rows, 0
+            )
+            grad_normed_b = grad_normed_b + mm(
+                "te,de->td", own_logits.astype(jnp.bfloat16), router_full
+            )
+            grad_norm_b, grad_gain_b = norm_back(grad_normed_b, scaled_b, inverse_b, gains[1:])
+            grad_middle = grad_hidden + grad_norm_b
+            plane_branch, *own_grad_in = exchange(
+                ("head_gather", (valid_column * grad_middle).astype(jnp.bfloat16)),
+                *(from_owner(grad_weight_sets[0][0]) if owned else []),
+                after=pending,
+            )
+            reached_terms = []
+        plane_branch = plane_branch.reshape(all_tokens, width)
         pending = []
         shared_terms = []
         if owned_total < experts_local:
@@ -2614,9 +2759,15 @@
             "attend_back",
         )
         grad_out_w = jnp.concatenate(
-            [grad_out_w, jnp.pad(grad_router, ((0, 0), (0, small_columns - EXPERTS)))], axis=1
+            [grad_out_w, jnp.pad(grad_router, ((0, 0), (0, small_columns - gate_lanes)))], axis=1
         ).astype(jnp.bfloat16)
-        swapped = [("blk_swap", grad_out_w.reshape(blocks_count, weight_rows, -1))]
+        alone = fused and layer_index > 0
+        if alone:
+            grad_out_w = lax.psum_scatter(grad_out_w, "blk", scatter_dimension=0, tiled=True)
+            pending.append(grad_out_w)
+            swapped = []
+        else:
+            swapped = [("blk_swap", grad_out_w.reshape(blocks_count, weight_rows, -1))]
         if owned:
             swapped += from_owner(grad_weight_sets[0][1])
         if fused:
@@ -2631,7 +2782,7 @@
                     jnp.broadcast_to(inverse_a, (slot_rows, 128)),
                     (before[STORED_TURNED], before[STORED_GATES], matrices(before[0], 1)),
                 )
-            (grad_projected, grad_normed_a, grad_out_w, *own_grad_down), further = unproject(
+            (grad_projected, grad_normed_a, *others), further = unproject(
                 grad_queries,
                 grad_pairs.reshape(
                     SEQUENCE_SLOTS, heads_count, blocks_count // 2, 2, resident, pair_columns
@@ -2640,11 +2791,14 @@
                 tile_cosine,
                 tile_sine,
                 [array for _, array in swapped],
-                shared_terms if layer_index else [],
+                [*reached_terms, *(shared_terms if layer_index else [])],
                 onward,
             )
             waiting = [] if layer_index else shared_terms
             grad_projected = grad_projected.reshape(all_tokens, -1)
+            if not alone:
+                grad_out_w, *others = others
+            own_grad_down = others
         else:
             grad_pairs = (
                 grad_pairs.reshape(
@@ -2669,12 +2823,23 @@
                 axis=-1,
             ).astype(jnp.bfloat16)
             grad_normed_a, grad_out_w, *own_grad_down = exchange(
-                ("head_swap", head_parts(mm("te,de->td", grad_projected, qkv_full))),
+                (
+                    "head_swap",
+                    head_parts(
+                        mm(
+                            "te,de->td",
+                            grad_projected,
+                            qkv_full[:, : query_columns + pair_columns],
+                        )
+                    ),
+                ),
                 *swapped,
                 after=shared_terms,
             )
             grad_normed_a = head_sum(grad_normed_a)
-        grad_out_w = jnp.sum(grad_out_w.astype(jnp.float32), axis=0)
+        grad_out_w = grad_out_w.astype(jnp.float32)
+        if not alone:
+            grad_out_w = jnp.sum(grad_out_w, axis=0)
         if fused and layer_index:
             grad_hidden, grad_gain_a, *further = further
             grad_gain_a = grad_gain_a[0]
@@ -2703,21 +2868,22 @@
                 .transpose(1, 2, 0, 3)
                 .reshape(heads_count, -1)
             )
-            grad_qkv, grad_gains = exchange(
+            grad_qkv, grad_gains, *qkv_done = exchange(
                 ("blk_swap", grad_qkv),
                 ("head_swap", grad_gains[:, None]),
+                *(
+                    ("head_swap", term.reshape(heads_count, weight_rows, -1))
+                    for term in qkv_list[1:]
+                ),
                 after=waiting,
             )
             grad_qkv = jnp.sum(grad_qkv.astype(jnp.float32), axis=0).astype(jnp.bfloat16)
             grad_gains = jnp.sum(grad_gains, axis=0).reshape(blocks_count, 1, -1)
-            qkv_list[0] = grad_qkv
-            *qkv_list, grad_gains = exchange(
-                *(
-                    ("head_swap", term.reshape(heads_count, weight_rows, -1))
-                    for term in qkv_list
-                ),
+            grad_qkv, grad_gains = exchange(
+                ("head_swap", grad_qkv.reshape(heads_count, weight_rows, -1)),
                 ("blk_swap", grad_gains),
             )
+            qkv_list = [grad_qkv, *qkv_done]
             qkv_list = [
                 jnp.concatenate(
                     [
@@ -2731,7 +2897,11 @@
             grad_gains = jnp.sum(grad_gains, axis=0).reshape(DECODER_LAYERS, 2, weight_rows)
 
         out_list[layer_index] = grad_out_w[:, :width]
-        router_list[layer_index] = grad_out_w[:, width : width + EXPERTS]
+        router_list[layer_index] = (
+            grad_out_w[:, width : width + gate_lanes]
+            .reshape(weight_rows, heads_count, room)[:, :, :experts_local]
+            .reshape(weight_rows, EXPERTS)
+        )
         terms = []
         for number, received in enumerate((own_grad_in, own_grad_down)):
             parts = owned_rows(received[0]) if owned else []

time: 1140 us -> 1100 us (0.965)
  Pallas kernels: 968 us -> 939 us
    pallas_call x0 -> x2, Pallas kernels: none -> 216 us  [depart(): pl.pallas_call(kernel, out_shape=[*outs, *more_outs], in_specs=[*specs, *...]
    pallas_call x3 -> x1, Pallas kernels: 228 us -> 87.8 us  [staged_call(): pl.pallas_call(kernel, out_shape=[out for plan in plans for out in plan[4...]
    pallas_call x6 -> x4, Pallas kernels: 182 us -> 77.4 us  [exchange(): pl.pallas_call(functools.partial(exchange_kernel, heads, blocks, plan, le...]
    dot_general x18 -> x16, matrix products: 37.7 us -> 36.6 us  [mm(): return jnp.einsum(spec, left, right, preferred_element_type=jnp.float32)]
  transfers between devices with their start and end apart: 11 -> 12, of which waited for: 0 -> 0; matrix products, arithmetic and copies ran while one was open for 9% -> 8% of each run, Pallas kernels for 61% -> 71%
where the time goes in v6:
time: 1100 us; the launch traced here: 1090 us
  Pallas kernels  939 us (85%)
  local copies, waits for them, and re-layouts  49 us (4%)
  other arithmetic  43.6 us (4%)
  matrix products  36.6 us (3%)
  between operations  15.6 us (1%)
    pallas_call x2, Pallas kernels, depart(): pl.pallas_call(kernel, out_shape=[*outs, *more_outs], in_specs=[*specs, *...  216 us
    pallas_call x2, Pallas kernels, enter(): pl.pallas_call(functools.partial(enter_kernel, heads, blocks, layer, len(...  183 us
    pallas_call x2, Pallas kernels, unproject(): pl.pallas_call(kernel, out_shape=[*outs, *more_outs], in_specs=[vmem] * 5...  160 us
    pallas_call x1, Pallas kernels, cross(): pl.pallas_call(kernel, out_shape=[*outs, *norm_outs, *more_outs], in_spec...  107 us
    pallas_call x1, Pallas kernels, staged_call(): pl.pallas_call(kernel, out_shape=[out for plan in plans for out in plan[4...  87.8 us
    pallas_call x4, Pallas kernels, exchange(): pl.pallas_call(functools.partial(exchange_kernel, heads, blocks, plan, le...  77.4 us
    pallas_call x4, Pallas kernels, attention_call(): pl.pallas_call(kernel, grid_spec=pltpu.PrefetchScalarGridSpec(num_scalar_...  53.4 us
    pallas_call x1, Pallas kernels, project(): pl.pallas_call(functools.partial(project_kernel, heads, blocks, PROJECT_P...  49.6 us
  transfers between devices with their start and end apart: 12, of which 0 were waited for; matrix products, arithmetic and copies ran while one was open for 8% of the time, Pallas kernels for 71%

profile of v6, /device:TPU:0, one launch (start us, length us, event | category | flops | bytes accessed | tf_op | source)
XLA Modules:
  0.0 1087.9 jit_solution(18131576856792463424)
XLA Ops:
  10.4 2.6 slice_bitcast_fusion
  15.8 13.2 %exchange.4 = (s32[4,32,128]{2,1,0:T(8,128)}, bf16[4,48,768]{2,1,0:T(8,128)(2,1)}) custom-call(s32[32,128]{1,0:T(8,128)} %bitcast.338, bf16[4,48,768]{2,1,0:T(8,128)(2,1)} %pad_maximum_fusion.4.refs_1_), custom_call_target="tpu_custom_call" | custom-call | bytes 115343360 | tf_op jit(solution)/shard_map/exchange/pallas_call | solution.py:215
  29.8 26.2 %exchange.5 = (bf16[8,4,48,768]{3,2,1,0:T(8,128)(2,1)}, bf16[8,48,1536]{2,1,0:T(8,128)(2,1)}, bf16[4,48,768]{2,1,0:T(8,128)(2,1)}) custom-call(bf16[4,48,768]{2,1,0:T(8,128)(2,1)} %get-tuple-element.95.refs_0_, bf16[48,1536]{1,0:T(8,128)(2,1)} %get-tuple-element.202.refs_1_, bf16[4,48,768]{2,1,0:T(8,128)(2,1)} %pad_maximum_fusion.5.refs_2_), custom_call_target="tpu_custom_call" | custom-call | bytes 115343360 | tf_op jit(solution)/shard_map/exchange/pallas_call | solution.py:215
  66.6 49.6 %project.1 = (bf16[4,128,1536]{2,1,0:T(8,128)(2,1)}, bf16[2,256,384]{2,1,0:T(8,128)(2,1)}, bf16[2,4,8,64,256]{4,3,2,1,0:T(8,128)(2,1)}, bf16[8,64,1536]{2,1,0:T(8,128)(2,1)}) custom-call(bf16[128,1536]{1,0:T(8,128)(2,1)} %multiply_convert_fusion.1.own_ref, bf16[1536,768]{1,0:T(8,128)(2,1)} %bitcast.261, ...), custom_call_target="tpu_custom_call" | custom-call | bytes 136314880 | tf_op jit(solution)/shard_map/project/pallas_call | solution.py:1051
  116.2 2.4 plans.2
  121.4 9.7 attend.2
  132.1 99.4 %enter.2 = (f32[128,1536]{1,0:T(8,128)}, f32[128,1536]{1,0:T(8,128)}, f32[128,128]{1,0:T(8,128)}, bf16[4,128,1536]{2,1,0:T(8,128)(2,1)}, bf16[8,112,1536]{2,1,0:...) custom-call(bf16[512,384]{1,0:T(8,128)(2,1)} %bitcast.305, ...), custom_call_target="tpu_custom_call" | custom-call | bytes 283115520 | tf_op jit(solution)/shard_map/enter/pallas_call | solution.py:777
  232.2 2.4 plans.3
  250.7 106.6 %cross.1 = (f32[128,1536]{1,0:T(8,128)}, bf16[10,112,1536]{2,1,0:T(8,128)(2,1)}, f32[128,1536]{1,0:T(8,128)}, f32[128,1536]{1,0:T(8,128)}, f32[128,128]{1,0:T(8,...) custom-call(bf16[896,512]{1,0:T(8,128)(2,1)} %fusion.6.refs_0_.refs_, ...), custom_call_target="tpu_custom_call" | custom-call | bytes 304087040 | tf_op jit(solution)/shard_map/cross/pallas_call | solution.py:1121
  357.3 9.6 attend.3
  366.9 83.8 %enter.3 = (f32[128,1536]{1,0:T(8,128)}, f32[128,1536]{1,0:T(8,128)}, f32[128,128]{1,0:T(8,128)}, bf16[4,128,1536]{2,1,0:T(8,128)(2,1)}, bf16[8,112,1536]{2,1,0:...) custom-call(bf16[512,384]{1,0:T(8,128)(2,1)} %bitcast.330, ...), custom_call_target="tpu_custom_call" | custom-call | bytes 283115520 | tf_op jit(solution)/shard_map/enter/pallas_call | solution.py:777
  457.5 87.8 %turn.1 = (f32[128,1536]{1,0:T(8,128)}, bf16[10,112,1536]{2,1,0:T(8,128)(2,1)}, bf16[4,128,1536]{2,1,0:T(8,128)(2,1)}, bf16[8,112,1536]{2,1,0:T(8,128)(2,1)}, bf...) custom-call(bf16[896,512]{1,0:T(8,128)(2,1)} %fusion.7.refs_0_.refs_7_, ...), custom_call_target="tpu_custom_call" | custom-call | bytes 272629760 | tf_op jit(solution)/shard_map/turn/pallas_call | solution.py:526
  545.4 3.8 convolution_convert_fusion.3.refs_19_
  550.5 4.5 convolution_convert_fusion.1.refs_18_
  559.7 111.2 %depart.2 = (f32[128,1536]{1,0:T(8,128)}, bf16[10,112,1536]{2,1,0:T(8,128)(2,1)}, bf16[1536,1024]{1,0:T(8,128)(2,1)}, bf16[512,1536]{1,0:T(8,128)(2,1)}, f32[4,1...) custom-call(f32[896,1024]{1,0:T(8,128)} %get-tuple-element.118.refs_, ...), custom_call_target="tpu_custom_call" | custom-call | bytes 346030080 | tf_op jit(solution)/shard_map/depart/pallas_call | solution.py:1894
  677.6 2.4 convolution_convert_fusion.7
  680.9 16.9 %attend_back.2 = (bf16[2,256,384]{2,1,0:T(8,128)(2,1)}, bf16[2,2048,256]{2,1,0:T(8,128)(2,1)}) custom-call(s32[3]{0:T(128)} %pad_add_fusion.1.info_ref, bf16[2,256,384]{2,1,0:T(8,128)(2,1)} %get-tuple-element.112.query_ref, bf16[2,2048,256]{2,1,0:T(8,128)(2,1)} %bitcast.349, bf16[2,256,384]{2,1,0:T(8,128)(2,1)} %bitcast.322), custom_call_target="tpu_custom_call" | custom-call | flops 2013265920 | bytes 8388608 | tf_op jit(solution)/shard_map/attend_back/pallas_call | solution.py:2151
  698.5 94.9 %unproject.2 = (bf16[4,128,640]{2,1,0:T(8,128)(2,1)}, f32[128,1536]{1,0:T(8,128)}, bf16[8,1,64,1536]{3,2,1,0:T(8,128)(2,1)}, f32[128,1536]{1,0:T(8,128)}, f32[1,...) custom-call(bf16[2,256,384]{2,1,0:T(8,128)(2,1)} %get-tuple-element., ...), custom_call_target="tpu_custom_call" | custom-call | bytes 335544320 | tf_op jit(solution)/shard_map/unproject/pallas_call | solution.py:1469
  793.5 2.5 bitcast_convert_fusion.1
  798.7 2.7 convolution_convert_fusion.2.refs_19_
  803.0 4.5 convolution_convert_fusion.refs_18_
  816.5 105.2 %depart.3 = (f32[128,1536]{1,0:T(8,128)}, bf16[10,112,1536]{2,1,0:T(8,128)(2,1)}, bf16[1536,1024]{1,0:T(8,128)(2,1)}, bf16[512,1536]{1,0:T(8,128)(2,1)}, f32[4,1...) custom-call(f32[896,1024]{1,0:T(8,128)} %get-tuple-element.103.refs_, ...), custom_call_target="tpu_custom_call" | custom-call | bytes 346030080 | tf_op jit(solution)/shard_map/depart/pallas_call | solution.py:1894
  921.8 2.5 convolution_convert_fusion.6
  926.9 17.1 %attend_back.3 = (bf16[2,256,384]{2,1,0:T(8,128)(2,1)}, bf16[2,2048,256]{2,1,0:T(8,128)(2,1)}) custom-call(s32[3]{0:T(128)} %pad_add_fusion.1.info_ref, bf16[2,256,384]{2,1,0:T(8,128)(2,1)} %get-tuple-element.97.query_ref, bf16[2,2048,256]{2,1,0:T(8,128)(2,1)} %bitcast.347, bf16[2,256,384]{2,1,0:T(8,128)(2,1)} %bitcast.321), custom_call_target="tpu_custom_call" | custom-call | flops 2013265920 | bytes 8388608 | tf_op jit(solution)/shard_map/attend_back/pallas_call | solution.py:2151
  946.0 64.8 %unproject.3 = (bf16[4,128,640]{2,1,0:T(8,128)(2,1)}, f32[128,1536]{1,0:T(8,128)}, bf16[8,48,1664]{2,1,0:T(8,128)(2,1)}, bf16[8,1,64,1536]{3,2,1,0:T(8,128)(2,1)}) custom-call(bf16[2,256,384]{2,1,0:T(8,128)(2,1)} %get-tuple-element.158.refs_0_, bf16[2,4,4,2,64,256]{5,4,3,2,1,0:T(8,128)(2,1)} %bitcast.294, bf16[1536,768]{1,0:T(8,128)(2,1)} %bitcast.264, ...), custom_call_target="tpu_custom_call" | custom-call | bytes 157286400 | tf_op jit(solution)/shard_map/unproject/pallas_call | solution.py:1469
  1010.8 2.5 bitcast_convert_fusion
  1018.0 2.3 multiply_add_fusion
  1020.3 4.8 maximum_convert_fusion.1
  1025.0 26.4 %exchange.6 = (bf16[8,4,48,640]{3,2,1,0:T(8,128)(2,1)}, f32[4,1,1536]{2,1,0:T(1,128)}, bf16[4,48,640]{2,1,0:T(8,128)(2,1)}) custom-call(bf16[8,4,48,640]{3,2,1,0:T(8,128)(2,1)} %bitcast.273, f32[4,1,1536]{2,1,0:T(1,128)} %broadcast_in_dim_reshape.3.refs_1_, bf16[4,48,640]{2,1,0:T(8,128)(2,1)} %bitcast.312, ...), custom_call_target="tpu_custom_call" | custom-call | bytes 115343360 | tf_op jit(solution)/shard_map/exchange/pallas_call | solution.py:215
  1053.3 2.6 reduce_sum.129.refs_0_
  1056.6 11.6 %exchange.7 = (bf16[4,48,640]{2,1,0:T(8,128)(2,1)}, f32[8,1,192]{2,1,0:T(1,128)}) custom-call(bf16[4,48,640]{2,1,0:T(8,128)(2,1)} %reduce_sum.129.refs_0_, f32[8,1,192]{2,1,0:T(1,128)} %reshape.617.refs_1_), custom_call_target="tpu_custom_call" | custom-call | bytes 115343360 | tf_op jit(solution)/shard_map/exchange/pallas_call | solution.py:215
  1072.4 8.4 maximum_convert_fusion
  (287 shorter events, 87.2 us)
Async XLA Ops:
  7.2 124.9 %all-gather.8.cloned.1.call-start = ((), (), s32[]{:S(2)}) async-start(), calls=%async_computation.6 | async-start | bytes 7077888 | tf_op jit(solution)/shard_map/all_gather | solution.py:2252
  56.0 181.9 %all-gather.18.cloned.1.call-start = ((), (), s32[]{:S(2)}) async-start(), calls=%async_computation.17 | async-start | bytes 2654208 | tf_op jit(solution)/shard_map/all_gather | solution.py:2473
  56.8 193.9 %all-gather.10.cloned.1.call-start = ((), (), s32[]{:S(2)}) async-start(), calls=%async_computation.7 | async-start | bytes 3538944 | tf_op jit(solution)/shard_map/all_gather | solution.py:2252
  57.5 309.4 %all-gather.12.cloned.1.call-start = ((), (), s32[]{:S(2)}) async-start(), calls=%async_computation.8 | async-start | bytes 1327104 | tf_op jit(solution)/shard_map/all_gather | solution.py:2474
  58.1 308.8 %all-gather.14.cloned.1.call-start = ((), (), s32[]{:S(2)}) async-start(), calls=%async_computation.9 | async-start | bytes 7077888 | tf_op jit(solution)/shard_map/all_gather | solution.py:2252
  132.1 104.6 %copy-start.32 = (bf16[2,64,1536]{2,1,0:T(8,128)(2,1)S(1)}, bf16[2,64,1536]{2,1,0:T(8,128)(2,1)}, u32[]{:S(2)}) copy-start(bf16[2,64,1536]{2,1,0:T(8,128)(2,1)} %param.21) | copy-start | bytes 1179652
  231.5 226.0 %all-gather.16.cloned.1.call-start = ((), (), s32[]{:S(2)}) async-start(), calls=%async_computation.10 | async-start | bytes 3538944 | tf_op jit(solution)/shard_map/all_gather | solution.py:2252
  232.1 465.7 %reduce-scatter.9.cloned.1.call-start = ((), (), s32[]{:S(2)}) async-start(), calls=%async_computation.12 | async-start | bytes 3538944 | tf_op jit(solution)/shard_map/reduce_scatter | solution.py:2741
  239.8 6.4 copy-start.7
  244.0 4.4 copy-start.11
  450.7 4.4 copy-start.13
  457.5 87.8 %copy-start.18 = (bf16[2,112,512]{2,1,0:T(8,128)(2,1)S(1)}, bf16[2,112,512]{2,1,0:T(8,128)(2,1)}, u32[]{:S(2)}) copy-start(bf16[2,112,512]{2,1,0:T(8,128)(2,1)} %multiply_convert_fusion.6.refs_1_) | copy-start | bytes 688132
  549.2 148.6 %reduce-scatter.7.cloned.1.call-start = ((), (), s32[]{:S(2)}) async-start(), calls=%async_computation.11 | async-start | bytes 7077888 | tf_op jit(solution)/shard_map/reduce_scatter | solution.py:2741
  555.1 258.2 %reduce-scatter.11.cloned.1.call-start = ((), (), s32[]{:S(2)}) async-start(), calls=%async_computation.13 | async-start | bytes 1437696 | tf_op jit(solution)/shard_map/reduce_scatter | solution.py:2766
  677.0 269.0 %reduce-scatter.13.cloned.1.call-start = ((), (), s32[]{:S(2)}) async-start(), calls=%async_computation.14 | async-start | bytes 2211840 | tf_op jit(solution)/shard_map/reduce_scatter | solution.py:2857
  698.5 94.9 %copy-start.51 = (bf16[4,128,1536]{2,1,0:T(8,128)(2,1)S(1)}, bf16[4,128,1536]{2,1,0:T(8,128)(2,1)}, u32[]{:S(2)}) copy-start(bf16[4,128,1536]{2,1,0:T(8,128)(2,1)} %get-tuple-element.163) | copy-start | bytes 4718596
  797.5 222.8 %reduce-scatter.17.cloned.1.call-start = ((), (), s32[]{:S(2)}) async-start(), calls=%async_computation.16 | async-start | bytes 3538944 | tf_op jit(solution)/shard_map/reduce_scatter | solution.py:2741
  801.4 223.6 %reduce-scatter.15.cloned.1.call-start = ((), (), s32[]{:S(2)}) async-start(), calls=%async_computation.15 | async-start | bytes 7077888 | tf_op jit(solution)/shard_map/reduce_scatter | solution.py:2741
  807.5 3.5 copy-start.36
  807.5 3.6 copy-start.25
  816.5 105.2 %copy-start.23 = (bf16[8,48,1536]{2,1,0:T(8,128)(2,1)S(1)}, bf16[8,48,1536]{2,1,0:T(8,128)(2,1)}, u32[]{:S(2)}) copy-start(bf16[8,48,1536]{2,1,0:T(8,128)(2,1)} %get-tuple-element.99) | copy-start | bytes 3538948
  921.8 3.3 copy-start.35
  926.8 17.2 %copy-start.45 = (f32[1,1536]{1,0:T(1,128)S(1)}, f32[1,1536]{1,0:T(1,128)}, u32[]{:S(2)}) copy-start(f32[1,1536]{1,0:T(1,128)} %get-tuple-element.170) | copy-start | bytes 18436
  926.8 17.2 %copy-start.46 = (f32[1,1536]{1,0:T(1,128)S(1)}, f32[1,1536]{1,0:T(1,128)}, u32[]{:S(2)}) copy-start(f32[1,1536]{1,0:T(1,128)} %get-tuple-element.169) | copy-start | bytes 18436
  926.8 17.2 %copy-start.31 = (bf16[384,512]{1,0:T(8,128)(2,1)S(1)}, bf16[384,512]{1,0:T(8,128)(2,1)}, u32[]{:S(2)}) copy-start(bf16[384,512]{1,0:T(8,128)(2,1)} %copy.218) | copy-start | bytes 1179652
  926.9 17.2 %copy-start.52 = (bf16[4,128,1536]{2,1,0:T(8,128)(2,1)S(1)}, bf16[4,128,1536]{2,1,0:T(8,128)(2,1)}, u32[]{:S(2)}) copy-start(bf16[4,128,1536]{2,1,0:T(8,128)(2,1)} %get-tuple-element.157) | copy-start | bytes 4718596
  946.0 64.8 %copy-start.50 = (bf16[4,128,1536]{2,1,0:T(8,128)(2,1)S(1)}, bf16[4,128,1536]{2,1,0:T(8,128)(2,1)}, u32[]{:S(2)}) copy-start(bf16[4,128,1536]{2,1,0:T(8,128)(2,1)} %get-tuple-element.166) | copy-start | bytes 4718596
  1017.1 3.2 copy-start.19
  1017.1 3.2 copy-start.20
  1051.5 4.4 copy-start.40
  1069.1 3.3 copy-start.14
  1069.1 3.3 copy-start.15
  (33 other events, 60.2 us)
Sparse Core Ops, SparseCore 0:
  56.1 65.3 all-gather.7
  123.4 48.9 all-gather.17
  174.4 51.0 all-gather.9
  227.2 25.1 all-gather.11
  254.7 76.6 all-gather.13
  333.2 35.1 all-gather.15
  549.3 62.7 reduce-scatter.8
  616.5 73.0 reduce-scatter.6
  692.9 47.5 reduce-scatter.10
  797.6 47.9 reduce-scatter.12
  849.6 72.8 reduce-scatter.16
  926.6 95.2 reduce-scatter.14

commit v7 on v6

--- a/solution.py
+++ b/solution.py
@@ -274,7 +274,7 @@
 
 STORED_TURNED, STORED_GATES = 12, 13
 DISPATCH_PIECES, DISPATCH_WINDOW, DISPATCH_LAG = 6, 3, 2
-COMBINE_PIECES = 6
+COMBINE_PIECES = 4
 
 
 def dispatch_stages(heads, blocks, by_columns, refs):
@@ -1875,7 +1875,9 @@
         grad_logits = shares * (
             grad_gates - jnp.sum(shares * grad_gates, axis=1, keepdims=True)
         )
-        grad = total_ref[...] + dot_last(grad_logits.astype(jnp.bfloat16), router_ref[...])
+        grad = total_ref[...] + jnp.dot(
+            grad_logits.astype(jnp.bfloat16), router_ref[...], preferred_element_type=jnp.float32
+        )
         scaled = scaled_ref[...]
         grad_gain_ref[...] = jnp.sum(grad * scaled, axis=0, keepdims=True)
         grad = grad * gain_ref[...]
@@ -1914,6 +1916,171 @@
         name="depart",
     )(*arrays, other, valid, gain, scaled, inverse, gates, router, *after)
     return values[:results], values[results:]
+
+
+def settle(summed, swapped, gains, after):
+    heads, blocks = lax.axis_size("head"), lax.axis_size("blk")
+    chips = blocks // 2
+    arrays = [array.reshape((chips, 2) + array.shape[1:]) for array in summed]
+    halves = [(chips,) + array.shape[2:] for array in arrays]
+    count = len(arrays)
+    vmem = pl.BlockSpec(memory_space=pltpu.VMEM)
+    anywhere = pl.BlockSpec(memory_space=pl.ANY)
+    outs = [
+        jax.ShapeDtypeStruct(halves[0][1:], jnp.bfloat16),
+        *(jax.ShapeDtypeStruct(half[1:], jnp.float32) for half in halves[1:]),
+        *(jax.ShapeDtypeStruct(array.shape, array.dtype) for array in swapped),
+        jax.ShapeDtypeStruct(gains.shape[1:], jnp.float32),
+    ]
+    out_specs = [vmem] * count + [anywhere] * len(swapped) + [vmem]
+
+    def kernel(*refs):
+        head, blk, head_peers, blk_peers = plane_peers(heads, blocks)
+        chip, core = blk // 2, lax.rem(blk, 2)
+        sibling = (head, chip * 2 + 1 - core)
+        chip_peers = [(head, lax.rem(chip + step, chips) * 2 + core) for step in range(1, chips)]
+        greet(head_peers + blk_peers)
+        sources, refs = refs[:count], refs[count:]
+        swap_refs, refs = refs[: len(swapped)], refs[len(swapped) :]
+        gains_ref, refs = refs[0], refs[1 + len(after) :]
+        made, refs = refs[:count], refs[count:]
+        swap_outs, refs = refs[: len(swapped)], refs[len(swapped) :]
+        gains_out, refs = refs[0], refs[1:]
+        near, refs = refs[:count], refs[count:]
+        sums, refs = refs[:count], refs[count:]
+        far, refs = refs[:count], refs[count:]
+        total_ref, gains_near, gains_sum, *sems = refs
+        near_sems, chip_sems, head_sems, gain_sems, row_sems = zip(sems[0:5], sems[5:10])
+        local_sems = sems[10]
+        near_copies = [
+            started(
+                remote(
+                    sources[item].at[:, 1 - core], near[item], near_sems, item, sibling
+                )
+            )
+            for item in range(count)
+        ]
+        gain_copies = [
+            started(
+                remote(
+                    gains_ref.at[peer[0]], gains_near.at[head], gain_sems, number, peer
+                )
+            )
+            for number, peer in enumerate(head_peers)
+        ]
+        others = []
+        for item in range(len(swapped)):
+            others += [
+                started(
+                    remote(
+                        swap_refs[item].at[peer[0]],
+                        swap_outs[item].at[head],
+                        head_sems,
+                        (item + 1) * heads + number,
+                        peer,
+                    )
+                )
+                for number, peer in enumerate(head_peers)
+            ]
+            others.append(
+                started(
+                    pltpu.make_async_copy(
+                        swap_refs[item].at[head], swap_outs[item].at[head], local_sems.at[item]
+                    )
+                )
+            )
+        chip_copies = []
+        for item in range(count):
+            near_copies[item].wait_recv()
+            sums[item][...] = (
+                sources[item][:, core].astype(jnp.float32) + near[item][...].astype(jnp.float32)
+            ).astype(jnp.bfloat16)
+            chip_copies.append(
+                [
+                    started(
+                        remote(
+                            sums[item].at[peer[1] // 2],
+                            far[item].at[chip],
+                            chip_sems,
+                            item * chips + number,
+                            peer,
+                        )
+                    )
+                    for number, peer in enumerate(chip_peers)
+                ]
+            )
+        total = gains_ref[head]
+        for number, peer in enumerate(head_peers):
+            gain_copies[number].wait_recv()
+            total = total + gains_near[lax.rem(2 * head + heads - peer[0], heads)]
+        gains_sum[...] = total
+        row_copies = [
+            started(
+                remote(gains_sum.at[peer[1]], gains_out.at[blk], row_sems, number, peer)
+            )
+            for number, peer in enumerate(blk_peers)
+        ]
+        gains_out[blk] = gains_sum[blk]
+        head_copies = []
+        for item in range(count):
+            for copy in chip_copies[item]:
+                copy.wait_recv()
+            total = sums[item][chip].astype(jnp.float32)
+            for peer in chip_peers:
+                total = total + far[item][peer[1] // 2].astype(jnp.float32)
+            if item:
+                made[item][...] = total
+                continue
+            total_ref[...] = total.astype(total_ref.dtype)
+            head_copies = [
+                started(
+                    remote(
+                        total_ref.at[peer[0]], made[0].at[head], head_sems, number, peer
+                    )
+                )
+                for number, peer in enumerate(head_peers)
+            ]
+            made[0][head] = total_ref[head]
+        for copy in head_copies + others + row_copies:
+            copy.wait()
+        for copy in near_copies + gain_copies:
+            copy.wait_send()
+        for copies in chip_copies:
+            for copy in copies:
+                copy.wait_send()
+
+    sems = [
+        pltpu.SemaphoreType.DMA((count,)),
+        pltpu.SemaphoreType.DMA((count * chips,)),
+        pltpu.SemaphoreType.DMA(((1 + len(swapped)) * heads,)),
+        pltpu.SemaphoreType.DMA((heads,)),
+        pltpu.SemaphoreType.DMA((blocks,)),
+    ]
+    results = pl.pallas_call(
+        kernel,
+        out_shape=outs,
+        in_specs=[vmem] * count + [anywhere] * len(swapped) + [vmem] + [anywhere] * len(after),
+        out_specs=out_specs,
+        scratch_shapes=[
+            *(pltpu.VMEM(half, jnp.bfloat16) for half in halves),
+            *(pltpu.VMEM(half, jnp.bfloat16) for half in halves),
+            *(pltpu.VMEM(half, jnp.bfloat16) for half in halves),
+            pltpu.VMEM(halves[0][1:], jnp.bfloat16),
+            pltpu.VMEM(gains.shape, jnp.float32),
+            pltpu.VMEM(gains.shape[1:], jnp.float32),
+            *sems,
+            *sems,
+            pltpu.SemaphoreType.DMA((max(1, len(swapped)),)),
+        ],
+        compiler_params=pltpu.CompilerParams(
+            collective_id=kernel_number("settle"),
+            has_side_effects=True,
+            vmem_limit_bytes=56 * 1024 * 1024,
+        ),
+        cost_estimate=pl.CostEstimate(flops=0, bytes_accessed=100 << 20, transcendentals=0),
+        name="settle",
+    )(*arrays, *swapped, gains, *after)
+    return results[:count], results[count:-1], results[-1]
 
 
 def head_parts(partial):
@@ -2456,8 +2623,9 @@
     def attention_set(wide, out_full):
         wide = wide.transpose(1, 0, 2, 3).reshape(width, -1)
         small = wide[:, query_columns + pair_columns :]
-        gains = small.T[gate_lanes : gate_lanes + 2].astype(jnp.float32)
-        return (wide, out_full.reshape(-1, width), small[:, :gate_lanes], gains)
+        small = small.T
+        gains = small[gate_lanes : gate_lanes + 2].astype(jnp.float32)
+        return (wide, out_full.reshape(-1, width), small[:gate_lanes], gains)
 
     wide, first_out, *next_sends = exchange(
         ("blk_pairs", first_send),
@@ -2576,7 +2744,7 @@
             normed_b = (scaled_b * gains[1:]).astype(jnp.bfloat16)
             plane_rows, incoming, gate_up = moe_in(normed_b, turned_places, None, weight_sets, 0)
         units = [gated(part) for part in gate_up]
-        logits = mm("td,de->te", plane_rows, router_full)
+        logits = mm("td,ed->te", plane_rows, router_full)
         peaks = jnp.max(jnp.where(chosen, logits, negative), axis=-1, keepdims=True)
         lifted = jnp.where(chosen, jnp.exp(logits - peaks), 0.0)
         gates_all = lifted / jnp.sum(lifted, axis=-1, keepdims=True)
@@ -2723,7 +2891,7 @@
                 grad_logits, head_index * slot_rows, slot_rows, 0
             )
             grad_normed_b = grad_normed_b + mm(
-                "te,de->td", own_logits.astype(jnp.bfloat16), router_full
+                "te,ed->td", own_logits.astype(jnp.bfloat16), router_full
             )
             grad_norm_b, grad_gain_b = norm_back(grad_normed_b, scaled_b, inverse_b, gains[1:])
             grad_middle = grad_hidden + grad_norm_b
@@ -2762,7 +2930,10 @@
             [grad_out_w, jnp.pad(grad_router, ((0, 0), (0, small_columns - gate_lanes)))], axis=1
         ).astype(jnp.bfloat16)
         alone = fused and layer_index > 0
-        if alone:
+        last = fused and not layer_index
+        if last:
+            swapped = []
+        elif alone:
             grad_out_w = lax.psum_scatter(grad_out_w, "blk", scatter_dimension=0, tiled=True)
             pending.append(grad_out_w)
             swapped = []
@@ -2796,8 +2967,6 @@
             )
             waiting = [] if layer_index else shared_terms
             grad_projected = grad_projected.reshape(all_tokens, -1)
-            if not alone:
-                grad_out_w, *others = others
             own_grad_down = others
         else:
             grad_pairs = (
@@ -2837,8 +3006,9 @@
                 after=shared_terms,
             )
             grad_normed_a = head_sum(grad_normed_a)
-        grad_out_w = grad_out_w.astype(jnp.float32)
-        if not alone:
+        if not last:
+            grad_out_w = grad_out_w.astype(jnp.float32)
+        if not alone and not last:
             grad_out_w = jnp.sum(grad_out_w, axis=0)
         if fused and layer_index:
             grad_hidden, grad_gain_a, *further = further
@@ -2862,27 +3032,38 @@
             gains_list[layer_index] = jnp.stack([grad_gain_a, grad_gain_b])
         else:
             gains_list[0] = jnp.stack([grad_gain_a, grad_gain_b])
+            lanes = 2 * DECODER_LAYERS * weight_rows // 8
             grad_gains = (
                 jnp.stack(gains_list)
                 .reshape(2 * DECODER_LAYERS, heads_count, blocks_count, weight_rows)
                 .transpose(1, 2, 0, 3)
-                .reshape(heads_count, -1)
-            )
-            grad_qkv, grad_gains, *qkv_done = exchange(
-                ("blk_swap", grad_qkv),
-                ("head_swap", grad_gains[:, None]),
-                *(
-                    ("head_swap", term.reshape(heads_count, weight_rows, -1))
-                    for term in qkv_list[1:]
-                ),
-                after=waiting,
-            )
-            grad_qkv = jnp.sum(grad_qkv.astype(jnp.float32), axis=0).astype(jnp.bfloat16)
-            grad_gains = jnp.sum(grad_gains, axis=0).reshape(blocks_count, 1, -1)
-            grad_qkv, grad_gains = exchange(
-                ("head_swap", grad_qkv.reshape(heads_count, weight_rows, -1)),
-                ("blk_swap", grad_gains),
-            )
+                .reshape(heads_count, blocks_count, 8, lanes)
+            )
+            if last:
+                (grad_qkv, grad_out_w), qkv_done, grad_gains = settle(
+                    [grad_qkv, grad_out_w.reshape(blocks_count, weight_rows, -1)],
+                    [term.reshape(heads_count, weight_rows, -1) for term in qkv_list[1:]],
+                    jnp.pad(grad_gains, ((0, 0), (0, 0), (0, 0), (0, 128 - lanes))),
+                    waiting,
+                )
+                grad_gains = grad_gains[..., :lanes]
+            else:
+                grad_gains = grad_gains.reshape(heads_count, 1, -1)
+                grad_qkv, grad_gains, *qkv_done = exchange(
+                    ("blk_swap", grad_qkv),
+                    ("head_swap", grad_gains),
+                    *(
+                        ("head_swap", term.reshape(heads_count, weight_rows, -1))
+                        for term in qkv_list[1:]
+                    ),
+                    after=waiting,
+                )
+                grad_qkv = jnp.sum(grad_qkv.astype(jnp.float32), axis=0).astype(jnp.bfloat16)
+                grad_gains = jnp.sum(grad_gains, axis=0).reshape(blocks_count, 1, -1)
+                grad_qkv, grad_gains = exchange(
+                    ("head_swap", grad_qkv.reshape(heads_count, weight_rows, -1)),
+                    ("blk_swap", grad_gains),
+                )
             qkv_list = [grad_qkv, *qkv_done]
             qkv_list = [
                 jnp.concatenate(

time: 1100 us -> 1060 us (0.964)
  Pallas kernels: 939 us -> 896 us
    pallas_call x4 -> x2, Pallas kernels: 77.4 us -> 39.4 us  [exchange(): pl.pallas_call(functools.partial(exchange_kernel, heads, blocks, plan, le...]
    pallas_call x0 -> x1, Pallas kernels: none -> 29.2 us  [settle(): pl.pallas_call(kernel, out_shape=outs, in_specs=[vmem] * count + [anywher...]
    pallas_call x2, Pallas kernels: 216 us -> 201 us  [depart(): pl.pallas_call(kernel, out_shape=[*outs, *more_outs], in_specs=[*specs, *...]
    pallas_call x2, Pallas kernels: 160 us -> 148 us  [unproject(): pl.pallas_call(kernel, out_shape=[*outs, *more_outs], in_specs=[vmem] * 5...]
  transfers between devices with their start and end apart: 12 -> 12, of which waited for: 0 -> 2; matrix products, arithmetic and copies ran while one was open for 8% -> 9% of each run, Pallas kernels for 71% -> 71%
where the time goes in v7:
time: 1060 us; the launch traced here: 1050 us
  Pallas kernels  896 us (85%)
  local copies, waits for them, and re-layouts  51.4 us (5%)
  other arithmetic  41.8 us (4%)
  matrix products  35 us (3%)
  between operations  15.8 us (1%)
    pallas_call x2, Pallas kernels, depart(): pl.pallas_call(kernel, out_shape=[*outs, *more_outs], in_specs=[*specs, *...  201 us
    pallas_call x2, Pallas kernels, enter(): pl.pallas_call(functools.partial(enter_kernel, heads, blocks, layer, len(...  184 us
    pallas_call x2, Pallas kernels, unproject(): pl.pallas_call(kernel, out_shape=[*outs, *more_outs], in_specs=[vmem] * 5...  148 us
    pallas_call x1, Pallas kernels, cross(): pl.pallas_call(kernel, out_shape=[*outs, *norm_outs, *more_outs], in_spec...  107 us
    pallas_call x1, Pallas kernels, staged_call(): pl.pallas_call(kernel, out_shape=[out for plan in plans for out in plan[4...  79 us
    pallas_call x4, Pallas kernels, attention_call(): pl.pallas_call(kernel, grid_spec=pltpu.PrefetchScalarGridSpec(num_scalar_...  53.9 us
    pallas_call x1, Pallas kernels, project(): pl.pallas_call(functools.partial(project_kernel, heads, blocks, PROJECT_P...  49.7 us
    pallas_call x2, Pallas kernels, exchange(): pl.pallas_call(functools.partial(exchange_kernel, heads, blocks, plan, le...  39.4 us
  transfers between devices with their start and end apart: 12, of which 2 were waited for; matrix products, arithmetic and copies ran while one was open for 9% of the time, Pallas kernels for 71%

profile of v7, /device:TPU:0, one launch (start us, length us, event | category | flops | bytes accessed | tf_op | source)
XLA Modules:
  0.0 1048.0 jit_solution(874584690362989113)
XLA Ops:
  10.4 2.6 slice_bitcast_fusion
  15.8 13.2 %exchange.2 = (s32[4,32,128]{2,1,0:T(8,128)}, bf16[4,48,768]{2,1,0:T(8,128)(2,1)}) custom-call(s32[32,128]{1,0:T(8,128)} %bitcast.340, bf16[4,48,768]{2,1,0:T(8,128)(2,1)} %pad_maximum_fusion.4.refs_1_), custom_call_target="tpu_custom_call" | custom-call | bytes 115343360 | tf_op jit(solution)/shard_map/exchange/pallas_call | solution.py:215
  29.8 26.2 %exchange.3 = (bf16[8,4,48,768]{3,2,1,0:T(8,128)(2,1)}, bf16[8,48,1536]{2,1,0:T(8,128)(2,1)}, bf16[4,48,768]{2,1,0:T(8,128)(2,1)}) custom-call(bf16[4,48,768]{2,1,0:T(8,128)(2,1)} %get-tuple-element.93.refs_0_, bf16[48,1536]{1,0:T(8,128)(2,1)} %get-tuple-element.198.refs_1_, bf16[4,48,768]{2,1,0:T(8,128)(2,1)} %pad_maximum_fusion.5.refs_2_), custom_call_target="tpu_custom_call" | custom-call | bytes 115343360 | tf_op jit(solution)/shard_map/exchange/pallas_call | solution.py:215
  67.1 49.7 %project.1 = (bf16[4,128,1536]{2,1,0:T(8,128)(2,1)}, bf16[2,256,384]{2,1,0:T(8,128)(2,1)}, bf16[2,4,8,64,256]{4,3,2,1,0:T(8,128)(2,1)}, bf16[8,64,1536]{2,1,0:T(8,128)(2,1)}) custom-call(bf16[128,1536]{1,0:T(8,128)(2,1)} %multiply_convert_fusion.1.own_ref, bf16[1536,768]{1,0:T(8,128)(2,1)} %bitcast.264, ...), custom_call_target="tpu_custom_call" | custom-call | bytes 136314880 | tf_op jit(solution)/shard_map/project/pallas_call | solution.py:1051
  116.9 2.4 plans.2
  122.0 9.8 attend.2
  132.8 99.0 %enter.2 = (f32[128,1536]{1,0:T(8,128)}, f32[128,1536]{1,0:T(8,128)}, f32[128,128]{1,0:T(8,128)}, bf16[4,128,1536]{2,1,0:T(8,128)(2,1)}, bf16[8,112,1536]{2,1,0:...) custom-call(bf16[512,384]{1,0:T(8,128)(2,1)} %bitcast.308, ...), custom_call_target="tpu_custom_call" | custom-call | bytes 283115520 | tf_op jit(solution)/shard_map/enter/pallas_call | solution.py:777
  232.6 2.4 plans.3
  244.3 2.2 fusion.50
  251.0 106.9 %cross.1 = (f32[128,1536]{1,0:T(8,128)}, bf16[10,112,1536]{2,1,0:T(8,128)(2,1)}, f32[128,1536]{1,0:T(8,128)}, f32[128,1536]{1,0:T(8,128)}, f32[128,128]{1,0:T(8,...) custom-call(bf16[896,512]{1,0:T(8,128)(2,1)} %fusion.6.refs_0_.refs_, ...), custom_call_target="tpu_custom_call" | custom-call | bytes 304087040 | tf_op jit(solution)/shard_map/cross/pallas_call | solution.py:1121
  358.0 9.8 attend.3
  367.8 84.8 %enter.3 = (f32[128,1536]{1,0:T(8,128)}, f32[128,1536]{1,0:T(8,128)}, f32[128,128]{1,0:T(8,128)}, bf16[4,128,1536]{2,1,0:T(8,128)(2,1)}, bf16[8,112,1536]{2,1,0:...) custom-call(bf16[512,384]{1,0:T(8,128)(2,1)} %bitcast.332, ...), custom_call_target="tpu_custom_call" | custom-call | bytes 283115520 | tf_op jit(solution)/shard_map/enter/pallas_call | solution.py:777
  459.3 79.0 %turn.1 = (f32[128,1536]{1,0:T(8,128)}, bf16[10,112,1536]{2,1,0:T(8,128)(2,1)}, bf16[4,128,1536]{2,1,0:T(8,128)(2,1)}, bf16[8,112,1536]{2,1,0:T(8,128)(2,1)}, bf...) custom-call(bf16[896,512]{1,0:T(8,128)(2,1)} %fusion.7.refs_0_.refs_7_, ...), custom_call_target="tpu_custom_call" | custom-call | bytes 272629760 | tf_op jit(solution)/shard_map/turn/pallas_call | solution.py:526
  538.3 3.8 convolution_convert_fusion.3.refs_19_
  543.5 4.5 convolution_convert_fusion.1.refs_18_
  551.1 102.7 %depart.2 = (f32[128,1536]{1,0:T(8,128)}, bf16[10,112,1536]{2,1,0:T(8,128)(2,1)}, bf16[1536,1024]{1,0:T(8,128)(2,1)}, bf16[512,1536]{1,0:T(8,128)(2,1)}, f32[4,1...) custom-call(f32[896,1024]{1,0:T(8,128)} %get-tuple-element.116.refs_, ...), custom_call_target="tpu_custom_call" | custom-call | bytes 346030080 | tf_op jit(solution)/shard_map/depart/pallas_call | solution.py:1896
  659.2 2.5 convolution_convert_fusion.7
  662.5 17.0 %attend_back.2 = (bf16[2,256,384]{2,1,0:T(8,128)(2,1)}, bf16[2,2048,256]{2,1,0:T(8,128)(2,1)}) custom-call(s32[3]{0:T(128)} %pad_add_fusion.1.info_ref, bf16[2,256,384]{2,1,0:T(8,128)(2,1)} %get-tuple-element.110.query_ref, bf16[2,2048,256]{2,1,0:T(8,128)(2,1)} %bitcast.351, bf16[2,256,384]{2,1,0:T(8,128)(2,1)} %bitcast.324), custom_call_target="tpu_custom_call" | custom-call | flops 2013265920 | bytes 8388608 | tf_op jit(solution)/shard_map/attend_back/pallas_call | solution.py:2318
  682.2 95.5 %unproject.2 = (bf16[4,128,640]{2,1,0:T(8,128)(2,1)}, f32[128,1536]{1,0:T(8,128)}, bf16[8,1,64,1536]{3,2,1,0:T(8,128)(2,1)}, f32[128,1536]{1,0:T(8,128)}, f32[1,...) custom-call(bf16[2,256,384]{2,1,0:T(8,128)(2,1)} %get-tuple-element., ...), custom_call_target="tpu_custom_call" | custom-call | bytes 335544320 | tf_op jit(solution)/shard_map/unproject/pallas_call | solution.py:1469
  777.7 2.5 bitcast_convert_fusion.1
  782.9 2.7 convolution_convert_fusion.2.refs_19_
  787.2 4.5 convolution_convert_fusion.refs_18_
  800.7 98.3 %depart.3 = (f32[128,1536]{1,0:T(8,128)}, bf16[10,112,1536]{2,1,0:T(8,128)(2,1)}, bf16[1536,1024]{1,0:T(8,128)(2,1)}, bf16[512,1536]{1,0:T(8,128)(2,1)}, f32[4,1...) custom-call(f32[896,1024]{1,0:T(8,128)} %get-tuple-element.101.refs_, ...), custom_call_target="tpu_custom_call" | custom-call | bytes 346030080 | tf_op jit(solution)/shard_map/depart/pallas_call | solution.py:1896
  899.1 2.5 convolution_convert_fusion.6
  904.1 17.3 %attend_back.3 = (bf16[2,256,384]{2,1,0:T(8,128)(2,1)}, bf16[2,2048,256]{2,1,0:T(8,128)(2,1)}) custom-call(s32[3]{0:T(128)} %pad_add_fusion.1.info_ref, bf16[2,256,384]{2,1,0:T(8,128)(2,1)} %get-tuple-element.95.query_ref, bf16[2,2048,256]{2,1,0:T(8,128)(2,1)} %bitcast.349, bf16[2,256,384]{2,1,0:T(8,128)(2,1)} %bitcast.323), custom_call_target="tpu_custom_call" | custom-call | flops 2013265920 | bytes 8388608 | tf_op jit(solution)/shard_map/attend_back/pallas_call | solution.py:2318
  923.5 52.4 %unproject.3 = (bf16[4,128,640]{2,1,0:T(8,128)(2,1)}, f32[128,1536]{1,0:T(8,128)}, bf16[8,1,64,1536]{3,2,1,0:T(8,128)(2,1)}) custom-call(bf16[2,256,384]{2,1,0:T(8,128)(2,1)} %get-tuple-element.156.refs_0_, bf16[2,4,4,2,64,256]{5,4,3,2,1,0:T(8,128)(2,1)} %bitcast.294, bf16[1536,768]{1,0:T(8,128)(2,1)} %bitcast.265, ...), custom_call_target="tpu_custom_call" | custom-call | bytes 157286400 | tf_op jit(solution)/shard_map/unproject/pallas_call | solution.py:1469
  975.9 2.5 bitcast_convert_fusion
  984.2 2.3 multiply_add_fusion
  986.5 4.8 maximum_convert_fusion.1
  991.3 2.7 reduce-scatter.15.cloned.1.call-done.refs_4_
  994.0 29.2 %settle.1 = (bf16[4,48,640]{2,1,0:T(8,128)(2,1)}, f32[48,1664]{1,0:T(8,128)}, bf16[4,48,640]{2,1,0:T(8,128)(2,1)}, f32[8,8,128]{2,1,0:T(8,128)}) custom-call(bf16[4,2,4,48,640]{4,3,2,1,0:T(8,128)(2,1)} %bitcast.271, bf16[4,2,48,1664]{3,2,1,0:T(8,128)(2,1)} %pad_maximum_fusion.refs_1_, bf16[4,48,640]{2,1,0:T(8,128)(2,1)} %bitcast.315, ...), custom_call_target="tpu_custom_call" | custom-call | bytes 104857600 | tf_op jit(solution)/shard_map/settle/pallas_call | solution.py:2059
  1032.4 8.4 maximum_convert_fusion
  (285 shorter events, 88.1 us)
Async XLA Ops:
  7.2 125.6 %all-gather.8.cloned.1.call-start = ((), (), s32[]{:S(2)}) async-start(), calls=%async_computation.6 | async-start | bytes 7077888 | tf_op jit(solution)/shard_map/all_gather | solution.py:2419
  56.0 182.2 %all-gather.18.cloned.1.call-start = ((), (), s32[]{:S(2)}) async-start(), calls=%async_computation.17 | async-start | bytes 2654208 | tf_op jit(solution)/shard_map/all_gather | solution.py:2641
  56.8 194.3 %all-gather.10.cloned.1.call-start = ((), (), s32[]{:S(2)}) async-start(), calls=%async_computation.7 | async-start | bytes 3538944 | tf_op jit(solution)/shard_map/all_gather | solution.py:2419
  57.5 310.3 %all-gather.12.cloned.1.call-start = ((), (), s32[]{:S(2)}) async-start(), calls=%async_computation.8 | async-start | bytes 1327104 | tf_op jit(solution)/shard_map/all_gather | solution.py:2642
  58.1 309.7 %all-gather.14.cloned.1.call-start = ((), (), s32[]{:S(2)}) async-start(), calls=%async_computation.9 | async-start | bytes 7077888 | tf_op jit(solution)/shard_map/all_gather | solution.py:2419
  132.8 104.3 %copy-start.33 = (bf16[2,64,1536]{2,1,0:T(8,128)(2,1)S(1)}, bf16[2,64,1536]{2,1,0:T(8,128)(2,1)}, u32[]{:S(2)}) copy-start(bf16[2,64,1536]{2,1,0:T(8,128)(2,1)} %param.21) | copy-start | bytes 1179652
  231.9 227.4 %all-gather.16.cloned.1.call-start = ((), (), s32[]{:S(2)}) async-start(), calls=%async_computation.10 | async-start | bytes 3538944 | tf_op jit(solution)/shard_map/all_gather | solution.py:2419
  232.4 447.0 %reduce-scatter.9.cloned.1.call-start = ((), (), s32[]{:S(2)}) async-start(), calls=%async_computation.12 | async-start | bytes 3538944 | tf_op jit(solution)/shard_map/reduce_scatter | solution.py:2909
  240.1 6.4 copy-start.7
  244.3 4.4 copy-start.13
  367.8 84.8 %copy-start.21 = (bf16[1536,128]{0,1:T(8,128)(2,1)S(1)}, bf16[1536,128]{0,1:T(8,128)(2,1)}, u32[]{:S(2)}) copy-start(bf16[1536,128]{0,1:T(8,128)(2,1)} %copy.244) | copy-start | bytes 1179652
  452.6 4.3 copy-start.15
  459.3 79.0 %copy-start.20 = (bf16[2,112,512]{2,1,0:T(8,128)(2,1)S(1)}, bf16[2,112,512]{2,1,0:T(8,128)(2,1)}, u32[]{:S(2)}) copy-start(bf16[2,112,512]{2,1,0:T(8,128)(2,1)} %multiply_convert_fusion.6.refs_1_) | copy-start | bytes 688132
  542.1 139.3 %reduce-scatter.7.cloned.1.call-start = ((), (), s32[]{:S(2)}) async-start(), calls=%async_computation.11 | async-start | bytes 7077888 | tf_op jit(solution)/shard_map/reduce_scatter | solution.py:2909
  548.1 249.3 %reduce-scatter.11.cloned.1.call-start = ((), (), s32[]{:S(2)}) async-start(), calls=%async_computation.13 | async-start | bytes 1437696 | tf_op jit(solution)/shard_map/reduce_scatter | solution.py:2937
  658.6 264.8 %reduce-scatter.13.cloned.1.call-start = ((), (), s32[]{:S(2)}) async-start(), calls=%async_computation.14 | async-start | bytes 2211840 | tf_op jit(solution)/shard_map/reduce_scatter | solution.py:3027
  682.2 95.5 %copy-start.51 = (bf16[4,128,1536]{2,1,0:T(8,128)(2,1)S(1)}, bf16[4,128,1536]{2,1,0:T(8,128)(2,1)}, u32[]{:S(2)}) copy-start(bf16[4,128,1536]{2,1,0:T(8,128)(2,1)} %get-tuple-element.160) | copy-start | bytes 4718596
  781.7 204.8 %reduce-scatter.17.cloned.1.call-start = ((), (), s32[]{:S(2)}) async-start(), calls=%async_computation.16 | async-start | bytes 3538944 | tf_op jit(solution)/shard_map/reduce_scatter | solution.py:2909
  785.6 208.3 %reduce-scatter.15.cloned.1.call-start = ((), (), s32[]{:S(2)}) async-start(), calls=%async_computation.15 | async-start | bytes 7077888 | tf_op jit(solution)/shard_map/reduce_scatter | solution.py:2909
  791.7 3.5 copy-start.37
  791.8 3.5 copy-start.27
  800.7 98.4 %copy-start.25 = (bf16[8,48,1536]{2,1,0:T(8,128)(2,1)S(1)}, bf16[8,48,1536]{2,1,0:T(8,128)(2,1)}, u32[]{:S(2)}) copy-start(bf16[8,48,1536]{2,1,0:T(8,128)(2,1)} %get-tuple-element.97) | copy-start | bytes 3538948
  904.1 17.3 %copy-start.45 = (f32[1,1536]{1,0:T(1,128)S(1)}, f32[1,1536]{1,0:T(1,128)}, u32[]{:S(2)}) copy-start(f32[1,1536]{1,0:T(1,128)} %get-tuple-element.168) | copy-start | bytes 18436
  904.1 17.3 %copy-start.46 = (f32[1,1536]{1,0:T(1,128)S(1)}, f32[1,1536]{1,0:T(1,128)}, u32[]{:S(2)}) copy-start(f32[1,1536]{1,0:T(1,128)} %get-tuple-element.167) | copy-start | bytes 18436
  904.1 17.4 %copy-start.32 = (bf16[384,512]{1,0:T(8,128)(2,1)S(1)}, bf16[384,512]{1,0:T(8,128)(2,1)}, u32[]{:S(2)}) copy-start(bf16[384,512]{1,0:T(8,128)(2,1)} %copy.229) | copy-start | bytes 1179652
  904.1 17.4 %copy-start.52 = (bf16[4,128,1536]{2,1,0:T(8,128)(2,1)S(1)}, bf16[4,128,1536]{2,1,0:T(8,128)(2,1)}, u32[]{:S(2)}) copy-start(bf16[4,128,1536]{2,1,0:T(8,128)(2,1)} %get-tuple-element.155) | copy-start | bytes 4718596
  923.5 52.4 %copy-start.50 = (bf16[4,128,1536]{2,1,0:T(8,128)(2,1)S(1)}, bf16[4,128,1536]{2,1,0:T(8,128)(2,1)}, u32[]{:S(2)}) copy-start(bf16[4,128,1536]{2,1,0:T(8,128)(2,1)} %get-tuple-element.163) | copy-start | bytes 4718596
  980.2 6.3 copy-start.22
  980.2 6.3 copy-start.23
  1023.2 6.0 copy-start.41
  1028.9 3.5 copy-start.16
  1028.9 3.5 copy-start.17
  (34 other events, 59.5 us)
Sparse Core Ops, SparseCore 0:
  56.1 65.3 all-gather.7
  123.4 49.6 all-gather.17
  175.1 51.8 all-gather.9
  228.6 24.1 all-gather.11
  255.2 78.1 all-gather.13
  335.2 34.8 all-gather.15
  542.3 67.7 reduce-scatter.8
  614.4 67.0 reduce-scatter.6
  684.8 47.3 reduce-scatter.10
  781.8 47.6 reduce-scatter.12
  833.5 68.2 reduce-scatter.16
  906.0 87.9 reduce-scatter.14
